TPU v7x, 512 devices: a whole 4x8x8 slice. The times are simulated.
512 devices in a mesh: dp: 32 (over z, y_hi), mp: 16 (over y_lo, x, core).
Axes of the slice: x: 4, y: 8 (y_hi: 4, y_lo: 2; y = y_hi * 2 + y_lo), z: 8, core: 2. Of those that a mesh axis runs over, the one named last changes fastest.
Arguments:
- attention: bfloat16 [4096, 8192], P('dp', 'mp'), may hold values from -6 to 6
- output_projection: bfloat16 [8192, 8192], P('mp', 'dp'), may hold values from -0.0625 to 0.0625
- residual: bfloat16 [4096, 8192], P('dp', 'mp'), may hold values from -6 to 6
- final_norm_gain: bfloat16 [8192], P('mp'), may hold values from 0.099609375 to 1.8984375
- draft_projection_weight: bfloat16 [8192, 4096], P(None, 'mp'), may hold values from -0.0625 to 0.0625
- adapter_down_weight: bfloat16 [8192, 512], P('mp', 'dp'), may hold values from -0.0625 to 0.0625
- adapter_up_weight: bfloat16 [4096, 512], P('mp', 'dp'), may hold values from -1.5 to 1.5
- token_tenant_index: int32 [4096], P('dp'), may hold values from 0 to 31, as said below
- tenant_token_count: int32 [32], replicated, may hold values from 32 to 511
Outputs:
- grad_down: float32 [8192, 512], P('mp', 'dp')
- grad_up: float32 [4096, 512], P('mp', 'dp')
Inputs may be any that keep to these rules, and one draw needn't show every extreme that they name: `token_tenant_index`: tokens come in runs of one tenant; every tenant has tokens.
All inputs are finite; a program needn't handle non-finite values.
Results may differ from a plain program's by a relative error of at most 0.03.
Values may be sent and summed in bfloat16 or wider, within the bound.
No kernel may reach another device: no remote copies, remote signals or barrier semaphores. Data moves between devices by JAX's collectives and lax.ppermute only.
A program may use at most 64 MiB of HBM per device.

v0:
```python
import jax
import jax.numpy as jnp
from jax import lax
from jax.sharding import PartitionSpec as P

MODEL_WIDTH = 8192
TENANT_COUNT = 32


EPSILON = 1e-06
ADAPTER_SCALE = 2.0
TOP_PRECISION = lax.Precision.HIGHEST


def select_tenant(values, tenant_indicator):
    spread = values.reshape(
        values.shape[0], tenant_indicator.shape[1], values.shape[1] // tenant_indicator.shape[1]
    )
    return jnp.sum(spread * tenant_indicator[:, :, None], axis=1)


def widen(values, tenant_indicator):
    return jnp.tile(values, (1, tenant_indicator.shape[1])) * jnp.repeat(
        tenant_indicator, values.shape[1], axis=1
    )


def sum_heads(partial_value):
    return lax.psum_scatter(
        partial_value.astype(jnp.bfloat16), "mp", scatter_dimension=1, tiled=True
    ).astype(jnp.float32)


def shards(
    attention,
    output_projection,
    residual,
    final_norm_gain,
    draft_projection_weight,
    adapter_down_weight,
    adapter_up_weight,
    token_tenant_index,
    tenant_token_count,
):
    row_count = attention.shape[0]
    out_block = draft_projection_weight.shape[1]
    proj_full, down_full, up_full = (
        lax.all_gather(output_projection, "dp", axis=1, tiled=True),
        lax.all_gather(adapter_down_weight, "dp", axis=1, tiled=True),
        lax.all_gather(adapter_up_weight, "dp", axis=1, tiled=True),
    )
    partial_value = jnp.dot(attention, proj_full, preferred_element_type=jnp.float32)
    projected = sum_heads(partial_value)
    hidden = residual.astype(jnp.float32) + projected
    scaled = hidden * final_norm_gain.astype(jnp.float32)[None, :]
    local_squares = jnp.sum(hidden * hidden, axis=1)
    tenant_indicator = (
        token_tenant_index[:, None] == jnp.arange(TENANT_COUNT, dtype=jnp.int32)[None, :]
    ).astype(jnp.float32)
    onehot_half = tenant_indicator.astype(jnp.bfloat16)
    down_weights = down_full.astype(jnp.float32)
    raw_low = select_tenant(
        jnp.dot(scaled, down_weights, precision=TOP_PRECISION), tenant_indicator
    )
    total_squares, summed_low = lax.psum((local_squares, raw_low), "mp")
    inv_rms = lax.rsqrt(total_squares / MODEL_WIDTH + EPSILON)
    normalized_features = scaled * inv_rms[:, None]
    low_codes = summed_low * inv_rms[:, None]
    local_features = normalized_features.astype(jnp.bfloat16)
    verifier_features = lax.all_gather(local_features, "mp", axis=1, tiled=True)
    low_rank_widened = widen(low_codes.astype(jnp.bfloat16), onehot_half)
    draft_output = jnp.dot(
        verifier_features, draft_projection_weight, preferred_element_type=jnp.float32
    )
    draft_output = draft_output + ADAPTER_SCALE * jnp.dot(
        low_rank_widened, up_full.T, preferred_element_type=jnp.float32
    )
    own_columns = lax.dynamic_slice_in_dim(
        verifier_features, lax.axis_index("mp") * out_block, out_block, 1
    )
    target = jnp.roll(own_columns, -1, axis=0).astype(jnp.float32)
    position = jnp.arange(row_count, dtype=jnp.int32)
    keep_mask = (position < row_count - 1) & (
        token_tenant_index == jnp.roll(token_tenant_index, -1)
    )
    weight = keep_mask.astype(jnp.float32) / jnp.dot(
        tenant_indicator, tenant_token_count.astype(jnp.float32), precision=TOP_PRECISION
    )
    grad_draft = (draft_output - target) * weight[:, None]
    gradient_rounded = grad_draft.astype(jnp.bfloat16)
    backward_partial = select_tenant(
        jnp.dot(gradient_rounded, up_full, preferred_element_type=jnp.float32), tenant_indicator
    )
    backward_low_rank = ADAPTER_SCALE * lax.psum(backward_partial, "mp")
    back_round = backward_low_rank.astype(jnp.bfloat16)
    grad_up = jnp.dot(gradient_rounded.T, low_rank_widened, preferred_element_type=jnp.float32)
    grad_down = jnp.dot(
        local_features.T, widen(back_round, onehot_half), preferred_element_type=jnp.float32
    )
    return (
        lax.psum_scatter(
            grad_down.astype(jnp.bfloat16), "dp", scatter_dimension=1, tiled=True
        ).astype(jnp.float32),
        lax.psum_scatter(
            grad_up.astype(jnp.bfloat16), "dp", scatter_dimension=1, tiled=True
        ).astype(jnp.float32),
    )


def solution(mesh):
    return jax.shard_map(
        shards,
        mesh=mesh,
        in_specs=(
            P("dp", "mp"),
            P("mp", "dp"),
            P("dp", "mp"),
            P("mp"),
            P(None, "mp"),
            P("mp", "dp"),
            P("mp", "dp"),
            P("dp"),
            P(),
        ),
        out_specs=(P("mp", "dp"), P("mp", "dp")),
        check_vma=False,
    )
```

profile of v0, /device:TPU:6, one launch (start us, length us, event | category | flops | bytes accessed | tf_op | source)
XLA Modules:
  0.0 815.2 jit_solution(10472356086609491391)
XLA Ops:
  7.2 0.0 copy-start
  7.2 0.0 all-gather.3.cloned.1.call-start
  7.2 0.7 all-gather.3.cloned.1.call-update
  7.9 0.0 copy-start.5
  7.9 0.0 copy-start.6
  7.9 0.0 copy-start.3
  7.9 0.0 copy-start.2
  8.0 0.0 reduce-scatter.4.cloned.1.call-start
  8.0 139.2 %all-gather.3.cloned.1.call-done = bf16[512,8192]{1,0:T(8,128)(2,1)} async-done(((bf16[512,256]{1,0:T(8,128)(2,1)}), bf16[512,8192]{1,0:T(8,128)(2,1)}) %all-gather.3.cloned.1.call-update) | async-done | bytes 8388624 | tf_op jit(solution)/shard_map/all_gather | solution.py:48
  147.2 0.0 copy-done
  147.2 6.0 convolution_convert_fusion
  153.2 0.0 copy-start.4
  153.2 0.0 copy-start.7
  153.2 0.0 reduce-scatter.4.cloned.1.call-update
  153.2 0.0 all-gather.5.cloned.1.call-start
  153.3 0.0 copy-done.5
  153.3 0.0 copy-done.6
  153.3 0.0 copy-done.3
  153.3 89.3 %all_gather.14 = bf16[512,512]{0,1:T(8,128)(2,1)S(1)} all-gather(bf16[512,16]{0,1:T(8,128)(2,1)S(1)} %copy-done.3), channel_id=1, replica_groups=mesh['dp'=32,'mp'=16] {'dp'}, dimensions={1}, use_global_device_ids=true | all-gather | bytes 540672 | tf_op jit(solution)/shard_map/all_gather | solution.py:49
  242.6 0.0 reduce-scatter.4.cloned.1.call-done
  242.6 0.0 copy-done.2
  242.6 1.5 fusion.6
  244.1 0.1 multiply_reduce_fusion.1
  244.2 1.0 multiply_reduce_fusion.2
  245.2 28.9 %all-reduce = (f32[128]{0:T(128)S(1)}, f32[128,16]{0,1:T(8,128)S(1)}) all-reduce(f32[128]{0:T(128)S(1)} %multiply_reduce_fusion.2, f32[128,16]{0,1:T(8,128)S(1)} %multiply_reduce_fusion.1), channel_id=1, replica_groups=mesh['dp'=32,'mp'=16] {'mp'}, use_global_device_ids=true, to_apply=%region_2.0 | all-reduce | flops 2176 | bytes 17408 | tf_op jit(solution)/shard_map/psum | solution.py:65
  274.1 1.7 multiply_convert_fusion
  275.8 0.0 all-gather.5.cloned.1.call-update
  275.8 0.0 reduce-scatter.8.cloned.1.call-start
  275.8 0.1 slice.18
  275.9 0.0 copy-done.4
  275.9 77.3 %all_gather.15 = bf16[256,512]{0,1:T(8,128)(2,1)S(1)} all-gather(bf16[256,16]{0,1:T(8,128)(2,1)S(1)} %copy-done.4), channel_id=1, replica_groups=mesh['dp'=32,'mp'=16] {'dp'}, dimensions={1}, use_global_device_ids=true | all-gather | bytes 270336 | tf_op jit(solution)/shard_map/all_gather | solution.py:50
  353.2 0.0 copy-done.7
  353.2 0.2 fusion.4
  353.4 0.0 all-gather.5.cloned.1.call-done
  353.5 0.7 constant_dynamic-slice_fusion
  354.1 0.9 dynamic-slice
  355.1 0.0 copy-start.1
  355.1 3.6 fusion.12
  358.7 0.2 fusion.3
  358.9 0.9 convolution_convert_fusion.2
  359.8 0.2 fusion.13
  360.0 0.0 reduce-scatter.8.cloned.1.call-update
  360.1 0.0 reduce-scatter.6.cloned.1.call-start
  360.2 27.2 %psum.23 = f32[128,16]{0,1:T(8,128)S(1)} all-reduce(f32[128,16]{0,1:T(8,128)S(1)} %multiply_reduce_fusion), channel_id=1, replica_groups=mesh['dp'=32,'mp'=16] {'mp'}, use_global_device_ids=true, to_apply=%region_6.7 | all-reduce | flops 2048 | bytes 16384 | tf_op jit(solution)/shard_map/psum | solution.py:94
  387.4 0.0 copy-done.1
  387.4 1.1 convolution_convert_fusion.1
  388.5 0.0 reduce-scatter.6.cloned.1.call-update
  388.5 193.4 %reduce-scatter.8.cloned.1.call-done = bf16[256,16]{0,1:T(8,128)(2,1)} async-done(((bf16[256,512]{0,1:T(8,128)(2,1)}), bf16[256,16]{0,1:T(8,128)(2,1)}) %reduce-scatter.8.cloned.1.call-update) | async-done | bytes 8208 | tf_op jit(solution)/shard_map/reduce_scatter | solution.py:104
  581.9 1.3 convert_element_type.72
  583.2 224.2 %reduce-scatter.6.cloned.1.call-done = bf16[512,16]{0,1:T(8,128)(2,1)} async-done(((bf16[512,512]{0,1:T(8,128)(2,1)}), bf16[512,16]{0,1:T(8,128)(2,1)}) %reduce-scatter.6.cloned.1.call-update) | async-done | bytes 16400 | tf_op jit(solution)/shard_map/reduce_scatter | solution.py:101
  807.4 1.3 convert_element_type.70
  (8 shorter events, 0.1 us)
Async XLA Ops:
  7.2 140.0 %copy-start = (bf16[128,512]{1,0:T(8,128)(2,1)S(1)}, bf16[128,512]{1,0:T(8,128)(2,1)}, u32[]{:S(2)}) copy-start(bf16[128,512]{1,0:T(8,128)(2,1)} %param.9) | copy-start | bytes 393220
  7.2 140.0 %all-gather.3.cloned.1.call-start = ((), (), s32[]{:S(2)}) async-start(), calls=%async_computation.3 | async-start | bytes 8650752 | tf_op jit(solution)/shard_map/all_gather | solution.py:48
  7.9 145.4 %copy-start.5 = (bf16[512]{0:T(512)(128)(2,1)S(1)}, bf16[512]{0:T(512)(128)(2,1)}, u32[]{:S(2)}) copy-start(bf16[512]{0:T(512)(128)(2,1)} %param.12) | copy-start | bytes 3076
  7.9 145.4 %copy-start.6 = (s32[128]{0:T(128)S(1)}, s32[128]{0:T(128)}, u32[]{:S(2)}) copy-start(s32[128]{0:T(128)} %param.16) | copy-start | bytes 1540
  7.9 145.4 %copy-start.3 = (bf16[512,16]{0,1:T(8,128)(2,1)S(1)}, bf16[512,16]{0,1:T(8,128)(2,1)}, u32[]{:S(2)}) copy-start(bf16[512,16]{0,1:T(8,128)(2,1)} %param.14) | copy-start | bytes 49156
  7.9 234.7 %copy-start.2 = (bf16[128,512]{1,0:T(8,128)(2,1)S(1)}, bf16[128,512]{1,0:T(8,128)(2,1)}, u32[]{:S(2)}) copy-start(bf16[128,512]{1,0:T(8,128)(2,1)} %param.11) | copy-start | bytes 393220
  8.0 234.6 %reduce-scatter.4.cloned.1.call-start = ((), (), s32[]{:S(2)}) async-start(), calls=%async_computation.4 | async-start | bytes 2228224 | tf_op jit(solution)/shard_map/reduce_scatter | solution.py:29
  153.2 122.7 %copy-start.4 = (bf16[256,16]{0,1:T(8,128)(2,1)S(1)}, bf16[256,16]{0,1:T(8,128)(2,1)}, u32[]{:S(2)}) copy-start(bf16[256,16]{0,1:T(8,128)(2,1)} %param.15) | copy-start | bytes 24580
  153.2 200.0 %copy-start.7 = (s32[32]{0:T(128)S(1)}, s32[32]{0:T(128)}, u32[]{:S(2)}) copy-start(s32[32]{0:T(128)} %param.17) | copy-start | bytes 388
  153.2 200.2 %all-gather.5.cloned.1.call-start = ((), (), s32[]{:S(2)}) async-start(), calls=%async_computation.5 | async-start | bytes 2228224 | tf_op jit(solution)/shard_map/all_gather | solution.py:70
  275.8 306.1 %reduce-scatter.8.cloned.1.call-start = ((), (), s32[]{:S(2)}) async-start(), calls=%async_computation.7 | async-start | bytes 270336 | tf_op jit(solution)/shard_map/reduce_scatter | solution.py:104
  355.1 32.4 %copy-start.1 = (bf16[128,512]{1,0:T(8,128)(2,1)S(1)}, bf16[128,512]{1,0:T(8,128)(2,1)}, u32[]{:S(2)}) copy-start(bf16[128,512]{1,0:T(8,128)(2,1)} %multiply_convert_fusion) | copy-start | bytes 393220
  360.1 447.3 %reduce-scatter.6.cloned.1.call-start = ((), (), s32[]{:S(2)}) async-start(), calls=%async_computation.6 | async-start | bytes 540672 | tf_op jit(solution)/shard_map/reduce_scatter | solution.py:101
Sparse Core Ops, SparseCore 0:
  11.1 136.0 all-gather.2
  153.3 74.1 reduce-scatter.3
  275.9 34.6 all-gather.4
  360.2 221.6 reduce-scatter.7
  586.7 220.5 reduce-scatter.5
where the time goes:
time: 816 us; the launch traced here: 815 us
  waiting for transfers between devices  557 us (68%)
  blocking collectives  223 us (27%)
  between operations  14 us (2%)
  matrix products  13.7 us (2%)
    reduce_scatter x1, waiting for transfers between devices, shards(): lax.psum_scatter(grad_down.astype(jnp.bfloat16), 'dp', scatter_dimension=...  224 us
    reduce_scatter x1, waiting for transfers between devices, shards(): lax.psum_scatter(grad_up.astype(jnp.bfloat16), 'dp', scatter_dimension=1,...  193 us
    all_gather x1, waiting for transfers between devices, shards(): lax.all_gather(output_projection, 'dp', axis=1, tiled=True)  139 us
    all_gather x1, blocking collectives, shards(): lax.all_gather(adapter_down_weight, 'dp', axis=1, tiled=True)  89.3 us
    all_gather x1, blocking collectives, shards(): lax.all_gather(adapter_up_weight, 'dp', axis=1, tiled=True)  77.3 us
    psum x1, blocking collectives, shards(): total_squares, summed_low = lax.psum((local_squares, raw_low), 'mp')  28.9 us
    psum x1, blocking collectives, shards(): backward_low_rank = ADAPTER_SCALE * lax.psum(backward_partial, 'mp')  27.2 us
  transfers between devices with their start and end apart: 5, of which 3 were waited for; matrix products, arithmetic and copies ran while one was open for 0% of the time, Pallas kernels for 0%

commit v1 on v0

v1 whole, which is shorter than its diff:
```python
import jax
import jax.numpy as jnp
from jax import lax
from jax.sharding import Mesh
from jax.sharding import PartitionSpec as P

EPSILON = 1e-06
ADAPTER_SCALE = 2.0
BF = jnp.bfloat16
F32 = jnp.float32

AXES = ("z", "yh", "yl", "x", "c")
SIZES = (8, 4, 2, 4, 2)
DP = ("z", "yh")
MP = ("yl", "x", "c")
CHIPS = ("yl", "x")


def dot(subscripts, left, right):
    return jnp.einsum(subscripts, left, right, preferred_element_type=F32)


def swap(value):
    return lax.ppermute(value, "c", [(0, 1), (1, 0)])


def exchange(value, axis):
    return lax.all_to_all(value, axis, 0, 0)


def gather(value, axis, size):
    return exchange(jnp.broadcast_to(value[None], (size,) + value.shape), axis)


def split(value):
    high = value.astype(BF)
    return high, (value - high.astype(F32)).astype(BF)


def half(value, which, length, axis=0):
    return lax.dynamic_slice_in_dim(value, which * length, length, axis)


def shards(attention, output_projection, residual, gain, draft_weight, down, up, tenant_of, tenant_count):
    n_z, n_yh, n_yl, n_x, _ = SIZES
    n_chips = n_yl * n_x
    tenants = tenant_count.shape[0]
    rank = down.shape[1]
    tokens, block = residual.shape
    cols = output_projection.shape[1]
    out_block = draft_weight.shape[1]
    width = block * 2 * n_chips
    mine = tokens // 2
    core = lax.axis_index("c")
    chip = lax.axis_index(CHIPS)
    other = 1 - core
    first = core == 0

    def ordered(own, others):
        return jnp.where(first, own, others), jnp.where(first, others, own)

    proj = lax.all_gather(output_projection, "z", axis=0)
    draft_weight_other = swap(draft_weight)
    pad = jnp.broadcast_to(gain[None], (16, block))
    kept = swap(jnp.concatenate([half(residual, other, mine), pad], axis=0))
    residual_parts = ordered(half(residual, core, mine), kept[:mine])
    gain_parts = ordered(gain[None], kept[mine : mine + 1])

    adapters = jnp.concatenate([down.T, up.T], axis=1)
    adapters = gather(adapters, "z", n_z).reshape(n_z * rank, block + out_block)
    joined = gather(jnp.concatenate([attention, adapters], axis=1), "yh", n_yh)
    attention_all = joined[:, :, :block]
    adapters_all = joined[:, :, block:].reshape(tenants * rank, block + out_block)
    adapters_other = swap(adapters_all)
    down_parts = ordered(adapters_all[:, :block], adapters_other[:, :block])
    up_own, up_other = adapters_all[:, block:], adapters_other[:, block:]

    rows = n_yh * mine
    send = half(attention_all, other, mine, 1).reshape(rows, block)
    keep = half(attention_all, core, mine, 1).reshape(rows, block)
    sent = swap(dot("tk,zkn->ztn", send, proj).astype(BF))
    pair = (dot("tk,zkn->ztn", keep, proj) + sent.astype(F32)).astype(BF)
    summed = jnp.sum(exchange(pair, CHIPS).astype(F32), axis=0).astype(BF)
    projected = exchange(summed.reshape(n_yh, mine, cols), "yh")

    half_yh = n_yh // 2
    scaled, squares = [], 0.0
    for part in range(2):
        piece = jnp.concatenate(
            [projected[half_yh * part + j] for j in range(half_yh)], axis=1
        ).astype(F32)
        hidden = residual_parts[part].astype(F32) + piece
        squares = squares + jnp.sum(hidden * hidden, axis=1, keepdims=True)
        scaled.append((hidden * gain_parts[part].astype(F32)).astype(BF))
    own_scaled = jnp.where(first, scaled[0], scaled[1])
    partner_scaled = swap(jnp.where(first, scaled[1], scaled[0]))

    slot = jnp.arange(tenants * rank, dtype=jnp.int32) // rank
    slot_tenant = (slot % n_z) * n_yh + slot // n_z
    own_tenant = half(tenant_of, core, mine)
    partner_tenant = half(tenant_of, other, mine)
    own_mask = slot_tenant[:, None] == own_tenant[None, :]
    partner_mask = slot_tenant[:, None] == partner_tenant[None, :]

    def select(values):
        chosen = jnp.where(own_mask, values, 0.0)
        return jnp.sum(chosen.reshape(tenants, rank, mine), axis=0)

    def widen(values, mask):
        return jnp.where(mask, jnp.tile(values, (tenants, 1)), BF(0))

    low_part = select(dot("jd,td->jt", down_parts[0], scaled[0]) + dot("jd,td->jt", down_parts[1], scaled[1]))
    extras = jnp.concatenate(split(low_part), axis=0).T
    message = jnp.concatenate(
        scaled + [extras, *split(squares), jnp.zeros((mine, 128 - 2 * rank - 2), BF)], axis=1
    )
    received = gather(message, CHIPS, n_chips)
    features = received[:, :, : 2 * block]
    totals = jnp.sum(received[:, :, 2 * block :].astype(F32), axis=0)
    square_column = totals[:, 2 * rank : 2 * rank + 1] + totals[:, 2 * rank + 1 : 2 * rank + 2]
    inv_column = lax.rsqrt(square_column / width + EPSILON)
    totals = totals.T
    inv_row = lax.rsqrt((totals[2 * rank : 2 * rank + 1] + totals[2 * rank + 1 : 2 * rank + 2]) / width + EPSILON)
    low_round = ((totals[:rank] + totals[rank : 2 * rank]) * inv_row).astype(BF)
    low_wide = widen(low_round, own_mask)

    target = lax.dynamic_slice(
        features, (chip // 2, 0, (chip % 2) * 2 * out_block), (1, mine, 2 * out_block)
    )[0]
    target = (target.astype(F32) * inv_column).astype(BF)
    next_row = swap(target[:16])[:1]
    target = jnp.concatenate([target[1:], next_row], axis=0)
    target_own = half(target, core, out_block, 1).astype(F32)
    target_other = half(target, other, out_block, 1).astype(F32)

    following = jnp.roll(tenant_of, -1)
    position = jnp.arange(tokens, dtype=jnp.int32)
    keep_mask = (position < tokens - 1) & (tenant_of == following)
    is_tenant = tenant_of[:, None] == jnp.arange(tenants, dtype=jnp.int32)[None, :]
    count = jnp.sum(jnp.where(is_tenant, tenant_count.astype(F32)[None, :], 0.0), axis=1)
    weight = half(keep_mask.astype(F32) / count, core, mine)[:, None]

    def draft(weights, ups):
        shaped = weights.reshape(n_chips, 2 * block, out_block)
        return dot("ktd,kdn->tn", features, shaped) * inv_column + ADAPTER_SCALE * dot("jt,jn->tn", low_wide, ups)

    grad_other = ((draft(draft_weight_other, up_other) - target_other) * weight).astype(BF)
    low_lanes = jnp.concatenate([low_round.T, jnp.zeros((mine, 128 - rank), BF)], axis=1)
    partner = swap(jnp.concatenate([grad_other, low_lanes], axis=1))
    grad_own = ((draft(draft_weight, up_own) - target_own) * weight).astype(BF)

    back_part = select(dot("jc,tc->jt", up_own, grad_own) + dot("jc,tc->jt", up_other, grad_other))
    back = jnp.sum(gather(back_part, CHIPS, n_chips), axis=0)
    back_scaled = (ADAPTER_SCALE * back * inv_row).astype(BF)
    back_partner = swap(back_scaled)

    grad_up = dot("jt,tc->jc", low_wide, grad_own) + dot(
        "jt,tc->jc", widen(partner[:, out_block : out_block + rank].T, partner_mask), partner[:, :out_block]
    )
    grad_down = dot("jt,td->jd", widen(back_scaled, own_mask), own_scaled) + dot(
        "jt,td->jd", widen(back_partner, partner_mask), partner_scaled
    )
    grads = jnp.concatenate([grad_down.astype(BF), grad_up.astype(BF)], axis=1)
    grads = exchange(grads.reshape(n_yh, n_z * rank, block + out_block), "yh")
    grads = jnp.sum(grads.astype(F32), axis=0).astype(BF)
    grads = exchange(grads.reshape(n_z, rank, block + out_block), "z")
    grads = jnp.sum(grads.astype(F32), axis=0)
    return grads[:, :block].T, grads[:, block:].T


def solution(mesh):
    split_mesh = Mesh(mesh.devices.reshape(SIZES), AXES)
    return jax.shard_map(
        shards,
        mesh=split_mesh,
        in_specs=(
            P(DP, MP),
            P(MP, DP),
            P(DP, MP),
            P(MP),
            P(None, MP),
            P(MP, DP),
            P(MP, DP),
            P(DP),
            P(),
        ),
        out_specs=(P(MP, DP), P(MP, DP)),
        check_vma=False,
    )
```

time: 816 us -> 209 us (0.26)
  waiting for transfers between devices: 557 us -> 64.1 us
  blocking collectives: 223 us -> 59.5 us
  starting transfers between devices: 0.2 us -> 43.7 us
    reduce_scatter x3 -> x0, waiting for transfers between devices: 418 us -> none  [the longest x1 224 us: shards(): lax.psum_scatter(grad_down.astype(jnp.bfloat16), 'dp', scatter_dimension=...]
    all_gather x2 -> x0, blocking collectives: 167 us -> none  [the longest x1 89.3 us: shards(): lax.all_gather(adapter_down_weight, 'dp', axis=1, tiled=True)]
    all_gather x2 -> x1, waiting for transfers between devices: 139 us -> 0.02 us  [shards(): proj = lax.all_gather(output_projection, 'z', axis=0)]
    all_to_all x0 -> x3, blocking collectives: none -> 59.5 us  [exchange(): return lax.all_to_all(value, axis, 0, 0)]
    all_to_all x0 -> x5, waiting for transfers between devices: none -> 59.5 us  [exchange(): return lax.all_to_all(value, axis, 0, 0)]
    psum x2 -> x0, blocking collectives: 56.1 us -> none  [the longest x1 28.9 us: shards(): total_squares, summed_low = lax.psum((local_squares, raw_low), 'mp')]
    all_to_all x0 -> x5, starting transfers between devices: none -> 27.6 us  [exchange(): return lax.all_to_all(value, axis, 0, 0)]
    ppermute x0 -> x8, starting transfers between devices: none -> 16 us  [swap(): return lax.ppermute(value, 'c', [(0, 1), (1, 0)])]
  transfers between devices with their start and end apart: 5 -> 14, of which waited for: 3 -> 8; matrix products, arithmetic and copies ran while one was open for 0% -> 8% of each run, Pallas kernels for 0% -> 0%
where the time goes in v1:
time: 209 us; the launch traced here: 206 us
  waiting for transfers between devices  64.1 us (31%)
  blocking collectives  59.5 us (28%)
  starting transfers between devices  43.7 us (21%)
  between operations  14.5 us (7%)
  matrix products  12.9 us (6%)
  local copies, waits for them, and re-layouts  6.95 us (3%)
  other arithmetic  4.77 us (2%)
    all_to_all x3, blocking collectives, exchange(): return lax.all_to_all(value, axis, 0, 0)  59.5 us
    all_to_all x5, waiting for transfers between devices, exchange(): return lax.all_to_all(value, axis, 0, 0)  59.5 us
    all_to_all x5, starting transfers between devices, exchange(): return lax.all_to_all(value, axis, 0, 0)  27.6 us
    ppermute x8, starting transfers between devices, swap(): return lax.ppermute(value, 'c', [(0, 1), (1, 0)])  16 us
    dot_general x14, matrix products, dot(): return jnp.einsum(subscripts, left, right, preferred_element_type=F32)  12.9 us
  transfers between devices with their start and end apart: 14, of which 8 were waited for; matrix products, arithmetic and copies ran while one was open for 8% of the time, Pallas kernels for 0%

profile of v1, /device:TPU:6, one launch (start us, length us, event | category | flops | bytes accessed | tf_op | source)
XLA Modules:
  0.0 206.5 jit_solution(1936641960519563535)
XLA Ops:
  7.2 0.7 all-gather.3.cloned.1.call-update
  7.9 0.7 pad_maximum_fusion.4
  8.7 20.6 %all_to_all.40 = bf16[8,16,768]{2,1,0:T(8,128)(2,1)S(1)} all-to-all(bf16[8,16,768]{2,1,0:T(8,128)(2,1)S(1)} %broadcast_in_dim.40), channel_id=1, replica_groups=mesh['z'=8,'yh'=4,'yl'=2,'x'=4,'c'=2] {'z'}, dimensions={0} | all-to-all | bytes 393216 | tf_op jit(solution)/shard_map/all_to_all | solution.py:28
  29.2 0.9 pad_maximum_fusion
  30.2 1.1 broadcast_in_dim.41
  31.3 7.1 %all-to-all-start.1 = ((bf16[4,128,1280]{2,1,0:T(8,128)(2,1)}), bf16[4,128,1280]{2,1,0:T(8,128)(2,1)S(1)}, u32[]{:S(2)}, u32[]{:S(2)}) async-start(bf16[4,128,1280]{2,1,0:T(8,128)(2,1)} %broadcast_in_dim.41), calls=%async_computation.1 | async-start | bytes 2621440 | tf_op jit(solution)/shard_map/all_to_all | solution.py:28
  38.4 29.4 %all-to-all-done.1 = bf16[4,128,1280]{2,1,0:T(8,128)(2,1)S(1)} async-done(((bf16[4,128,1280]{2,1,0:T(8,128)(2,1)}), bf16[4,128,1280]{2,1,0:T(8,128)(2,1)S(1)}, u32[]{:S(2)}, u32[]{:S(2)}) %all-to-all-start.1) | async-done | bytes 1310752 | tf_op jit(solution)/shard_map/all_to_all | solution.py:28
  67.9 2.4 %fusion.1 = bf16[8,256,256]{2,1,0:T(8,128)(2,1)S(1)} fusion(bf16[256,512,1]{1,0,2:T(8,128)(2,1)S(1)} %bitcast.110, bf16[8,512,256]{2,1,0:T(8,128)(2,1)} %bitcast.96), kind=kOutput, calls=%fused_computation.3 | convolution fusion | flops 537395200 | bytes 3407872 | tf_op jit(solution)/shard_map/tk,zkn->ztn/dot_general | solution.py:20
  70.4 1.9 collective-permute-start.1
  72.3 2.6 %collective-permute-done.1 = bf16[8,256,256]{2,1,0:T(8,128)(2,1)S(1)} collective-permute-done((bf16[8,256,256]{2,1,0:T(8,128)(2,1)S(1)}, bf16[8,256,256]{2,1,0:T(8,128)(2,1)S(1)}, u32[]{:S(2)}, u32[]{:S(2)}) %collective-permute-start.1) | collective-permute-done | bytes 1048608 | tf_op jit(solution)/shard_map/ppermute | solution.py:24
  75.0 1.7 fusion
  76.7 4.9 %all-to-all-start.2 = ((bf16[8,256,256]{2,1,0:T(8,128)(2,1)}), bf16[8,256,256]{2,1,0:T(8,128)(2,1)S(1)}, u32[]{:S(2)}, u32[]{:S(2)}) async-start(bf16[8,256,256]{2,1,0:T(8,128)(2,1)} %fusion), calls=%async_computation.2 | async-start | bytes 2097152 | tf_op jit(solution)/shard_map/all_to_all | solution.py:28
  81.6 1.9 collective-permute-start
  83.7 11.3 %all-to-all-done.2 = bf16[8,256,256]{2,1,0:T(8,128)(2,1)S(1)} async-done(((bf16[8,256,256]{2,1,0:T(8,128)(2,1)}), bf16[8,256,256]{2,1,0:T(8,128)(2,1)S(1)}, u32[]{:S(2)}, u32[]{:S(2)}) %all-to-all-start.2) | async-done | bytes 1048608 | tf_op jit(solution)/shard_map/all_to_all | solution.py:28
  95.0 0.8 reduce_sum.96
  95.8 5.0 %all-to-all-start.3 = ((bf16[4,64,256]{2,1,0:T(8,128)(2,1)}), bf16[4,64,256]{2,1,0:T(8,128)(2,1)S(1)}, u32[]{:S(2)}, u32[]{:S(2)}) async-start(bf16[4,64,256]{2,1,0:T(8,128)(2,1)} %bitcast.11), calls=%async_computation.3 | async-start | bytes 262144 | tf_op jit(solution)/shard_map/all_to_all | solution.py:28
  100.8 1.9 collective-permute-start.2
  102.8 7.1 %all-to-all-done.3 = bf16[4,64,256]{2,1,0:T(8,128)(2,1)S(1)} async-done(((bf16[4,64,256]{2,1,0:T(8,128)(2,1)}), bf16[4,64,256]{2,1,0:T(8,128)(2,1)S(1)}, u32[]{:S(2)}, u32[]{:S(2)}) %all-to-all-start.3) | async-done | bytes 131104 | tf_op jit(solution)/shard_map/all_to_all | solution.py:28
  109.9 0.2 multiply_reduce_fusion
  110.0 0.1 copy.52
  110.1 0.1 copy.53
  110.3 0.3 fusion.13
  110.6 0.3 fusion.4
  110.9 0.1 copy.50
  111.2 0.1 concatenate.40
  111.3 1.2 broadcast_in_dim.79
  112.5 5.4 %all-to-all-start.4 = ((bf16[8,64,1152]{2,1,0:T(8,128)(2,1)}), bf16[8,64,1152]{2,1,0:T(8,128)(2,1)S(1)}, u32[]{:S(2)}, u32[]{:S(2)}) async-start(bf16[8,64,1152]{2,1,0:T(8,128)(2,1)} %broadcast_in_dim.79), calls=%async_computation.4 | async-start | bytes 2359296 | tf_op jit(solution)/shard_map/all_to_all | solution.py:28
  117.9 1.9 collective-permute-start.4
  120.0 0.1 fusion.65
  120.2 2.4 %collective-permute-start.6 = (bf16[64,512]{1,0:T(8,128)(2,1)S(1)}, bf16[64,512]{1,0:T(8,128)(2,1)S(1)}, u32[]{:S(2)}, u32[]{:S(2)}) collective-permute-start(bf16[64,512]{1,0:T(8,128)(2,1)S(1)} %get-tuple-element.4), channel_id=1, source_target_pairs={{0,1},{1,0},{2,3},{3,2},{4,5},{5,4},{6,7},{7,6},{8,9},{9,8},{10,11... | collective-permute-start | bytes 196616 | tf_op jit(solution)/shard_map/ppermute | solution.py:24
  122.6 8.1 %all-to-all-done.4 = bf16[8,64,1152]{2,1,0:T(8,128)(2,1)S(1)} async-done(((bf16[8,64,1152]{2,1,0:T(8,128)(2,1)}), bf16[8,64,1152]{2,1,0:T(8,128)(2,1)S(1)}, u32[]{:S(2)}, u32[]{:S(2)}) %all-to-all-start.4) | async-done | bytes 1179680 | tf_op jit(solution)/shard_map/all_to_all | solution.py:28
  130.7 0.2 fusion.43
  131.1 0.1 copy.55
  131.2 0.1 slice.129
  131.4 0.2 fusion.49
  131.7 1.9 collective-permute-start.3
  133.7 0.2 convolution_multiply_fusion.1
  133.9 0.2 convolution_multiply_fusion
  134.2 0.6 collective-permute-done.3
  134.8 3.0 %multiply_convert_fusion.2 = bf16[64,256]{1,0:T(8,128)(2,1)S(1)} fusion(s32[]{:T(128)S(6)} %select_n.154, bf16[63,512]{1,0:T(8,128)(2,1)S(1)} %slice.137, bf16[1,512]{1,0:T(2,128)(2,1)S(1)} %slice.139, f32[64]{0:T(128)S(1)} %dynamic_slice.37, f32[64,256]{1,0:T(8,128)S(1)} %convolution_multiply_fusion.1, f32[64]{0:T(128)S(1)} %fusion.49, ...), kind=kOutput, calls=%fused_computation.61 | convolution fusion | flops 268582912 | bytes 5409796 | tf_op jit(solution)/shard_map/ktd,kdn->tn/dot_general | solution.py:20
  137.8 0.2 fusion.24
  138.0 0.3 fusion.70
  138.3 3.0 %fusion.12 = bf16[64,256]{1,0:T(8,128)(2,1)S(1)} fusion(f32[64,256]{1,0:T(8,128)S(1)} %convolution_multiply_fusion, bf16[8,1024,256]{2,1,0:T(8,128)(2,1)} %bitcast.26, s32[]{:T(128)S(6)} %select_n.156, bf16[63,512]{1,0:T(8,128)(2,1)S(1)} %slice.137, bf16[1,512]{1,0:T(2,128)(2,1)S(1)} %slice.139, f32[64]{0:T(128)S(1)} %dynamic_slice.37, f32[64]{0:T(128)S(1)} %fusion.49, ...), kind=kOutput, calls=%fused_computation.22 | convolution fusion | flops 268582912 | bytes 5409796 | tf_op jit(solution)/shard_map/ktd,kdn->tn/dot_general | solution.py:20
  141.4 2.1 %collective-permute-start.7 = (bf16[64,384]{1,0:T(8,128)(2,1)S(1)}, bf16[64,384]{1,0:T(8,128)(2,1)S(1)}, u32[]{:S(2)}, u32[]{:S(2)}) collective-permute-start(bf16[64,384]{1,0:T(8,128)(2,1)S(1)} %maximum_maximum_fusion), channel_id=1, source_target_pairs={{0,1},{1,0},{2,3},{3,2},{4,5},{5,4},{6,7},{7,6},{8,9},{9,8},{10,11... | collective-permute-start | bytes 147464 | tf_op jit(solution)/shard_map/ppermute | solution.py:24
  143.5 0.2 fusion.5
  143.7 0.1 copy.56
  143.9 0.7 reshape.179
  144.6 5.3 %all-to-all-start.5 = ((f32[8,1,1024]{2,1,0:T(1,128)}), f32[8,1,1024]{2,1,0:T(1,128)S(1)}, u32[]{:S(2)}, u32[]{:S(2)}) async-start(f32[8,1,1024]{2,1,0:T(1,128)} %reshape.179), calls=%async_computation.5 | async-start | bytes 65536 | tf_op jit(solution)/shard_map/all_to_all | solution.py:28
  150.1 0.3 fusion.3
  150.3 3.7 %all-to-all-done.5 = f32[8,1,1024]{2,1,0:T(1,128)S(1)} async-done(((f32[8,1,1024]{2,1,0:T(1,128)}), f32[8,1,1024]{2,1,0:T(1,128)S(1)}, u32[]{:S(2)}, u32[]{:S(2)}) %all-to-all-start.5) | async-done | bytes 32800 | tf_op jit(solution)/shard_map/all_to_all | solution.py:28
  154.0 0.5 broadcast.138
  154.5 0.7 reduce.6
  155.4 1.9 collective-permute-start.5
  157.3 0.1 copy.57
  157.4 0.4 fusion.28
  157.8 0.6 collective-permute-done.5
  158.6 0.4 fusion.2
  158.9 0.1 copy_bitcast_fusion
  159.1 26.0 %all_to_all.41 = bf16[4,128,768]{1,2,0:T(8,128)(2,1)S(1)} all-to-all(bf16[4,128,768]{1,2,0:T(8,128)(2,1)S(1)} %copy_bitcast_fusion), channel_id=1, replica_groups=mesh['z'=8,'yh'=4,'yl'=2,'x'=4,'c'=2] {'yh'}, dimensions={0} | all-to-all | bytes 1572864 | tf_op jit(solution)/shard_map/all_to_all | solution.py:28
  185.1 0.2 reduce_sum.104
  185.3 0.1 copy.63
  185.4 12.9 %all_to_all.42 = bf16[8,16,768]{2,1,0:T(8,128)(2,1)S(1)} all-to-all(bf16[8,16,768]{2,1,0:T(8,128)(2,1)S(1)} %bitcast.111), channel_id=1, replica_groups=mesh['z'=8,'yh'=4,'yl'=2,'x'=4,'c'=2] {'z'}, dimensions={0} | all-to-all | bytes 393216 | tf_op jit(solution)/shard_map/all_to_all | solution.py:28
  198.4 0.6 slice_bitcast_fusion.5
  199.0 0.6 slice_bitcast_fusion
  (66 shorter events, 1.9 us)
Async XLA Ops:
  7.2 60.8 %all-gather.3.cloned.1.call-start = ((), (), s32[]{:S(2)}) async-start(), calls=%async_computation.8 | async-start | bytes 2359296 | tf_op jit(solution)/shard_map/all_gather | solution.py:62
  31.3 36.5 %all-to-all-start.1 = ((bf16[4,128,1280]{2,1,0:T(8,128)(2,1)}), bf16[4,128,1280]{2,1,0:T(8,128)(2,1)S(1)}, u32[]{:S(2)}, u32[]{:S(2)}) async-start(bf16[4,128,1280]{2,1,0:T(8,128)(2,1)} %broadcast_in_dim.41), calls=%async_computation.1 | async-start | bytes 2621440 | tf_op jit(solution)/shard_map/all_to_all | solution.py:28
  67.9 7.0 %copy-start = (bf16[4096,256]{1,0:T(8,128)(2,1)S(1)}, bf16[4096,256]{1,0:T(8,128)(2,1)}, u32[]{:S(2)}) copy-start(bf16[4096,256]{1,0:T(8,128)(2,1)} %all-gather.3.cloned.1.call-done) | copy-start | bytes 6291460
  70.4 4.6 %collective-permute-start.1 = (bf16[8,256,256]{2,1,0:T(8,128)(2,1)S(1)}, bf16[8,256,256]{2,1,0:T(8,128)(2,1)S(1)}, u32[]{:S(2)}, u32[]{:S(2)}) collective-permute-start(bf16[8,256,256]{2,1,0:T(8,128)(2,1)S(1)} %fusion.1), channel_id=1, source_target_pairs={{0,1},{1,0},{2,3},{3,2},{4,5},{5,4},{6,7},{7,6},{8,9},{9,8},{10,11... | collective-permute-start | bytes 3145736 | tf_op jit(solution)/shard_map/ppermute | solution.py:24
  76.7 4.9 %copy-start.1 = (bf16[128,512]{1,0:T(8,128)(2,1)S(1)}, bf16[128,512]{1,0:T(8,128)(2,1)}, u32[]{:S(2)}) copy-start(bf16[128,512]{1,0:T(8,128)(2,1)} %param.11) | copy-start | bytes 393220
  76.7 4.9 %copy-start.3 = (bf16[512]{0:T(512)(128)(2,1)S(1)}, bf16[512]{0:T(512)(128)(2,1)}, u32[]{:S(2)}) copy-start(bf16[512]{0:T(512)(128)(2,1)} %param.12) | copy-start | bytes 3076
  76.7 6.9 %copy-start.2 = (s32[128]{0:T(128)S(1)}, s32[128]{0:T(128)}, u32[]{:S(2)}) copy-start(s32[128]{0:T(128)} %param.16) | copy-start | bytes 1540
  76.7 18.3 %all-to-all-start.2 = ((bf16[8,256,256]{2,1,0:T(8,128)(2,1)}), bf16[8,256,256]{2,1,0:T(8,128)(2,1)S(1)}, u32[]{:S(2)}, u32[]{:S(2)}) async-start(bf16[8,256,256]{2,1,0:T(8,128)(2,1)} %fusion), calls=%async_computation.2 | async-start | bytes 2097152 | tf_op jit(solution)/shard_map/all_to_all | solution.py:28
  81.6 19.1 %collective-permute-start = (bf16[80,512]{1,0:T(8,128)(2,1)S(1)}, bf16[80,512]{1,0:T(8,128)(2,1)S(1)}, u32[]{:S(2)}, u32[]{:S(2)}) collective-permute-start(bf16[80,512]{1,0:T(8,128)(2,1)S(1)} %pad_maximum_fusion.1), channel_id=1, source_target_pairs={{0,1},{1,0},{2,3},{3,2},{4,5},{5,4},{6,7},{7,6},{8,9},{9,8},{10,11... | collective-permute-start | bytes 245768 | tf_op jit(solution)/shard_map/ppermute | solution.py:24
  95.8 14.1 %all-to-all-start.3 = ((bf16[4,64,256]{2,1,0:T(8,128)(2,1)}), bf16[4,64,256]{2,1,0:T(8,128)(2,1)S(1)}, u32[]{:S(2)}, u32[]{:S(2)}) async-start(bf16[4,64,256]{2,1,0:T(8,128)(2,1)} %bitcast.11), calls=%async_computation.3 | async-start | bytes 262144 | tf_op jit(solution)/shard_map/all_to_all | solution.py:28
  100.8 9.5 %collective-permute-start.2 = (bf16[512,768]{1,0:T(8,128)(2,1)S(1)}, bf16[512,768]{1,0:T(8,128)(2,1)S(1)}, u32[]{:S(2)}, u32[]{:S(2)}) collective-permute-start(bf16[512,768]{1,0:T(8,128)(2,1)S(1)} %bitcast.102), channel_id=1, source_target_pairs={{0,1},{1,0},{2,3},{3,2},{4,5},{5,4},{6,7},{7,6},{8,9},{9,8},{10,11... | collective-permute-start | bytes 2359304 | tf_op jit(solution)/shard_map/ppermute | solution.py:24
  111.1 8.8 %copy-start.4 = (s32[32]{0:T(128)S(1)}, s32[32]{0:T(128)}, u32[]{:S(2)}) copy-start(s32[32]{0:T(128)} %param.17) | copy-start | bytes 388
  112.5 18.2 %all-to-all-start.4 = ((bf16[8,64,1152]{2,1,0:T(8,128)(2,1)}), bf16[8,64,1152]{2,1,0:T(8,128)(2,1)S(1)}, u32[]{:S(2)}, u32[]{:S(2)}) async-start(bf16[8,64,1152]{2,1,0:T(8,128)(2,1)} %broadcast_in_dim.79), calls=%async_computation.4 | async-start | bytes 2359296 | tf_op jit(solution)/shard_map/all_to_all | solution.py:28
  117.9 20.4 %collective-permute-start.4 = (bf16[8192,256]{1,0:T(8,128)(2,1)}, bf16[8192,256]{1,0:T(8,128)(2,1)}, u32[]{:S(2)}, u32[]{:S(2)}) collective-permute-start(bf16[8192,256]{1,0:T(8,128)(2,1)} %param.13), channel_id=1, source_target_pairs={{0,1},{1,0},{2,3},{3,2},{4,5},{5,4},{6,7},{7,6},{8,9},{9,8},{10,11... | collective-permute-start | bytes 12582920 | tf_op jit(solution)/shard_map/ppermute | solution.py:24
  120.2 38.3 %collective-permute-start.6 = (bf16[64,512]{1,0:T(8,128)(2,1)S(1)}, bf16[64,512]{1,0:T(8,128)(2,1)S(1)}, u32[]{:S(2)}, u32[]{:S(2)}) collective-permute-start(bf16[64,512]{1,0:T(8,128)(2,1)S(1)} %get-tuple-element.4), channel_id=1, source_target_pairs={{0,1},{1,0},{2,3},{3,2},{4,5},{5,4},{6,7},{7,6},{8,9},{9,8},{10,11... | collective-permute-start | bytes 196616 | tf_op jit(solution)/shard_map/ppermute | solution.py:24
  131.7 3.1 %collective-permute-start.3 = (bf16[16,512]{1,0:T(8,128)(2,1)S(1)}, bf16[16,512]{1,0:T(8,128)(2,1)S(1)}, u32[]{:S(2)}, u32[]{:S(2)}) collective-permute-start(bf16[16,512]{1,0:T(8,128)(2,1)S(1)} %slice.138), channel_id=1, source_target_pairs={{0,1},{1,0},{2,3},{3,2},{4,5},{5,4},{6,7},{7,6},{8,9},{9,8},{10,11... | collective-permute-start | bytes 49160 | tf_op jit(solution)/shard_map/ppermute | solution.py:24
  141.4 8.5 %collective-permute-start.7 = (bf16[64,384]{1,0:T(8,128)(2,1)S(1)}, bf16[64,384]{1,0:T(8,128)(2,1)S(1)}, u32[]{:S(2)}, u32[]{:S(2)}) collective-permute-start(bf16[64,384]{1,0:T(8,128)(2,1)S(1)} %maximum_maximum_fusion), channel_id=1, source_target_pairs={{0,1},{1,0},{2,3},{3,2},{4,5},{5,4},{6,7},{7,6},{8,9},{9,8},{10,11... | collective-permute-start | bytes 147464 | tf_op jit(solution)/shard_map/ppermute | solution.py:24
  144.6 9.5 %all-to-all-start.5 = ((f32[8,1,1024]{2,1,0:T(1,128)}), f32[8,1,1024]{2,1,0:T(1,128)S(1)}, u32[]{:S(2)}, u32[]{:S(2)}) async-start(f32[8,1,1024]{2,1,0:T(1,128)} %reshape.179), calls=%async_computation.5 | async-start | bytes 65536 | tf_op jit(solution)/shard_map/all_to_all | solution.py:28
  155.4 3.1 %collective-permute-start.5 = (bf16[16,64]{1,0:T(8,128)(2,1)S(1)}, bf16[16,64]{1,0:T(8,128)(2,1)S(1)}, u32[]{:S(2)}, u32[]{:S(2)}) collective-permute-start(bf16[16,64]{1,0:T(8,128)(2,1)S(1)} %multiply_convert_fusion.3), channel_id=1, source_target_pairs={{0,1},{1,0},{2,3},{3,2},{4,5},{5,4},{6,7},{7,6},{8,9},{9,8},{10,11... | collective-permute-start | bytes 6152 | tf_op jit(solution)/shard_map/ppermute | solution.py:24
Sparse Core Ops, SparseCore 0:
  10.1 49.2 all-gather.2

commit v2 on v1

--- a/solution.py
+++ b/solution.py
@@ -67,13 +67,18 @@
     gain_parts = ordered(gain[None], kept[mine : mine + 1])
 
     adapters = jnp.concatenate([down.T, up.T], axis=1)
-    adapters = gather(adapters, "z", n_z).reshape(n_z * rank, block + out_block)
-    joined = gather(jnp.concatenate([attention, adapters], axis=1), "yh", n_yh)
-    attention_all = joined[:, :, :block]
-    adapters_all = joined[:, :, block:].reshape(tenants * rank, block + out_block)
-    adapters_other = swap(adapters_all)
-    down_parts = ordered(adapters_all[:, :block], adapters_other[:, :block])
-    up_own, up_other = adapters_all[:, block:], adapters_other[:, block:]
+    adapters_kept = swap(adapters)
+    packed = [
+        *ordered(adapters[:, :block], adapters_kept[:, :block]),
+        jnp.concatenate([adapters[:, block:], adapters_kept[:, block:]], axis=1),
+    ]
+    joined = gather(jnp.concatenate([attention, *packed], axis=0), "yh", n_yh)
+    attention_all = joined[:, :tokens]
+    adapters_yh, proj = lax.optimization_barrier((joined[:, tokens:], proj))
+    adapters_all = lax.all_gather(adapters_yh.reshape(n_yh * 3 * rank, block), "z", axis=0)
+    adapters_all = adapters_all.reshape(tenants, 3, rank, block)
+    down_parts = [adapters_all[:, part].reshape(tenants * rank, block) for part in range(2)]
+    ups = adapters_all[:, 2].reshape(tenants * rank, 2 * out_block)
 
     rows = n_yh * mine
     send = half(attention_all, other, mine, 1).reshape(rows, block)
@@ -95,8 +100,7 @@
     own_scaled = jnp.where(first, scaled[0], scaled[1])
     partner_scaled = swap(jnp.where(first, scaled[1], scaled[0]))
 
-    slot = jnp.arange(tenants * rank, dtype=jnp.int32) // rank
-    slot_tenant = (slot % n_z) * n_yh + slot // n_z
+    slot_tenant = jnp.arange(tenants * rank, dtype=jnp.int32) // rank
     own_tenant = half(tenant_of, core, mine)
     partner_tenant = half(tenant_of, other, mine)
     own_mask = slot_tenant[:, None] == own_tenant[None, :]
@@ -130,8 +134,7 @@
     target = (target.astype(F32) * inv_column).astype(BF)
     next_row = swap(target[:16])[:1]
     target = jnp.concatenate([target[1:], next_row], axis=0)
-    target_own = half(target, core, out_block, 1).astype(F32)
-    target_other = half(target, other, out_block, 1).astype(F32)
+    target = jnp.concatenate([half(target, core, out_block, 1), half(target, other, out_block, 1)], axis=1)
 
     following = jnp.roll(tenant_of, -1)
     position = jnp.arange(tokens, dtype=jnp.int32)
@@ -140,30 +143,32 @@
     count = jnp.sum(jnp.where(is_tenant, tenant_count.astype(F32)[None, :], 0.0), axis=1)
     weight = half(keep_mask.astype(F32) / count, core, mine)[:, None]
 
-    def draft(weights, ups):
-        shaped = weights.reshape(n_chips, 2 * block, out_block)
-        return dot("ktd,kdn->tn", features, shaped) * inv_column + ADAPTER_SCALE * dot("jt,jn->tn", low_wide, ups)
+    both_weights = jnp.concatenate([draft_weight, draft_weight_other], axis=1)
+    draft = dot("ktd,kdn->tn", features, both_weights.reshape(n_chips, 2 * block, 2 * out_block)) * inv_column
+    draft = draft + ADAPTER_SCALE * dot("jt,jn->tn", low_wide, ups)
+    grad = ((draft - target.astype(F32)) * weight).astype(BF)
+    grad_own = grad[:, :out_block]
 
-    grad_other = ((draft(draft_weight_other, up_other) - target_other) * weight).astype(BF)
-    low_lanes = jnp.concatenate([low_round.T, jnp.zeros((mine, 128 - rank), BF)], axis=1)
-    partner = swap(jnp.concatenate([grad_other, low_lanes], axis=1))
-    grad_own = ((draft(draft_weight, up_own) - target_own) * weight).astype(BF)
-
-    back_part = select(dot("jc,tc->jt", up_own, grad_own) + dot("jc,tc->jt", up_other, grad_other))
-    back = jnp.sum(gather(back_part, CHIPS, n_chips), axis=0)
-    back_scaled = (ADAPTER_SCALE * back * inv_row).astype(BF)
-    back_partner = swap(back_scaled)
+    back_part = select(dot("jc,tc->jt", ups, grad))
+    low_lanes = jnp.concatenate([low_round.T, *split(inv_column), jnp.zeros((mine, 126 - rank), BF)], axis=1)
+    partner = jnp.concatenate([grad[:, out_block:], low_lanes], axis=1)
+    back_part, partner = lax.optimization_barrier((back_part, partner))
+    backs = gather(back_part, MP, 2 * n_chips)
+    partner = swap(partner)
+    backs = jnp.sum(backs.reshape(n_chips, 2, rank, mine), axis=0)
+    partner_codes = partner[:, out_block:].T
+    inv_partner = partner_codes[rank : rank + 1].astype(F32) + partner_codes[rank + 1 : rank + 2].astype(F32)
+    back_scaled = (ADAPTER_SCALE * half(backs, core, 1)[0] * inv_row).astype(BF)
+    back_partner = (ADAPTER_SCALE * half(backs, other, 1)[0] * inv_partner).astype(BF)
 
     grad_up = dot("jt,tc->jc", low_wide, grad_own) + dot(
-        "jt,tc->jc", widen(partner[:, out_block : out_block + rank].T, partner_mask), partner[:, :out_block]
+        "jt,tc->jc", widen(partner_codes[:rank], partner_mask), partner[:, :out_block]
     )
     grad_down = dot("jt,td->jd", widen(back_scaled, own_mask), own_scaled) + dot(
         "jt,td->jd", widen(back_partner, partner_mask), partner_scaled
     )
     grads = jnp.concatenate([grad_down.astype(BF), grad_up.astype(BF)], axis=1)
-    grads = exchange(grads.reshape(n_yh, n_z * rank, block + out_block), "yh")
-    grads = jnp.sum(grads.astype(F32), axis=0).astype(BF)
-    grads = exchange(grads.reshape(n_z, rank, block + out_block), "z")
+    grads = exchange(grads.reshape(tenants, rank, block + out_block), DP)
     grads = jnp.sum(grads.astype(F32), axis=0)
     return grads[:, :block].T, grads[:, block:].T
 

time: 209 us -> 198 us (0.947)
  blocking collectives: 59.5 us -> 35.7 us
  other arithmetic: 4.77 us -> 12.3 us
  local copies, waits for them, and re-layouts: 6.95 us -> 10.4 us
  waiting for transfers between devices: 64.1 us -> 67.2 us
    all_to_all x5, waiting for transfers between devices: 59.5 us -> 28.6 us  [exchange(): return lax.all_to_all(value, axis, 0, 0)]
    all_to_all x3 -> x1, blocking collectives: 59.5 us -> 35.7 us  [exchange(): return lax.all_to_all(value, axis, 0, 0)]
    all_gather x1, waiting for transfers between devices: 0.02 us -> 17.6 us  [shards(): proj = lax.all_gather(output_projection, 'z', axis=0)]
    all_gather x0 -> x1, waiting for transfers between devices: none -> 11.3 us  [shards(): lax.all_gather(adapters_yh.reshape(n_yh * 3 * rank, block), 'z', axis=0)]
    concatenate x2 -> x4, other arithmetic: 0.94 us -> 8.37 us  [the longest x1 7.3 us: shards(): both_weights = jnp.concatenate([draft_weight, draft_weight_other], axis=1)]
    ppermute x8 -> x7, waiting for transfers between devices: 3.86 us -> 8.99 us  [swap(): return lax.ppermute(value, 'c', [(0, 1), (1, 0)])]
    slice x2 -> x7, local copies, waits for them, and re-layouts: 0.09 us -> 2.37 us  [the longest x1 1.48 us: shards(): ups = adapters_all[:, 2].reshape(tenants * rank, 2 * out_block)]
    ppermute x8 -> x7, starting transfers between devices: 16 us -> 14 us  [swap(): return lax.ppermute(value, 'c', [(0, 1), (1, 0)])]
  transfers between devices with their start and end apart: 14 -> 14, of which waited for: 8 -> 10; matrix products, arithmetic and copies ran while one was open for 8% -> 15% of each run, Pallas kernels for 0% -> 0%
where the time goes in v2:
time: 198 us; the launch traced here: 196 us
  waiting for transfers between devices  67.2 us (34%)
  starting transfers between devices  43.5 us (22%)
  blocking collectives  35.7 us (18%)
  between operations  14.5 us (7%)
  matrix products  12.6 us (6%)
  other arithmetic  12.3 us (6%)
  local copies, waits for them, and re-layouts  10.4 us (5%)
    all_to_all x1, blocking collectives, exchange(): return lax.all_to_all(value, axis, 0, 0)  35.7 us
    all_to_all x5, starting transfers between devices, exchange(): return lax.all_to_all(value, axis, 0, 0)  29.4 us
    all_to_all x5, waiting for transfers between devices, exchange(): return lax.all_to_all(value, axis, 0, 0)  28.6 us
    all_gather x1, waiting for transfers between devices, shards(): proj = lax.all_gather(output_projection, 'z', axis=0)  17.6 us
    ppermute x7, starting transfers between devices, swap(): return lax.ppermute(value, 'c', [(0, 1), (1, 0)])  14 us
    dot_general x11, matrix products, dot(): return jnp.einsum(subscripts, left, right, preferred_element_type=F32)  12.6 us
    all_gather x1, waiting for transfers between devices, shards(): lax.all_gather(adapters_yh.reshape(n_yh * 3 * rank, block), 'z', axis=0)  11.3 us
    ppermute x7, waiting for transfers between devices, swap(): return lax.ppermute(value, 'c', [(0, 1), (1, 0)])  8.99 us
  transfers between devices with their start and end apart: 14, of which 10 were waited for; matrix products, arithmetic and copies ran while one was open for 15% of the time, Pallas kernels for 0%

profile of v2, /device:TPU:6, one launch (start us, length us, event | category | flops | bytes accessed | tf_op | source)
XLA Modules:
  0.0 196.1 jit_solution(12904031052409706777)
XLA Ops:
  7.2 0.7 all-gather.6.cloned.1.call-update
  7.9 0.7 pad_maximum_fusion.5
  8.6 1.9 collective-permute-start
  10.6 1.2 collective-permute-done
  11.7 0.7 broadcast_select_fusion.4
  12.4 0.9 maximum_maximum_fusion
  13.4 0.9 broadcast_in_dim.40
  14.3 7.1 %all-to-all-start = ((bf16[4,176,512]{2,1,0:T(8,128)(2,1)}), bf16[4,176,512]{2,1,0:T(8,128)(2,1)S(1)}, u32[]{:S(2)}, u32[]{:S(2)}) async-start(bf16[4,176,512]{2,1,0:T(8,128)(2,1)} %broadcast_in_dim.40), calls=%async_computation | async-start | bytes 1441792 | tf_op jit(solution)/shard_map/all_to_all | solution.py:28
  21.4 19.5 %all-to-all-done = bf16[4,176,512]{2,1,0:T(8,128)(2,1)S(1)} async-done(((bf16[4,176,512]{2,1,0:T(8,128)(2,1)}), bf16[4,176,512]{2,1,0:T(8,128)(2,1)S(1)}, u32[]{:S(2)}, u32[]{:S(2)}) %all-to-all-start) | async-done | bytes 720928 | tf_op jit(solution)/shard_map/all_to_all | solution.py:28
  41.0 0.7 slice.144
  41.7 17.6 %all-gather.6.cloned.1.call-done = bf16[4096,256]{1,0:T(8,128)(2,1)} async-done(((bf16[512,256]{1,0:T(8,128)(2,1)}), bf16[4096,256]{1,0:T(8,128)(2,1)}) %all-gather.6.cloned.1.call-update) | async-done | bytes 2097168 | tf_op jit(solution)/shard_map/all_gather | solution.py:62
  59.4 3.5 %fusion.1 = bf16[8,256,256]{1,2,0:T(8,128)(2,1)} fusion(bf16[8,512,256]{2,1,0:T(8,128)(2,1)} %bitcast.102, bf16[256,512,1]{1,0,2:T(8,128)(2,1)S(1)} %bitcast.116), kind=kOutput, calls=%fused_computation.5 | convolution fusion | flops 537395200 | bytes 3407872 | tf_op jit(solution)/shard_map/tk,zkn->ztn/dot_general | solution.py:20
  62.8 1.9 collective-permute-start.2
  64.8 2.8 %collective-permute-done.2 = bf16[8,256,256]{1,2,0:T(8,128)(2,1)S(1)} collective-permute-done((bf16[8,256,256]{1,2,0:T(8,128)(2,1)}, bf16[8,256,256]{1,2,0:T(8,128)(2,1)S(1)}, u32[]{:S(2)}, u32[]{:S(2)}) %collective-permute-start.2) | collective-permute-done | bytes 1048608 | tf_op jit(solution)/shard_map/ppermute | solution.py:24
  67.6 1.7 fusion
  69.3 5.8 %all-to-all-start.1 = ((bf16[8,256,256]{1,2,0:T(8,128)(2,1)}), bf16[8,256,256]{1,2,0:T(8,128)(2,1)S(1)}, u32[]{:S(2)}, u32[]{:S(2)}) async-start(bf16[8,256,256]{1,2,0:T(8,128)(2,1)} %fusion), calls=%async_computation.1 | async-start | bytes 2097152 | tf_op jit(solution)/shard_map/all_to_all | solution.py:28
  75.2 1.9 collective-permute-start.3
  77.2 2.4 %collective-permute-start.1 = (bf16[80,512]{1,0:T(8,128)(2,1)S(1)}, bf16[80,512]{1,0:T(8,128)(2,1)S(1)}, u32[]{:S(2)}, u32[]{:S(2)}) collective-permute-start(bf16[80,512]{1,0:T(8,128)(2,1)S(1)} %pad_maximum_fusion.2), channel_id=1, source_target_pairs={{0,1},{1,0},{2,3},{3,2},{4,5},{5,4},{6,7},{7,6},{8,9},{9,8},{10,11... | collective-permute-start | bytes 245768 | tf_op jit(solution)/shard_map/ppermute | solution.py:24
  79.7 4.7 %collective-permute-done.1 = bf16[80,512]{1,0:T(8,128)(2,1)S(1)} collective-permute-done((bf16[80,512]{1,0:T(8,128)(2,1)S(1)}, bf16[80,512]{1,0:T(8,128)(2,1)S(1)}, u32[]{:S(2)}, u32[]{:S(2)}) %collective-permute-start.1) | collective-permute-done | bytes 81952 | tf_op jit(solution)/shard_map/ppermute | solution.py:24
  84.4 4.2 %all-to-all-done.1 = bf16[8,256,256]{1,2,0:T(8,128)(2,1)S(1)} async-done(((bf16[8,256,256]{1,2,0:T(8,128)(2,1)}), bf16[8,256,256]{1,2,0:T(8,128)(2,1)S(1)}, u32[]{:S(2)}, u32[]{:S(2)}) %all-to-all-start.1) | async-done | bytes 1048608 | tf_op jit(solution)/shard_map/all_to_all | solution.py:28
  88.6 0.1 reduce_sum.84
  88.7 0.8 copy.92
  89.5 5.8 %all-to-all-start.2 = ((bf16[4,64,256]{2,1,0:T(8,128)(2,1)}), bf16[4,64,256]{2,1,0:T(8,128)(2,1)S(1)}, u32[]{:S(2)}, u32[]{:S(2)}) async-start(bf16[4,64,256]{2,1,0:T(8,128)(2,1)} %bitcast.12), calls=%async_computation.2 | async-start | bytes 262144 | tf_op jit(solution)/shard_map/all_to_all | solution.py:28
  95.3 11.3 %all-gather.4.cloned.1.call-done = bf16[8,192,512]{2,1,0:T(8,128)(2,1)} async-done(((bf16[1,192,512]{2,1,0:T(8,128)(2,1)}), bf16[8,192,512]{2,1,0:T(8,128)(2,1)}) %all-gather.4.cloned.1.call-update) | async-done | bytes 1572880 | tf_op jit(solution)/shard_map/all_gather | solution.py:78
  106.6 1.5 fusion.52
  108.2 0.3 fusion.55
  108.5 0.3 fusion.4
  108.8 0.1 copy.93
  109.1 0.2 multiply_reduce_fusion
  109.3 0.1 copy.95
  109.4 0.1 copy.96
  109.6 1.2 broadcast_in_dim.74
  110.9 5.7 %all-to-all-start.3 = ((bf16[8,64,1152]{2,1,0:T(8,128)(2,1)}), bf16[8,64,1152]{2,1,0:T(8,128)(2,1)S(1)}, u32[]{:S(2)}, u32[]{:S(2)}) async-start(bf16[8,64,1152]{2,1,0:T(8,128)(2,1)} %broadcast_in_dim.74), calls=%async_computation.3 | async-start | bytes 2359296 | tf_op jit(solution)/shard_map/all_to_all | solution.py:28
  116.7 0.1 fusion.45
  117.0 7.3 %pad_maximum_fusion = bf16[8192,512]{1,0:T(8,128)(2,1)} fusion(bf16[8192,256]{1,0:T(8,128)(2,1)} %collective-permute-done.3, bf16[8192,256]{1,0:T(8,128)(2,1)} %param.13), kind=kLoop, calls=%fused_computation | loop fusion | flops 16777216 | bytes 16777216 | tf_op jit(solution)/shard_map/concatenate | solution.py:146
  124.3 1.9 collective-permute-start.6
  126.2 1.2 all-to-all-done.3
  127.5 0.2 fusion.30
  128.2 0.1 slice.155
  128.4 1.9 collective-permute-start.4
  130.3 0.1 compare_select_fusion
  130.5 0.2 convolution_multiply_fusion
  130.9 0.1 copy.101
  131.0 0.1 copy.102
  131.1 0.4 collective-permute-done.4
  131.6 4.9 %fusion.9 = bf16[64,512]{1,0:T(8,128)(2,1)S(1)} fusion(f32[64,512]{1,0:T(8,128)S(1)} %convolution_multiply_fusion, bf16[8,1024,512]{2,1,0:T(8,128)(2,1)} %bitcast.101, bf16[64,256]{1,0:T(8,128)(2,1)S(1)} %get-tuple-element.31, bf16[64,256]{1,0:T(8,128)(2,1)S(1)} %get-tuple-element.30, f32[64]{0:T(128)S(1)} %dynamic_slice.44, f32[64]{0:T(128)S(1)} %bitcast.132, ...), kind=kOutput, calls=%fused_computation.19 | convolution fusion | flops 537165824 | bytes 9700352 | tf_op jit(solution)/shard_map/ktd,kdn->tn/dot_general | solution.py:20
  136.5 0.3 convolution_select_fusion
  136.8 0.1 copy.100
  137.1 2.1 %collective-permute-start.5 = (bf16[64,384]{1,0:T(8,128)(2,1)S(1)}, bf16[64,384]{1,0:T(8,128)(2,1)S(1)}, u32[]{:S(2)}, u32[]{:S(2)}) collective-permute-start(bf16[64,384]{1,0:T(8,128)(2,1)S(1)} %concatenate.55), channel_id=1, source_target_pairs={{0,1},{1,0},{2,3},{3,2},{4,5},{5,4},{6,7},{7,6},{8,9},{9,8},{10,11... | collective-permute-start | bytes 147464 | tf_op jit(solution)/shard_map/ppermute | solution.py:24
  139.2 0.3 fusion.12
  139.5 0.7 reshape.215
  140.2 4.9 %all-to-all-start.4 = ((f32[16,1,1024]{2,1,0:T(1,128)}), f32[16,1,1024]{2,1,0:T(1,128)S(1)}, u32[]{:S(2)}, u32[]{:S(2)}) async-start(f32[16,1,1024]{2,1,0:T(1,128)} %reshape.215), calls=%async_computation.4 | async-start | bytes 131072 | tf_op jit(solution)/shard_map/all_to_all | solution.py:28
  145.4 0.3 fusion.3
  145.7 0.2 multiply_reduce_fusion.2
  145.9 3.6 %all-to-all-done.4 = f32[16,1,1024]{2,1,0:T(1,128)S(1)} async-done(((f32[16,1,1024]{2,1,0:T(1,128)}), f32[16,1,1024]{2,1,0:T(1,128)S(1)}, u32[]{:S(2)}, u32[]{:S(2)}) %all-to-all-start.4) | async-done | bytes 65568 | tf_op jit(solution)/shard_map/all_to_all | solution.py:28
  149.5 0.5 broadcast.158
  150.0 0.8 reduce.5
  151.0 0.4 fusion.11
  151.5 0.4 fusion.2
  152.0 0.3 copy.108
  152.3 35.7 %all_to_all.30 = bf16[32,16,768]{2,1,0:T(8,128)(2,1)S(1)} all-to-all(bf16[32,16,768]{2,1,0:T(8,128)(2,1)S(1)} %bitcast.106), channel_id=1, replica_groups=mesh['z'=8,'yh'=4,'yl'=2,'x'=4,'c'=2] {'z','yh'}, dimensions={0} | all-to-all | bytes 1572864 | tf_op jit(solution)/shard_map/all_to_all | solution.py:28
  187.9 0.1 convert_reduce_fusion
  188.0 0.6 slice_bitcast_fusion
  188.6 0.6 slice_bitcast_fusion.5
  (75 shorter events, 2.5 us)
Async XLA Ops:
  7.2 52.2 %all-gather.6.cloned.1.call-start = ((), (), s32[]{:S(2)}) async-start(), calls=%async_computation.7 | async-start | bytes 2359296 | tf_op jit(solution)/shard_map/all_gather | solution.py:62
  8.6 3.1 %collective-permute-start = (bf16[16,768]{1,0:T(8,128)(2,1)S(1)}, bf16[16,768]{1,0:T(8,128)(2,1)S(1)}, u32[]{:S(2)}, u32[]{:S(2)}) collective-permute-start(bf16[16,768]{1,0:T(8,128)(2,1)S(1)} %pad_maximum_fusion.5), channel_id=1, source_target_pairs={{0,1},{1,0},{2,3},{3,2},{4,5},{5,4},{6,7},{7,6},{8,9},{9,8},{10,11... | collective-permute-start | bytes 73736 | tf_op jit(solution)/shard_map/ppermute | solution.py:24
  14.3 26.6 %all-to-all-start = ((bf16[4,176,512]{2,1,0:T(8,128)(2,1)}), bf16[4,176,512]{2,1,0:T(8,128)(2,1)S(1)}, u32[]{:S(2)}, u32[]{:S(2)}) async-start(bf16[4,176,512]{2,1,0:T(8,128)(2,1)} %broadcast_in_dim.40), calls=%async_computation | async-start | bytes 1441792 | tf_op jit(solution)/shard_map/all_to_all | solution.py:28
  21.4 85.2 %all-gather.4.cloned.1.call-start = ((), (), s32[]{:S(2)}) async-start(), calls=%async_computation.6 | async-start | bytes 1769472 | tf_op jit(solution)/shard_map/all_gather | solution.py:78
  59.3 8.2 %copy-start = (bf16[4096,256]{1,0:T(8,128)(2,1)S(1)}, bf16[4096,256]{1,0:T(8,128)(2,1)}, u32[]{:S(2)}) copy-start(bf16[4096,256]{1,0:T(8,128)(2,1)} %all-gather.6.cloned.1.call-done) | copy-start | bytes 6291460
  62.8 4.8 %collective-permute-start.2 = (bf16[8,256,256]{1,2,0:T(8,128)(2,1)}, bf16[8,256,256]{1,2,0:T(8,128)(2,1)S(1)}, u32[]{:S(2)}, u32[]{:S(2)}) collective-permute-start(bf16[8,256,256]{1,2,0:T(8,128)(2,1)} %fusion.1), channel_id=1, source_target_pairs={{0,1},{1,0},{2,3},{3,2},{4,5},{5,4},{6,7},{7,6},{8,9},{9,8},{10,11... | collective-permute-start | bytes 3145736 | tf_op jit(solution)/shard_map/ppermute | solution.py:24
  69.3 7.8 %copy-start.1 = (bf16[128,512]{1,0:T(8,128)(2,1)S(1)}, bf16[128,512]{1,0:T(8,128)(2,1)}, u32[]{:S(2)}) copy-start(bf16[128,512]{1,0:T(8,128)(2,1)} %param.11) | copy-start | bytes 393220
  69.3 7.8 %copy-start.3 = (bf16[512]{0:T(512)(128)(2,1)S(1)}, bf16[512]{0:T(512)(128)(2,1)}, u32[]{:S(2)}) copy-start(bf16[512]{0:T(512)(128)(2,1)} %param.12) | copy-start | bytes 3076
  69.3 10.3 %copy-start.2 = (s32[128]{0:T(128)S(1)}, s32[128]{0:T(128)}, u32[]{:S(2)}) copy-start(s32[128]{0:T(128)} %param.16) | copy-start | bytes 1540
  69.3 19.2 %all-to-all-start.1 = ((bf16[8,256,256]{1,2,0:T(8,128)(2,1)}), bf16[8,256,256]{1,2,0:T(8,128)(2,1)S(1)}, u32[]{:S(2)}, u32[]{:S(2)}) async-start(bf16[8,256,256]{1,2,0:T(8,128)(2,1)} %fusion), calls=%async_computation.1 | async-start | bytes 2097152 | tf_op jit(solution)/shard_map/all_to_all | solution.py:28
  75.2 41.8 %collective-permute-start.3 = (bf16[8192,256]{1,0:T(8,128)(2,1)}, bf16[8192,256]{1,0:T(8,128)(2,1)}, u32[]{:S(2)}, u32[]{:S(2)}) collective-permute-start(bf16[8192,256]{1,0:T(8,128)(2,1)} %param.13), channel_id=1, source_target_pairs={{0,1},{1,0},{2,3},{3,2},{4,5},{5,4},{6,7},{7,6},{8,9},{9,8},{10,11... | collective-permute-start | bytes 12582920 | tf_op jit(solution)/shard_map/ppermute | solution.py:24
  77.2 7.2 %collective-permute-start.1 = (bf16[80,512]{1,0:T(8,128)(2,1)S(1)}, bf16[80,512]{1,0:T(8,128)(2,1)S(1)}, u32[]{:S(2)}, u32[]{:S(2)}) collective-permute-start(bf16[80,512]{1,0:T(8,128)(2,1)S(1)} %pad_maximum_fusion.2), channel_id=1, source_target_pairs={{0,1},{1,0},{2,3},{3,2},{4,5},{5,4},{6,7},{7,6},{8,9},{9,8},{10,11... | collective-permute-start | bytes 245768 | tf_op jit(solution)/shard_map/ppermute | solution.py:24
  89.5 18.6 %all-to-all-start.2 = ((bf16[4,64,256]{2,1,0:T(8,128)(2,1)}), bf16[4,64,256]{2,1,0:T(8,128)(2,1)S(1)}, u32[]{:S(2)}, u32[]{:S(2)}) async-start(bf16[4,64,256]{2,1,0:T(8,128)(2,1)} %bitcast.12), calls=%async_computation.2 | async-start | bytes 262144 | tf_op jit(solution)/shard_map/all_to_all | solution.py:28
  109.2 7.4 %copy-start.4 = (s32[32]{0:T(128)S(1)}, s32[32]{0:T(128)}, u32[]{:S(2)}) copy-start(s32[32]{0:T(128)} %param.17) | copy-start | bytes 388
  110.9 16.6 %all-to-all-start.3 = ((bf16[8,64,1152]{2,1,0:T(8,128)(2,1)}), bf16[8,64,1152]{2,1,0:T(8,128)(2,1)S(1)}, u32[]{:S(2)}, u32[]{:S(2)}) async-start(bf16[8,64,1152]{2,1,0:T(8,128)(2,1)} %broadcast_in_dim.74), calls=%async_computation.3 | async-start | bytes 2359296 | tf_op jit(solution)/shard_map/all_to_all | solution.py:28
  124.3 27.3 %collective-permute-start.6 = (bf16[64,512]{1,0:T(8,128)(2,1)S(1)}, bf16[64,512]{1,0:T(8,128)(2,1)S(1)}, u32[]{:S(2)}, u32[]{:S(2)}) collective-permute-start(bf16[64,512]{1,0:T(8,128)(2,1)S(1)} %get-tuple-element.12), channel_id=1, source_target_pairs={{0,1},{1,0},{2,3},{3,2},{4,5},{5,4},{6,7},{7,6},{8,9},{9,8},{10,11... | collective-permute-start | bytes 196616 | tf_op jit(solution)/shard_map/ppermute | solution.py:24
  128.4 3.1 %collective-permute-start.4 = (bf16[16,512]{1,0:T(8,128)(2,1)S(1)}, bf16[16,512]{1,0:T(8,128)(2,1)S(1)}, u32[]{:S(2)}, u32[]{:S(2)}) collective-permute-start(bf16[16,512]{1,0:T(8,128)(2,1)S(1)} %slice.164), channel_id=1, source_target_pairs={{0,1},{1,0},{2,3},{3,2},{4,5},{5,4},{6,7},{7,6},{8,9},{9,8},{10,11... | collective-permute-start | bytes 49160 | tf_op jit(solution)/shard_map/ppermute | solution.py:24
  137.1 8.1 %collective-permute-start.5 = (bf16[64,384]{1,0:T(8,128)(2,1)S(1)}, bf16[64,384]{1,0:T(8,128)(2,1)S(1)}, u32[]{:S(2)}, u32[]{:S(2)}) collective-permute-start(bf16[64,384]{1,0:T(8,128)(2,1)S(1)} %concatenate.55), channel_id=1, source_target_pairs={{0,1},{1,0},{2,3},{3,2},{4,5},{5,4},{6,7},{7,6},{8,9},{9,8},{10,11... | collective-permute-start | bytes 147464 | tf_op jit(solution)/shard_map/ppermute | solution.py:24
  140.2 9.2 %all-to-all-start.4 = ((f32[16,1,1024]{2,1,0:T(1,128)}), f32[16,1,1024]{2,1,0:T(1,128)S(1)}, u32[]{:S(2)}, u32[]{:S(2)}) async-start(f32[16,1,1024]{2,1,0:T(1,128)} %reshape.215), calls=%async_computation.4 | async-start | bytes 131072 | tf_op jit(solution)/shard_map/all_to_all | solution.py:28
Sparse Core Ops, SparseCore 0:
  10.1 49.2 all-gather.5
  64.9 41.6 all-gather.3

commit v3 on v2

--- a/solution.py
+++ b/solution.py
@@ -56,37 +56,48 @@
     other = 1 - core
     first = core == 0
 
+    yh = lax.axis_index("yh")
+    turned = (yh - jnp.arange(n_yh, dtype=jnp.int32)) % n_yh
+
+    def around(value):
+        return [value] + [
+            lax.ppermute(value, "yh", [(i, (i + s) % n_yh) for i in range(n_yh)]) for s in range(1, n_yh)
+        ]
+
     def ordered(own, others):
         return jnp.where(first, own, others), jnp.where(first, others, own)
 
-    proj = lax.all_gather(output_projection, "z", axis=0)
+    upper = jnp.concatenate([up.T, jnp.zeros((rank, block - out_block), BF)], axis=1)
+    joined = gather(jnp.concatenate([attention, down.T, upper], axis=0), "z", n_z)
+    proj = jnp.concatenate(around(output_projection), axis=1)
     draft_weight_other = swap(draft_weight)
     pad = jnp.broadcast_to(gain[None], (16, block))
     kept = swap(jnp.concatenate([half(residual, other, mine), pad], axis=0))
     residual_parts = ordered(half(residual, core, mine), kept[:mine])
     gain_parts = ordered(gain[None], kept[mine : mine + 1])
 
-    adapters = jnp.concatenate([down.T, up.T], axis=1)
-    adapters_kept = swap(adapters)
-    packed = [
-        *ordered(adapters[:, :block], adapters_kept[:, :block]),
-        jnp.concatenate([adapters[:, block:], adapters_kept[:, block:]], axis=1),
-    ]
-    joined = gather(jnp.concatenate([attention, *packed], axis=0), "yh", n_yh)
-    attention_all = joined[:, :tokens]
-    adapters_yh, proj = lax.optimization_barrier((joined[:, tokens:], proj))
-    adapters_all = lax.all_gather(adapters_yh.reshape(n_yh * 3 * rank, block), "z", axis=0)
-    adapters_all = adapters_all.reshape(tenants, 3, rank, block)
-    down_parts = [adapters_all[:, part].reshape(tenants * rank, block) for part in range(2)]
-    ups = adapters_all[:, 2].reshape(tenants * rank, 2 * out_block)
-
-    rows = n_yh * mine
-    send = half(attention_all, other, mine, 1).reshape(rows, block)
-    keep = half(attention_all, core, mine, 1).reshape(rows, block)
-    sent = swap(dot("tk,zkn->ztn", send, proj).astype(BF))
-    pair = (dot("tk,zkn->ztn", keep, proj) + sent.astype(F32)).astype(BF)
-    summed = jnp.sum(exchange(pair, CHIPS).astype(F32), axis=0).astype(BF)
-    projected = exchange(summed.reshape(n_yh, mine, cols), "yh")
+    rows = n_z * mine
+    send = half(joined[:, :tokens], other, mine, 1).reshape(rows, block)
+    keep = half(joined[:, :tokens], core, mine, 1).reshape(rows, block)
+    sent = swap(dot("tk,kn->tn", send, proj).astype(BF))
+    pair = (dot("tk,kn->tn", keep, proj) + sent.astype(F32)).astype(BF)
+    adapters = jnp.concatenate(
+        [joined[:, tokens : tokens + rank], joined[:, tokens + rank :, :out_block]], axis=2
+    ).reshape(n_z * rank, block + out_block)
+    pair, adapters = lax.optimization_barrier((pair, adapters))
+
+    summed = jnp.sum(exchange(pair.reshape(n_chips, mine, n_yh * cols), CHIPS).astype(F32), axis=0).astype(BF)
+    summed = jnp.stack([summed[:, s * cols : (s + 1) * cols] for s in range(n_yh)])
+    projected = lax.ppermute(
+        summed[turned],
+        ("z", "yl", "x"),
+        [(z * n_chips + k, k * n_chips + z) for z in range(n_z) for k in range(n_chips)],
+    )
+
+    adapters_all = jnp.stack(around(adapters))[turned].reshape(tenants * rank, block + out_block)
+    adapters_other = swap(adapters_all)
+    down_parts = ordered(adapters_all[:, :block], adapters_other[:, :block])
+    ups = jnp.concatenate([adapters_all[:, block:], adapters_other[:, block:]], axis=1)
 
     half_yh = n_yh // 2
     scaled, squares = [], 0.0
@@ -100,7 +111,8 @@
     own_scaled = jnp.where(first, scaled[0], scaled[1])
     partner_scaled = swap(jnp.where(first, scaled[1], scaled[0]))
 
-    slot_tenant = jnp.arange(tenants * rank, dtype=jnp.int32) // rank
+    slot = jnp.arange(tenants * rank, dtype=jnp.int32) // rank
+    slot_tenant = (slot % n_z) * n_yh + slot // n_z
     own_tenant = half(tenant_of, core, mine)
     partner_tenant = half(tenant_of, other, mine)
     own_mask = slot_tenant[:, None] == own_tenant[None, :]
@@ -168,7 +180,7 @@
         "jt,td->jd", widen(back_partner, partner_mask), partner_scaled
     )
     grads = jnp.concatenate([grad_down.astype(BF), grad_up.astype(BF)], axis=1)
-    grads = exchange(grads.reshape(tenants, rank, block + out_block), DP)
+    grads = exchange(grads.reshape(tenants, rank, block + out_block), ("yh", "z"))
     grads = jnp.sum(grads.astype(F32), axis=0)
     return grads[:, :block].T, grads[:, block:].T
 

time: 198 us -> 202 us (1.020)
  starting transfers between devices: 43.5 us -> 88 us
  waiting for transfers between devices: 67.2 us -> 42.3 us
  between operations: 14.5 us -> 1.32 us
  local copies, waits for them, and re-layouts: 10.4 us -> 14 us
  blocking collectives: 35.7 us -> 32.3 us
    ppermute x0 -> x7, starting transfers between devices: none -> 34.4 us  [the longest x6 29.2 us: around(): lax.ppermute(value, 'yh', [(i, (i + s) % n_yh) for i in range(n_yh)])]
    ppermute x0 -> x7, waiting for transfers between devices: none -> 32.4 us  [the longest x6 25.7 us: around(): lax.ppermute(value, 'yh', [(i, (i + s) % n_yh) for i in range(n_yh)])]
    all_gather x2 -> x0, waiting for transfers between devices: 28.9 us -> none  [the longest x1 17.6 us: shards(): proj = lax.all_gather(output_projection, 'z', axis=0)]
    all_to_all x5 -> x4, waiting for transfers between devices: 28.6 us -> 6.68 us  [exchange(): return lax.all_to_all(value, axis, 0, 0)]
    all_to_all x5 -> x4, starting transfers between devices: 29.4 us -> 39.6 us  [exchange(): return lax.all_to_all(value, axis, 0, 0)]
    ppermute x7, waiting for transfers between devices: 8.99 us -> 3.2 us  [swap(): return lax.ppermute(value, 'c', [(0, 1), (1, 0)])]
    all_to_all x1, blocking collectives: 35.7 us -> 32.3 us  [exchange(): return lax.all_to_all(value, axis, 0, 0)]
    unnamed x14 -> x19, local copies, waits for them, and re-layouts: 0.99 us -> 4.29 us
  transfers between devices with their start and end apart: 14 -> 18, of which waited for: 10 -> 10; matrix products, arithmetic and copies ran while one was open for 15% -> 14% of each run, Pallas kernels for 0% -> 0%
where the time goes in v3:
time: 202 us; the launch traced here: 201 us
  starting transfers between devices  88 us (44%)
  waiting for transfers between devices  42.3 us (21%)
  blocking collectives  32.3 us (16%)
  local copies, waits for them, and re-layouts  14 us (7%)
  matrix products  11.8 us (6%)
  other arithmetic  10.9 us (5%)
    all_to_all x4, starting transfers between devices, exchange(): return lax.all_to_all(value, axis, 0, 0)  39.6 us
    all_to_all x1, blocking collectives, exchange(): return lax.all_to_all(value, axis, 0, 0)  32.3 us
    ppermute x6, starting transfers between devices, around(): lax.ppermute(value, 'yh', [(i, (i + s) % n_yh) for i in range(n_yh)])  29.2 us
    ppermute x6, waiting for transfers between devices, around(): lax.ppermute(value, 'yh', [(i, (i + s) % n_yh) for i in range(n_yh)])  25.7 us
    ppermute x7, starting transfers between devices, swap(): return lax.ppermute(value, 'c', [(0, 1), (1, 0)])  14.1 us
    dot_general x11, matrix products, dot(): return jnp.einsum(subscripts, left, right, preferred_element_type=F32)  11.8 us
    concatenate x1, other arithmetic, shards(): both_weights = jnp.concatenate([draft_weight, draft_weight_other], axis=1)  7.29 us
    ppermute x1, waiting for transfers between devices, shards(): lax.ppermute(summed[turned], ('z', 'yl', 'x'), [(z * n_chips + k, k * n_c...  6.68 us
  transfers between devices with their start and end apart: 18, of which 10 were waited for; matrix products, arithmetic and copies ran while one was open for 14% of the time, Pallas kernels for 0%

profile of v3, /device:TPU:6, one launch (start us, length us, event | category | flops | bytes accessed | tf_op | source)
XLA Modules:
  0.0 200.6 jit_solution(15322576886550902712)
XLA Ops:
  0.6 1.0 fusion.18
  1.6 1.2 broadcast_in_dim.34
  2.8 10.3 %all-to-all-start = ((bf16[8,160,512]{2,1,0:T(8,128)(2,1)}), bf16[8,160,512]{2,1,0:T(8,128)(2,1)S(1)}, u32[]{:S(2)}, u32[]{:S(2)}) async-start(bf16[8,160,512]{2,1,0:T(8,128)(2,1)} %broadcast_in_dim.34), calls=%async_computation | async-start | bytes 2621440 | tf_op jit(solution)/shard_map/all_to_all | solution.py:28
  13.1 4.5 %collective-permute-start = (bf16[512,256]{1,0:T(8,128)(2,1)S(1)}, bf16[512,256]{1,0:T(8,128)(2,1)S(1)}, u32[]{:S(2)}, u32[]{:S(2)}) collective-permute-start(bf16[512,256]{1,0:T(8,128)(2,1)S(1)} %copy-done.1), channel_id=1, source_target_pairs={{0,16},{16,32},{32,48},{48,0},{1,17},{17,33},{33,49},{49,1},{2,18}... | collective-permute-start | bytes 786440 | tf_op jit(solution)/shard_map/ppermute | solution.py:64
  17.6 5.9 %collective-permute-start.1 = (bf16[512,256]{1,0:T(8,128)(2,1)S(1)}, bf16[512,256]{1,0:T(8,128)(2,1)S(1)}, u32[]{:S(2)}, u32[]{:S(2)}) collective-permute-start(bf16[512,256]{1,0:T(8,128)(2,1)S(1)} %copy-done.1), channel_id=1, source_target_pairs={{0,32},{16,48},{32,0},{48,16},{1,33},{17,49},{33,1},{49,17},{2,34}... | collective-permute-start | bytes 786440 | tf_op jit(solution)/shard_map/ppermute | solution.py:64
  23.6 5.3 %collective-permute-start.2 = (bf16[512,256]{1,0:T(8,128)(2,1)S(1)}, bf16[512,256]{1,0:T(8,128)(2,1)S(1)}, u32[]{:S(2)}, u32[]{:S(2)}) collective-permute-start(bf16[512,256]{1,0:T(8,128)(2,1)S(1)} %copy-done.1), channel_id=1, source_target_pairs={{0,48},{16,0},{32,16},{48,32},{1,49},{17,1},{33,17},{49,33},{2,50}... | collective-permute-start | bytes 786440 | tf_op jit(solution)/shard_map/ppermute | solution.py:64
  28.8 0.8 constant_dynamic-update-slice_fusion.3
  29.6 1.7 collective-permute-done
  31.3 0.7 constant_dynamic-update-slice_fusion.2
  32.1 7.5 %collective-permute-done.1 = bf16[512,256]{1,0:T(8,128)(2,1)S(1)} collective-permute-done((bf16[512,256]{1,0:T(8,128)(2,1)S(1)}, bf16[512,256]{1,0:T(8,128)(2,1)S(1)}, u32[]{:S(2)}, u32[]{:S(2)}) %collective-permute-start.1) | collective-permute-done | bytes 262176 | tf_op jit(solution)/shard_map/ppermute | solution.py:64
  39.6 0.7 constant_dynamic-update-slice_fusion.1
  40.3 6.5 %collective-permute-done.2 = bf16[512,256]{1,0:T(8,128)(2,1)S(1)} collective-permute-done((bf16[512,256]{1,0:T(8,128)(2,1)S(1)}, bf16[512,256]{1,0:T(8,128)(2,1)S(1)}, u32[]{:S(2)}, u32[]{:S(2)}) %collective-permute-start.2) | collective-permute-done | bytes 262176 | tf_op jit(solution)/shard_map/ppermute | solution.py:64
  46.8 0.8 constant_dynamic-update-slice_fusion
  47.7 1.0 copy-done.2
  48.8 0.7 convolution_convert_fusion
  49.5 1.9 collective-permute-start.3
  51.5 2.6 %collective-permute-done.3 = bf16[512,1024]{1,0:T(8,128)(2,1)S(1)} collective-permute-done((bf16[512,1024]{1,0:T(8,128)(2,1)S(1)}, bf16[512,1024]{1,0:T(8,128)(2,1)S(1)}, u32[]{:S(2)}, u32[]{:S(2)}) %collective-permute-start.3) | collective-permute-done | bytes 1048608 | tf_op jit(solution)/shard_map/ppermute | solution.py:24
  54.1 1.7 add_convert_fusion
  55.7 4.9 %all-to-all-start.1 = ((bf16[8,64,1024]{2,1,0:T(8,128)(2,1)}), bf16[8,64,1024]{2,1,0:T(8,128)(2,1)S(1)}, u32[]{:S(2)}, u32[]{:S(2)}) async-start(bf16[8,64,1024]{2,1,0:T(8,128)(2,1)} %bitcast.11), calls=%async_computation.1 | async-start | bytes 2097152 | tf_op jit(solution)/shard_map/all_to_all | solution.py:28
  60.7 1.9 collective-permute-start.10
  62.6 2.4 %collective-permute-start.8 = (bf16[80,512]{1,0:T(8,128)(2,1)S(1)}, bf16[80,512]{1,0:T(8,128)(2,1)S(1)}, u32[]{:S(2)}, u32[]{:S(2)}) collective-permute-start(bf16[80,512]{1,0:T(8,128)(2,1)S(1)} %pad_maximum_fusion.8), channel_id=1, source_target_pairs={{0,1},{1,0},{2,3},{3,2},{4,5},{5,4},{6,7},{7,6},{8,9},{9,8},{10,11... | collective-permute-start | bytes 245768 | tf_op jit(solution)/shard_map/ppermute | solution.py:24
  65.2 5.3 %collective-permute-start.6 = (bf16[128,768]{1,0:T(8,128)(2,1)S(1)}, bf16[128,768]{1,0:T(8,128)(2,1)S(1)}, u32[]{:S(2)}, u32[]{:S(2)}) collective-permute-start(bf16[128,768]{1,0:T(8,128)(2,1)S(1)} %bitcast.104), channel_id=1, source_target_pairs={{0,48},{16,0},{32,16},{48,32},{1,49},{17,1},{33,17},{49,33},{2,50}... | collective-permute-start | bytes 589832 | tf_op jit(solution)/shard_map/ppermute | solution.py:64
  70.5 4.7 %collective-permute-start.5 = (bf16[128,768]{1,0:T(8,128)(2,1)S(1)}, bf16[128,768]{1,0:T(8,128)(2,1)S(1)}, u32[]{:S(2)}, u32[]{:S(2)}) collective-permute-start(bf16[128,768]{1,0:T(8,128)(2,1)S(1)} %bitcast.105), channel_id=1, source_target_pairs={{0,32},{16,48},{32,0},{48,16},{1,33},{17,49},{33,1},{49,17},{2,34}... | collective-permute-start | bytes 589832 | tf_op jit(solution)/shard_map/ppermute | solution.py:64
  75.1 3.6 %collective-permute-start.4 = (bf16[128,768]{1,0:T(8,128)(2,1)S(1)}, bf16[128,768]{1,0:T(8,128)(2,1)S(1)}, u32[]{:S(2)}, u32[]{:S(2)}) collective-permute-start(bf16[128,768]{1,0:T(8,128)(2,1)S(1)} %bitcast.106), channel_id=1, source_target_pairs={{0,16},{16,32},{32,48},{48,0},{1,17},{17,33},{33,49},{49,1},{2,18}... | collective-permute-start | bytes 589832 | tf_op jit(solution)/shard_map/ppermute | solution.py:64
  78.8 9.8 %collective-permute-done.5 = bf16[128,768]{1,0:T(8,128)(2,1)S(1)} collective-permute-done((bf16[128,768]{1,0:T(8,128)(2,1)S(1)}, bf16[128,768]{1,0:T(8,128)(2,1)S(1)}, u32[]{:S(2)}, u32[]{:S(2)}) %collective-permute-start.5) | collective-permute-done | bytes 196640 | tf_op jit(solution)/shard_map/ppermute | solution.py:64
  88.5 0.2 collective-permute-done.4
  88.9 0.6 gather_fusion
  89.5 1.9 collective-permute-start.7
  91.4 0.2 reduce_sum.84
  91.6 0.6 gather_fusion.1
  92.2 5.2 %collective-permute-start.9 = (bf16[4,64,256]{2,1,0:T(8,128)(2,1)S(1)}, bf16[4,64,256]{2,1,0:T(8,128)(2,1)S(1)}, u32[]{:S(2)}, u32[]{:S(2)}) collective-permute-start(bf16[4,64,256]{2,1,0:T(8,128)(2,1)S(1)} %gather_fusion.1), channel_id=1, source_target_pairs={{0,0},{2,64},{4,128},{6,192},{8,256},{10,320},{12,384},{14,448},{6... | collective-permute-start | bytes 393224 | tf_op jit(solution)/shard_map/ppermute | solution.py:91
  97.4 6.7 %collective-permute-done.9 = bf16[4,64,256]{2,1,0:T(8,128)(2,1)S(1)} collective-permute-done((bf16[4,64,256]{2,1,0:T(8,128)(2,1)S(1)}, bf16[4,64,256]{2,1,0:T(8,128)(2,1)S(1)}, u32[]{:S(2)}, u32[]{:S(2)}) %collective-permute-start.9) | collective-permute-done | bytes 131104 | tf_op jit(solution)/shard_map/ppermute | solution.py:91
  104.2 1.3 fusion.8
  105.5 1.3 fusion.2
  106.9 0.1 copy.62
  107.2 0.2 multiply_reduce_fusion
  107.7 1.2 broadcast_in_dim.43
  108.9 19.0 %all-to-all-start.2 = ((bf16[8,64,1152]{2,1,0:T(8,128)(2,1)}), bf16[8,64,1152]{2,1,0:T(8,128)(2,1)S(1)}, u32[]{:S(2)}, u32[]{:S(2)}) async-start(bf16[8,64,1152]{2,1,0:T(8,128)(2,1)} %broadcast_in_dim.43), calls=%async_computation.2 | async-start | bytes 2359296 | tf_op jit(solution)/shard_map/all_to_all | solution.py:28
  128.3 7.3 %pad_maximum_fusion = bf16[8192,512]{1,0:T(8,128)(2,1)} fusion(bf16[8192,256]{1,0:T(8,128)(2,1)} %collective-permute-done.10, bf16[8192,256]{1,0:T(8,128)(2,1)} %param.13), kind=kLoop, calls=%fused_computation.2 | loop fusion | flops 16777216 | bytes 16777216 | tf_op jit(solution)/shard_map/concatenate | solution.py:158
  135.6 1.0 slice.167
  136.6 1.9 collective-permute-start.13
  138.5 3.1 %all-to-all-done.2 = bf16[8,64,1152]{2,1,0:T(8,128)(2,1)S(1)} async-done(((bf16[8,64,1152]{2,1,0:T(8,128)(2,1)}), bf16[8,64,1152]{2,1,0:T(8,128)(2,1)S(1)}, u32[]{:S(2)}, u32[]{:S(2)}) %all-to-all-start.2) | async-done | bytes 1179680 | tf_op jit(solution)/shard_map/all_to_all | solution.py:28
  141.7 0.2 fusion.37
  142.5 0.1 slice.180
  142.7 1.9 collective-permute-start.11
  144.6 0.2 convolution_multiply_fusion
  145.2 0.6 collective-permute-done.11
  145.9 4.9 %fusion.7 = bf16[64,512]{1,0:T(8,128)(2,1)S(1)} fusion(f32[64,512]{1,0:T(8,128)S(1)} %convolution_multiply_fusion, bf16[8,1024,512]{2,1,0:T(8,128)(2,1)} %bitcast.93, bf16[64,256]{1,0:T(8,128)(2,1)S(1)} %get-tuple-element.32, bf16[64,256]{1,0:T(8,128)(2,1)S(1)} %get-tuple-element.31, f32[64]{0:T(128)S(1)} %dynamic_slice.44, f32[64]{0:T(128)S(1)} %bitcast.125, ...), kind=kOutput, calls=%fused_computation.19 | convolution fusion | flops 537165824 | bytes 9700352 | tf_op jit(solution)/shard_map/ktd,kdn->tn/dot_general | solution.py:20
  150.8 0.3 convolution_select_fusion
  151.4 2.1 %collective-permute-start.12 = (bf16[64,384]{1,0:T(8,128)(2,1)S(1)}, bf16[64,384]{1,0:T(8,128)(2,1)S(1)}, u32[]{:S(2)}, u32[]{:S(2)}) collective-permute-start(bf16[64,384]{1,0:T(8,128)(2,1)S(1)} %concatenate.63), channel_id=1, source_target_pairs={{0,1},{1,0},{2,3},{3,2},{4,5},{5,4},{6,7},{7,6},{8,9},{9,8},{10,11... | collective-permute-start | bytes 147464 | tf_op jit(solution)/shard_map/ppermute | solution.py:24
  153.5 0.3 fusion.32
  153.8 0.7 reshape.256
  154.6 5.4 %all-to-all-start.3 = ((f32[16,1,1024]{2,1,0:T(1,128)}), f32[16,1,1024]{2,1,0:T(1,128)S(1)}, u32[]{:S(2)}, u32[]{:S(2)}) async-start(f32[16,1,1024]{2,1,0:T(1,128)} %reshape.256), calls=%async_computation.3 | async-start | bytes 131072 | tf_op jit(solution)/shard_map/all_to_all | solution.py:28
  160.2 0.3 fusion.1
  160.5 0.2 multiply_reduce_fusion.2
  160.6 3.6 %all-to-all-done.3 = f32[16,1,1024]{2,1,0:T(1,128)S(1)} async-done(((f32[16,1,1024]{2,1,0:T(1,128)}), f32[16,1,1024]{2,1,0:T(1,128)S(1)}, u32[]{:S(2)}, u32[]{:S(2)}) %all-to-all-start.3) | async-done | bytes 65568 | tf_op jit(solution)/shard_map/all_to_all | solution.py:28
  164.2 0.5 broadcast.221
  164.7 0.8 reduce.5
  165.8 0.4 fusion.20
  166.3 0.4 fusion
  166.7 0.3 copy.77
  167.0 32.3 %all_to_all.25 = bf16[32,16,768]{2,1,0:T(8,128)(2,1)S(1)} all-to-all(bf16[32,16,768]{2,1,0:T(8,128)(2,1)S(1)} %bitcast.94), channel_id=1, replica_groups=mesh['z'=8,'yh'=4,'yl'=2,'x'=4,'c'=2] {'yh','z'}, dimensions={0} | all-to-all | bytes 1572864 | tf_op jit(solution)/shard_map/all_to_all | solution.py:28
  199.4 0.6 slice_bitcast_fusion
  200.0 0.6 slice_bitcast_fusion.9
  (91 shorter events, 3.5 us)
Async XLA Ops:
  1.6 11.5 %copy-start.1 = (bf16[512,256]{1,0:T(8,128)(2,1)S(1)}, bf16[512,256]{1,0:T(8,128)(2,1)}, u32[]{:S(2)}) copy-start(bf16[512,256]{1,0:T(8,128)(2,1)} %param.10) | copy-start | bytes 786436
  2.8 44.8 %all-to-all-start = ((bf16[8,160,512]{2,1,0:T(8,128)(2,1)}), bf16[8,160,512]{2,1,0:T(8,128)(2,1)S(1)}, u32[]{:S(2)}, u32[]{:S(2)}) async-start(bf16[8,160,512]{2,1,0:T(8,128)(2,1)} %broadcast_in_dim.34), calls=%async_computation | async-start | bytes 2621440 | tf_op jit(solution)/shard_map/all_to_all | solution.py:28
  13.1 18.2 %collective-permute-start = (bf16[512,256]{1,0:T(8,128)(2,1)S(1)}, bf16[512,256]{1,0:T(8,128)(2,1)S(1)}, u32[]{:S(2)}, u32[]{:S(2)}) collective-permute-start(bf16[512,256]{1,0:T(8,128)(2,1)S(1)} %copy-done.1), channel_id=1, source_target_pairs={{0,16},{16,32},{32,48},{48,0},{1,17},{17,33},{33,49},{49,1},{2,18}... | collective-permute-start | bytes 786440 | tf_op jit(solution)/shard_map/ppermute | solution.py:64
  17.6 22.0 %collective-permute-start.1 = (bf16[512,256]{1,0:T(8,128)(2,1)S(1)}, bf16[512,256]{1,0:T(8,128)(2,1)S(1)}, u32[]{:S(2)}, u32[]{:S(2)}) collective-permute-start(bf16[512,256]{1,0:T(8,128)(2,1)S(1)} %copy-done.1), channel_id=1, source_target_pairs={{0,32},{16,48},{32,0},{48,16},{1,33},{17,49},{33,1},{49,17},{2,34}... | collective-permute-start | bytes 786440 | tf_op jit(solution)/shard_map/ppermute | solution.py:64
  23.6 23.2 %collective-permute-start.2 = (bf16[512,256]{1,0:T(8,128)(2,1)S(1)}, bf16[512,256]{1,0:T(8,128)(2,1)S(1)}, u32[]{:S(2)}, u32[]{:S(2)}) collective-permute-start(bf16[512,256]{1,0:T(8,128)(2,1)S(1)} %copy-done.1), channel_id=1, source_target_pairs={{0,48},{16,0},{32,16},{48,32},{1,49},{17,1},{33,17},{49,33},{2,50}... | collective-permute-start | bytes 786440 | tf_op jit(solution)/shard_map/ppermute | solution.py:64
  47.6 1.2 copy-start.2
  49.5 4.6 %collective-permute-start.3 = (bf16[512,1024]{1,0:T(8,128)(2,1)S(1)}, bf16[512,1024]{1,0:T(8,128)(2,1)S(1)}, u32[]{:S(2)}, u32[]{:S(2)}) collective-permute-start(bf16[512,1024]{1,0:T(8,128)(2,1)S(1)} %convolution_convert_fusion), channel_id=1, source_target_pairs={{0,1},{1,0},{2,3},{3,2},{4,5},{5,4},{6,7},{7,6},{8,9},{9,8},{10,11... | collective-permute-start | bytes 3145736 | tf_op jit(solution)/shard_map/ppermute | solution.py:24
  54.1 8.5 %copy-start = (bf16[128,512]{1,0:T(8,128)(2,1)S(1)}, bf16[128,512]{1,0:T(8,128)(2,1)}, u32[]{:S(2)}) copy-start(bf16[128,512]{1,0:T(8,128)(2,1)} %param.11) | copy-start | bytes 393220
  55.7 6.9 %copy-start.4 = (bf16[512]{0:T(512)(128)(2,1)S(1)}, bf16[512]{0:T(512)(128)(2,1)}, u32[]{:S(2)}) copy-start(bf16[512]{0:T(512)(128)(2,1)} %param.12) | copy-start | bytes 3076
  55.7 9.3 %copy-start.3 = (s32[128]{0:T(128)S(1)}, s32[128]{0:T(128)}, u32[]{:S(2)}) copy-start(s32[128]{0:T(128)} %param.16) | copy-start | bytes 1540
  55.7 35.7 %all-to-all-start.1 = ((bf16[8,64,1024]{2,1,0:T(8,128)(2,1)}), bf16[8,64,1024]{2,1,0:T(8,128)(2,1)S(1)}, u32[]{:S(2)}, u32[]{:S(2)}) async-start(bf16[8,64,1024]{2,1,0:T(8,128)(2,1)} %bitcast.11), calls=%async_computation.1 | async-start | bytes 2097152 | tf_op jit(solution)/shard_map/all_to_all | solution.py:28
  60.7 67.6 %collective-permute-start.10 = (bf16[8192,256]{1,0:T(8,128)(2,1)}, bf16[8192,256]{1,0:T(8,128)(2,1)}, u32[]{:S(2)}, u32[]{:S(2)}) collective-permute-start(bf16[8192,256]{1,0:T(8,128)(2,1)} %param.13), channel_id=1, source_target_pairs={{0,1},{1,0},{2,3},{3,2},{4,5},{5,4},{6,7},{7,6},{8,9},{9,8},{10,11... | collective-permute-start | bytes 12582920 | tf_op jit(solution)/shard_map/ppermute | solution.py:24
  62.6 34.8 %collective-permute-start.8 = (bf16[80,512]{1,0:T(8,128)(2,1)S(1)}, bf16[80,512]{1,0:T(8,128)(2,1)S(1)}, u32[]{:S(2)}, u32[]{:S(2)}) collective-permute-start(bf16[80,512]{1,0:T(8,128)(2,1)S(1)} %pad_maximum_fusion.8), channel_id=1, source_target_pairs={{0,1},{1,0},{2,3},{3,2},{4,5},{5,4},{6,7},{7,6},{8,9},{9,8},{10,11... | collective-permute-start | bytes 245768 | tf_op jit(solution)/shard_map/ppermute | solution.py:24
  65.2 13.6 %collective-permute-start.6 = (bf16[128,768]{1,0:T(8,128)(2,1)S(1)}, bf16[128,768]{1,0:T(8,128)(2,1)S(1)}, u32[]{:S(2)}, u32[]{:S(2)}) collective-permute-start(bf16[128,768]{1,0:T(8,128)(2,1)S(1)} %bitcast.104), channel_id=1, source_target_pairs={{0,48},{16,0},{32,16},{48,32},{1,49},{17,1},{33,17},{49,33},{2,50}... | collective-permute-start | bytes 589832 | tf_op jit(solution)/shard_map/ppermute | solution.py:64
  70.5 18.1 %collective-permute-start.5 = (bf16[128,768]{1,0:T(8,128)(2,1)S(1)}, bf16[128,768]{1,0:T(8,128)(2,1)S(1)}, u32[]{:S(2)}, u32[]{:S(2)}) collective-permute-start(bf16[128,768]{1,0:T(8,128)(2,1)S(1)} %bitcast.105), channel_id=1, source_target_pairs={{0,32},{16,48},{32,0},{48,16},{1,33},{17,49},{33,1},{49,17},{2,34}... | collective-permute-start | bytes 589832 | tf_op jit(solution)/shard_map/ppermute | solution.py:64
  75.1 13.6 %collective-permute-start.4 = (bf16[128,768]{1,0:T(8,128)(2,1)S(1)}, bf16[128,768]{1,0:T(8,128)(2,1)S(1)}, u32[]{:S(2)}, u32[]{:S(2)}) collective-permute-start(bf16[128,768]{1,0:T(8,128)(2,1)S(1)} %bitcast.106), channel_id=1, source_target_pairs={{0,16},{16,32},{32,48},{48,0},{1,17},{17,33},{33,49},{49,1},{2,18}... | collective-permute-start | bytes 589832 | tf_op jit(solution)/shard_map/ppermute | solution.py:64
  89.5 14.7 %collective-permute-start.7 = (bf16[512,768]{1,0:T(8,128)(2,1)S(1)}, bf16[512,768]{1,0:T(8,128)(2,1)}, u32[]{:S(2)}, u32[]{:S(2)}) collective-permute-start(bf16[512,768]{1,0:T(8,128)(2,1)S(1)} %bitcast.98), channel_id=1, source_target_pairs={{0,1},{1,0},{2,3},{3,2},{4,5},{5,4},{6,7},{7,6},{8,9},{9,8},{10,11... | collective-permute-start | bytes 2359304 | tf_op jit(solution)/shard_map/ppermute | solution.py:24
  92.2 11.9 %collective-permute-start.9 = (bf16[4,64,256]{2,1,0:T(8,128)(2,1)S(1)}, bf16[4,64,256]{2,1,0:T(8,128)(2,1)S(1)}, u32[]{:S(2)}, u32[]{:S(2)}) collective-permute-start(bf16[4,64,256]{2,1,0:T(8,128)(2,1)S(1)} %gather_fusion.1), channel_id=1, source_target_pairs={{0,0},{2,64},{4,128},{6,192},{8,256},{10,320},{12,384},{14,448},{6... | collective-permute-start | bytes 393224 | tf_op jit(solution)/shard_map/ppermute | solution.py:91
  107.3 20.7 %copy-start.5 = (s32[32]{0:T(128)S(1)}, s32[32]{0:T(128)}, u32[]{:S(2)}) copy-start(s32[32]{0:T(128)} %param.17) | copy-start | bytes 388
  108.9 32.7 %all-to-all-start.2 = ((bf16[8,64,1152]{2,1,0:T(8,128)(2,1)}), bf16[8,64,1152]{2,1,0:T(8,128)(2,1)S(1)}, u32[]{:S(2)}, u32[]{:S(2)}) async-start(bf16[8,64,1152]{2,1,0:T(8,128)(2,1)} %broadcast_in_dim.43), calls=%async_computation.2 | async-start | bytes 2359296 | tf_op jit(solution)/shard_map/all_to_all | solution.py:28
  136.6 29.7 %collective-permute-start.13 = (bf16[64,512]{1,0:T(8,128)(2,1)S(1)}, bf16[64,512]{1,0:T(8,128)(2,1)S(1)}, u32[]{:S(2)}, u32[]{:S(2)}) collective-permute-start(bf16[64,512]{1,0:T(8,128)(2,1)S(1)} %get-tuple-element.12), channel_id=1, source_target_pairs={{0,1},{1,0},{2,3},{3,2},{4,5},{5,4},{6,7},{7,6},{8,9},{9,8},{10,11... | collective-permute-start | bytes 196616 | tf_op jit(solution)/shard_map/ppermute | solution.py:24
  142.7 3.1 %collective-permute-start.11 = (bf16[16,512]{1,0:T(8,128)(2,1)S(1)}, bf16[16,512]{1,0:T(8,128)(2,1)S(1)}, u32[]{:S(2)}, u32[]{:S(2)}) collective-permute-start(bf16[16,512]{1,0:T(8,128)(2,1)S(1)} %slice.189), channel_id=1, source_target_pairs={{0,1},{1,0},{2,3},{3,2},{4,5},{5,4},{6,7},{7,6},{8,9},{9,8},{10,11... | collective-permute-start | bytes 49160 | tf_op jit(solution)/shard_map/ppermute | solution.py:24
  151.4 8.5 %collective-permute-start.12 = (bf16[64,384]{1,0:T(8,128)(2,1)S(1)}, bf16[64,384]{1,0:T(8,128)(2,1)S(1)}, u32[]{:S(2)}, u32[]{:S(2)}) collective-permute-start(bf16[64,384]{1,0:T(8,128)(2,1)S(1)} %concatenate.63), channel_id=1, source_target_pairs={{0,1},{1,0},{2,3},{3,2},{4,5},{5,4},{6,7},{7,6},{8,9},{9,8},{10,11... | collective-permute-start | bytes 147464 | tf_op jit(solution)/shard_map/ppermute | solution.py:24
  154.6 9.7 %all-to-all-start.3 = ((f32[16,1,1024]{2,1,0:T(1,128)}), f32[16,1,1024]{2,1,0:T(1,128)S(1)}, u32[]{:S(2)}, u32[]{:S(2)}) async-start(f32[16,1,1024]{2,1,0:T(1,128)} %reshape.256), calls=%async_computation.3 | async-start | bytes 131072 | tf_op jit(solution)/shard_map/all_to_all | solution.py:28

commit v4 on v3

--- a/solution.py
+++ b/solution.py
@@ -57,59 +57,71 @@
     first = core == 0
 
     yh = lax.axis_index("yh")
-    turned = (yh - jnp.arange(n_yh, dtype=jnp.int32)) % n_yh
-
-    def around(value):
-        return [value] + [
-            lax.ppermute(value, "yh", [(i, (i + s) % n_yh) for i in range(n_yh)]) for s in range(1, n_yh)
-        ]
+
+    def shift(value, step):
+        return lax.ppermute(value, "yh", [(i, (i + step) % n_yh) for i in range(n_yh)])
+
+    def farther(before, after):
+        size = before.shape[0] // 2
+        return jnp.concatenate([shift(before[:size], 1), shift(after[size:], -1)], axis=0)
 
     def ordered(own, others):
         return jnp.where(first, own, others), jnp.where(first, others, own)
 
     upper = jnp.concatenate([up.T, jnp.zeros((rank, block - out_block), BF)], axis=1)
     joined = gather(jnp.concatenate([attention, down.T, upper], axis=0), "z", n_z)
-    proj = jnp.concatenate(around(output_projection), axis=1)
+    before, after = shift(output_projection, 1), shift(output_projection, -1)
+    proj = jnp.zeros((block, n_yh * cols), BF)
+    for step, piece in enumerate([output_projection, before, farther(before, after), after]):
+        proj = lax.dynamic_update_slice(proj, piece, (0, (yh - step) % n_yh * cols))
     draft_weight_other = swap(draft_weight)
     pad = jnp.broadcast_to(gain[None], (16, block))
     kept = swap(jnp.concatenate([half(residual, other, mine), pad], axis=0))
-    residual_parts = ordered(half(residual, core, mine), kept[:mine])
-    gain_parts = ordered(gain[None], kept[mine : mine + 1])
+    chip_rows = jnp.concatenate(
+        ordered(jnp.concatenate([half(residual, core, mine), pad], axis=0), kept), axis=1
+    )
+
+    piece = 2 * block // n_chips
+    chip_rows = chip_rows.reshape(mine + 16, n_chips, piece).transpose(1, 0, 2)
+    joined, chip_rows = lax.optimization_barrier((joined, chip_rows))
+    chip_rows = exchange(chip_rows, CHIPS)
+    residual_part, gain_part = chip_rows[:, :mine].astype(F32), chip_rows[:, mine : mine + 1].astype(F32)
 
     rows = n_z * mine
     send = half(joined[:, :tokens], other, mine, 1).reshape(rows, block)
     keep = half(joined[:, :tokens], core, mine, 1).reshape(rows, block)
     sent = swap(dot("tk,kn->tn", send, proj).astype(BF))
     pair = (dot("tk,kn->tn", keep, proj) + sent.astype(F32)).astype(BF)
+    pair = pair.reshape(rows, n_chips, piece).transpose(1, 0, 2)
+    summed = jnp.sum(exchange(pair, CHIPS).astype(F32), axis=0).astype(BF)
     adapters = jnp.concatenate(
         [joined[:, tokens : tokens + rank], joined[:, tokens + rank :, :out_block]], axis=2
     ).reshape(n_z * rank, block + out_block)
-    pair, adapters = lax.optimization_barrier((pair, adapters))
-
-    summed = jnp.sum(exchange(pair.reshape(n_chips, mine, n_yh * cols), CHIPS).astype(F32), axis=0).astype(BF)
-    summed = jnp.stack([summed[:, s * cols : (s + 1) * cols] for s in range(n_yh)])
-    projected = lax.ppermute(
-        summed[turned],
-        ("z", "yl", "x"),
-        [(z * n_chips + k, k * n_chips + z) for z in range(n_z) for k in range(n_chips)],
-    )
-
-    adapters_all = jnp.stack(around(adapters))[turned].reshape(tenants * rank, block + out_block)
+    summed, adapters = lax.optimization_barrier((summed, adapters))
+    projected = exchange(summed.reshape(n_z, mine, piece), "z").astype(F32)
+    before, after = shift(adapters, 1), shift(adapters, -1)
+
+    hidden = residual_part + projected
+    squares = jnp.sum(jnp.sum(hidden * hidden, axis=0), axis=1, keepdims=True)
+    scaled = (hidden * gain_part).astype(BF)
+    message = jnp.concatenate(
+        [scaled[z] for z in range(n_z)] + [*split(squares), jnp.zeros((mine, 126), BF)], axis=1
+    )
+    message, before, after = lax.optimization_barrier((message, before, after))
+    received = gather(message, CHIPS, n_chips)
+    features = received[:, :, : 2 * block].reshape(n_chips, mine, n_z, piece)
+    features = features.transpose(2, 1, 0, 3).reshape(n_z, mine, 2 * block)
+    totals = jnp.sum(received[:, :, 2 * block :].astype(F32), axis=0)
+    inv_column = lax.rsqrt((totals[:, :1] + totals[:, 1:2]) / width + EPSILON)
+    inv_row = jnp.broadcast_to(inv_column, (mine, 128)).T[:1]
+
+    adapters_all = jnp.zeros((n_yh, n_z * rank, block + out_block), BF)
+    for step, part in enumerate([adapters, before, farther(before, after), after]):
+        adapters_all = lax.dynamic_update_slice(adapters_all, part[None], ((yh - step) % n_yh, 0, 0))
+    adapters_all = adapters_all.reshape(tenants * rank, block + out_block)
     adapters_other = swap(adapters_all)
-    down_parts = ordered(adapters_all[:, :block], adapters_other[:, :block])
+    downs = jnp.concatenate(ordered(adapters_all[:, :block], adapters_other[:, :block]), axis=1)
     ups = jnp.concatenate([adapters_all[:, block:], adapters_other[:, block:]], axis=1)
-
-    half_yh = n_yh // 2
-    scaled, squares = [], 0.0
-    for part in range(2):
-        piece = jnp.concatenate(
-            [projected[half_yh * part + j] for j in range(half_yh)], axis=1
-        ).astype(F32)
-        hidden = residual_parts[part].astype(F32) + piece
-        squares = squares + jnp.sum(hidden * hidden, axis=1, keepdims=True)
-        scaled.append((hidden * gain_parts[part].astype(F32)).astype(BF))
-    own_scaled = jnp.where(first, scaled[0], scaled[1])
-    partner_scaled = swap(jnp.where(first, scaled[1], scaled[0]))
 
     slot = jnp.arange(tenants * rank, dtype=jnp.int32) // rank
     slot_tenant = (slot % n_z) * n_yh + slot // n_z
@@ -125,19 +137,11 @@
     def widen(values, mask):
         return jnp.where(mask, jnp.tile(values, (tenants, 1)), BF(0))
 
-    low_part = select(dot("jd,td->jt", down_parts[0], scaled[0]) + dot("jd,td->jt", down_parts[1], scaled[1]))
-    extras = jnp.concatenate(split(low_part), axis=0).T
-    message = jnp.concatenate(
-        scaled + [extras, *split(squares), jnp.zeros((mine, 128 - 2 * rank - 2), BF)], axis=1
-    )
-    received = gather(message, CHIPS, n_chips)
-    features = received[:, :, : 2 * block]
-    totals = jnp.sum(received[:, :, 2 * block :].astype(F32), axis=0)
-    square_column = totals[:, 2 * rank : 2 * rank + 1] + totals[:, 2 * rank + 1 : 2 * rank + 2]
-    inv_column = lax.rsqrt(square_column / width + EPSILON)
-    totals = totals.T
-    inv_row = lax.rsqrt((totals[2 * rank : 2 * rank + 1] + totals[2 * rank + 1 : 2 * rank + 2]) / width + EPSILON)
-    low_round = ((totals[:rank] + totals[rank : 2 * rank]) * inv_row).astype(BF)
+    chip_features = lax.dynamic_index_in_dim(features, chip, 0, keepdims=False)
+    own_scaled = half(chip_features, core, block, 1)
+    low_part = select(dot("jd,td->jt", downs, chip_features))
+    low_round = (jnp.sum(gather(low_part, CHIPS, n_chips), axis=0) * inv_row).astype(BF)
+    partner_scaled = swap(half(chip_features, other, block, 1))
     low_wide = widen(low_round, own_mask)
 
     target = lax.dynamic_slice(

time: 202 us -> 224 us (1.11)
  waiting for transfers between devices: 42.3 us -> 57.8 us
  blocking collectives: 32.3 us -> 35.1 us
  other arithmetic: 10.9 us -> 13.7 us
    all_to_all x4 -> x7, waiting for transfers between devices: 6.68 us -> 17.1 us  [exchange(): return lax.all_to_all(value, axis, 0, 0)]
    all_to_all x4 -> x7, starting transfers between devices: 39.6 us -> 46 us  [exchange(): return lax.all_to_all(value, axis, 0, 0)]
    ppermute x7 -> x8, starting transfers between devices: 34.4 us -> 29.6 us  [shift(): lax.ppermute(value, 'yh', [(i, (i + step) % n_yh) for i in range(n_yh)])]
    ppermute x7 -> x8, waiting for transfers between devices: 32.4 us -> 37 us  [shift(): lax.ppermute(value, 'yh', [(i, (i + step) % n_yh) for i in range(n_yh)])]
    all_to_all x1, blocking collectives: 32.3 us -> 35.1 us  [exchange(): return lax.all_to_all(value, axis, 0, 0)]
    dot_general x11 -> x10, matrix products: 11.8 us -> 9.98 us  [dot(): return jnp.einsum(subscripts, left, right, preferred_element_type=F32)]
  transfers between devices with their start and end apart: 18 -> 22, of which waited for: 10 -> 12; matrix products, arithmetic and copies ran while one was open for 14% -> 12% of each run, Pallas kernels for 0% -> 0%
where the time goes in v4:
time: 224 us; the launch traced here: 222 us
  starting transfers between devices  89.5 us (40%)
  waiting for transfers between devices  57.8 us (26%)
  blocking collectives  35.1 us (16%)
  local copies, waits for them, and re-layouts  14.1 us (6%)
  other arithmetic  13.7 us (6%)
  matrix products  9.98 us (4%)
    all_to_all x7, starting transfers between devices, exchange(): return lax.all_to_all(value, axis, 0, 0)  46 us
    ppermute x8, waiting for transfers between devices, shift(): lax.ppermute(value, 'yh', [(i, (i + step) % n_yh) for i in range(n_yh)])  37 us
    all_to_all x1, blocking collectives, exchange(): return lax.all_to_all(value, axis, 0, 0)  35.1 us
    ppermute x8, starting transfers between devices, shift(): lax.ppermute(value, 'yh', [(i, (i + step) % n_yh) for i in range(n_yh)])  29.6 us
    all_to_all x7, waiting for transfers between devices, exchange(): return lax.all_to_all(value, axis, 0, 0)  17.1 us
    ppermute x7, starting transfers between devices, swap(): return lax.ppermute(value, 'c', [(0, 1), (1, 0)])  13.9 us
    dot_general x10, matrix products, dot(): return jnp.einsum(subscripts, left, right, preferred_element_type=F32)  9.98 us
    concatenate x1, other arithmetic, shards(): both_weights = jnp.concatenate([draft_weight, draft_weight_other], axis=1)  7.29 us
  transfers between devices with their start and end apart: 22, of which 12 were waited for; matrix products, arithmetic and copies ran while one was open for 12% of the time, Pallas kernels for 0%

profile of v4, /device:TPU:6, one launch (start us, length us, event | category | flops | bytes accessed | tf_op | source)
XLA Modules:
  0.0 221.6 jit_solution(4024951948594173886)
XLA Ops:
  0.6 1.0 fusion.13
  1.6 1.2 broadcast_in_dim.94
  2.8 10.3 %all-to-all-start = ((bf16[8,160,512]{2,1,0:T(8,128)(2,1)}), bf16[8,160,512]{2,1,0:T(8,128)(2,1)S(1)}, u32[]{:S(2)}, u32[]{:S(2)}) async-start(bf16[8,160,512]{2,1,0:T(8,128)(2,1)} %broadcast_in_dim.94), calls=%async_computation | async-start | bytes 2621440 | tf_op jit(solution)/shard_map/all_to_all | solution.py:28
  13.1 4.5 %collective-permute-start.1 = (bf16[512,256]{1,0:T(8,128)(2,1)S(1)}, bf16[512,256]{1,0:T(8,128)(2,1)S(1)}, u32[]{:S(2)}, u32[]{:S(2)}) collective-permute-start(bf16[512,256]{1,0:T(8,128)(2,1)S(1)} %copy-done), channel_id=1, source_target_pairs={{0,16},{16,32},{32,48},{48,0},{1,17},{17,33},{33,49},{49,1},{2,18}... | collective-permute-start | bytes 786440 | tf_op jit(solution)/shard_map/ppermute | solution.py:62
  17.6 3.6 %collective-permute-start.3 = (bf16[512,256]{1,0:T(8,128)(2,1)S(1)}, bf16[512,256]{1,0:T(8,128)(2,1)S(1)}, u32[]{:S(2)}, u32[]{:S(2)}) collective-permute-start(bf16[512,256]{1,0:T(8,128)(2,1)S(1)} %copy-done), channel_id=1, source_target_pairs={{0,48},{16,0},{32,16},{48,32},{1,49},{17,1},{33,17},{49,33},{2,50}... | collective-permute-start | bytes 786440 | tf_op jit(solution)/shard_map/ppermute | solution.py:62
  21.3 1.9 collective-permute-start
  23.5 1.0 collective-permute-done
  24.5 10.3 %collective-permute-done.3 = bf16[512,256]{1,0:T(8,128)(2,1)S(1)} collective-permute-done((bf16[512,256]{1,0:T(8,128)(2,1)S(1)}, bf16[512,256]{1,0:T(8,128)(2,1)S(1)}, u32[]{:S(2)}, u32[]{:S(2)}) %collective-permute-start.3) | collective-permute-done | bytes 262176 | tf_op jit(solution)/shard_map/ppermute | solution.py:62
  34.8 3.9 %collective-permute-start.4 = (bf16[256,256]{1,0:T(8,128)(2,1)S(1)}, bf16[256,256]{1,0:T(8,128)(2,1)S(1)}, u32[]{:S(2)}, u32[]{:S(2)}) collective-permute-start(bf16[256,256]{1,0:T(8,128)(2,1)S(1)} %slice.161), channel_id=1, source_target_pairs={{0,48},{16,0},{32,16},{48,32},{1,49},{17,1},{33,17},{49,33},{2,50}... | collective-permute-start | bytes 393224 | tf_op jit(solution)/shard_map/ppermute | solution.py:62
  38.8 3.0 %collective-permute-start.2 = (bf16[256,256]{1,0:T(8,128)(2,1)S(1)}, bf16[256,256]{1,0:T(8,128)(2,1)S(1)}, u32[]{:S(2)}, u32[]{:S(2)}) collective-permute-start(bf16[256,256]{1,0:T(8,128)(2,1)S(1)} %slice.160), channel_id=1, source_target_pairs={{0,16},{16,32},{32,48},{48,0},{1,17},{17,33},{33,49},{49,1},{2,18}... | collective-permute-start | bytes 393224 | tf_op jit(solution)/shard_map/ppermute | solution.py:62
  41.8 2.1 collective-permute-done.4
  43.9 3.9 %collective-permute-done.2 = bf16[256,256]{1,0:T(8,128)(2,1)S(1)} collective-permute-done((bf16[256,256]{1,0:T(8,128)(2,1)S(1)}, bf16[256,256]{1,0:T(8,128)(2,1)S(1)}, u32[]{:S(2)}, u32[]{:S(2)}) %collective-permute-start.2) | collective-permute-done | bytes 131104 | tf_op jit(solution)/shard_map/ppermute | solution.py:62
  48.1 0.7 convolution_convert_fusion
  48.8 1.9 collective-permute-start.5
  50.7 2.6 %collective-permute-done.5 = bf16[512,1024]{1,0:T(8,128)(2,1)S(1)} collective-permute-done((bf16[512,1024]{1,0:T(8,128)(2,1)S(1)}, bf16[512,1024]{1,0:T(8,128)(2,1)S(1)}, u32[]{:S(2)}, u32[]{:S(2)}) %collective-permute-start.5) | collective-permute-done | bytes 1048608 | tf_op jit(solution)/shard_map/ppermute | solution.py:24
  53.4 0.7 fusion
  54.1 1.2 copy.213
  55.3 5.4 %all-to-all-start.1 = ((bf16[8,512,128]{2,1,0:T(8,128)(2,1)}), bf16[8,512,128]{2,1,0:T(8,128)(2,1)S(1)}, u32[]{:S(2)}, u32[]{:S(2)}) async-start(bf16[8,512,128]{2,1,0:T(8,128)(2,1)} %bitcast.121), calls=%async_computation.1 | async-start | bytes 2097152 | tf_op jit(solution)/shard_map/all_to_all | solution.py:28
  60.7 1.9 collective-permute-start.11
  62.7 0.6 fusion.44
  63.4 0.7 copy.191
  64.1 10.0 %all-to-all-done.1 = bf16[8,512,128]{2,1,0:T(8,128)(2,1)S(1)} async-done(((bf16[8,512,128]{2,1,0:T(8,128)(2,1)}), bf16[8,512,128]{2,1,0:T(8,128)(2,1)S(1)}, u32[]{:S(2)}, u32[]{:S(2)}) %all-to-all-start.1) | async-done | bytes 1048608 | tf_op jit(solution)/shard_map/all_to_all | solution.py:28
  74.1 5.4 %all-to-all-start.2 = ((bf16[8,80,128]{2,1,0:T(8,128)(2,1)}), bf16[8,80,128]{2,1,0:T(8,128)(2,1)S(1)}, u32[]{:S(2)}, u32[]{:S(2)}) async-start(bf16[8,80,128]{2,1,0:T(8,128)(2,1)} %copy.191), calls=%async_computation.2 | async-start | bytes 327680 | tf_op jit(solution)/shard_map/all_to_all | solution.py:28
  79.6 0.8 reduce_sum.90
  80.4 3.6 %all-to-all-done.2 = bf16[8,80,128]{2,1,0:T(8,128)(2,1)S(1)} async-done(((bf16[8,80,128]{2,1,0:T(8,128)(2,1)}), bf16[8,80,128]{2,1,0:T(8,128)(2,1)S(1)}, u32[]{:S(2)}, u32[]{:S(2)}) %all-to-all-start.2) | async-done | bytes 163872 | tf_op jit(solution)/shard_map/all_to_all | solution.py:28
  84.0 6.3 %all-to-all-start.3 = ((bf16[8,64,128]{2,1,0:T(8,128)(2,1)}), bf16[8,64,128]{2,1,0:T(8,128)(2,1)S(1)}, u32[]{:S(2)}, u32[]{:S(2)}) async-start(bf16[8,64,128]{2,1,0:T(8,128)(2,1)} %bitcast.8), calls=%async_computation.3 | async-start | bytes 262144 | tf_op jit(solution)/shard_map/all_to_all | solution.py:28
  90.3 0.7 fusion.63
  90.9 0.6 dynamic_slice.59
  91.5 4.9 %collective-permute-start.6 = (bf16[128,768]{1,0:T(8,128)(2,1)S(1)}, bf16[128,768]{1,0:T(8,128)(2,1)S(1)}, u32[]{:S(2)}, u32[]{:S(2)}) collective-permute-start(bf16[128,768]{1,0:T(8,128)(2,1)S(1)} %bitcast.134), channel_id=1, source_target_pairs={{0,16},{16,32},{32,48},{48,0},{1,17},{17,33},{33,49},{49,1},{2,18}... | collective-permute-start | bytes 589832 | tf_op jit(solution)/shard_map/ppermute | solution.py:62
  96.4 3.1 %collective-permute-start.7 = (bf16[128,768]{1,0:T(8,128)(2,1)S(1)}, bf16[128,768]{1,0:T(8,128)(2,1)S(1)}, u32[]{:S(2)}, u32[]{:S(2)}) collective-permute-start(bf16[128,768]{1,0:T(8,128)(2,1)S(1)} %bitcast.135), channel_id=1, source_target_pairs={{0,48},{16,0},{32,16},{48,32},{1,49},{17,1},{33,17},{49,33},{2,50}... | collective-permute-start | bytes 589832 | tf_op jit(solution)/shard_map/ppermute | solution.py:62
  100.0 1.4 collective-permute-done.6
  101.5 8.4 %collective-permute-done.7 = bf16[128,768]{1,0:T(8,128)(2,1)S(1)} collective-permute-done((bf16[128,768]{1,0:T(8,128)(2,1)S(1)}, bf16[128,768]{1,0:T(8,128)(2,1)S(1)}, u32[]{:S(2)}, u32[]{:S(2)}) %collective-permute-start.7) | collective-permute-done | bytes 196640 | tf_op jit(solution)/shard_map/ppermute | solution.py:62
  109.9 1.2 broadcast_in_dim.102
  111.1 5.7 %all-to-all-start.4 = ((bf16[8,64,1152]{2,1,0:T(8,128)(2,1)}), bf16[8,64,1152]{2,1,0:T(8,128)(2,1)S(1)}, u32[]{:S(2)}, u32[]{:S(2)}) async-start(bf16[8,64,1152]{2,1,0:T(8,128)(2,1)} %broadcast_in_dim.102), calls=%async_computation.4 | async-start | bytes 2359296 | tf_op jit(solution)/shard_map/all_to_all | solution.py:28
  116.9 2.7 %collective-permute-start.9 = (bf16[64,768]{1,0:T(8,128)(2,1)S(1)}, bf16[64,768]{1,0:T(8,128)(2,1)S(1)}, u32[]{:S(2)}, u32[]{:S(2)}) collective-permute-start(bf16[64,768]{1,0:T(8,128)(2,1)S(1)} %slice.137), channel_id=1, source_target_pairs={{0,48},{16,0},{32,16},{48,32},{1,49},{17,1},{33,17},{49,33},{2,50}... | collective-permute-start | bytes 294920 | tf_op jit(solution)/shard_map/ppermute | solution.py:62
  119.6 4.0 %collective-permute-start.8 = (bf16[64,768]{1,0:T(8,128)(2,1)S(1)}, bf16[64,768]{1,0:T(8,128)(2,1)S(1)}, u32[]{:S(2)}, u32[]{:S(2)}) collective-permute-start(bf16[64,768]{1,0:T(8,128)(2,1)S(1)} %slice.136), channel_id=1, source_target_pairs={{0,16},{16,32},{32,48},{48,0},{1,17},{17,33},{33,49},{49,1},{2,18}... | collective-permute-start | bytes 294920 | tf_op jit(solution)/shard_map/ppermute | solution.py:62
  123.7 0.7 collective-permute-done.9
  124.4 10.2 %collective-permute-done.8 = bf16[64,768]{1,0:T(8,128)(2,1)S(1)} collective-permute-done((bf16[64,768]{1,0:T(8,128)(2,1)S(1)}, bf16[64,768]{1,0:T(8,128)(2,1)S(1)}, u32[]{:S(2)}, u32[]{:S(2)}) %collective-permute-start.8) | collective-permute-done | bytes 98336 | tf_op jit(solution)/shard_map/ppermute | solution.py:62
  134.6 1.9 collective-permute-start.10
  136.6 7.3 %pad_maximum_fusion = bf16[8192,512]{1,0:T(8,128)(2,1)} fusion(bf16[8192,256]{1,0:T(8,128)(2,1)} %collective-permute-done.11, bf16[8192,256]{1,0:T(8,128)(2,1)} %param.13), kind=kLoop, calls=%fused_computation | loop fusion | flops 16777216 | bytes 16777216 | tf_op jit(solution)/shard_map/concatenate | solution.py:162
  143.9 0.7 slice.173
  144.6 1.1 broadcast_select_fusion.1
  146.2 0.7 copy.194
  146.9 0.5 reshape.258
  147.5 1.7 convolution_select_fusion.1
  149.3 0.7 reshape.268
  150.1 7.1 %all-to-all-start.5 = ((f32[8,1,1024]{2,1,0:T(1,128)}), f32[8,1,1024]{2,1,0:T(1,128)S(1)}, u32[]{:S(2)}, u32[]{:S(2)}) async-start(f32[8,1,1024]{2,1,0:T(1,128)} %reshape.268), calls=%async_computation.5 | async-start | bytes 65536 | tf_op jit(solution)/shard_map/all_to_all | solution.py:28
  157.5 1.9 collective-permute-start.12
  159.8 2.4 %collective-permute-start.14 = (bf16[64,512]{1,0:T(8,128)(2,1)S(1)}, bf16[64,512]{1,0:T(8,128)(2,1)S(1)}, u32[]{:S(2)}, u32[]{:S(2)}) collective-permute-start(bf16[64,512]{1,0:T(8,128)(2,1)S(1)} %dynamic-slice_bitcast_fusion), channel_id=1, source_target_pairs={{0,1},{1,0},{2,3},{3,2},{4,5},{5,4},{6,7},{7,6},{8,9},{9,8},{10,11... | collective-permute-start | bytes 196616 | tf_op jit(solution)/shard_map/ppermute | solution.py:24
  162.3 0.5 broadcast.248
  162.8 0.7 reduce.4
  164.1 4.9 %fusion.7 = bf16[64,512]{1,0:T(8,128)(2,1)S(1)} fusion(f32[64,512]{1,0:T(8,128)S(1)} %convolution_multiply_fusion, bf16[8,64,1024]{2,1,0:T(8,128)(2,1)S(1)} %reshape.258, bf16[8,1024,512]{2,1,0:T(8,128)(2,1)} %bitcast.125, bf16[64,256]{1,0:T(8,128)(2,1)S(1)} %get-tuple-element.41, bf16[64,256]{1,0:T(8,128)(2,1)S(1)} %get-tuple-element.40, ...), kind=kOutput, calls=%fused_computation.17 | convolution fusion | flops 537165824 | bytes 9699840 | tf_op jit(solution)/shard_map/ktd,kdn->tn/dot_general | solution.py:20
  169.7 1.9 collective-permute-start.13
  171.7 0.3 fusion.27
  172.0 0.7 reshape.270
  172.7 5.8 %all-to-all-start.6 = ((f32[16,1,1024]{2,1,0:T(1,128)}), f32[16,1,1024]{2,1,0:T(1,128)S(1)}, u32[]{:S(2)}, u32[]{:S(2)}) async-start(f32[16,1,1024]{2,1,0:T(1,128)} %reshape.270), calls=%async_computation.6 | async-start | bytes 131072 | tf_op jit(solution)/shard_map/all_to_all | solution.py:28
  178.8 0.3 fusion.2
  179.3 3.6 %all-to-all-done.6 = f32[16,1,1024]{2,1,0:T(1,128)S(1)} async-done(((f32[16,1,1024]{2,1,0:T(1,128)}), f32[16,1,1024]{2,1,0:T(1,128)S(1)}, u32[]{:S(2)}, u32[]{:S(2)}) %all-to-all-start.6) | async-done | bytes 65568 | tf_op jit(solution)/shard_map/all_to_all | solution.py:28
  182.8 0.8 reduce.5
  183.9 0.4 fusion.17
  184.5 0.4 fusion.1
  185.2 35.1 %all_to_all.40 = bf16[32,16,768]{2,1,0:T(8,128)(2,1)S(1)} all-to-all(bf16[32,16,768]{2,1,0:T(8,128)(2,1)S(1)} %bitcast.131), channel_id=1, replica_groups=mesh['z'=8,'yh'=4,'yl'=2,'x'=4,'c'=2] {'yh','z'}, dimensions={0} | all-to-all | bytes 1572864 | tf_op jit(solution)/shard_map/all_to_all | solution.py:28
  220.4 0.6 slice_bitcast_fusion
  221.0 0.6 slice_bitcast_fusion.1
  (119 shorter events, 5.4 us)
Async XLA Ops:
  1.6 11.5 %copy-start = (bf16[512,256]{1,0:T(8,128)(2,1)S(1)}, bf16[512,256]{1,0:T(8,128)(2,1)}, u32[]{:S(2)}) copy-start(bf16[512,256]{1,0:T(8,128)(2,1)} %param.10) | copy-start | bytes 786436
  1.6 19.6 %copy-start.2 = (bf16[128,512]{1,0:T(8,128)(2,1)S(1)}, bf16[128,512]{1,0:T(8,128)(2,1)}, u32[]{:S(2)}) copy-start(bf16[128,512]{1,0:T(8,128)(2,1)} %param.11) | copy-start | bytes 393220
  1.6 19.7 %copy-start.7 = (bf16[512]{0:T(512)(128)(2,1)S(1)}, bf16[512]{0:T(512)(128)(2,1)}, u32[]{:S(2)}) copy-start(bf16[512]{0:T(512)(128)(2,1)} %param.12) | copy-start | bytes 3076
  2.8 45.1 %all-to-all-start = ((bf16[8,160,512]{2,1,0:T(8,128)(2,1)}), bf16[8,160,512]{2,1,0:T(8,128)(2,1)S(1)}, u32[]{:S(2)}, u32[]{:S(2)}) async-start(bf16[8,160,512]{2,1,0:T(8,128)(2,1)} %broadcast_in_dim.94), calls=%async_computation | async-start | bytes 2621440 | tf_op jit(solution)/shard_map/all_to_all | solution.py:28
  13.1 25.6 %collective-permute-start.1 = (bf16[512,256]{1,0:T(8,128)(2,1)S(1)}, bf16[512,256]{1,0:T(8,128)(2,1)S(1)}, u32[]{:S(2)}, u32[]{:S(2)}) collective-permute-start(bf16[512,256]{1,0:T(8,128)(2,1)S(1)} %copy-done), channel_id=1, source_target_pairs={{0,16},{16,32},{32,48},{48,0},{1,17},{17,33},{33,49},{49,1},{2,18}... | collective-permute-start | bytes 786440 | tf_op jit(solution)/shard_map/ppermute | solution.py:62
  17.6 17.2 %collective-permute-start.3 = (bf16[512,256]{1,0:T(8,128)(2,1)S(1)}, bf16[512,256]{1,0:T(8,128)(2,1)S(1)}, u32[]{:S(2)}, u32[]{:S(2)}) collective-permute-start(bf16[512,256]{1,0:T(8,128)(2,1)S(1)} %copy-done), channel_id=1, source_target_pairs={{0,48},{16,0},{32,16},{48,32},{1,49},{17,1},{33,17},{49,33},{2,50}... | collective-permute-start | bytes 786440 | tf_op jit(solution)/shard_map/ppermute | solution.py:62
  21.3 3.2 %collective-permute-start = (bf16[80,512]{1,0:T(8,128)(2,1)S(1)}, bf16[80,512]{1,0:T(8,128)(2,1)S(1)}, u32[]{:S(2)}, u32[]{:S(2)}) collective-permute-start(bf16[80,512]{1,0:T(8,128)(2,1)S(1)} %pad_maximum_fusion.6), channel_id=1, source_target_pairs={{0,1},{1,0},{2,3},{3,2},{4,5},{5,4},{6,7},{7,6},{8,9},{9,8},{10,11... | collective-permute-start | bytes 245768 | tf_op jit(solution)/shard_map/ppermute | solution.py:24
  34.8 9.1 %collective-permute-start.4 = (bf16[256,256]{1,0:T(8,128)(2,1)S(1)}, bf16[256,256]{1,0:T(8,128)(2,1)S(1)}, u32[]{:S(2)}, u32[]{:S(2)}) collective-permute-start(bf16[256,256]{1,0:T(8,128)(2,1)S(1)} %slice.161), channel_id=1, source_target_pairs={{0,48},{16,0},{32,16},{48,32},{1,49},{17,1},{33,17},{49,33},{2,50}... | collective-permute-start | bytes 393224 | tf_op jit(solution)/shard_map/ppermute | solution.py:62
  38.8 9.1 %collective-permute-start.2 = (bf16[256,256]{1,0:T(8,128)(2,1)S(1)}, bf16[256,256]{1,0:T(8,128)(2,1)S(1)}, u32[]{:S(2)}, u32[]{:S(2)}) collective-permute-start(bf16[256,256]{1,0:T(8,128)(2,1)S(1)} %slice.160), channel_id=1, source_target_pairs={{0,16},{16,32},{32,48},{48,0},{1,17},{17,33},{33,49},{49,1},{2,18}... | collective-permute-start | bytes 393224 | tf_op jit(solution)/shard_map/ppermute | solution.py:62
  48.8 4.6 %collective-permute-start.5 = (bf16[512,1024]{1,0:T(8,128)(2,1)S(1)}, bf16[512,1024]{1,0:T(8,128)(2,1)S(1)}, u32[]{:S(2)}, u32[]{:S(2)}) collective-permute-start(bf16[512,1024]{1,0:T(8,128)(2,1)S(1)} %convolution_convert_fusion), channel_id=1, source_target_pairs={{0,1},{1,0},{2,3},{3,2},{4,5},{5,4},{6,7},{7,6},{8,9},{9,8},{10,11... | collective-permute-start | bytes 3145736 | tf_op jit(solution)/shard_map/ppermute | solution.py:24
  54.1 8.6 %copy-start.9 = (s32[32]{0:T(128)S(1)}, s32[32]{0:T(128)}, u32[]{:S(2)}) copy-start(s32[32]{0:T(128)} %param.17) | copy-start | bytes 388
  54.1 8.6 %copy-start.4 = (s32[128]{0:T(128)S(1)}, s32[128]{0:T(128)}, u32[]{:S(2)}) copy-start(s32[128]{0:T(128)} %param.16) | copy-start | bytes 1540
  55.3 18.8 %all-to-all-start.1 = ((bf16[8,512,128]{2,1,0:T(8,128)(2,1)}), bf16[8,512,128]{2,1,0:T(8,128)(2,1)S(1)}, u32[]{:S(2)}, u32[]{:S(2)}) async-start(bf16[8,512,128]{2,1,0:T(8,128)(2,1)} %bitcast.121), calls=%async_computation.1 | async-start | bytes 2097152 | tf_op jit(solution)/shard_map/all_to_all | solution.py:28
  60.7 75.8 %collective-permute-start.11 = (bf16[8192,256]{1,0:T(8,128)(2,1)}, bf16[8192,256]{1,0:T(8,128)(2,1)}, u32[]{:S(2)}, u32[]{:S(2)}) collective-permute-start(bf16[8192,256]{1,0:T(8,128)(2,1)} %param.13), channel_id=1, source_target_pairs={{0,1},{1,0},{2,3},{3,2},{4,5},{5,4},{6,7},{7,6},{8,9},{9,8},{10,11... | collective-permute-start | bytes 12582920 | tf_op jit(solution)/shard_map/ppermute | solution.py:24
  74.1 9.9 %all-to-all-start.2 = ((bf16[8,80,128]{2,1,0:T(8,128)(2,1)}), bf16[8,80,128]{2,1,0:T(8,128)(2,1)S(1)}, u32[]{:S(2)}, u32[]{:S(2)}) async-start(bf16[8,80,128]{2,1,0:T(8,128)(2,1)} %copy.191), calls=%async_computation.2 | async-start | bytes 327680 | tf_op jit(solution)/shard_map/all_to_all | solution.py:28
  84.0 15.5 %all-to-all-start.3 = ((bf16[8,64,128]{2,1,0:T(8,128)(2,1)}), bf16[8,64,128]{2,1,0:T(8,128)(2,1)S(1)}, u32[]{:S(2)}, u32[]{:S(2)}) async-start(bf16[8,64,128]{2,1,0:T(8,128)(2,1)} %bitcast.8), calls=%async_computation.3 | async-start | bytes 262144 | tf_op jit(solution)/shard_map/all_to_all | solution.py:28
  91.5 10.0 %collective-permute-start.6 = (bf16[128,768]{1,0:T(8,128)(2,1)S(1)}, bf16[128,768]{1,0:T(8,128)(2,1)S(1)}, u32[]{:S(2)}, u32[]{:S(2)}) collective-permute-start(bf16[128,768]{1,0:T(8,128)(2,1)S(1)} %bitcast.134), channel_id=1, source_target_pairs={{0,16},{16,32},{32,48},{48,0},{1,17},{17,33},{33,49},{49,1},{2,18}... | collective-permute-start | bytes 589832 | tf_op jit(solution)/shard_map/ppermute | solution.py:62
  96.4 13.5 %collective-permute-start.7 = (bf16[128,768]{1,0:T(8,128)(2,1)S(1)}, bf16[128,768]{1,0:T(8,128)(2,1)S(1)}, u32[]{:S(2)}, u32[]{:S(2)}) collective-permute-start(bf16[128,768]{1,0:T(8,128)(2,1)S(1)} %bitcast.135), channel_id=1, source_target_pairs={{0,48},{16,0},{32,16},{48,32},{1,49},{17,1},{33,17},{49,33},{2,50}... | collective-permute-start | bytes 589832 | tf_op jit(solution)/shard_map/ppermute | solution.py:62
  111.1 34.6 %all-to-all-start.4 = ((bf16[8,64,1152]{2,1,0:T(8,128)(2,1)}), bf16[8,64,1152]{2,1,0:T(8,128)(2,1)S(1)}, u32[]{:S(2)}, u32[]{:S(2)}) async-start(bf16[8,64,1152]{2,1,0:T(8,128)(2,1)} %broadcast_in_dim.102), calls=%async_computation.4 | async-start | bytes 2359296 | tf_op jit(solution)/shard_map/all_to_all | solution.py:28
  116.9 7.5 %collective-permute-start.9 = (bf16[64,768]{1,0:T(8,128)(2,1)S(1)}, bf16[64,768]{1,0:T(8,128)(2,1)S(1)}, u32[]{:S(2)}, u32[]{:S(2)}) collective-permute-start(bf16[64,768]{1,0:T(8,128)(2,1)S(1)} %slice.137), channel_id=1, source_target_pairs={{0,48},{16,0},{32,16},{48,32},{1,49},{17,1},{33,17},{49,33},{2,50}... | collective-permute-start | bytes 294920 | tf_op jit(solution)/shard_map/ppermute | solution.py:62
  119.6 14.9 %collective-permute-start.8 = (bf16[64,768]{1,0:T(8,128)(2,1)S(1)}, bf16[64,768]{1,0:T(8,128)(2,1)S(1)}, u32[]{:S(2)}, u32[]{:S(2)}) collective-permute-start(bf16[64,768]{1,0:T(8,128)(2,1)S(1)} %slice.136), channel_id=1, source_target_pairs={{0,16},{16,32},{32,48},{48,0},{1,17},{17,33},{33,49},{49,1},{2,18}... | collective-permute-start | bytes 294920 | tf_op jit(solution)/shard_map/ppermute | solution.py:62
  134.6 9.3 %collective-permute-start.10 = (bf16[512,768]{1,0:T(8,128)(2,1)S(1)}, bf16[512,768]{1,0:T(8,128)(2,1)S(1)}, u32[]{:S(2)}, u32[]{:S(2)}) collective-permute-start(bf16[512,768]{1,0:T(8,128)(2,1)S(1)} %bitcast.128), channel_id=1, source_target_pairs={{0,1},{1,0},{2,3},{3,2},{4,5},{5,4},{6,7},{7,6},{8,9},{9,8},{10,11... | collective-permute-start | bytes 2359304 | tf_op jit(solution)/shard_map/ppermute | solution.py:24
  147.4 16.4 %copy-start.1 = (bf16[512,256]{1,0:T(8,128)(2,1)S(1)}, bf16[512,256]{1,0:T(8,128)(2,1)}, u32[]{:S(2)}) copy-start(bf16[512,256]{1,0:T(8,128)(2,1)} %slice.173) | copy-start | bytes 786436
  147.4 16.4 %copy-start.3 = (s32[512]{0:T(512)S(1)}, s32[512]{0:T(512)}, u32[]{:S(2)}) copy-start(s32[512]{0:T(512)} %fusion.44) | copy-start | bytes 6148
  147.5 16.4 %copy-start.6 = (s32[64]{0:T(128)S(1)}, s32[64]{0:T(128)}, u32[]{:S(2)}) copy-start(s32[64]{0:T(128)} %get-tuple-element.47) | copy-start | bytes 772
  149.1 14.9 %copy-start.8 = (f32[64]{0:T(128)S(1)}, f32[64]{0:T(128)}, u32[]{:S(2)}) copy-start(f32[64]{0:T(128)} %dynamic_slice.59) | copy-start | bytes 772
  150.1 12.3 %all-to-all-start.5 = ((f32[8,1,1024]{2,1,0:T(1,128)}), f32[8,1,1024]{2,1,0:T(1,128)S(1)}, u32[]{:S(2)}, u32[]{:S(2)}) async-start(f32[8,1,1024]{2,1,0:T(1,128)} %reshape.268), calls=%async_computation.5 | async-start | bytes 65536 | tf_op jit(solution)/shard_map/all_to_all | solution.py:28
  157.5 4.7 %collective-permute-start.12 = (bf16[16,512]{1,0:T(8,128)(2,1)S(1)}, bf16[16,512]{1,0:T(8,128)(2,1)S(1)}, u32[]{:S(2)}, u32[]{:S(2)}) collective-permute-start(bf16[16,512]{1,0:T(8,128)(2,1)S(1)} %slice.181), channel_id=1, source_target_pairs={{0,1},{1,0},{2,3},{3,2},{4,5},{5,4},{6,7},{7,6},{8,9},{9,8},{10,11... | collective-permute-start | bytes 49160 | tf_op jit(solution)/shard_map/ppermute | solution.py:24
  159.8 24.7 %collective-permute-start.14 = (bf16[64,512]{1,0:T(8,128)(2,1)S(1)}, bf16[64,512]{1,0:T(8,128)(2,1)S(1)}, u32[]{:S(2)}, u32[]{:S(2)}) collective-permute-start(bf16[64,512]{1,0:T(8,128)(2,1)S(1)} %dynamic-slice_bitcast_fusion), channel_id=1, source_target_pairs={{0,1},{1,0},{2,3},{3,2},{4,5},{5,4},{6,7},{7,6},{8,9},{9,8},{10,11... | collective-permute-start | bytes 196616 | tf_op jit(solution)/shard_map/ppermute | solution.py:24
  169.0 9.7 %copy-start.5 = (s32[64]{0:T(128)S(1)}, s32[64]{0:T(128)}, u32[]{:S(2)}) copy-start(s32[64]{0:T(128)} %get-tuple-element.46) | copy-start | bytes 772
  169.7 8.8 %collective-permute-start.13 = (bf16[64,384]{1,0:T(8,128)(2,1)S(1)}, bf16[64,384]{1,0:T(8,128)(2,1)S(1)}, u32[]{:S(2)}, u32[]{:S(2)}) collective-permute-start(bf16[64,384]{1,0:T(8,128)(2,1)S(1)} %concatenate.67), channel_id=1, source_target_pairs={{0,1},{1,0},{2,3},{3,2},{4,5},{5,4},{6,7},{7,6},{8,9},{9,8},{10,11... | collective-permute-start | bytes 147464 | tf_op jit(solution)/shard_map/ppermute | solution.py:24
  172.7 10.1 %all-to-all-start.6 = ((f32[16,1,1024]{2,1,0:T(1,128)}), f32[16,1,1024]{2,1,0:T(1,128)S(1)}, u32[]{:S(2)}, u32[]{:S(2)}) async-start(f32[16,1,1024]{2,1,0:T(1,128)} %reshape.270), calls=%async_computation.6 | async-start | bytes 131072 | tf_op jit(solution)/shard_map/all_to_all | solution.py:28

commit v5 on v4

--- a/solution.py
+++ b/solution.py
@@ -61,20 +61,16 @@
     def shift(value, step):
         return lax.ppermute(value, "yh", [(i, (i + step) % n_yh) for i in range(n_yh)])
 
-    def farther(before, after):
-        size = before.shape[0] // 2
-        return jnp.concatenate([shift(before[:size], 1), shift(after[size:], -1)], axis=0)
-
     def ordered(own, others):
         return jnp.where(first, own, others), jnp.where(first, others, own)
 
     upper = jnp.concatenate([up.T, jnp.zeros((rank, block - out_block), BF)], axis=1)
     joined = gather(jnp.concatenate([attention, down.T, upper], axis=0), "z", n_z)
-    before, after = shift(output_projection, 1), shift(output_projection, -1)
     proj = jnp.zeros((block, n_yh * cols), BF)
-    for step, piece in enumerate([output_projection, before, farther(before, after), after]):
-        proj = lax.dynamic_update_slice(proj, piece, (0, (yh - step) % n_yh * cols))
-    draft_weight_other = swap(draft_weight)
+    for step in range(n_yh):
+        part = shift(output_projection, step) if step else output_projection
+        proj = lax.dynamic_update_slice(proj, part, (0, (yh - step) % n_yh * cols))
+    both_weights = jnp.concatenate([draft_weight, swap(draft_weight)], axis=1)
     pad = jnp.broadcast_to(gain[None], (16, block))
     kept = swap(jnp.concatenate([half(residual, other, mine), pad], axis=0))
     chip_rows = jnp.concatenate(
@@ -83,7 +79,7 @@
 
     piece = 2 * block // n_chips
     chip_rows = chip_rows.reshape(mine + 16, n_chips, piece).transpose(1, 0, 2)
-    joined, chip_rows = lax.optimization_barrier((joined, chip_rows))
+    joined, chip_rows, both_weights = lax.optimization_barrier((joined, chip_rows, both_weights))
     chip_rows = exchange(chip_rows, CHIPS)
     residual_part, gain_part = chip_rows[:, :mine].astype(F32), chip_rows[:, mine : mine + 1].astype(F32)
 
@@ -93,13 +89,13 @@
     sent = swap(dot("tk,kn->tn", send, proj).astype(BF))
     pair = (dot("tk,kn->tn", keep, proj) + sent.astype(F32)).astype(BF)
     pair = pair.reshape(rows, n_chips, piece).transpose(1, 0, 2)
-    summed = jnp.sum(exchange(pair, CHIPS).astype(F32), axis=0).astype(BF)
     adapters = jnp.concatenate(
         [joined[:, tokens : tokens + rank], joined[:, tokens + rank :, :out_block]], axis=2
     ).reshape(n_z * rank, block + out_block)
-    summed, adapters = lax.optimization_barrier((summed, adapters))
+    pair, adapters, residual_part, gain_part = lax.optimization_barrier((pair, adapters, residual_part, gain_part))
+    summed = jnp.sum(exchange(pair, CHIPS).astype(F32), axis=0).astype(BF)
+    adapters_parts = [adapters] + [shift(adapters, step) for step in range(1, n_yh)]
     projected = exchange(summed.reshape(n_z, mine, piece), "z").astype(F32)
-    before, after = shift(adapters, 1), shift(adapters, -1)
 
     hidden = residual_part + projected
     squares = jnp.sum(jnp.sum(hidden * hidden, axis=0), axis=1, keepdims=True)
@@ -107,7 +103,7 @@
     message = jnp.concatenate(
         [scaled[z] for z in range(n_z)] + [*split(squares), jnp.zeros((mine, 126), BF)], axis=1
     )
-    message, before, after = lax.optimization_barrier((message, before, after))
+    message, *adapters_parts = lax.optimization_barrier((message, *adapters_parts))
     received = gather(message, CHIPS, n_chips)
     features = received[:, :, : 2 * block].reshape(n_chips, mine, n_z, piece)
     features = features.transpose(2, 1, 0, 3).reshape(n_z, mine, 2 * block)
@@ -116,7 +112,7 @@
     inv_row = jnp.broadcast_to(inv_column, (mine, 128)).T[:1]
 
     adapters_all = jnp.zeros((n_yh, n_z * rank, block + out_block), BF)
-    for step, part in enumerate([adapters, before, farther(before, after), after]):
+    for step, part in enumerate(adapters_parts):
         adapters_all = lax.dynamic_update_slice(adapters_all, part[None], ((yh - step) % n_yh, 0, 0))
     adapters_all = adapters_all.reshape(tenants * rank, block + out_block)
     adapters_other = swap(adapters_all)
@@ -159,9 +155,9 @@
     count = jnp.sum(jnp.where(is_tenant, tenant_count.astype(F32)[None, :], 0.0), axis=1)
     weight = half(keep_mask.astype(F32) / count, core, mine)[:, None]
 
-    both_weights = jnp.concatenate([draft_weight, draft_weight_other], axis=1)
-    draft = dot("ktd,kdn->tn", features, both_weights.reshape(n_chips, 2 * block, 2 * out_block)) * inv_column
-    draft = draft + ADAPTER_SCALE * dot("jt,jn->tn", low_wide, ups)
+    draft = dot("ktd,kdn->tn", features, both_weights.reshape(n_chips, 2 * block, 2 * out_block))
+    draft, low_wide = lax.optimization_barrier((draft, low_wide))
+    draft = draft * inv_column + ADAPTER_SCALE * dot("jt,jn->tn", low_wide, ups)
     grad = ((draft - target.astype(F32)) * weight).astype(BF)
     grad_own = grad[:, :out_block]
 

time: 224 us -> 226 us (level)
  blocking collectives: 35.1 us -> 55.7 us
  waiting for transfers between devices: 57.8 us -> 43.4 us
  starting transfers between devices: 89.5 us -> 82.7 us
    all_to_all x1 -> x2, blocking collectives: 35.1 us -> 55.7 us  [exchange(): return lax.all_to_all(value, axis, 0, 0)]
    ppermute x8 -> x6, waiting for transfers between devices: 37 us -> 25.3 us  [shift(): lax.ppermute(value, 'yh', [(i, (i + step) % n_yh) for i in range(n_yh)])]
    all_to_all x7 -> x6, starting transfers between devices: 46 us -> 38.3 us  [exchange(): return lax.all_to_all(value, axis, 0, 0)]
    ppermute x7, waiting for transfers between devices: 3.63 us -> 1.01 us  [swap(): return lax.ppermute(value, 'c', [(0, 1), (1, 0)])]
    ppermute x8 -> x6, starting transfers between devices: 29.6 us -> 30.4 us  [shift(): lax.ppermute(value, 'yh', [(i, (i + step) % n_yh) for i in range(n_yh)])]
    all_to_all x7 -> x6, waiting for transfers between devices: 17.1 us -> 17.1 us  [exchange(): return lax.all_to_all(value, axis, 0, 0)]
  transfers between devices with their start and end apart: 22 -> 19, of which waited for: 12 -> 8; matrix products, arithmetic and copies ran while one was open for 12% -> 12% of each run, Pallas kernels for 0% -> 0%
where the time goes in v5:
time: 226 us; the launch traced here: 224 us
  starting transfers between devices  82.7 us (37%)
  blocking collectives  55.7 us (25%)
  waiting for transfers between devices  43.4 us (19%)
  local copies, waits for them, and re-layouts  15.2 us (7%)
  other arithmetic  13.4 us (6%)
  matrix products  11.7 us (5%)
    all_to_all x2, blocking collectives, exchange(): return lax.all_to_all(value, axis, 0, 0)  55.7 us
    all_to_all x6, starting transfers between devices, exchange(): return lax.all_to_all(value, axis, 0, 0)  38.3 us
    ppermute x6, starting transfers between devices, shift(): lax.ppermute(value, 'yh', [(i, (i + step) % n_yh) for i in range(n_yh)])  30.4 us
    ppermute x6, waiting for transfers between devices, shift(): lax.ppermute(value, 'yh', [(i, (i + step) % n_yh) for i in range(n_yh)])  25.3 us
    all_to_all x6, waiting for transfers between devices, exchange(): return lax.all_to_all(value, axis, 0, 0)  17.1 us
    ppermute x7, starting transfers between devices, swap(): return lax.ppermute(value, 'c', [(0, 1), (1, 0)])  13.9 us
    dot_general x10, matrix products, dot(): return jnp.einsum(subscripts, left, right, preferred_element_type=F32)  11.7 us
    concatenate x1, other arithmetic, shards(): both_weights = jnp.concatenate([draft_weight, swap(draft_weight)], axis=1)  7.3 us
  transfers between devices with their start and end apart: 19, of which 8 were waited for; matrix products, arithmetic and copies ran while one was open for 12% of the time, Pallas kernels for 0%

profile of v5, /device:TPU:6, one launch (start us, length us, event | category | flops | bytes accessed | tf_op | source)
XLA Modules:
  0.0 223.7 jit_solution(18288507522396174319)
XLA Ops:
  0.6 1.9 collective-permute-start.1
  2.6 1.0 fusion.11
  3.6 1.2 broadcast_in_dim.94
  4.8 10.3 %all-to-all-start = ((bf16[8,160,512]{2,1,0:T(8,128)(2,1)}), bf16[8,160,512]{2,1,0:T(8,128)(2,1)S(1)}, u32[]{:S(2)}, u32[]{:S(2)}) async-start(bf16[8,160,512]{2,1,0:T(8,128)(2,1)} %broadcast_in_dim.94), calls=%async_computation | async-start | bytes 2621440 | tf_op jit(solution)/shard_map/all_to_all | solution.py:28
  15.1 4.5 %collective-permute-start.2 = (bf16[512,256]{1,0:T(8,128)(2,1)S(1)}, bf16[512,256]{1,0:T(8,128)(2,1)}, u32[]{:S(2)}, u32[]{:S(2)}) collective-permute-start(bf16[512,256]{1,0:T(8,128)(2,1)S(1)} %copy-done.1), channel_id=1, source_target_pairs={{0,16},{16,32},{32,48},{48,0},{1,17},{17,33},{33,49},{49,1},{2,18}... | collective-permute-start | bytes 786440 | tf_op jit(solution)/shard_map/ppermute | solution.py:62
  19.6 5.9 %collective-permute-start.3 = (bf16[512,256]{1,0:T(8,128)(2,1)S(1)}, bf16[512,256]{1,0:T(8,128)(2,1)S(1)}, u32[]{:S(2)}, u32[]{:S(2)}) collective-permute-start(bf16[512,256]{1,0:T(8,128)(2,1)S(1)} %copy-done.1), channel_id=1, source_target_pairs={{0,32},{16,48},{32,0},{48,16},{1,33},{17,49},{33,1},{49,17},{2,34}... | collective-permute-start | bytes 786440 | tf_op jit(solution)/shard_map/ppermute | solution.py:62
  25.5 5.3 %collective-permute-start.4 = (bf16[512,256]{1,0:T(8,128)(2,1)S(1)}, bf16[512,256]{1,0:T(8,128)(2,1)S(1)}, u32[]{:S(2)}, u32[]{:S(2)}) collective-permute-start(bf16[512,256]{1,0:T(8,128)(2,1)S(1)} %copy-done.1), channel_id=1, source_target_pairs={{0,48},{16,0},{32,16},{48,32},{1,49},{17,1},{33,17},{49,33},{2,50}... | collective-permute-start | bytes 786440 | tf_op jit(solution)/shard_map/ppermute | solution.py:62
  30.9 1.9 collective-permute-start
  33.1 1.0 collective-permute-done
  34.2 1.0 constant_dynamic-update-slice_fusion.2
  35.1 6.7 %collective-permute-done.3 = bf16[512,256]{1,0:T(8,128)(2,1)S(1)} collective-permute-done((bf16[512,256]{1,0:T(8,128)(2,1)S(1)}, bf16[512,256]{1,0:T(8,128)(2,1)S(1)}, u32[]{:S(2)}, u32[]{:S(2)}) %collective-permute-start.3) | collective-permute-done | bytes 262176 | tf_op jit(solution)/shard_map/ppermute | solution.py:62
  41.8 7.6 %collective-permute-done.4 = bf16[512,256]{1,0:T(8,128)(2,1)S(1)} collective-permute-done((bf16[512,256]{1,0:T(8,128)(2,1)S(1)}, bf16[512,256]{1,0:T(8,128)(2,1)S(1)}, u32[]{:S(2)}, u32[]{:S(2)}) %collective-permute-start.4) | collective-permute-done | bytes 262176 | tf_op jit(solution)/shard_map/ppermute | solution.py:62
  49.5 7.3 %pad_maximum_fusion = bf16[8192,512]{1,0:T(8,128)(2,1)} fusion(bf16[8192,256]{1,0:T(8,128)(2,1)} %collective-permute-done.1, bf16[8192,256]{1,0:T(8,128)(2,1)} %param.13), kind=kLoop, calls=%fused_computation | loop fusion | flops 16777216 | bytes 16777216 | tf_op jit(solution)/shard_map/concatenate | solution.py:73
  57.0 1.8 convolution_convert_fusion
  58.7 1.9 collective-permute-start.5
  60.7 0.7 copy.191
  61.3 4.8 %all-to-all-start.1 = ((bf16[8,80,128]{2,1,0:T(8,128)(2,1)}), bf16[8,80,128]{2,1,0:T(8,128)(2,1)S(1)}, u32[]{:S(2)}, u32[]{:S(2)}) async-start(bf16[8,80,128]{2,1,0:T(8,128)(2,1)} %copy.191), calls=%async_computation.1 | async-start | bytes 327680 | tf_op jit(solution)/shard_map/all_to_all | solution.py:28
  66.2 4.6 %all-to-all-done.1 = bf16[8,80,128]{2,1,0:T(8,128)(2,1)S(1)} async-done(((bf16[8,80,128]{2,1,0:T(8,128)(2,1)}), bf16[8,80,128]{2,1,0:T(8,128)(2,1)S(1)}, u32[]{:S(2)}, u32[]{:S(2)}) %all-to-all-start.1) | async-done | bytes 163872 | tf_op jit(solution)/shard_map/all_to_all | solution.py:28
  70.8 1.9 fusion
  73.0 17.9 %all_to_all.40 = bf16[8,512,128]{2,1,0:T(8,128)(2,1)S(1)} all-to-all(bf16[8,512,128]{2,1,0:T(8,128)(2,1)S(1)} %bitcast.116), channel_id=1, replica_groups=mesh['z'=8,'yh'=4,'yl'=2,'x'=4,'c'=2] {'yl','x'}, dimensions={0} | all-to-all | bytes 2097152 | tf_op jit(solution)/shard_map/all_to_all | solution.py:28
  90.9 0.8 reduce_sum.90
  91.7 6.9 %all-to-all-start.3 = ((bf16[8,64,128]{2,1,0:T(8,128)(2,1)}), bf16[8,64,128]{2,1,0:T(8,128)(2,1)S(1)}, u32[]{:S(2)}, u32[]{:S(2)}) async-start(bf16[8,64,128]{2,1,0:T(8,128)(2,1)} %bitcast.7), calls=%async_computation.3 | async-start | bytes 262144 | tf_op jit(solution)/shard_map/all_to_all | solution.py:28
  98.6 4.5 %collective-permute-start.6 = (bf16[128,768]{1,0:T(8,128)(2,1)S(1)}, bf16[128,768]{1,0:T(8,128)(2,1)S(1)}, u32[]{:S(2)}, u32[]{:S(2)}) collective-permute-start(bf16[128,768]{1,0:T(8,128)(2,1)S(1)} %bitcast.125), channel_id=1, source_target_pairs={{0,16},{16,32},{32,48},{48,0},{1,17},{17,33},{33,49},{49,1},{2,18}... | collective-permute-start | bytes 589832 | tf_op jit(solution)/shard_map/ppermute | solution.py:62
  103.1 5.1 %collective-permute-start.7 = (bf16[128,768]{1,0:T(8,128)(2,1)S(1)}, bf16[128,768]{1,0:T(8,128)(2,1)S(1)}, u32[]{:S(2)}, u32[]{:S(2)}) collective-permute-start(bf16[128,768]{1,0:T(8,128)(2,1)S(1)} %bitcast.126), channel_id=1, source_target_pairs={{0,32},{16,48},{32,0},{48,16},{1,33},{17,49},{33,1},{49,17},{2,34}... | collective-permute-start | bytes 589832 | tf_op jit(solution)/shard_map/ppermute | solution.py:62
  108.2 5.2 %collective-permute-start.8 = (bf16[128,768]{1,0:T(8,128)(2,1)S(1)}, bf16[128,768]{1,0:T(8,128)(2,1)S(1)}, u32[]{:S(2)}, u32[]{:S(2)}) collective-permute-start(bf16[128,768]{1,0:T(8,128)(2,1)S(1)} %bitcast.127), channel_id=1, source_target_pairs={{0,48},{16,0},{32,16},{48,32},{1,49},{17,1},{33,17},{49,33},{2,50}... | collective-permute-start | bytes 589832 | tf_op jit(solution)/shard_map/ppermute | solution.py:62
  113.9 6.2 %collective-permute-done.7 = bf16[128,768]{1,0:T(8,128)(2,1)S(1)} collective-permute-done((bf16[128,768]{1,0:T(8,128)(2,1)S(1)}, bf16[128,768]{1,0:T(8,128)(2,1)S(1)}, u32[]{:S(2)}, u32[]{:S(2)}) %collective-permute-start.7) | collective-permute-done | bytes 196640 | tf_op jit(solution)/shard_map/ppermute | solution.py:62
  120.1 4.8 %collective-permute-done.8 = bf16[128,768]{1,0:T(8,128)(2,1)S(1)} collective-permute-done((bf16[128,768]{1,0:T(8,128)(2,1)S(1)}, bf16[128,768]{1,0:T(8,128)(2,1)S(1)}, u32[]{:S(2)}, u32[]{:S(2)}) %collective-permute-start.8) | collective-permute-done | bytes 196640 | tf_op jit(solution)/shard_map/ppermute | solution.py:62
  124.9 1.2 broadcast_in_dim.102
  126.2 5.3 %all-to-all-start.4 = ((bf16[8,64,1152]{2,1,0:T(8,128)(2,1)}), bf16[8,64,1152]{2,1,0:T(8,128)(2,1)S(1)}, u32[]{:S(2)}, u32[]{:S(2)}) async-start(bf16[8,64,1152]{2,1,0:T(8,128)(2,1)} %broadcast_in_dim.102), calls=%async_computation.4 | async-start | bytes 2359296 | tf_op jit(solution)/shard_map/all_to_all | solution.py:28
  131.7 1.9 collective-permute-start.9
  133.9 0.7 dynamic_slice.59
  134.6 0.6 fusion.59
  135.2 0.6 fusion.42
  135.9 0.7 slice.155
  136.6 0.9 broadcast_select_fusion.1
  137.5 8.9 %all-to-all-done.4 = bf16[8,64,1152]{2,1,0:T(8,128)(2,1)S(1)} async-done(((bf16[8,64,1152]{2,1,0:T(8,128)(2,1)}), bf16[8,64,1152]{2,1,0:T(8,128)(2,1)S(1)}, u32[]{:S(2)}, u32[]{:S(2)}) %all-to-all-start.4) | async-done | bytes 1179680 | tf_op jit(solution)/shard_map/all_to_all | solution.py:28
  146.5 0.6 copy.207
  147.1 0.6 copy.208
  147.8 0.3 copy.211
  148.2 0.7 copy.194
  148.8 0.5 reshape.258
  149.4 1.1 convolution_select_fusion.1
  150.7 0.7 reshape.267
  151.4 5.2 %all-to-all-start.5 = ((f32[8,1,1024]{2,1,0:T(1,128)}), f32[8,1,1024]{2,1,0:T(1,128)S(1)}, u32[]{:S(2)}, u32[]{:S(2)}) async-start(f32[8,1,1024]{2,1,0:T(1,128)} %reshape.267), calls=%async_computation.5 | async-start | bytes 65536 | tf_op jit(solution)/shard_map/all_to_all | solution.py:28
  156.8 1.9 collective-permute-start.10
  158.7 5.0 %convolution_bitcast_fusion = f32[64,512]{1,0:T(8,128)S(1)} fusion(bf16[8,64,1024]{2,1,0:T(8,128)(2,1)S(1)} %reshape.258, bf16[8,1024,512]{2,1,0:T(8,128)(2,1)} %bitcast.115), kind=kOutput, calls=%fused_computation.15 | convolution fusion | flops 536870912 | bytes 9568256 | tf_op jit(solution)/shard_map/ktd,kdn->tn/dot_general | solution.py:20
  164.1 2.4 %collective-permute-start.12 = (bf16[64,512]{1,0:T(8,128)(2,1)S(1)}, bf16[64,512]{1,0:T(8,128)(2,1)S(1)}, u32[]{:S(2)}, u32[]{:S(2)}) collective-permute-start(bf16[64,512]{1,0:T(8,128)(2,1)S(1)} %dynamic-slice_bitcast_fusion), channel_id=1, source_target_pairs={{0,1},{1,0},{2,3},{3,2},{4,5},{5,4},{6,7},{7,6},{8,9},{9,8},{10,11... | collective-permute-start | bytes 196616 | tf_op jit(solution)/shard_map/ppermute | solution.py:24
  166.6 0.5 broadcast.248
  167.1 0.7 reduce.4
  168.2 0.2 fusion.6
  168.4 0.3 convolution_select_fusion
  169.1 1.9 collective-permute-start.11
  171.1 0.3 fusion.25
  171.3 0.7 reshape.269
  172.1 5.8 %all-to-all-start.6 = ((f32[16,1,1024]{2,1,0:T(1,128)}), f32[16,1,1024]{2,1,0:T(1,128)S(1)}, u32[]{:S(2)}, u32[]{:S(2)}) async-start(f32[16,1,1024]{2,1,0:T(1,128)} %reshape.269), calls=%async_computation.6 | async-start | bytes 131072 | tf_op jit(solution)/shard_map/all_to_all | solution.py:28
  178.2 0.3 fusion.2
  178.6 3.6 %all-to-all-done.6 = f32[16,1,1024]{2,1,0:T(1,128)S(1)} async-done(((f32[16,1,1024]{2,1,0:T(1,128)}), f32[16,1,1024]{2,1,0:T(1,128)S(1)}, u32[]{:S(2)}, u32[]{:S(2)}) %all-to-all-start.6) | async-done | bytes 65568 | tf_op jit(solution)/shard_map/all_to_all | solution.py:28
  182.2 0.8 reduce.5
  183.3 0.4 fusion.15
  183.9 0.4 fusion.1
  184.3 0.3 copy.206
  184.6 37.8 %all_to_all.41 = bf16[32,16,768]{2,1,0:T(8,128)(2,1)S(1)} all-to-all(bf16[32,16,768]{2,1,0:T(8,128)(2,1)S(1)} %bitcast.122), channel_id=1, replica_groups=mesh['z'=8,'yh'=4,'yl'=2,'x'=4,'c'=2] {'yh','z'}, dimensions={0} | all-to-all | bytes 1572864 | tf_op jit(solution)/shard_map/all_to_all | solution.py:28
  222.5 0.6 slice_bitcast_fusion
  223.1 0.6 slice_bitcast_fusion.1
  (118 shorter events, 4.4 us)
Async XLA Ops:
  0.6 48.8 %collective-permute-start.1 = (bf16[8192,256]{1,0:T(8,128)(2,1)}, bf16[8192,256]{1,0:T(8,128)(2,1)}, u32[]{:S(2)}, u32[]{:S(2)}) collective-permute-start(bf16[8192,256]{1,0:T(8,128)(2,1)} %param.13), channel_id=1, source_target_pairs={{0,1},{1,0},{2,3},{3,2},{4,5},{5,4},{6,7},{7,6},{8,9},{9,8},{10,11... | collective-permute-start | bytes 12582920 | tf_op jit(solution)/shard_map/ppermute | solution.py:24
  3.5 11.6 %copy-start.1 = (bf16[512,256]{1,0:T(8,128)(2,1)S(1)}, bf16[512,256]{1,0:T(8,128)(2,1)}, u32[]{:S(2)}) copy-start(bf16[512,256]{1,0:T(8,128)(2,1)} %param.10) | copy-start | bytes 786436
  3.5 27.3 %copy-start.3 = (bf16[128,512]{1,0:T(8,128)(2,1)S(1)}, bf16[128,512]{1,0:T(8,128)(2,1)}, u32[]{:S(2)}) copy-start(bf16[128,512]{1,0:T(8,128)(2,1)} %param.11) | copy-start | bytes 393220
  3.5 27.3 %copy-start.10 = (bf16[512]{0:T(512)(128)(2,1)S(1)}, bf16[512]{0:T(512)(128)(2,1)}, u32[]{:S(2)}) copy-start(bf16[512]{0:T(512)(128)(2,1)} %param.12) | copy-start | bytes 3076
  4.8 52.0 %all-to-all-start = ((bf16[8,160,512]{2,1,0:T(8,128)(2,1)}), bf16[8,160,512]{2,1,0:T(8,128)(2,1)S(1)}, u32[]{:S(2)}, u32[]{:S(2)}) async-start(bf16[8,160,512]{2,1,0:T(8,128)(2,1)} %broadcast_in_dim.94), calls=%async_computation | async-start | bytes 2621440 | tf_op jit(solution)/shard_map/all_to_all | solution.py:28
  15.1 19.1 %collective-permute-start.2 = (bf16[512,256]{1,0:T(8,128)(2,1)S(1)}, bf16[512,256]{1,0:T(8,128)(2,1)}, u32[]{:S(2)}, u32[]{:S(2)}) collective-permute-start(bf16[512,256]{1,0:T(8,128)(2,1)S(1)} %copy-done.1), channel_id=1, source_target_pairs={{0,16},{16,32},{32,48},{48,0},{1,17},{17,33},{33,49},{49,1},{2,18}... | collective-permute-start | bytes 786440 | tf_op jit(solution)/shard_map/ppermute | solution.py:62
  19.6 22.2 %collective-permute-start.3 = (bf16[512,256]{1,0:T(8,128)(2,1)S(1)}, bf16[512,256]{1,0:T(8,128)(2,1)S(1)}, u32[]{:S(2)}, u32[]{:S(2)}) collective-permute-start(bf16[512,256]{1,0:T(8,128)(2,1)S(1)} %copy-done.1), channel_id=1, source_target_pairs={{0,32},{16,48},{32,0},{48,16},{1,33},{17,49},{33,1},{49,17},{2,34}... | collective-permute-start | bytes 786440 | tf_op jit(solution)/shard_map/ppermute | solution.py:62
  25.5 23.9 %collective-permute-start.4 = (bf16[512,256]{1,0:T(8,128)(2,1)S(1)}, bf16[512,256]{1,0:T(8,128)(2,1)S(1)}, u32[]{:S(2)}, u32[]{:S(2)}) collective-permute-start(bf16[512,256]{1,0:T(8,128)(2,1)S(1)} %copy-done.1), channel_id=1, source_target_pairs={{0,48},{16,0},{32,16},{48,32},{1,49},{17,1},{33,17},{49,33},{2,50}... | collective-permute-start | bytes 786440 | tf_op jit(solution)/shard_map/ppermute | solution.py:62
  30.9 3.2 %collective-permute-start = (bf16[80,512]{1,0:T(8,128)(2,1)S(1)}, bf16[80,512]{1,0:T(8,128)(2,1)S(1)}, u32[]{:S(2)}, u32[]{:S(2)}) collective-permute-start(bf16[80,512]{1,0:T(8,128)(2,1)S(1)} %pad_maximum_fusion.6), channel_id=1, source_target_pairs={{0,1},{1,0},{2,3},{3,2},{4,5},{5,4},{6,7},{7,6},{8,9},{9,8},{10,11... | collective-permute-start | bytes 245768 | tf_op jit(solution)/shard_map/ppermute | solution.py:24
  58.7 12.1 %collective-permute-start.5 = (bf16[512,1024]{1,0:T(8,128)(2,1)}, bf16[512,1024]{1,0:T(8,128)(2,1)}, u32[]{:S(2)}, u32[]{:S(2)}) collective-permute-start(bf16[512,1024]{1,0:T(8,128)(2,1)} %convolution_convert_fusion), channel_id=1, source_target_pairs={{0,1},{1,0},{2,3},{3,2},{4,5},{5,4},{6,7},{7,6},{8,9},{9,8},{10,11... | collective-permute-start | bytes 3145736 | tf_op jit(solution)/shard_map/ppermute | solution.py:24
  61.3 9.4 %all-to-all-start.1 = ((bf16[8,80,128]{2,1,0:T(8,128)(2,1)}), bf16[8,80,128]{2,1,0:T(8,128)(2,1)S(1)}, u32[]{:S(2)}, u32[]{:S(2)}) async-start(bf16[8,80,128]{2,1,0:T(8,128)(2,1)} %copy.191), calls=%async_computation.1 | async-start | bytes 327680 | tf_op jit(solution)/shard_map/all_to_all | solution.py:28
  91.7 21.7 %all-to-all-start.3 = ((bf16[8,64,128]{2,1,0:T(8,128)(2,1)}), bf16[8,64,128]{2,1,0:T(8,128)(2,1)S(1)}, u32[]{:S(2)}, u32[]{:S(2)}) async-start(bf16[8,64,128]{2,1,0:T(8,128)(2,1)} %bitcast.7), calls=%async_computation.3 | async-start | bytes 262144 | tf_op jit(solution)/shard_map/all_to_all | solution.py:28
  98.6 15.3 %collective-permute-start.6 = (bf16[128,768]{1,0:T(8,128)(2,1)S(1)}, bf16[128,768]{1,0:T(8,128)(2,1)S(1)}, u32[]{:S(2)}, u32[]{:S(2)}) collective-permute-start(bf16[128,768]{1,0:T(8,128)(2,1)S(1)} %bitcast.125), channel_id=1, source_target_pairs={{0,16},{16,32},{32,48},{48,0},{1,17},{17,33},{33,49},{49,1},{2,18}... | collective-permute-start | bytes 589832 | tf_op jit(solution)/shard_map/ppermute | solution.py:62
  103.1 17.0 %collective-permute-start.7 = (bf16[128,768]{1,0:T(8,128)(2,1)S(1)}, bf16[128,768]{1,0:T(8,128)(2,1)S(1)}, u32[]{:S(2)}, u32[]{:S(2)}) collective-permute-start(bf16[128,768]{1,0:T(8,128)(2,1)S(1)} %bitcast.126), channel_id=1, source_target_pairs={{0,32},{16,48},{32,0},{48,16},{1,33},{17,49},{33,1},{49,17},{2,34}... | collective-permute-start | bytes 589832 | tf_op jit(solution)/shard_map/ppermute | solution.py:62
  108.2 16.8 %collective-permute-start.8 = (bf16[128,768]{1,0:T(8,128)(2,1)S(1)}, bf16[128,768]{1,0:T(8,128)(2,1)S(1)}, u32[]{:S(2)}, u32[]{:S(2)}) collective-permute-start(bf16[128,768]{1,0:T(8,128)(2,1)S(1)} %bitcast.127), channel_id=1, source_target_pairs={{0,48},{16,0},{32,16},{48,32},{1,49},{17,1},{33,17},{49,33},{2,50}... | collective-permute-start | bytes 589832 | tf_op jit(solution)/shard_map/ppermute | solution.py:62
  126.2 7.5 %copy-start.11 = (s32[32]{0:T(128)S(1)}, s32[32]{0:T(128)}, u32[]{:S(2)}) copy-start(s32[32]{0:T(128)} %param.17) | copy-start | bytes 388
  126.2 7.5 %copy-start.5 = (s32[128]{0:T(128)S(1)}, s32[128]{0:T(128)}, u32[]{:S(2)}) copy-start(s32[128]{0:T(128)} %param.16) | copy-start | bytes 1540
  126.2 20.2 %all-to-all-start.4 = ((bf16[8,64,1152]{2,1,0:T(8,128)(2,1)}), bf16[8,64,1152]{2,1,0:T(8,128)(2,1)S(1)}, u32[]{:S(2)}, u32[]{:S(2)}) async-start(bf16[8,64,1152]{2,1,0:T(8,128)(2,1)} %broadcast_in_dim.102), calls=%async_computation.4 | async-start | bytes 2359296 | tf_op jit(solution)/shard_map/all_to_all | solution.py:28
  131.7 4.2 %collective-permute-start.9 = (bf16[512,768]{1,0:T(8,128)(2,1)S(1)}, bf16[512,768]{1,0:T(8,128)(2,1)S(1)}, u32[]{:S(2)}, u32[]{:S(2)}) collective-permute-start(bf16[512,768]{1,0:T(8,128)(2,1)S(1)} %bitcast.119), channel_id=1, source_target_pairs={{0,1},{1,0},{2,3},{3,2},{4,5},{5,4},{6,7},{7,6},{8,9},{9,8},{10,11... | collective-permute-start | bytes 2359304 | tf_op jit(solution)/shard_map/ppermute | solution.py:24
  148.1 1.2 copy-start
  149.3 7.3 %copy-start.8 = (f32[64,1]{0,1:T(1,128)S(1)}, f32[64,1]{0,1:T(1,128)}, u32[]{:S(2)}) copy-start(f32[64,1]{0,1:T(1,128)} %copy.207) | copy-start | bytes 772
  149.4 7.3 %copy-start.9 = (f32[64,1]{0,1:T(1,128)S(1)}, f32[64,1]{0,1:T(1,128)}, u32[]{:S(2)}) copy-start(f32[64,1]{0,1:T(1,128)} %copy.208) | copy-start | bytes 772
  151.4 15.2 %all-to-all-start.5 = ((f32[8,1,1024]{2,1,0:T(1,128)}), f32[8,1,1024]{2,1,0:T(1,128)S(1)}, u32[]{:S(2)}, u32[]{:S(2)}) async-start(f32[8,1,1024]{2,1,0:T(1,128)} %reshape.267), calls=%async_computation.5 | async-start | bytes 65536 | tf_op jit(solution)/shard_map/all_to_all | solution.py:28
  156.8 9.7 %collective-permute-start.10 = (bf16[16,512]{1,0:T(8,128)(2,1)S(1)}, bf16[16,512]{1,0:T(8,128)(2,1)S(1)}, u32[]{:S(2)}, u32[]{:S(2)}) collective-permute-start(bf16[16,512]{1,0:T(8,128)(2,1)S(1)} %slice.163), channel_id=1, source_target_pairs={{0,1},{1,0},{2,3},{3,2},{4,5},{5,4},{6,7},{7,6},{8,9},{9,8},{10,11... | collective-permute-start | bytes 49160 | tf_op jit(solution)/shard_map/ppermute | solution.py:24
  158.7 9.4 %copy-start.4 = (s32[512]{0:T(512)S(1)}, s32[512]{0:T(512)}, u32[]{:S(2)}) copy-start(s32[512]{0:T(512)} %fusion.42) | copy-start | bytes 6148
  158.7 9.4 %copy-start.7 = (s32[64]{0:T(128)S(1)}, s32[64]{0:T(128)}, u32[]{:S(2)}) copy-start(s32[64]{0:T(128)} %get-tuple-element.61) | copy-start | bytes 772
  158.7 9.5 %copy-start.2 = (bf16[512,256]{1,0:T(8,128)(2,1)S(1)}, bf16[512,256]{1,0:T(8,128)(2,1)}, u32[]{:S(2)}) copy-start(bf16[512,256]{1,0:T(8,128)(2,1)} %slice.155) | copy-start | bytes 786436
  158.7 9.5 %copy-start.12 = (f32[64]{0:T(128)S(1)}, f32[64]{0:T(128)}, u32[]{:S(2)}) copy-start(f32[64]{0:T(128)} %dynamic_slice.59) | copy-start | bytes 772
  164.1 19.8 %collective-permute-start.12 = (bf16[64,512]{1,0:T(8,128)(2,1)S(1)}, bf16[64,512]{1,0:T(8,128)(2,1)S(1)}, u32[]{:S(2)}, u32[]{:S(2)}) collective-permute-start(bf16[64,512]{1,0:T(8,128)(2,1)S(1)} %dynamic-slice_bitcast_fusion), channel_id=1, source_target_pairs={{0,1},{1,0},{2,3},{3,2},{4,5},{5,4},{6,7},{7,6},{8,9},{9,8},{10,11... | collective-permute-start | bytes 196616 | tf_op jit(solution)/shard_map/ppermute | solution.py:24
  168.2 10.0 %copy-start.6 = (s32[64]{0:T(128)S(1)}, s32[64]{0:T(128)}, u32[]{:S(2)}) copy-start(s32[64]{0:T(128)} %get-tuple-element.60) | copy-start | bytes 772
  169.1 8.8 %collective-permute-start.11 = (bf16[64,384]{1,0:T(8,128)(2,1)S(1)}, bf16[64,384]{1,0:T(8,128)(2,1)S(1)}, u32[]{:S(2)}, u32[]{:S(2)}) collective-permute-start(bf16[64,384]{1,0:T(8,128)(2,1)S(1)} %concatenate.59), channel_id=1, source_target_pairs={{0,1},{1,0},{2,3},{3,2},{4,5},{5,4},{6,7},{7,6},{8,9},{9,8},{10,11... | collective-permute-start | bytes 147464 | tf_op jit(solution)/shard_map/ppermute | solution.py:24
  172.1 10.1 %all-to-all-start.6 = ((f32[16,1,1024]{2,1,0:T(1,128)}), f32[16,1,1024]{2,1,0:T(1,128)S(1)}, u32[]{:S(2)}, u32[]{:S(2)}) async-start(f32[16,1,1024]{2,1,0:T(1,128)} %reshape.269), calls=%async_computation.6 | async-start | bytes 131072 | tf_op jit(solution)/shard_map/all_to_all | solution.py:28

commit v6 on v3

--- a/solution.py
+++ b/solution.py
@@ -56,55 +56,45 @@
     other = 1 - core
     first = core == 0
 
-    yh = lax.axis_index("yh")
-    turned = (yh - jnp.arange(n_yh, dtype=jnp.int32)) % n_yh
-
-    def around(value):
-        return [value] + [
-            lax.ppermute(value, "yh", [(i, (i + s) % n_yh) for i in range(n_yh)]) for s in range(1, n_yh)
-        ]
-
     def ordered(own, others):
         return jnp.where(first, own, others), jnp.where(first, others, own)
 
     upper = jnp.concatenate([up.T, jnp.zeros((rank, block - out_block), BF)], axis=1)
-    joined = gather(jnp.concatenate([attention, down.T, upper], axis=0), "z", n_z)
-    proj = jnp.concatenate(around(output_projection), axis=1)
+    joined = lax.all_gather(jnp.concatenate([attention, down.T, upper], axis=0), "z", axis=0)
+    pieces = gather(output_projection, "yh", n_yh)
+    proj = jnp.concatenate([pieces[j] for j in range(n_yh)], axis=1)
     draft_weight_other = swap(draft_weight)
     pad = jnp.broadcast_to(gain[None], (16, block))
     kept = swap(jnp.concatenate([half(residual, other, mine), pad], axis=0))
     residual_parts = ordered(half(residual, core, mine), kept[:mine])
     gain_parts = ordered(gain[None], kept[mine : mine + 1])
 
-    rows = n_z * mine
-    send = half(joined[:, :tokens], other, mine, 1).reshape(rows, block)
-    keep = half(joined[:, :tokens], core, mine, 1).reshape(rows, block)
-    sent = swap(dot("tk,kn->tn", send, proj).astype(BF))
-    pair = (dot("tk,kn->tn", keep, proj) + sent.astype(F32)).astype(BF)
     adapters = jnp.concatenate(
-        [joined[:, tokens : tokens + rank], joined[:, tokens + rank :, :out_block]], axis=2
-    ).reshape(n_z * rank, block + out_block)
-    pair, adapters = lax.optimization_barrier((pair, adapters))
-
-    summed = jnp.sum(exchange(pair.reshape(n_chips, mine, n_yh * cols), CHIPS).astype(F32), axis=0).astype(BF)
-    summed = jnp.stack([summed[:, s * cols : (s + 1) * cols] for s in range(n_yh)])
-    projected = lax.ppermute(
-        summed[turned],
-        ("z", "yl", "x"),
-        [(z * n_chips + k, k * n_chips + z) for z in range(n_z) for k in range(n_chips)],
-    )
-
-    adapters_all = jnp.stack(around(adapters))[turned].reshape(tenants * rank, block + out_block)
+        [joined[:, tokens : tokens + rank], joined[:, tokens + rank :]], axis=2
+    ).reshape(n_z * rank, 2 * block)
+    adapters_all = lax.all_gather(adapters, "yh", axis=0).reshape(tenants * rank, 2 * block)
+    adapters_all = adapters_all[:, : block + out_block]
     adapters_other = swap(adapters_all)
     down_parts = ordered(adapters_all[:, :block], adapters_other[:, :block])
     ups = jnp.concatenate([adapters_all[:, block:], adapters_other[:, block:]], axis=1)
 
-    half_yh = n_yh // 2
+    z = lax.axis_index("z")
+    order = (z + jnp.arange(n_z, dtype=jnp.int32)) % n_z
+    rows = n_z * mine
+    send = half(joined[:, :tokens], other, mine, 1)[order].reshape(rows, block)
+    keep = half(joined[:, :tokens], core, mine, 1)[order].reshape(rows, block)
+    sent = swap(dot("tk,kn->tn", send, proj).astype(BF))
+    pair = (dot("tk,kn->tn", keep, proj) + sent.astype(F32)).astype(BF)
+
+    summed = jnp.sum(exchange(pair.reshape(n_chips, mine, n_yh * cols), CHIPS).astype(F32), axis=0).astype(BF)
+    places = [(i, k) for i in range(n_z) for k in range(n_chips)]
+    homes = [(i * n_chips + k, (i + k) % n_z * n_chips + k) for i, k in places]
+    chips = [(i * n_chips + k, i * n_chips + (i - k) % n_chips) for i, k in places]
+    projected = lax.ppermute(lax.ppermute(summed, ("z", "yl", "x"), homes), ("z", "yl", "x"), chips)
+
     scaled, squares = [], 0.0
     for part in range(2):
-        piece = jnp.concatenate(
-            [projected[half_yh * part + j] for j in range(half_yh)], axis=1
-        ).astype(F32)
+        piece = projected[:, part * block : (part + 1) * block].astype(F32)
         hidden = residual_parts[part].astype(F32) + piece
         squares = squares + jnp.sum(hidden * hidden, axis=1, keepdims=True)
         scaled.append((hidden * gain_parts[part].astype(F32)).astype(BF))

time: 202 us -> 234 us (1.16)
  waiting for transfers between devices: 42.3 us -> 97.3 us
  starting transfers between devices: 88 us -> 46.3 us
  between operations: 1.32 us -> 14.6 us
    all_gather x0 -> x2, waiting for transfers between devices: none -> 47.3 us  [the longest x1 33.6 us: shards(): lax.all_gather(adapters, 'yh', axis=0).reshape(tenants * rank, 2 * block)]
    ppermute x7 -> x2, starting transfers between devices: 34.4 us -> 9.41 us  [the longest x1 5.81 us: shards(): lax.ppermute(summed, ('z', 'yl', 'x'), homes)]
    all_to_all x4, waiting for transfers between devices: 6.68 us -> 31.7 us  [exchange(): return lax.all_to_all(value, axis, 0, 0)]
    ppermute x7 -> x2, waiting for transfers between devices: 32.4 us -> 15.4 us  [the longest x1 9.73 us: shards(): lax.ppermute(summed, ('z', 'yl', 'x'), homes)]
    all_to_all x4, starting transfers between devices: 39.6 us -> 22.8 us  [exchange(): return lax.all_to_all(value, axis, 0, 0)]
    unnamed x19 -> x14, local copies, waits for them, and re-layouts: 4.29 us -> 0.99 us
    slice x2, local copies, waits for them, and re-layouts: 0.07 us -> 2.6 us  [the longest x1 1.33 us: shards(): keep = half(joined[:, :tokens], core, mine, 1)[order].reshape(rows, block)]
  transfers between devices with their start and end apart: 18 -> 15, of which waited for: 10 -> 9; matrix products, arithmetic and copies ran while one was open for 14% -> 13% of each run, Pallas kernels for 0% -> 0%
where the time goes in v6:
time: 234 us; the launch traced here: 233 us
  waiting for transfers between devices  97.3 us (42%)
  starting transfers between devices  46.3 us (20%)
  blocking collectives  34 us (15%)
  between operations  14.6 us (6%)
  local copies, waits for them, and re-layouts  14.3 us (6%)
  matrix products  14 us (6%)
  other arithmetic  12.1 us (5%)
    all_to_all x1, blocking collectives, exchange(): return lax.all_to_all(value, axis, 0, 0)  34 us
    all_gather x1, waiting for transfers between devices, shards(): lax.all_gather(adapters, 'yh', axis=0).reshape(tenants * rank, 2 * block)  33.6 us
    all_to_all x4, waiting for transfers between devices, exchange(): return lax.all_to_all(value, axis, 0, 0)  31.7 us
    all_to_all x4, starting transfers between devices, exchange(): return lax.all_to_all(value, axis, 0, 0)  22.8 us
    ppermute x7, starting transfers between devices, swap(): return lax.ppermute(value, 'c', [(0, 1), (1, 0)])  14.1 us
    dot_general x11, matrix products, dot(): return jnp.einsum(subscripts, left, right, preferred_element_type=F32)  14 us
    all_gather x1, waiting for transfers between devices, shards(): lax.all_gather(jnp.concatenate([attention, down.T, upper], axis=0), 'z',...  13.7 us
    ppermute x1, waiting for transfers between devices, shards(): lax.ppermute(summed, ('z', 'yl', 'x'), homes)  9.73 us
  transfers between devices with their start and end apart: 15, of which 9 were waited for; matrix products, arithmetic and copies ran while one was open for 13% of the time, Pallas kernels for 0%

profile of v6, /device:TPU:6, one launch (start us, length us, event | category | flops | bytes accessed | tf_op | source)
XLA Modules:
  0.0 232.8 jit_solution(13119331716173512661)
XLA Ops:
  7.2 1.6 fusion.19
  8.9 2.0 broadcast_in_dim.39
  10.9 7.1 %all-to-all-start = ((bf16[4,512,256]{2,1,0:T(8,128)(2,1)}), bf16[4,512,256]{2,1,0:T(8,128)(2,1)S(1)}, u32[]{:S(2)}, u32[]{:S(2)}) async-start(bf16[4,512,256]{2,1,0:T(8,128)(2,1)} %broadcast_in_dim.39), calls=%async_computation | async-start | bytes 2097152 | tf_op jit(solution)/shard_map/all_to_all | solution.py:28
  18.0 25.7 %all-to-all-done = bf16[4,512,256]{2,1,0:T(8,128)(2,1)S(1)} async-done(((bf16[4,512,256]{2,1,0:T(8,128)(2,1)}), bf16[4,512,256]{2,1,0:T(8,128)(2,1)S(1)}, u32[]{:S(2)}, u32[]{:S(2)}) %all-to-all-start) | async-done | bytes 1048608 | tf_op jit(solution)/shard_map/all_to_all | solution.py:28
  43.7 13.7 %all-gather.6.cloned.1.call-done = bf16[1280,512]{1,0:T(8,128)(2,1)} async-done(((bf16[160,512]{1,0:T(8,128)(2,1)}), bf16[1280,512]{1,0:T(8,128)(2,1)}) %all-gather.6.cloned.1.call-update) | async-done | bytes 1310736 | tf_op jit(solution)/shard_map/all_gather | solution.py:63
  57.4 1.3 slice.167
  58.9 0.6 gather_fusion.1
  59.5 1.7 convolution_convert_fusion
  61.1 1.9 collective-permute-start.2
  63.1 0.6 gather_fusion
  63.7 2.4 %collective-permute-done.2 = bf16[512,1024]{1,0:T(8,128)(2,1)} collective-permute-done((bf16[512,1024]{1,0:T(8,128)(2,1)}, bf16[512,1024]{1,0:T(8,128)(2,1)}, u32[]{:S(2)}, u32[]{:S(2)}) %collective-permute-start.2) | collective-permute-done | bytes 1048608 | tf_op jit(solution)/shard_map/ppermute | solution.py:24
  66.0 2.9 %add_convert_fusion = bf16[512,1024]{1,0:T(8,128)(2,1)} fusion(bf16[512,1024]{1,0:T(8,128)(2,1)} %collective-permute-done.2, bf16[512,512]{1,0:T(8,128)(2,1)S(1)} %bitcast.99, bf16[512,256]{1,0:T(8,128)(2,1)S(1)} %get-tuple-element.20, bf16[512,256]{1,0:T(8,128)(2,1)S(1)} %get-tuple-element.21, bf16[512,256]{1,0:T(8,128)(2,1)S(1)} %get-tuple-element.22, ...), kind=kOutput, calls=%fused_computation.3 | convolution fusion | flops 542638080 | bytes 3670016 | tf_op jit(solution)/shard_map/tk,kn->tn/dot_general | solution.py:20
  69.0 5.8 %all-to-all-start.1 = ((bf16[8,64,1024]{2,1,0:T(8,128)(2,1)}), bf16[8,64,1024]{2,1,0:T(8,128)(2,1)S(1)}, u32[]{:S(2)}, u32[]{:S(2)}) async-start(bf16[8,64,1024]{2,1,0:T(8,128)(2,1)} %bitcast.12), calls=%async_computation.1 | async-start | bytes 2097152 | tf_op jit(solution)/shard_map/all_to_all | solution.py:28
  74.8 1.0 fusion.72
  75.8 0.7 pad_maximum_fusion.6
  76.5 1.9 collective-permute-start.5
  78.5 33.6 %all-gather.4.cloned.1.call-done = bf16[4,128,1024]{2,1,0:T(8,128)(2,1)} async-done(((bf16[1,128,1024]{2,1,0:T(8,128)(2,1)}), bf16[4,128,1024]{2,1,0:T(8,128)(2,1)}) %all-gather.4.cloned.1.call-update) | async-done | bytes 1048592 | tf_op jit(solution)/shard_map/all_gather | solution.py:75
  112.1 1.3 slice.164
  113.4 1.9 collective-permute-start
  115.3 2.4 %collective-permute-start.1 = (bf16[80,512]{1,0:T(8,128)(2,1)S(1)}, bf16[80,512]{1,0:T(8,128)(2,1)S(1)}, u32[]{:S(2)}, u32[]{:S(2)}) collective-permute-start(bf16[80,512]{1,0:T(8,128)(2,1)S(1)} %pad_maximum_fusion.11), channel_id=1, source_target_pairs={{0,1},{1,0},{2,3},{3,2},{4,5},{5,4},{6,7},{7,6},{8,9},{9,8},{10,11... | collective-permute-start | bytes 245768 | tf_op jit(solution)/shard_map/ppermute | solution.py:24
  117.7 0.2 reduce_sum.84
  117.9 5.8 %collective-permute-start.3 = (bf16[64,1024]{1,0:T(8,128)(2,1)S(1)}, bf16[64,1024]{1,0:T(8,128)(2,1)S(1)}, u32[]{:S(2)}, u32[]{:S(2)}) collective-permute-start(bf16[64,1024]{1,0:T(8,128)(2,1)S(1)} %reduce_sum.84), channel_id=1, source_target_pairs={{0,0},{2,66},{4,132},{6,198},{8,264},{10,330},{12,396},{14,462},{6... | collective-permute-start | bytes 393224 | tf_op jit(solution)/shard_map/ppermute | solution.py:93
  123.9 9.7 %collective-permute-done.3 = bf16[64,1024]{1,0:T(8,128)(2,1)S(1)} collective-permute-done((bf16[64,1024]{1,0:T(8,128)(2,1)S(1)}, bf16[64,1024]{1,0:T(8,128)(2,1)S(1)}, u32[]{:S(2)}, u32[]{:S(2)}) %collective-permute-start.3) | collective-permute-done | bytes 131104 | tf_op jit(solution)/shard_map/ppermute | solution.py:93
  133.6 3.6 %collective-permute-start.4 = (bf16[64,1024]{1,0:T(8,128)(2,1)S(1)}, bf16[64,1024]{1,0:T(8,128)(2,1)S(1)}, u32[]{:S(2)}, u32[]{:S(2)}) collective-permute-start(bf16[64,1024]{1,0:T(8,128)(2,1)S(1)} %collective-permute-done.3), channel_id=1, source_target_pairs={{0,0},{2,14},{4,12},{6,10},{8,8},{10,6},{12,4},{14,2},{64,66},{66,... | collective-permute-start | bytes 393224 | tf_op jit(solution)/shard_map/ppermute | solution.py:93
  137.2 5.6 %collective-permute-done.4 = bf16[64,1024]{1,0:T(8,128)(2,1)S(1)} collective-permute-done((bf16[64,1024]{1,0:T(8,128)(2,1)S(1)}, bf16[64,1024]{1,0:T(8,128)(2,1)S(1)}, u32[]{:S(2)}, u32[]{:S(2)}) %collective-permute-start.4) | collective-permute-done | bytes 131104 | tf_op jit(solution)/shard_map/ppermute | solution.py:93
  142.9 1.3 fusion.8
  144.3 1.3 fusion.2
  145.6 0.1 copy.62
  145.9 0.2 multiply_reduce_fusion
  146.1 0.1 copy.64
  146.2 0.1 copy.65
  146.4 1.2 broadcast_in_dim.43
  147.7 4.5 %all-to-all-start.2 = ((bf16[8,64,1152]{2,1,0:T(8,128)(2,1)}), bf16[8,64,1152]{2,1,0:T(8,128)(2,1)S(1)}, u32[]{:S(2)}, u32[]{:S(2)}) async-start(bf16[8,64,1152]{2,1,0:T(8,128)(2,1)} %broadcast_in_dim.43), calls=%async_computation.2 | async-start | bytes 2359296 | tf_op jit(solution)/shard_map/all_to_all | solution.py:28
  152.3 0.1 fusion.58
  152.6 7.3 %pad_maximum_fusion = bf16[8192,512]{1,0:T(8,128)(2,1)} fusion(bf16[8192,256]{1,0:T(8,128)(2,1)} %collective-permute-done.5, bf16[8192,256]{1,0:T(8,128)(2,1)} %param.13), kind=kLoop, calls=%fused_computation.2 | loop fusion | flops 16777216 | bytes 16777216 | tf_op jit(solution)/shard_map/concatenate | solution.py:148
  159.9 1.0 slice.165
  160.8 1.9 collective-permute-start.8
  162.8 2.4 %all-to-all-done.2 = bf16[8,64,1152]{2,1,0:T(8,128)(2,1)S(1)} async-done(((bf16[8,64,1152]{2,1,0:T(8,128)(2,1)}), bf16[8,64,1152]{2,1,0:T(8,128)(2,1)S(1)}, u32[]{:S(2)}, u32[]{:S(2)}) %all-to-all-start.2) | async-done | bytes 1179680 | tf_op jit(solution)/shard_map/all_to_all | solution.py:28
  165.3 0.2 fusion.38
  166.0 0.1 slice.177
  166.3 1.9 collective-permute-start.6
  168.2 0.2 convolution_multiply_fusion
  168.5 0.1 copy.71
  168.6 0.1 copy.72
  168.7 0.6 collective-permute-done.6
  169.4 4.9 %fusion.7 = bf16[64,512]{1,0:T(8,128)(2,1)S(1)} fusion(f32[64,512]{1,0:T(8,128)S(1)} %convolution_multiply_fusion, bf16[8,1024,512]{2,1,0:T(8,128)(2,1)} %bitcast.80, bf16[64,256]{1,0:T(8,128)(2,1)S(1)} %get-tuple-element.26, bf16[64,256]{1,0:T(8,128)(2,1)S(1)} %get-tuple-element.25, f32[64]{0:T(128)S(1)} %dynamic_slice.44, f32[64]{0:T(128)S(1)} %bitcast.108, ...), kind=kOutput, calls=%fused_computation.19 | convolution fusion | flops 537165824 | bytes 9700352 | tf_op jit(solution)/shard_map/ktd,kdn->tn/dot_general | solution.py:20
  174.4 0.3 convolution_select_fusion
  174.7 0.1 copy.70
  175.0 2.1 collective-permute-start.7
  177.1 0.3 fusion.33
  177.4 0.7 reshape.253
  178.1 5.4 %all-to-all-start.3 = ((f32[16,1,1024]{2,1,0:T(1,128)}), f32[16,1,1024]{2,1,0:T(1,128)S(1)}, u32[]{:S(2)}, u32[]{:S(2)}) async-start(f32[16,1,1024]{2,1,0:T(1,128)} %reshape.253), calls=%async_computation.3 | async-start | bytes 131072 | tf_op jit(solution)/shard_map/all_to_all | solution.py:28
  183.7 0.3 fusion.1
  184.0 0.2 multiply_reduce_fusion.2
  184.2 3.6 %all-to-all-done.3 = f32[16,1,1024]{2,1,0:T(1,128)S(1)} async-done(((f32[16,1,1024]{2,1,0:T(1,128)}), f32[16,1,1024]{2,1,0:T(1,128)S(1)}, u32[]{:S(2)}, u32[]{:S(2)}) %all-to-all-start.3) | async-done | bytes 65568 | tf_op jit(solution)/shard_map/all_to_all | solution.py:28
  187.8 0.5 broadcast.221
  188.3 0.8 reduce.5
  189.3 0.4 fusion.21
  189.9 0.4 fusion
  190.3 0.3 copy.77
  190.6 34.0 %all_to_all.25 = bf16[32,16,768]{2,1,0:T(8,128)(2,1)S(1)} all-to-all(bf16[32,16,768]{2,1,0:T(8,128)(2,1)S(1)} %bitcast.81), channel_id=1, replica_groups=mesh['z'=8,'yh'=4,'yl'=2,'x'=4,'c'=2] {'yh','z'}, dimensions={0} | all-to-all | bytes 1572864 | tf_op jit(solution)/shard_map/all_to_all | solution.py:28
  224.6 0.1 convert_reduce_fusion
  224.7 0.6 slice_bitcast_fusion.4
  225.3 0.6 slice_bitcast_fusion.5
  (78 shorter events, 2.6 us)
Async XLA Ops:
  7.2 50.3 %all-gather.6.cloned.1.call-start = ((), (), s32[]{:S(2)}) async-start(), calls=%async_computation.6 | async-start | bytes 1474560 | tf_op jit(solution)/shard_map/all_gather | solution.py:63
  10.9 32.8 %all-to-all-start = ((bf16[4,512,256]{2,1,0:T(8,128)(2,1)}), bf16[4,512,256]{2,1,0:T(8,128)(2,1)S(1)}, u32[]{:S(2)}, u32[]{:S(2)}) async-start(bf16[4,512,256]{2,1,0:T(8,128)(2,1)} %broadcast_in_dim.39), calls=%async_computation | async-start | bytes 2097152 | tf_op jit(solution)/shard_map/all_to_all | solution.py:28
  61.1 4.9 %collective-permute-start.2 = (bf16[512,1024]{1,0:T(8,128)(2,1)}, bf16[512,1024]{1,0:T(8,128)(2,1)}, u32[]{:S(2)}, u32[]{:S(2)}) collective-permute-start(bf16[512,1024]{1,0:T(8,128)(2,1)} %convolution_convert_fusion), channel_id=1, source_target_pairs={{0,1},{1,0},{2,3},{3,2},{4,5},{5,4},{6,7},{7,6},{8,9},{9,8},{10,11... | collective-permute-start | bytes 3145736 | tf_op jit(solution)/shard_map/ppermute | solution.py:24
  69.0 9.5 %copy-start.1 = (bf16[128,512]{1,0:T(8,128)(2,1)S(1)}, bf16[128,512]{1,0:T(8,128)(2,1)}, u32[]{:S(2)}) copy-start(bf16[128,512]{1,0:T(8,128)(2,1)} %param.11) | copy-start | bytes 393220
  69.0 46.3 %copy-start.3 = (bf16[512]{0:T(512)(128)(2,1)S(1)}, bf16[512]{0:T(512)(128)(2,1)}, u32[]{:S(2)}) copy-start(bf16[512]{0:T(512)(128)(2,1)} %param.12) | copy-start | bytes 3076
  69.0 48.8 %all-to-all-start.1 = ((bf16[8,64,1024]{2,1,0:T(8,128)(2,1)}), bf16[8,64,1024]{2,1,0:T(8,128)(2,1)S(1)}, u32[]{:S(2)}, u32[]{:S(2)}) async-start(bf16[8,64,1024]{2,1,0:T(8,128)(2,1)} %bitcast.12), calls=%async_computation.1 | async-start | bytes 2097152 | tf_op jit(solution)/shard_map/all_to_all | solution.py:28
  74.8 49.0 %copy-start.2 = (s32[128]{0:T(128)S(1)}, s32[128]{0:T(128)}, u32[]{:S(2)}) copy-start(s32[128]{0:T(128)} %param.16) | copy-start | bytes 1540
  74.8 37.3 %all-gather.4.cloned.1.call-start = ((), (), s32[]{:S(2)}) async-start(), calls=%async_computation.5 | async-start | bytes 1310720 | tf_op jit(solution)/shard_map/all_gather | solution.py:75
  76.5 76.0 %collective-permute-start.5 = (bf16[8192,256]{1,0:T(8,128)(2,1)}, bf16[8192,256]{1,0:T(8,128)(2,1)}, u32[]{:S(2)}, u32[]{:S(2)}) collective-permute-start(bf16[8192,256]{1,0:T(8,128)(2,1)} %param.13), channel_id=1, source_target_pairs={{0,1},{1,0},{2,3},{3,2},{4,5},{5,4},{6,7},{7,6},{8,9},{9,8},{10,11... | collective-permute-start | bytes 12582920 | tf_op jit(solution)/shard_map/ppermute | solution.py:24
  112.1 30.8 %copy-start = (bf16[4,128,1024]{2,1,0:T(8,128)(2,1)S(1)}, bf16[4,128,1024]{2,1,0:T(8,128)(2,1)}, u32[]{:S(2)}) copy-start(bf16[4,128,1024]{2,1,0:T(8,128)(2,1)} %all-gather.4.cloned.1.call-done) | copy-start | bytes 3145732
  113.4 29.6 %collective-permute-start = (bf16[512,768]{1,0:T(8,128)(2,1)S(1)}, bf16[512,768]{1,0:T(8,128)(2,1)}, u32[]{:S(2)}, u32[]{:S(2)}) collective-permute-start(bf16[512,768]{1,0:T(8,128)(2,1)S(1)} %slice.164), channel_id=1, source_target_pairs={{0,1},{1,0},{2,3},{3,2},{4,5},{5,4},{6,7},{7,6},{8,9},{9,8},{10,11... | collective-permute-start | bytes 2359304 | tf_op jit(solution)/shard_map/ppermute | solution.py:24
  115.3 21.9 %collective-permute-start.1 = (bf16[80,512]{1,0:T(8,128)(2,1)S(1)}, bf16[80,512]{1,0:T(8,128)(2,1)S(1)}, u32[]{:S(2)}, u32[]{:S(2)}) collective-permute-start(bf16[80,512]{1,0:T(8,128)(2,1)S(1)} %pad_maximum_fusion.11), channel_id=1, source_target_pairs={{0,1},{1,0},{2,3},{3,2},{4,5},{5,4},{6,7},{7,6},{8,9},{9,8},{10,11... | collective-permute-start | bytes 245768 | tf_op jit(solution)/shard_map/ppermute | solution.py:24
  117.9 15.7 %collective-permute-start.3 = (bf16[64,1024]{1,0:T(8,128)(2,1)S(1)}, bf16[64,1024]{1,0:T(8,128)(2,1)S(1)}, u32[]{:S(2)}, u32[]{:S(2)}) collective-permute-start(bf16[64,1024]{1,0:T(8,128)(2,1)S(1)} %reduce_sum.84), channel_id=1, source_target_pairs={{0,0},{2,66},{4,132},{6,198},{8,264},{10,330},{12,396},{14,462},{6... | collective-permute-start | bytes 393224 | tf_op jit(solution)/shard_map/ppermute | solution.py:93
  133.6 9.3 %collective-permute-start.4 = (bf16[64,1024]{1,0:T(8,128)(2,1)S(1)}, bf16[64,1024]{1,0:T(8,128)(2,1)S(1)}, u32[]{:S(2)}, u32[]{:S(2)}) collective-permute-start(bf16[64,1024]{1,0:T(8,128)(2,1)S(1)} %collective-permute-done.3), channel_id=1, source_target_pairs={{0,0},{2,14},{4,12},{6,10},{8,8},{10,6},{12,4},{14,2},{64,66},{66,... | collective-permute-start | bytes 393224 | tf_op jit(solution)/shard_map/ppermute | solution.py:93
  146.0 6.2 %copy-start.4 = (s32[32]{0:T(128)S(1)}, s32[32]{0:T(128)}, u32[]{:S(2)}) copy-start(s32[32]{0:T(128)} %param.17) | copy-start | bytes 388
  147.7 17.5 %all-to-all-start.2 = ((bf16[8,64,1152]{2,1,0:T(8,128)(2,1)}), bf16[8,64,1152]{2,1,0:T(8,128)(2,1)S(1)}, u32[]{:S(2)}, u32[]{:S(2)}) async-start(bf16[8,64,1152]{2,1,0:T(8,128)(2,1)} %broadcast_in_dim.43), calls=%async_computation.2 | async-start | bytes 2359296 | tf_op jit(solution)/shard_map/all_to_all | solution.py:28
  160.8 29.0 %collective-permute-start.8 = (bf16[64,512]{1,0:T(8,128)(2,1)S(1)}, bf16[64,512]{1,0:T(8,128)(2,1)S(1)}, u32[]{:S(2)}, u32[]{:S(2)}) collective-permute-start(bf16[64,512]{1,0:T(8,128)(2,1)S(1)} %get-tuple-element.8), channel_id=1, source_target_pairs={{0,1},{1,0},{2,3},{3,2},{4,5},{5,4},{6,7},{7,6},{8,9},{9,8},{10,11... | collective-permute-start | bytes 196616 | tf_op jit(solution)/shard_map/ppermute | solution.py:24
  166.3 3.1 %collective-permute-start.6 = (bf16[16,512]{1,0:T(8,128)(2,1)S(1)}, bf16[16,512]{1,0:T(8,128)(2,1)S(1)}, u32[]{:S(2)}, u32[]{:S(2)}) collective-permute-start(bf16[16,512]{1,0:T(8,128)(2,1)S(1)} %slice.186), channel_id=1, source_target_pairs={{0,1},{1,0},{2,3},{3,2},{4,5},{5,4},{6,7},{7,6},{8,9},{9,8},{10,11... | collective-permute-start | bytes 49160 | tf_op jit(solution)/shard_map/ppermute | solution.py:24
  175.0 8.5 %collective-permute-start.7 = (bf16[64,384]{1,0:T(8,128)(2,1)S(1)}, bf16[64,384]{1,0:T(8,128)(2,1)S(1)}, u32[]{:S(2)}, u32[]{:S(2)}) collective-permute-start(bf16[64,384]{1,0:T(8,128)(2,1)S(1)} %concatenate.55), channel_id=1, source_target_pairs={{0,1},{1,0},{2,3},{3,2},{4,5},{5,4},{6,7},{7,6},{8,9},{9,8},{10,11... | collective-permute-start | bytes 147464 | tf_op jit(solution)/shard_map/ppermute | solution.py:24
  178.1 9.7 %all-to-all-start.3 = ((f32[16,1,1024]{2,1,0:T(1,128)}), f32[16,1,1024]{2,1,0:T(1,128)S(1)}, u32[]{:S(2)}, u32[]{:S(2)}) async-start(f32[16,1,1024]{2,1,0:T(1,128)} %reshape.253), calls=%async_computation.3 | async-start | bytes 131072 | tf_op jit(solution)/shard_map/all_to_all | solution.py:28
Sparse Core Ops, SparseCore 0:
  10.1 47.3 all-gather.5
  77.7 34.3 all-gather.3

commit v7 on v5

--- a/solution.py
+++ b/solution.py
@@ -57,64 +57,63 @@
     first = core == 0
 
     yh = lax.axis_index("yh")
-
-    def shift(value, step):
-        return lax.ppermute(value, "yh", [(i, (i + step) % n_yh) for i in range(n_yh)])
+    turned = (yh - jnp.arange(n_yh, dtype=jnp.int32)) % n_yh
+
+    def around(value):
+        return [value] + [
+            lax.ppermute(value, "yh", [(i, (i + s) % n_yh) for i in range(n_yh)]) for s in range(1, n_yh)
+        ]
 
     def ordered(own, others):
         return jnp.where(first, own, others), jnp.where(first, others, own)
 
     upper = jnp.concatenate([up.T, jnp.zeros((rank, block - out_block), BF)], axis=1)
     joined = gather(jnp.concatenate([attention, down.T, upper], axis=0), "z", n_z)
-    proj = jnp.zeros((block, n_yh * cols), BF)
-    for step in range(n_yh):
-        part = shift(output_projection, step) if step else output_projection
-        proj = lax.dynamic_update_slice(proj, part, (0, (yh - step) % n_yh * cols))
-    both_weights = jnp.concatenate([draft_weight, swap(draft_weight)], axis=1)
+    proj = jnp.concatenate(around(output_projection), axis=1)
+    draft_weight_other = swap(draft_weight)
     pad = jnp.broadcast_to(gain[None], (16, block))
     kept = swap(jnp.concatenate([half(residual, other, mine), pad], axis=0))
     chip_rows = jnp.concatenate(
         ordered(jnp.concatenate([half(residual, core, mine), pad], axis=0), kept), axis=1
     )
-
-    piece = 2 * block // n_chips
-    chip_rows = chip_rows.reshape(mine + 16, n_chips, piece).transpose(1, 0, 2)
-    joined, chip_rows, both_weights = lax.optimization_barrier((joined, chip_rows, both_weights))
-    chip_rows = exchange(chip_rows, CHIPS)
-    residual_part, gain_part = chip_rows[:, :mine].astype(F32), chip_rows[:, mine : mine + 1].astype(F32)
+    places = [(i, k) for i in range(n_z) for k in range(n_chips)]
+    homes = [(i * n_chips + k, (i + k) % n_z * n_chips + k) for i, k in places]
+    chips = [(i * n_chips + k, i * n_chips + (i - k) % n_chips) for i, k in places]
+    chip_rows = lax.ppermute(chip_rows, ("z", "yl", "x"), chips)
+    joined, chip_rows = lax.optimization_barrier((joined, chip_rows))
+    residual_part, gain_part = chip_rows[:mine].astype(F32), chip_rows[mine : mine + 1].astype(F32)
 
     rows = n_z * mine
-    send = half(joined[:, :tokens], other, mine, 1).reshape(rows, block)
-    keep = half(joined[:, :tokens], core, mine, 1).reshape(rows, block)
+    z = lax.axis_index("z")
+    order = (z + jnp.arange(n_z, dtype=jnp.int32)) % n_z
+    send = half(joined[:, :tokens], other, mine, 1)[order].reshape(rows, block)
+    keep = half(joined[:, :tokens], core, mine, 1)[order].reshape(rows, block)
     sent = swap(dot("tk,kn->tn", send, proj).astype(BF))
     pair = (dot("tk,kn->tn", keep, proj) + sent.astype(F32)).astype(BF)
-    pair = pair.reshape(rows, n_chips, piece).transpose(1, 0, 2)
     adapters = jnp.concatenate(
         [joined[:, tokens : tokens + rank], joined[:, tokens + rank :, :out_block]], axis=2
     ).reshape(n_z * rank, block + out_block)
-    pair, adapters, residual_part, gain_part = lax.optimization_barrier((pair, adapters, residual_part, gain_part))
-    summed = jnp.sum(exchange(pair, CHIPS).astype(F32), axis=0).astype(BF)
-    adapters_parts = [adapters] + [shift(adapters, step) for step in range(1, n_yh)]
-    projected = exchange(summed.reshape(n_z, mine, piece), "z").astype(F32)
-
-    hidden = residual_part + projected
-    squares = jnp.sum(jnp.sum(hidden * hidden, axis=0), axis=1, keepdims=True)
+    pair, adapters = lax.optimization_barrier((pair, adapters))
+    parts = around(adapters)
+
+    summed = jnp.sum(exchange(pair.reshape(n_chips, mine, n_yh * cols), CHIPS).astype(F32), axis=0).astype(BF)
+    summed, parts[1], parts[3] = lax.optimization_barrier((summed, parts[1], parts[3]))
+    summed = jnp.stack([summed[:, s * cols : (s + 1) * cols] for s in range(n_yh)])
+    projected = lax.ppermute(summed[turned], ("z", "yl", "x"), homes)
+    projected, parts[2] = lax.optimization_barrier((projected, parts[2]))
+
+    hidden = residual_part + jnp.concatenate([projected[j] for j in range(n_yh)], axis=1).astype(F32)
+    squares = jnp.sum(hidden * hidden, axis=1, keepdims=True)
     scaled = (hidden * gain_part).astype(BF)
-    message = jnp.concatenate(
-        [scaled[z] for z in range(n_z)] + [*split(squares), jnp.zeros((mine, 126), BF)], axis=1
-    )
-    message, *adapters_parts = lax.optimization_barrier((message, *adapters_parts))
+    message = jnp.concatenate([scaled, *split(squares), jnp.zeros((mine, 126), BF)], axis=1)
     received = gather(message, CHIPS, n_chips)
-    features = received[:, :, : 2 * block].reshape(n_chips, mine, n_z, piece)
-    features = features.transpose(2, 1, 0, 3).reshape(n_z, mine, 2 * block)
+    blocks = (z - jnp.arange(n_chips, dtype=jnp.int32)) % n_chips
+    features = received[:, :, : 2 * block][blocks]
     totals = jnp.sum(received[:, :, 2 * block :].astype(F32), axis=0)
     inv_column = lax.rsqrt((totals[:, :1] + totals[:, 1:2]) / width + EPSILON)
     inv_row = jnp.broadcast_to(inv_column, (mine, 128)).T[:1]
 
-    adapters_all = jnp.zeros((n_yh, n_z * rank, block + out_block), BF)
-    for step, part in enumerate(adapters_parts):
-        adapters_all = lax.dynamic_update_slice(adapters_all, part[None], ((yh - step) % n_yh, 0, 0))
-    adapters_all = adapters_all.reshape(tenants * rank, block + out_block)
+    adapters_all = jnp.stack(parts)[turned].reshape(tenants * rank, block + out_block)
     adapters_other = swap(adapters_all)
     downs = jnp.concatenate(ordered(adapters_all[:, :block], adapters_other[:, :block]), axis=1)
     ups = jnp.concatenate([adapters_all[:, block:], adapters_other[:, block:]], axis=1)
@@ -155,6 +154,7 @@
     count = jnp.sum(jnp.where(is_tenant, tenant_count.astype(F32)[None, :], 0.0), axis=1)
     weight = half(keep_mask.astype(F32) / count, core, mine)[:, None]
 
+    both_weights = jnp.concatenate([draft_weight, draft_weight_other], axis=1)
     draft = dot("ktd,kdn->tn", features, both_weights.reshape(n_chips, 2 * block, 2 * out_block))
     draft, low_wide = lax.optimization_barrier((draft, low_wide))
     draft = draft * inv_column + ADAPTER_SCALE * dot("jt,jn->tn", low_wide, ups)

time: 226 us -> 202 us (0.89)
  blocking collectives: 55.7 us -> 34.7 us
  waiting for transfers between devices: 43.4 us -> 40.3 us
  starting transfers between devices: 82.7 us -> 79.9 us
    all_to_all x2 -> x1, blocking collectives: 55.7 us -> 34.7 us  [exchange(): return lax.all_to_all(value, axis, 0, 0)]
    all_to_all x6 -> x5, starting transfers between devices: 38.3 us -> 31.3 us  [exchange(): return lax.all_to_all(value, axis, 0, 0)]
    all_to_all x6 -> x5, waiting for transfers between devices: 17.1 us -> 12.3 us  [exchange(): return lax.all_to_all(value, axis, 0, 0)]
    ppermute x6 -> x8, starting transfers between devices: 30.4 us -> 34.1 us  [the longest x6 28.8 us: around(): lax.ppermute(value, 'yh', [(i, (i + s) % n_yh) for i in range(n_yh)])]
    gather x0 -> x5, local copies, waits for them, and re-layouts: none -> 3.06 us  [the longest x1 0.74 us: shards(): features = received[:, :, :2 * block][blocks]]
    ppermute x6 -> x8, waiting for transfers between devices: 25.3 us -> 27.5 us  [the longest x6 18.7 us: around(): lax.ppermute(value, 'yh', [(i, (i + s) % n_yh) for i in range(n_yh)])]
    concatenate x1 -> x2, other arithmetic: 7.3 us -> 7.31 us  [the longest x1 7.3 us: shards(): both_weights = jnp.concatenate([draft_weight, draft_weight_other], axis=1)]
  transfers between devices with their start and end apart: 19 -> 20, of which waited for: 8 -> 9; matrix products, arithmetic and copies ran while one was open for 12% -> 17% of each run, Pallas kernels for 0% -> 0%
where the time goes in v7:
time: 202 us; the launch traced here: 200 us
  starting transfers between devices  79.9 us (40%)
  waiting for transfers between devices  40.3 us (20%)
  blocking collectives  34.7 us (17%)
  local copies, waits for them, and re-layouts  16.6 us (8%)
  other arithmetic  13.6 us (7%)
  matrix products  13.5 us (7%)
    all_to_all x1, blocking collectives, exchange(): return lax.all_to_all(value, axis, 0, 0)  34.7 us
    all_to_all x5, starting transfers between devices, exchange(): return lax.all_to_all(value, axis, 0, 0)  31.3 us
    ppermute x6, starting transfers between devices, around(): lax.ppermute(value, 'yh', [(i, (i + s) % n_yh) for i in range(n_yh)])  28.8 us
    ppermute x6, waiting for transfers between devices, around(): lax.ppermute(value, 'yh', [(i, (i + s) % n_yh) for i in range(n_yh)])  18.7 us
    ppermute x7, starting transfers between devices, swap(): return lax.ppermute(value, 'c', [(0, 1), (1, 0)])  14.4 us
    dot_general x10, matrix products, dot(): return jnp.einsum(subscripts, left, right, preferred_element_type=F32)  13.5 us
    all_to_all x5, waiting for transfers between devices, exchange(): return lax.all_to_all(value, axis, 0, 0)  12.3 us
    concatenate x1, other arithmetic, shards(): both_weights = jnp.concatenate([draft_weight, draft_weight_other], axis=1)  7.3 us
  transfers between devices with their start and end apart: 20, of which 9 were waited for; matrix products, arithmetic and copies ran while one was open for 17% of the time, Pallas kernels for 0%

profile of v7, /device:TPU:6, one launch (start us, length us, event | category | flops | bytes accessed | tf_op | source)
XLA Modules:
  0.0 199.8 jit_solution(5986613860084477046)
XLA Ops:
  0.6 1.0 fusion.10
  1.6 1.2 broadcast_in_dim.36
  2.8 10.3 %all-to-all-start = ((bf16[8,160,512]{2,1,0:T(8,128)(2,1)}), bf16[8,160,512]{2,1,0:T(8,128)(2,1)S(1)}, u32[]{:S(2)}, u32[]{:S(2)}) async-start(bf16[8,160,512]{2,1,0:T(8,128)(2,1)} %broadcast_in_dim.36), calls=%async_computation | async-start | bytes 2621440 | tf_op jit(solution)/shard_map/all_to_all | solution.py:28
  13.1 7.7 %collective-permute-start.3 = (bf16[512,256]{1,0:T(8,128)(2,1)S(1)}, bf16[512,256]{1,0:T(8,128)(2,1)S(1)}, u32[]{:S(2)}, u32[]{:S(2)}) collective-permute-start(bf16[512,256]{1,0:T(8,128)(2,1)S(1)} %copy-done.1), channel_id=1, source_target_pairs={{0,32},{16,48},{32,0},{48,16},{1,33},{17,49},{33,1},{49,17},{2,34}... | collective-permute-start | bytes 786440 | tf_op jit(solution)/shard_map/ppermute | solution.py:64
  20.9 2.7 %collective-permute-start.2 = (bf16[512,256]{1,0:T(8,128)(2,1)S(1)}, bf16[512,256]{1,0:T(8,128)(2,1)S(1)}, u32[]{:S(2)}, u32[]{:S(2)}) collective-permute-start(bf16[512,256]{1,0:T(8,128)(2,1)S(1)} %copy-done.1), channel_id=1, source_target_pairs={{0,16},{16,32},{32,48},{48,0},{1,17},{17,33},{33,49},{49,1},{2,18}... | collective-permute-start | bytes 786440 | tf_op jit(solution)/shard_map/ppermute | solution.py:64
  23.6 5.3 %collective-permute-start.4 = (bf16[512,256]{1,0:T(8,128)(2,1)S(1)}, bf16[512,256]{1,0:T(8,128)(2,1)S(1)}, u32[]{:S(2)}, u32[]{:S(2)}) collective-permute-start(bf16[512,256]{1,0:T(8,128)(2,1)S(1)} %copy-done.1), channel_id=1, source_target_pairs={{0,48},{16,0},{32,16},{48,32},{1,49},{17,1},{33,17},{49,33},{2,50}... | collective-permute-start | bytes 786440 | tf_op jit(solution)/shard_map/ppermute | solution.py:64
  28.9 1.9 collective-permute-start
  30.9 0.7 constant_dynamic-update-slice_fusion.3
  31.6 0.5 collective-permute-done
  32.1 3.4 %collective-permute-start.1 = (bf16[80,1024]{1,0:T(8,128)(2,1)S(1)}, bf16[80,1024]{1,0:T(8,128)(2,1)S(1)}, u32[]{:S(2)}, u32[]{:S(2)}) collective-permute-start(bf16[80,1024]{1,0:T(8,128)(2,1)S(1)} %pad_maximum_fusion.7), channel_id=1, source_target_pairs={{0,0},{2,14},{4,12},{6,10},{8,8},{10,6},{12,4},{14,2},{64,66},{66,... | collective-permute-start | bytes 491528 | tf_op jit(solution)/shard_map/ppermute | solution.py:82
  35.6 8.8 %collective-permute-done.2 = bf16[512,256]{1,0:T(8,128)(2,1)S(1)} collective-permute-done((bf16[512,256]{1,0:T(8,128)(2,1)S(1)}, bf16[512,256]{1,0:T(8,128)(2,1)S(1)}, u32[]{:S(2)}, u32[]{:S(2)}) %collective-permute-start.2) | collective-permute-done | bytes 262176 | tf_op jit(solution)/shard_map/ppermute | solution.py:64
  44.4 0.7 constant_dynamic-update-slice_fusion.2
  45.1 0.8 constant_dynamic-update-slice_fusion.1
  45.9 0.8 constant_dynamic-update-slice_fusion
  46.7 1.8 collective-permute-done.1
  48.7 0.6 gather_fusion.1
  49.3 2.9 %convolution_convert_fusion = bf16[512,1024]{1,0:T(8,128)(2,1)} fusion(bf16[512,512]{1,0:T(8,128)(2,1)S(1)} %bitcast.110, bf16[512,1024]{1,0:T(8,128)(2,1)} %constant_dynamic-update-slice_fusion), kind=kOutput, calls=%fused_computation.8 | convolution fusion | flops 537395200 | bytes 2621440 | tf_op jit(solution)/shard_map/tk,kn->tn/dot_general | solution.py:20
  52.2 1.9 collective-permute-start.5
  54.1 2.4 %collective-permute-start.11 = (bf16[8192,256]{1,0:T(8,128)(2,1)}, bf16[8192,256]{1,0:T(8,128)(2,1)}, u32[]{:S(2)}, u32[]{:S(2)}) collective-permute-start(bf16[8192,256]{1,0:T(8,128)(2,1)} %param.13), channel_id=1, source_target_pairs={{0,1},{1,0},{2,3},{3,2},{4,5},{5,4},{6,7},{7,6},{8,9},{9,8},{10,11... | collective-permute-start | bytes 12582920 | tf_op jit(solution)/shard_map/ppermute | solution.py:24
  56.6 0.6 gather_fusion
  57.2 3.3 %add_convert_fusion = bf16[512,1024]{1,0:T(8,128)(2,1)} fusion(bf16[512,1024]{1,0:T(8,128)(2,1)} %collective-permute-done.5, bf16[512,512]{1,0:T(8,128)(2,1)S(1)} %bitcast.109, bf16[512,1024]{1,0:T(8,128)(2,1)} %constant_dynamic-update-slice_fusion), kind=kOutput, calls=%fused_computation.6 | convolution fusion | flops 538443776 | bytes 3670016 | tf_op jit(solution)/shard_map/tk,kn->tn/dot_general | solution.py:20
  60.5 5.4 %all-to-all-start.1 = ((bf16[8,64,1024]{2,1,0:T(8,128)(2,1)}), bf16[8,64,1024]{2,1,0:T(8,128)(2,1)S(1)}, u32[]{:S(2)}, u32[]{:S(2)}) async-start(bf16[8,64,1024]{2,1,0:T(8,128)(2,1)} %bitcast.7), calls=%async_computation.1 | async-start | bytes 2097152 | tf_op jit(solution)/shard_map/all_to_all | solution.py:28
  66.1 4.8 %collective-permute-start.7 = (bf16[128,768]{1,0:T(8,128)(2,1)S(1)}, bf16[128,768]{1,0:T(8,128)(2,1)S(1)}, u32[]{:S(2)}, u32[]{:S(2)}) collective-permute-start(bf16[128,768]{1,0:T(8,128)(2,1)S(1)} %bitcast.101), channel_id=1, source_target_pairs={{0,48},{16,0},{32,16},{48,32},{1,49},{17,1},{33,17},{49,33},{2,50}... | collective-permute-start | bytes 589832 | tf_op jit(solution)/shard_map/ppermute | solution.py:64
  70.9 1.9 collective-permute-start.6
  72.9 0.7 dynamic_slice.59
  73.6 6.4 %collective-permute-start.9 = (bf16[128,768]{1,0:T(8,128)(2,1)S(1)}, bf16[128,768]{1,0:T(8,128)(2,1)S(1)}, u32[]{:S(2)}, u32[]{:S(2)}) collective-permute-start(bf16[128,768]{1,0:T(8,128)(2,1)S(1)} %bitcast.103), channel_id=1, source_target_pairs={{0,32},{16,48},{32,0},{48,16},{1,33},{17,49},{33,1},{49,17},{2,34}... | collective-permute-start | bytes 589832 | tf_op jit(solution)/shard_map/ppermute | solution.py:64
  80.0 4.6 %all-to-all-done.1 = bf16[8,64,1024]{2,1,0:T(8,128)(2,1)S(1)} async-done(((bf16[8,64,1024]{2,1,0:T(8,128)(2,1)}), bf16[8,64,1024]{2,1,0:T(8,128)(2,1)S(1)}, u32[]{:S(2)}, u32[]{:S(2)}) %all-to-all-start.1) | async-done | bytes 1048608 | tf_op jit(solution)/shard_map/all_to_all | solution.py:28
  84.8 6.1 %collective-permute-done.6 = bf16[128,768]{1,0:T(8,128)(2,1)S(1)} collective-permute-done((bf16[128,768]{1,0:T(8,128)(2,1)S(1)}, bf16[128,768]{1,0:T(8,128)(2,1)S(1)}, u32[]{:S(2)}, u32[]{:S(2)}) %collective-permute-start.6) | collective-permute-done | bytes 196640 | tf_op jit(solution)/shard_map/ppermute | solution.py:64
  91.0 0.6 gather_fusion.2
  91.5 1.9 collective-permute-start.8
  93.5 3.7 %collective-permute-done.9 = bf16[128,768]{1,0:T(8,128)(2,1)S(1)} collective-permute-done((bf16[128,768]{1,0:T(8,128)(2,1)S(1)}, bf16[128,768]{1,0:T(8,128)(2,1)S(1)}, u32[]{:S(2)}, u32[]{:S(2)}) %collective-permute-start.9) | collective-permute-done | bytes 196640 | tf_op jit(solution)/shard_map/ppermute | solution.py:64
  97.2 7.0 %collective-permute-done.8 = bf16[4,64,256]{2,1,0:T(8,128)(2,1)S(1)} collective-permute-done((bf16[4,64,256]{2,1,0:T(8,128)(2,1)S(1)}, bf16[4,64,256]{2,1,0:T(8,128)(2,1)S(1)}, u32[]{:S(2)}, u32[]{:S(2)}) %collective-permute-start.8) | collective-permute-done | bytes 131104 | tf_op jit(solution)/shard_map/ppermute | solution.py:102
  104.7 1.2 broadcast_in_dim.39
  105.9 4.5 %all-to-all-start.2 = ((bf16[8,64,1152]{2,1,0:T(8,128)(2,1)}), bf16[8,64,1152]{2,1,0:T(8,128)(2,1)S(1)}, u32[]{:S(2)}, u32[]{:S(2)}) async-start(bf16[8,64,1152]{2,1,0:T(8,128)(2,1)} %broadcast_in_dim.39), calls=%async_computation.2 | async-start | bytes 2359296 | tf_op jit(solution)/shard_map/all_to_all | solution.py:28
  110.5 0.7 fusion.64
  111.1 0.6 fusion.41
  111.7 0.6 pad_clamp_fusion
  112.4 0.6 gather_fusion.3
  113.1 1.9 collective-permute-start.10
  115.0 7.3 %pad_maximum_fusion = bf16[8192,512]{1,0:T(8,128)(2,1)} fusion(bf16[8192,256]{1,0:T(8,128)(2,1)} %collective-permute-done.11, bf16[8192,256]{1,0:T(8,128)(2,1)} %param.13), kind=kLoop, calls=%fused_computation.5 | loop fusion | flops 16777216 | bytes 16777216 | tf_op jit(solution)/shard_map/concatenate | solution.py:157
  122.3 0.8 slice.155
  123.1 0.9 broadcast_select_fusion.1
  124.4 0.7 gather_fusion.4
  125.2 2.4 %collective-permute-start.12 = (bf16[16,512]{1,0:T(8,128)(2,1)S(1)}, bf16[16,512]{1,0:T(8,128)(2,1)S(1)}, u32[]{:S(2)}, u32[]{:S(2)}) collective-permute-start(bf16[16,512]{1,0:T(8,128)(2,1)S(1)} %slice.163), channel_id=1, source_target_pairs={{0,1},{1,0},{2,3},{3,2},{4,5},{5,4},{6,7},{7,6},{8,9},{9,8},{10,11... | collective-permute-start | bytes 49160 | tf_op jit(solution)/shard_map/ppermute | solution.py:24
  127.8 1.9 collective-permute-start.14
  129.7 5.0 %convolution_bitcast_fusion = f32[64,512]{1,0:T(8,128)S(1)} fusion(bf16[8,64,1024]{2,1,0:T(8,128)(2,1)S(1)} %gather_fusion.4, bf16[8,1024,512]{2,1,0:T(8,128)(2,1)} %bitcast.94), kind=kOutput, calls=%fused_computation.19 | convolution fusion | flops 536870912 | bytes 9568256 | tf_op jit(solution)/shard_map/ktd,kdn->tn/dot_general | solution.py:20
  134.8 0.4 convolution_select_fusion.1
  135.6 0.7 reshape.439
  136.4 5.7 %all-to-all-start.3 = ((f32[8,1,1024]{2,1,0:T(1,128)}), f32[8,1,1024]{2,1,0:T(1,128)S(1)}, u32[]{:S(2)}, u32[]{:S(2)}) async-start(f32[8,1,1024]{2,1,0:T(1,128)} %reshape.439), calls=%async_computation.3 | async-start | bytes 65536 | tf_op jit(solution)/shard_map/all_to_all | solution.py:28
  142.2 4.1 %all-to-all-done.3 = f32[8,1,1024]{2,1,0:T(1,128)S(1)} async-done(((f32[8,1,1024]{2,1,0:T(1,128)}), f32[8,1,1024]{2,1,0:T(1,128)S(1)}, u32[]{:S(2)}, u32[]{:S(2)}) %all-to-all-start.3) | async-done | bytes 32800 | tf_op jit(solution)/shard_map/all_to_all | solution.py:28
  146.3 0.5 broadcast.449
  146.8 0.7 reduce.3
  148.1 0.3 convolution_select_fusion
  148.8 1.9 collective-permute-start.13
  151.0 0.7 reshape.441
  151.7 5.4 %all-to-all-start.4 = ((f32[16,1,1024]{2,1,0:T(1,128)}), f32[16,1,1024]{2,1,0:T(1,128)S(1)}, u32[]{:S(2)}, u32[]{:S(2)}) async-start(f32[16,1,1024]{2,1,0:T(1,128)} %reshape.441), calls=%async_computation.4 | async-start | bytes 131072 | tf_op jit(solution)/shard_map/all_to_all | solution.py:28
  157.4 0.3 fusion.1
  157.8 3.6 %all-to-all-done.4 = f32[16,1,1024]{2,1,0:T(1,128)S(1)} async-done(((f32[16,1,1024]{2,1,0:T(1,128)}), f32[16,1,1024]{2,1,0:T(1,128)S(1)}, u32[]{:S(2)}, u32[]{:S(2)}) %all-to-all-start.4) | async-done | bytes 65568 | tf_op jit(solution)/shard_map/all_to_all | solution.py:28
  161.4 0.8 reduce.4
  162.5 0.4 fusion.14
  163.1 0.4 fusion
  163.8 34.7 %all_to_all.30 = bf16[32,16,768]{2,1,0:T(8,128)(2,1)S(1)} all-to-all(bf16[32,16,768]{2,1,0:T(8,128)(2,1)S(1)} %bitcast.98), channel_id=1, replica_groups=mesh['z'=8,'yh'=4,'yl'=2,'x'=4,'c'=2] {'yh','z'}, dimensions={0} | all-to-all | bytes 1572864 | tf_op jit(solution)/shard_map/all_to_all | solution.py:28
  198.6 0.6 slice_bitcast_fusion.9
  199.2 0.6 slice_bitcast_fusion
  (114 shorter events, 5.0 us)
Async XLA Ops:
  1.6 11.5 %copy-start.1 = (bf16[512,256]{1,0:T(8,128)(2,1)S(1)}, bf16[512,256]{1,0:T(8,128)(2,1)}, u32[]{:S(2)}) copy-start(bf16[512,256]{1,0:T(8,128)(2,1)} %param.10) | copy-start | bytes 786436
  1.6 27.3 %copy-start.3 = (bf16[128,512]{1,0:T(8,128)(2,1)S(1)}, bf16[128,512]{1,0:T(8,128)(2,1)}, u32[]{:S(2)}) copy-start(bf16[128,512]{1,0:T(8,128)(2,1)} %param.11) | copy-start | bytes 393220
  1.6 27.3 %copy-start.8 = (bf16[512]{0:T(512)(128)(2,1)S(1)}, bf16[512]{0:T(512)(128)(2,1)}, u32[]{:S(2)}) copy-start(bf16[512]{0:T(512)(128)(2,1)} %param.12) | copy-start | bytes 3076
  2.8 45.7 %all-to-all-start = ((bf16[8,160,512]{2,1,0:T(8,128)(2,1)}), bf16[8,160,512]{2,1,0:T(8,128)(2,1)S(1)}, u32[]{:S(2)}, u32[]{:S(2)}) async-start(bf16[8,160,512]{2,1,0:T(8,128)(2,1)} %broadcast_in_dim.36), calls=%async_computation | async-start | bytes 2621440 | tf_op jit(solution)/shard_map/all_to_all | solution.py:28
  13.1 32.0 %collective-permute-start.3 = (bf16[512,256]{1,0:T(8,128)(2,1)S(1)}, bf16[512,256]{1,0:T(8,128)(2,1)S(1)}, u32[]{:S(2)}, u32[]{:S(2)}) collective-permute-start(bf16[512,256]{1,0:T(8,128)(2,1)S(1)} %copy-done.1), channel_id=1, source_target_pairs={{0,32},{16,48},{32,0},{48,16},{1,33},{17,49},{33,1},{49,17},{2,34}... | collective-permute-start | bytes 786440 | tf_op jit(solution)/shard_map/ppermute | solution.py:64
  20.9 23.5 %collective-permute-start.2 = (bf16[512,256]{1,0:T(8,128)(2,1)S(1)}, bf16[512,256]{1,0:T(8,128)(2,1)S(1)}, u32[]{:S(2)}, u32[]{:S(2)}) collective-permute-start(bf16[512,256]{1,0:T(8,128)(2,1)S(1)} %copy-done.1), channel_id=1, source_target_pairs={{0,16},{16,32},{32,48},{48,0},{1,17},{17,33},{33,49},{49,1},{2,18}... | collective-permute-start | bytes 786440 | tf_op jit(solution)/shard_map/ppermute | solution.py:64
  23.6 22.3 %collective-permute-start.4 = (bf16[512,256]{1,0:T(8,128)(2,1)S(1)}, bf16[512,256]{1,0:T(8,128)(2,1)S(1)}, u32[]{:S(2)}, u32[]{:S(2)}) collective-permute-start(bf16[512,256]{1,0:T(8,128)(2,1)S(1)} %copy-done.1), channel_id=1, source_target_pairs={{0,48},{16,0},{32,16},{48,32},{1,49},{17,1},{33,17},{49,33},{2,50}... | collective-permute-start | bytes 786440 | tf_op jit(solution)/shard_map/ppermute | solution.py:64
  28.9 3.2 %collective-permute-start = (bf16[80,512]{1,0:T(8,128)(2,1)S(1)}, bf16[80,512]{1,0:T(8,128)(2,1)S(1)}, u32[]{:S(2)}, u32[]{:S(2)}) collective-permute-start(bf16[80,512]{1,0:T(8,128)(2,1)S(1)} %pad_maximum_fusion.10), channel_id=1, source_target_pairs={{0,1},{1,0},{2,3},{3,2},{4,5},{5,4},{6,7},{7,6},{8,9},{9,8},{10,11... | collective-permute-start | bytes 245768 | tf_op jit(solution)/shard_map/ppermute | solution.py:24
  32.1 16.4 %collective-permute-start.1 = (bf16[80,1024]{1,0:T(8,128)(2,1)S(1)}, bf16[80,1024]{1,0:T(8,128)(2,1)S(1)}, u32[]{:S(2)}, u32[]{:S(2)}) collective-permute-start(bf16[80,1024]{1,0:T(8,128)(2,1)S(1)} %pad_maximum_fusion.7), channel_id=1, source_target_pairs={{0,0},{2,14},{4,12},{6,10},{8,8},{10,6},{12,4},{14,2},{64,66},{66,... | collective-permute-start | bytes 491528 | tf_op jit(solution)/shard_map/ppermute | solution.py:82
  52.2 5.0 %collective-permute-start.5 = (bf16[512,1024]{1,0:T(8,128)(2,1)}, bf16[512,1024]{1,0:T(8,128)(2,1)}, u32[]{:S(2)}, u32[]{:S(2)}) collective-permute-start(bf16[512,1024]{1,0:T(8,128)(2,1)} %convolution_convert_fusion), channel_id=1, source_target_pairs={{0,1},{1,0},{2,3},{3,2},{4,5},{5,4},{6,7},{7,6},{8,9},{9,8},{10,11... | collective-permute-start | bytes 3145736 | tf_op jit(solution)/shard_map/ppermute | solution.py:24
  54.1 60.8 %collective-permute-start.11 = (bf16[8192,256]{1,0:T(8,128)(2,1)}, bf16[8192,256]{1,0:T(8,128)(2,1)}, u32[]{:S(2)}, u32[]{:S(2)}) collective-permute-start(bf16[8192,256]{1,0:T(8,128)(2,1)} %param.13), channel_id=1, source_target_pairs={{0,1},{1,0},{2,3},{3,2},{4,5},{5,4},{6,7},{7,6},{8,9},{9,8},{10,11... | collective-permute-start | bytes 12582920 | tf_op jit(solution)/shard_map/ppermute | solution.py:24
  57.2 8.7 %copy-start.9 = (s32[32]{0:T(128)S(1)}, s32[32]{0:T(128)}, u32[]{:S(2)}) copy-start(s32[32]{0:T(128)} %param.17) | copy-start | bytes 388
  60.5 5.4 %copy-start.5 = (s32[128]{0:T(128)S(1)}, s32[128]{0:T(128)}, u32[]{:S(2)}) copy-start(s32[128]{0:T(128)} %param.16) | copy-start | bytes 1540
  60.5 24.1 %all-to-all-start.1 = ((bf16[8,64,1024]{2,1,0:T(8,128)(2,1)}), bf16[8,64,1024]{2,1,0:T(8,128)(2,1)S(1)}, u32[]{:S(2)}, u32[]{:S(2)}) async-start(bf16[8,64,1024]{2,1,0:T(8,128)(2,1)} %bitcast.7), calls=%async_computation.1 | async-start | bytes 2097152 | tf_op jit(solution)/shard_map/all_to_all | solution.py:28
  66.1 18.7 %collective-permute-start.7 = (bf16[128,768]{1,0:T(8,128)(2,1)S(1)}, bf16[128,768]{1,0:T(8,128)(2,1)S(1)}, u32[]{:S(2)}, u32[]{:S(2)}) collective-permute-start(bf16[128,768]{1,0:T(8,128)(2,1)S(1)} %bitcast.101), channel_id=1, source_target_pairs={{0,48},{16,0},{32,16},{48,32},{1,49},{17,1},{33,17},{49,33},{2,50}... | collective-permute-start | bytes 589832 | tf_op jit(solution)/shard_map/ppermute | solution.py:64
  70.9 20.0 %collective-permute-start.6 = (bf16[128,768]{1,0:T(8,128)(2,1)S(1)}, bf16[128,768]{1,0:T(8,128)(2,1)S(1)}, u32[]{:S(2)}, u32[]{:S(2)}) collective-permute-start(bf16[128,768]{1,0:T(8,128)(2,1)S(1)} %bitcast.102), channel_id=1, source_target_pairs={{0,16},{16,32},{32,48},{48,0},{1,17},{17,33},{33,49},{49,1},{2,18}... | collective-permute-start | bytes 589832 | tf_op jit(solution)/shard_map/ppermute | solution.py:64
  73.6 23.6 %collective-permute-start.9 = (bf16[128,768]{1,0:T(8,128)(2,1)S(1)}, bf16[128,768]{1,0:T(8,128)(2,1)S(1)}, u32[]{:S(2)}, u32[]{:S(2)}) collective-permute-start(bf16[128,768]{1,0:T(8,128)(2,1)S(1)} %bitcast.103), channel_id=1, source_target_pairs={{0,32},{16,48},{32,0},{48,16},{1,33},{17,49},{33,1},{49,17},{2,34}... | collective-permute-start | bytes 589832 | tf_op jit(solution)/shard_map/ppermute | solution.py:64
  91.5 12.6 %collective-permute-start.8 = (bf16[4,64,256]{2,1,0:T(8,128)(2,1)S(1)}, bf16[4,64,256]{2,1,0:T(8,128)(2,1)S(1)}, u32[]{:S(2)}, u32[]{:S(2)}) collective-permute-start(bf16[4,64,256]{2,1,0:T(8,128)(2,1)S(1)} %gather_fusion.2), channel_id=1, source_target_pairs={{0,0},{2,66},{4,132},{6,198},{8,264},{10,330},{12,396},{14,462},{6... | collective-permute-start | bytes 393224 | tf_op jit(solution)/shard_map/ppermute | solution.py:102
  105.9 18.0 %all-to-all-start.2 = ((bf16[8,64,1152]{2,1,0:T(8,128)(2,1)}), bf16[8,64,1152]{2,1,0:T(8,128)(2,1)S(1)}, u32[]{:S(2)}, u32[]{:S(2)}) async-start(bf16[8,64,1152]{2,1,0:T(8,128)(2,1)} %broadcast_in_dim.39), calls=%async_computation.2 | async-start | bytes 2359296 | tf_op jit(solution)/shard_map/all_to_all | solution.py:28
  113.1 9.3 %collective-permute-start.10 = (bf16[512,768]{1,0:T(8,128)(2,1)S(1)}, bf16[512,768]{1,0:T(8,128)(2,1)S(1)}, u32[]{:S(2)}, u32[]{:S(2)}) collective-permute-start(bf16[512,768]{1,0:T(8,128)(2,1)S(1)} %bitcast.95), channel_id=1, source_target_pairs={{0,1},{1,0},{2,3},{3,2},{4,5},{5,4},{6,7},{7,6},{8,9},{9,8},{10,11... | collective-permute-start | bytes 2359304 | tf_op jit(solution)/shard_map/ppermute | solution.py:24
  125.2 16.8 %collective-permute-start.12 = (bf16[16,512]{1,0:T(8,128)(2,1)S(1)}, bf16[16,512]{1,0:T(8,128)(2,1)S(1)}, u32[]{:S(2)}, u32[]{:S(2)}) collective-permute-start(bf16[16,512]{1,0:T(8,128)(2,1)S(1)} %slice.163), channel_id=1, source_target_pairs={{0,1},{1,0},{2,3},{3,2},{4,5},{5,4},{6,7},{7,6},{8,9},{9,8},{10,11... | collective-permute-start | bytes 49160 | tf_op jit(solution)/shard_map/ppermute | solution.py:24
  127.8 35.3 %collective-permute-start.14 = (bf16[64,512]{1,0:T(8,128)(2,1)S(1)}, bf16[64,512]{1,0:T(8,128)(2,1)S(1)}, u32[]{:S(2)}, u32[]{:S(2)}) collective-permute-start(bf16[64,512]{1,0:T(8,128)(2,1)S(1)} %dynamic-slice_bitcast_fusion), channel_id=1, source_target_pairs={{0,1},{1,0},{2,3},{3,2},{4,5},{5,4},{6,7},{7,6},{8,9},{9,8},{10,11... | collective-permute-start | bytes 196616 | tf_op jit(solution)/shard_map/ppermute | solution.py:24
  129.7 5.0 %copy-start = (bf16[512,512]{1,0:T(8,128)(2,1)S(1)}, bf16[512,512]{1,0:T(8,128)(2,1)}, u32[]{:S(2)}) copy-start(bf16[512,512]{1,0:T(8,128)(2,1)} %get-tuple-element.31) | copy-start | bytes 1572868
  129.7 5.0 %copy-start.4 = (s32[512]{0:T(512)S(1)}, s32[512]{0:T(512)}, u32[]{:S(2)}) copy-start(s32[512]{0:T(512)} %fusion.41) | copy-start | bytes 6148
  129.7 5.0 %copy-start.7 = (s32[64]{0:T(128)S(1)}, s32[64]{0:T(128)}, u32[]{:S(2)}) copy-start(s32[64]{0:T(128)} %get-tuple-element.55) | copy-start | bytes 772
  134.7 13.1 %copy-start.2 = (bf16[512,256]{1,0:T(8,128)(2,1)S(1)}, bf16[512,256]{1,0:T(8,128)(2,1)}, u32[]{:S(2)}) copy-start(bf16[512,256]{1,0:T(8,128)(2,1)} %slice.155) | copy-start | bytes 786436
  134.7 13.1 %copy-start.10 = (f32[64]{0:T(128)S(1)}, f32[64]{0:T(128)}, u32[]{:S(2)}) copy-start(f32[64]{0:T(128)} %dynamic_slice.59) | copy-start | bytes 772
  136.4 9.9 %all-to-all-start.3 = ((f32[8,1,1024]{2,1,0:T(1,128)}), f32[8,1,1024]{2,1,0:T(1,128)S(1)}, u32[]{:S(2)}, u32[]{:S(2)}) async-start(f32[8,1,1024]{2,1,0:T(1,128)} %reshape.439), calls=%async_computation.3 | async-start | bytes 65536 | tf_op jit(solution)/shard_map/all_to_all | solution.py:28
  147.9 9.5 %copy-start.6 = (s32[64]{0:T(128)S(1)}, s32[64]{0:T(128)}, u32[]{:S(2)}) copy-start(s32[64]{0:T(128)} %get-tuple-element.54) | copy-start | bytes 772
  148.8 8.3 %collective-permute-start.13 = (bf16[64,384]{1,0:T(8,128)(2,1)S(1)}, bf16[64,384]{1,0:T(8,128)(2,1)S(1)}, u32[]{:S(2)}, u32[]{:S(2)}) collective-permute-start(bf16[64,384]{1,0:T(8,128)(2,1)S(1)} %concatenate.67), channel_id=1, source_target_pairs={{0,1},{1,0},{2,3},{3,2},{4,5},{5,4},{6,7},{7,6},{8,9},{9,8},{10,11... | collective-permute-start | bytes 147464 | tf_op jit(solution)/shard_map/ppermute | solution.py:24
  151.7 9.7 %all-to-all-start.4 = ((f32[16,1,1024]{2,1,0:T(1,128)}), f32[16,1,1024]{2,1,0:T(1,128)S(1)}, u32[]{:S(2)}, u32[]{:S(2)}) async-start(f32[16,1,1024]{2,1,0:T(1,128)} %reshape.441), calls=%async_computation.4 | async-start | bytes 131072 | tf_op jit(solution)/shard_map/all_to_all | solution.py:28

commit v8 on v7

--- a/solution.py
+++ b/solution.py
@@ -134,10 +134,8 @@
 
     chip_features = lax.dynamic_index_in_dim(features, chip, 0, keepdims=False)
     own_scaled = half(chip_features, core, block, 1)
-    low_part = select(dot("jd,td->jt", downs, chip_features))
-    low_round = (jnp.sum(gather(low_part, CHIPS, n_chips), axis=0) * inv_row).astype(BF)
     partner_scaled = swap(half(chip_features, other, block, 1))
-    low_wide = widen(low_round, own_mask)
+    low_part = select(dot("jd,td->jt", downs, chip_features)) * inv_row
 
     target = lax.dynamic_slice(
         features, (chip // 2, 0, (chip % 2) * 2 * out_block), (1, mine, 2 * out_block)
@@ -152,33 +150,53 @@
     keep_mask = (position < tokens - 1) & (tenant_of == following)
     is_tenant = tenant_of[:, None] == jnp.arange(tenants, dtype=jnp.int32)[None, :]
     count = jnp.sum(jnp.where(is_tenant, tenant_count.astype(F32)[None, :], 0.0), axis=1)
-    weight = half(keep_mask.astype(F32) / count, core, mine)[:, None]
-
-    both_weights = jnp.concatenate([draft_weight, draft_weight_other], axis=1)
-    draft = dot("ktd,kdn->tn", features, both_weights.reshape(n_chips, 2 * block, 2 * out_block))
-    draft, low_wide = lax.optimization_barrier((draft, low_wide))
-    draft = draft * inv_column + ADAPTER_SCALE * dot("jt,jn->tn", low_wide, ups)
-    grad = ((draft - target.astype(F32)) * weight).astype(BF)
-    grad_own = grad[:, :out_block]
-
-    back_part = select(dot("jc,tc->jt", ups, grad))
-    low_lanes = jnp.concatenate([low_round.T, *split(inv_column), jnp.zeros((mine, 126 - rank), BF)], axis=1)
-    partner = jnp.concatenate([grad[:, out_block:], low_lanes], axis=1)
-    back_part, partner = lax.optimization_barrier((back_part, partner))
-    backs = gather(back_part, MP, 2 * n_chips)
-    partner = swap(partner)
-    backs = jnp.sum(backs.reshape(n_chips, 2, rank, mine), axis=0)
-    partner_codes = partner[:, out_block:].T
-    inv_partner = partner_codes[rank : rank + 1].astype(F32) + partner_codes[rank + 1 : rank + 2].astype(F32)
-    back_scaled = (ADAPTER_SCALE * half(backs, core, 1)[0] * inv_row).astype(BF)
-    back_partner = (ADAPTER_SCALE * half(backs, other, 1)[0] * inv_partner).astype(BF)
-
-    grad_up = dot("jt,tc->jc", low_wide, grad_own) + dot(
-        "jt,tc->jc", widen(partner_codes[:rank], partner_mask), partner[:, :out_block]
-    )
-    grad_down = dot("jt,td->jd", widen(back_scaled, own_mask), own_scaled) + dot(
-        "jt,td->jd", widen(back_partner, partner_mask), partner_scaled
-    )
+    weights = keep_mask.astype(F32) / count
+    weight, weight_row = half(weights, core, mine)[:, None], half(weights, core, mine)[None]
+    partner_weight, partner_weight_row = half(weights, other, mine)[:, None], half(weights, other, mine)[None]
+
+    def plain(columns, part):
+        draft = dot("ktd,kdn->tn", features, columns.reshape(n_chips, 2 * block, out_block))
+        return (draft * inv_column - target[:, part * out_block : (part + 1) * out_block].astype(F32)) * weight
+
+    plain_other = plain(draft_weight_other, 1).astype(BF)
+    lanes = jnp.concatenate([*split(inv_column), jnp.zeros((mine, 126), BF)], axis=1)
+    partner = swap(jnp.concatenate([plain_other, lanes], axis=1))
+    plain_own = plain(draft_weight, 0)
+
+    back_part = select(dot("jc,tc->jt", ups, jnp.concatenate([plain_own.astype(BF), plain_other], axis=1)))
+    some = tenants * rank // 2
+    some_ups = half(ups, core, some)
+    same = slot[:some, None] == slot[None, :some]
+    square_part = jnp.where(same, dot("jc,ic->ji", some_ups, some_ups), 0.0)
+    square_part = jnp.sum(square_part.reshape(tenants // 2, rank, some), axis=0)
+    codes = jnp.concatenate([low_part, back_part], axis=1)
+    codes = gather(jnp.concatenate([*split(codes), square_part.astype(BF)], axis=1), MP, 2 * n_chips)
+    codes = jnp.sum(codes.reshape(n_chips, 2, rank, 4 * mine + some).astype(F32), axis=0)
+    square = jnp.concatenate([codes[0, :, 4 * mine :], codes[1, :, 4 * mine :]], axis=1).astype(BF)
+    codes = codes[:, :, : 2 * mine] + codes[:, :, 2 * mine : 4 * mine]
+    partner_inv = partner[:, out_block:].T
+    partner_inv = partner_inv[:1].astype(F32) + partner_inv[1:2].astype(F32)
+
+    def finish(code, mask, plain_grad, column, row, inv):
+        low_wide = widen(code[:, :mine].astype(BF), mask)
+        term = ADAPTER_SCALE * dot("jt,jn->tn", low_wide, ups[:, :out_block])
+        grad = (plain_grad + term * column).astype(BF)
+        back = code[:, mine:] + ADAPTER_SCALE * dot("rj,jt->rt", square, low_wide) * row
+        return low_wide, grad, widen((ADAPTER_SCALE * back * inv).astype(BF), mask)
+
+    low_wide, grad, back_wide = finish(
+        half(codes, core, 1)[0], own_mask, plain_own, weight, weight_row, inv_row
+    )
+    partner_low, partner_grad, partner_back = finish(
+        half(codes, other, 1)[0],
+        partner_mask,
+        partner[:, :out_block].astype(F32),
+        partner_weight,
+        partner_weight_row,
+        partner_inv,
+    )
+    grad_up = dot("jt,tc->jc", low_wide, grad) + dot("jt,tc->jc", partner_low, partner_grad)
+    grad_down = dot("jt,td->jd", back_wide, own_scaled) + dot("jt,td->jd", partner_back, partner_scaled)
     grads = jnp.concatenate([grad_down.astype(BF), grad_up.astype(BF)], axis=1)
     grads = exchange(grads.reshape(tenants, rank, block + out_block), ("yh", "z"))
     grads = jnp.sum(grads.astype(F32), axis=0)

time: 202 us -> 194 us (0.960)
  the two profiles are of different devices: /device:TPU:6 before, /device:TPU:76 now
where the time goes in v8:
time: 194 us; the launch traced here: 193 us
  starting transfers between devices  83.6 us (43%)
  blocking collectives  37.2 us (19%)
  waiting for transfers between devices  27.8 us (14%)
  matrix products  19.6 us (10%)
  local copies, waits for them, and re-layouts  15.7 us (8%)
  other arithmetic  7.27 us (4%)
    all_to_all x1, blocking collectives, exchange(): return lax.all_to_all(value, axis, 0, 0)  37.2 us
    all_to_all x4, starting transfers between devices, exchange(): return lax.all_to_all(value, axis, 0, 0)  32.6 us
    ppermute x6, starting transfers between devices, around(): lax.ppermute(value, 'yh', [(i, (i + s) % n_yh) for i in range(n_yh)])  28.1 us
    dot_general x13, matrix products, dot(): return jnp.einsum(subscripts, left, right, preferred_element_type=F32)  19.6 us
    ppermute x6, waiting for transfers between devices, around(): lax.ppermute(value, 'yh', [(i, (i + s) % n_yh) for i in range(n_yh)])  17.2 us
    ppermute x7, starting transfers between devices, swap(): return lax.ppermute(value, 'c', [(0, 1), (1, 0)])  13.9 us
    ppermute x1, starting transfers between devices, shards(): projected = lax.ppermute(summed[turned], ('z', 'yl', 'x'), homes)  5.1 us
    all_to_all x4, waiting for transfers between devices, exchange(): return lax.all_to_all(value, axis, 0, 0)  4.75 us
  transfers between devices with their start and end apart: 19, of which 10 were waited for; matrix products, arithmetic and copies ran while one was open for 14% of the time, Pallas kernels for 0%

profile of v8, /device:TPU:76, one launch (start us, length us, event | category | flops | bytes accessed | tf_op | source)
XLA Modules:
  0.0 192.8 jit_solution(7830719501795207704)
XLA Ops:
  0.6 1.0 fusion.22
  1.6 1.2 broadcast_in_dim.34
  2.8 10.0 %all-to-all-start = ((bf16[8,160,512]{2,1,0:T(8,128)(2,1)}), bf16[8,160,512]{2,1,0:T(8,128)(2,1)S(1)}, u32[]{:S(2)}, u32[]{:S(2)}) async-start(bf16[8,160,512]{2,1,0:T(8,128)(2,1)} %broadcast_in_dim.34), calls=%async_computation | async-start | bytes 2621440 | tf_op jit(solution)/shard_map/all_to_all | solution.py:28
  12.8 4.5 %collective-permute-start.2 = (bf16[512,256]{1,0:T(8,128)(2,1)S(1)}, bf16[512,256]{1,0:T(8,128)(2,1)S(1)}, u32[]{:S(2)}, u32[]{:S(2)}) collective-permute-start(bf16[512,256]{1,0:T(8,128)(2,1)S(1)} %copy-done), channel_id=1, source_target_pairs={{0,16},{16,32},{32,48},{48,0},{1,17},{17,33},{33,49},{49,1},{2,18}... | collective-permute-start | bytes 786440 | tf_op jit(solution)/shard_map/ppermute | solution.py:64
  17.3 5.0 %collective-permute-start.3 = (bf16[512,256]{1,0:T(8,128)(2,1)S(1)}, bf16[512,256]{1,0:T(8,128)(2,1)S(1)}, u32[]{:S(2)}, u32[]{:S(2)}) collective-permute-start(bf16[512,256]{1,0:T(8,128)(2,1)S(1)} %copy-done), channel_id=1, source_target_pairs={{0,32},{16,48},{32,0},{48,16},{1,33},{17,49},{33,1},{49,17},{2,34}... | collective-permute-start | bytes 786440 | tf_op jit(solution)/shard_map/ppermute | solution.py:64
  22.3 5.3 %collective-permute-start.4 = (bf16[512,256]{1,0:T(8,128)(2,1)S(1)}, bf16[512,256]{1,0:T(8,128)(2,1)S(1)}, u32[]{:S(2)}, u32[]{:S(2)}) collective-permute-start(bf16[512,256]{1,0:T(8,128)(2,1)S(1)} %copy-done), channel_id=1, source_target_pairs={{0,48},{16,0},{32,16},{48,32},{1,49},{17,1},{33,17},{49,33},{2,50}... | collective-permute-start | bytes 786440 | tf_op jit(solution)/shard_map/ppermute | solution.py:64
  27.7 1.9 collective-permute-start
  29.6 0.8 constant_dynamic-update-slice_fusion.3
  30.9 3.9 %collective-permute-start.1 = (bf16[80,1024]{1,0:T(8,128)(2,1)S(1)}, bf16[80,1024]{1,0:T(8,128)(2,1)S(1)}, u32[]{:S(2)}, u32[]{:S(2)}) collective-permute-start(bf16[80,1024]{1,0:T(8,128)(2,1)S(1)} %pad_maximum_fusion.5), channel_id=1, source_target_pairs={{0,0},{2,14},{4,12},{6,10},{8,8},{10,6},{12,4},{14,2},{64,66},{66,... | collective-permute-start | bytes 491528 | tf_op jit(solution)/shard_map/ppermute | solution.py:82
  34.8 0.7 constant_dynamic-update-slice_fusion.2
  35.5 1.2 collective-permute-done.3
  36.7 0.8 constant_dynamic-update-slice_fusion.1
  37.5 8.4 %collective-permute-done.4 = bf16[512,256]{1,0:T(8,128)(2,1)S(1)} collective-permute-done((bf16[512,256]{1,0:T(8,128)(2,1)S(1)}, bf16[512,256]{1,0:T(8,128)(2,1)S(1)}, u32[]{:S(2)}, u32[]{:S(2)}) %collective-permute-start.4) | collective-permute-done | bytes 262176 | tf_op jit(solution)/shard_map/ppermute | solution.py:64
  45.8 0.8 constant_dynamic-update-slice_fusion
  46.6 0.8 collective-permute-done.1
  47.6 0.6 gather_fusion.1
  48.2 2.9 %convolution_convert_fusion = bf16[512,1024]{1,0:T(8,128)(2,1)} fusion(bf16[512,512]{1,0:T(8,128)(2,1)S(1)} %bitcast.123, bf16[512,1024]{1,0:T(8,128)(2,1)} %constant_dynamic-update-slice_fusion), kind=kOutput, calls=%fused_computation.7 | convolution fusion | flops 537395200 | bytes 2621440 | tf_op jit(solution)/shard_map/tk,kn->tn/dot_general | solution.py:20
  51.1 1.9 collective-permute-start.5
  53.0 0.6 gather_fusion
  53.6 2.3 %collective-permute-done.5 = bf16[512,1024]{1,0:T(8,128)(2,1)} collective-permute-done((bf16[512,1024]{1,0:T(8,128)(2,1)}, bf16[512,1024]{1,0:T(8,128)(2,1)}, u32[]{:S(2)}, u32[]{:S(2)}) %collective-permute-start.5) | collective-permute-done | bytes 1048608 | tf_op jit(solution)/shard_map/ppermute | solution.py:24
  56.0 3.3 %add_convert_fusion = bf16[512,1024]{1,0:T(8,128)(2,1)} fusion(bf16[512,1024]{1,0:T(8,128)(2,1)} %collective-permute-done.5, bf16[512,512]{1,0:T(8,128)(2,1)S(1)} %bitcast.122, bf16[512,1024]{1,0:T(8,128)(2,1)} %constant_dynamic-update-slice_fusion), kind=kOutput, calls=%fused_computation.5 | convolution fusion | flops 538443776 | bytes 3670016 | tf_op jit(solution)/shard_map/tk,kn->tn/dot_general | solution.py:20
  59.3 7.4 %all-to-all-start.1 = ((bf16[8,64,1024]{2,1,0:T(8,128)(2,1)}), bf16[8,64,1024]{2,1,0:T(8,128)(2,1)S(1)}, u32[]{:S(2)}, u32[]{:S(2)}) async-start(bf16[8,64,1024]{2,1,0:T(8,128)(2,1)} %bitcast.7), calls=%async_computation.1 | async-start | bytes 2097152 | tf_op jit(solution)/shard_map/all_to_all | solution.py:28
  66.6 3.0 %collective-permute-start.6 = (bf16[128,768]{1,0:T(8,128)(2,1)S(1)}, bf16[128,768]{1,0:T(8,128)(2,1)S(1)}, u32[]{:S(2)}, u32[]{:S(2)}) collective-permute-start(bf16[128,768]{1,0:T(8,128)(2,1)S(1)} %bitcast.115), channel_id=1, source_target_pairs={{0,16},{16,32},{32,48},{48,0},{1,17},{17,33},{33,49},{49,1},{2,18}... | collective-permute-start | bytes 589832 | tf_op jit(solution)/shard_map/ppermute | solution.py:64
  69.7 4.9 %collective-permute-start.7 = (bf16[128,768]{1,0:T(8,128)(2,1)S(1)}, bf16[128,768]{1,0:T(8,128)(2,1)S(1)}, u32[]{:S(2)}, u32[]{:S(2)}) collective-permute-start(bf16[128,768]{1,0:T(8,128)(2,1)S(1)} %bitcast.116), channel_id=1, source_target_pairs={{0,48},{16,0},{32,16},{48,32},{1,49},{17,1},{33,17},{49,33},{2,50}... | collective-permute-start | bytes 589832 | tf_op jit(solution)/shard_map/ppermute | solution.py:64
  74.6 1.9 collective-permute-start.12
  76.5 5.4 %collective-permute-start.9 = (bf16[128,768]{1,0:T(8,128)(2,1)S(1)}, bf16[128,768]{1,0:T(8,128)(2,1)S(1)}, u32[]{:S(2)}, u32[]{:S(2)}) collective-permute-start(bf16[128,768]{1,0:T(8,128)(2,1)S(1)} %bitcast.117), channel_id=1, source_target_pairs={{0,32},{16,48},{32,0},{48,16},{1,33},{17,49},{33,1},{49,17},{2,34}... | collective-permute-start | bytes 589832 | tf_op jit(solution)/shard_map/ppermute | solution.py:64
  81.9 2.5 %all-to-all-done.1 = bf16[8,64,1024]{2,1,0:T(8,128)(2,1)S(1)} async-done(((bf16[8,64,1024]{2,1,0:T(8,128)(2,1)}), bf16[8,64,1024]{2,1,0:T(8,128)(2,1)S(1)}, u32[]{:S(2)}, u32[]{:S(2)}) %all-to-all-start.1) | async-done | bytes 1048608 | tf_op jit(solution)/shard_map/all_to_all | solution.py:28
  84.6 4.6 %collective-permute-done.7 = bf16[128,768]{1,0:T(8,128)(2,1)S(1)} collective-permute-done((bf16[128,768]{1,0:T(8,128)(2,1)S(1)}, bf16[128,768]{1,0:T(8,128)(2,1)S(1)}, u32[]{:S(2)}, u32[]{:S(2)}) %collective-permute-start.7) | collective-permute-done | bytes 196640 | tf_op jit(solution)/shard_map/ppermute | solution.py:64
  89.8 5.1 %collective-permute-start.8 = (bf16[4,64,256]{2,1,0:T(8,128)(2,1)S(1)}, bf16[4,64,256]{2,1,0:T(8,128)(2,1)S(1)}, u32[]{:S(2)}, u32[]{:S(2)}) collective-permute-start(bf16[4,64,256]{2,1,0:T(8,128)(2,1)S(1)} %gather_fusion.2), channel_id=1, source_target_pairs={{0,0},{2,66},{4,132},{6,198},{8,264},{10,330},{12,396},{14,462},{6... | collective-permute-start | bytes 393224 | tf_op jit(solution)/shard_map/ppermute | solution.py:102
  94.9 3.1 %collective-permute-done.9 = bf16[128,768]{1,0:T(8,128)(2,1)S(1)} collective-permute-done((bf16[128,768]{1,0:T(8,128)(2,1)S(1)}, bf16[128,768]{1,0:T(8,128)(2,1)S(1)}, u32[]{:S(2)}, u32[]{:S(2)}) %collective-permute-start.9) | collective-permute-done | bytes 196640 | tf_op jit(solution)/shard_map/ppermute | solution.py:64
  98.1 2.2 %collective-permute-done.8 = bf16[4,64,256]{2,1,0:T(8,128)(2,1)S(1)} collective-permute-done((bf16[4,64,256]{2,1,0:T(8,128)(2,1)S(1)}, bf16[4,64,256]{2,1,0:T(8,128)(2,1)S(1)}, u32[]{:S(2)}, u32[]{:S(2)}) %collective-permute-start.8) | collective-permute-done | bytes 131104 | tf_op jit(solution)/shard_map/ppermute | solution.py:102
  100.8 1.2 broadcast_in_dim.40
  102.0 8.9 %all-to-all-start.2 = ((bf16[8,64,1152]{2,1,0:T(8,128)(2,1)}), bf16[8,64,1152]{2,1,0:T(8,128)(2,1)S(1)}, u32[]{:S(2)}, u32[]{:S(2)}) async-start(bf16[8,64,1152]{2,1,0:T(8,128)(2,1)} %broadcast_in_dim.40), calls=%async_computation.2 | async-start | bytes 2359296 | tf_op jit(solution)/shard_map/all_to_all | solution.py:28
  111.0 0.6 slice.158
  111.6 0.7 fusion.87
  112.4 0.6 gather_fusion.3
  113.0 1.9 collective-permute-start.10
  115.1 0.7 broadcast_multiply_fusion.2
  115.7 0.6 fusion.55
  116.3 0.6 pad_clamp_fusion
  116.9 0.6 fusion.43
  117.6 1.0 convolution_select_fusion
  118.7 0.6 reduce_sum.93
  119.3 0.9 broadcast_select_fusion.1
  120.2 2.2 %all-to-all-done.2 = bf16[8,64,1152]{2,1,0:T(8,128)(2,1)S(1)} async-done(((bf16[8,64,1152]{2,1,0:T(8,128)(2,1)}), bf16[8,64,1152]{2,1,0:T(8,128)(2,1)S(1)}, u32[]{:S(2)}, u32[]{:S(2)}) %all-to-all-start.2) | async-done | bytes 1179680 | tf_op jit(solution)/shard_map/all_to_all | solution.py:28
  122.5 0.6 copy.44
  123.1 0.6 copy.45
  123.9 0.7 gather_fusion.4
  124.8 1.9 collective-permute-start.11
  126.7 1.5 convolution_select_fusion.2
  128.7 3.0 %fusion.34 = (bf16[64,256]{1,0:T(8,128)(2,1)S(1)}, f32[64,256]{1,0:T(8,128)S(1)}) fusion(f32[64]{0:T(128)S(1)} %copy-done.13, s32[]{:T(128)S(6)} %select_n.261, bf16[1,512]{1,0:T(2,128)(2,1)S(1)} %slice.193, bf16[63,512]{1,0:T(8,128)(2,1)S(1)} %slice.191, f32[64]{0:T(128)S(1)} %bitcast.133, bf16[8,64,1024]{2,1,0:T(8,128)(2,1)S(1)} %gather_fusion.4, ...), kind=kOutput, calls=%fused_computation.86 | convolution fusion | flops 268566528 | bytes 5407236 | tf_op jit(solution)/shard_map/ktd,kdn->tn/dot_general | solution.py:20
  131.8 3.0 %fusion.7 = bf16[64,256]{1,0:T(8,128)(2,1)S(1)} fusion(bf16[8,64,1024]{2,1,0:T(8,128)(2,1)S(1)} %gather_fusion.4, bf16[8,1024,256]{2,1,0:T(8,128)(2,1)} %bitcast.30, s32[]{:T(128)S(6)} %select_n.263, bf16[63,512]{1,0:T(8,128)(2,1)S(1)} %slice.191, bf16[1,512]{1,0:T(2,128)(2,1)S(1)} %slice.193, f32[64]{0:T(128)S(1)} %copy-done.13, f32[64]{0:T(128)S(1)} %bitcast.134), kind=kOutput, calls=%fused_computation.24 | convolution fusion | flops 268566528 | bytes 5341700 | tf_op jit(solution)/shard_map/ktd,kdn->tn/dot_general | solution.py:20
  135.5 0.7 broadcast_in_dim.47
  136.2 6.3 %all-to-all-start.3 = ((bf16[16,16,512]{2,1,0:T(8,128)(2,1)}), bf16[16,16,512]{2,1,0:T(8,128)(2,1)S(1)}, u32[]{:S(2)}, u32[]{:S(2)}) async-start(bf16[16,16,512]{2,1,0:T(8,128)(2,1)} %broadcast_in_dim.47), calls=%async_computation.3 | async-start | bytes 524288 | tf_op jit(solution)/shard_map/all_to_all | solution.py:28
  142.7 2.1 %collective-permute-start.13 = (bf16[64,384]{1,0:T(8,128)(2,1)S(1)}, bf16[64,384]{1,0:T(8,128)(2,1)S(1)}, u32[]{:S(2)}, u32[]{:S(2)}) collective-permute-start(bf16[64,384]{1,0:T(8,128)(2,1)S(1)} %pad_maximum_fusion.10), channel_id=1, source_target_pairs={{0,1},{1,0},{2,3},{3,2},{4,5},{5,4},{6,7},{7,6},{8,9},{9,8},{10,11... | collective-permute-start | bytes 147464 | tf_op jit(solution)/shard_map/ppermute | solution.py:24
  144.7 0.7 dynamic-slice_bitcast_fusion
  145.4 2.3 %collective-permute-start.14 = (bf16[64,512]{1,0:T(8,128)(2,1)}, bf16[64,512]{1,0:T(8,128)(2,1)}, u32[]{:S(2)}, u32[]{:S(2)}) collective-permute-start(bf16[64,512]{1,0:T(8,128)(2,1)} %dynamic-slice_bitcast_fusion), channel_id=1, source_target_pairs={{0,1},{1,0},{2,3},{3,2},{4,5},{5,4},{6,7},{7,6},{8,9},{9,8},{10,11... | collective-permute-start | bytes 196616 | tf_op jit(solution)/shard_map/ppermute | solution.py:24
  147.7 0.8 multiply_reduce_fusion.1
  150.3 1.3 fusion.1
  151.7 0.9 fusion.15
  152.7 1.2 fusion
  154.3 37.2 %all_to_all.25 = bf16[32,16,768]{2,1,0:T(8,128)(2,1)S(1)} all-to-all(bf16[32,16,768]{2,1,0:T(8,128)(2,1)S(1)} %bitcast.111), channel_id=1, replica_groups=mesh['z'=8,'yh'=4,'yl'=2,'x'=4,'c'=2] {'yh','z'}, dimensions={0} | all-to-all | bytes 1572864 | tf_op jit(solution)/shard_map/all_to_all | solution.py:28
  191.6 0.6 slice_bitcast_fusion
  192.2 0.6 slice_bitcast_fusion.9
  (139 shorter events, 6.2 us)
Async XLA Ops:
  1.6 11.2 %copy-start = (bf16[512,256]{1,0:T(8,128)(2,1)S(1)}, bf16[512,256]{1,0:T(8,128)(2,1)}, u32[]{:S(2)}) copy-start(bf16[512,256]{1,0:T(8,128)(2,1)} %param.10) | copy-start | bytes 786436
  1.6 26.0 %copy-start.5 = (bf16[128,512]{1,0:T(8,128)(2,1)S(1)}, bf16[128,512]{1,0:T(8,128)(2,1)}, u32[]{:S(2)}) copy-start(bf16[128,512]{1,0:T(8,128)(2,1)} %param.11) | copy-start | bytes 393220
  1.6 26.0 %copy-start.24 = (bf16[512]{0:T(512)(128)(2,1)S(1)}, bf16[512]{0:T(512)(128)(2,1)}, u32[]{:S(2)}) copy-start(bf16[512]{0:T(512)(128)(2,1)} %param.12) | copy-start | bytes 3076
  2.8 44.6 %all-to-all-start = ((bf16[8,160,512]{2,1,0:T(8,128)(2,1)}), bf16[8,160,512]{2,1,0:T(8,128)(2,1)S(1)}, u32[]{:S(2)}, u32[]{:S(2)}) async-start(bf16[8,160,512]{2,1,0:T(8,128)(2,1)} %broadcast_in_dim.34), calls=%async_computation | async-start | bytes 2621440 | tf_op jit(solution)/shard_map/all_to_all | solution.py:28
  12.8 22.0 %collective-permute-start.2 = (bf16[512,256]{1,0:T(8,128)(2,1)S(1)}, bf16[512,256]{1,0:T(8,128)(2,1)S(1)}, u32[]{:S(2)}, u32[]{:S(2)}) collective-permute-start(bf16[512,256]{1,0:T(8,128)(2,1)S(1)} %copy-done), channel_id=1, source_target_pairs={{0,16},{16,32},{32,48},{48,0},{1,17},{17,33},{33,49},{49,1},{2,18}... | collective-permute-start | bytes 786440 | tf_op jit(solution)/shard_map/ppermute | solution.py:64
  17.3 19.5 %collective-permute-start.3 = (bf16[512,256]{1,0:T(8,128)(2,1)S(1)}, bf16[512,256]{1,0:T(8,128)(2,1)S(1)}, u32[]{:S(2)}, u32[]{:S(2)}) collective-permute-start(bf16[512,256]{1,0:T(8,128)(2,1)S(1)} %copy-done), channel_id=1, source_target_pairs={{0,32},{16,48},{32,0},{48,16},{1,33},{17,49},{33,1},{49,17},{2,34}... | collective-permute-start | bytes 786440 | tf_op jit(solution)/shard_map/ppermute | solution.py:64
  22.3 23.5 %collective-permute-start.4 = (bf16[512,256]{1,0:T(8,128)(2,1)S(1)}, bf16[512,256]{1,0:T(8,128)(2,1)S(1)}, u32[]{:S(2)}, u32[]{:S(2)}) collective-permute-start(bf16[512,256]{1,0:T(8,128)(2,1)S(1)} %copy-done), channel_id=1, source_target_pairs={{0,48},{16,0},{32,16},{48,32},{1,49},{17,1},{33,17},{49,33},{2,50}... | collective-permute-start | bytes 786440 | tf_op jit(solution)/shard_map/ppermute | solution.py:64
  27.7 3.2 %collective-permute-start = (bf16[80,512]{1,0:T(8,128)(2,1)S(1)}, bf16[80,512]{1,0:T(8,128)(2,1)S(1)}, u32[]{:S(2)}, u32[]{:S(2)}) collective-permute-start(bf16[80,512]{1,0:T(8,128)(2,1)S(1)} %pad_maximum_fusion.8), channel_id=1, source_target_pairs={{0,1},{1,0},{2,3},{3,2},{4,5},{5,4},{6,7},{7,6},{8,9},{9,8},{10,11... | collective-permute-start | bytes 245768 | tf_op jit(solution)/shard_map/ppermute | solution.py:24
  30.9 16.5 %collective-permute-start.1 = (bf16[80,1024]{1,0:T(8,128)(2,1)S(1)}, bf16[80,1024]{1,0:T(8,128)(2,1)S(1)}, u32[]{:S(2)}, u32[]{:S(2)}) collective-permute-start(bf16[80,1024]{1,0:T(8,128)(2,1)S(1)} %pad_maximum_fusion.5), channel_id=1, source_target_pairs={{0,0},{2,14},{4,12},{6,10},{8,8},{10,6},{12,4},{14,2},{64,66},{66,... | collective-permute-start | bytes 491528 | tf_op jit(solution)/shard_map/ppermute | solution.py:82
  51.1 4.9 %collective-permute-start.5 = (bf16[512,1024]{1,0:T(8,128)(2,1)}, bf16[512,1024]{1,0:T(8,128)(2,1)}, u32[]{:S(2)}, u32[]{:S(2)}) collective-permute-start(bf16[512,1024]{1,0:T(8,128)(2,1)} %convolution_convert_fusion), channel_id=1, source_target_pairs={{0,1},{1,0},{2,3},{3,2},{4,5},{5,4},{6,7},{7,6},{8,9},{9,8},{10,11... | collective-permute-start | bytes 3145736 | tf_op jit(solution)/shard_map/ppermute | solution.py:24
  59.3 25.2 %all-to-all-start.1 = ((bf16[8,64,1024]{2,1,0:T(8,128)(2,1)}), bf16[8,64,1024]{2,1,0:T(8,128)(2,1)S(1)}, u32[]{:S(2)}, u32[]{:S(2)}) async-start(bf16[8,64,1024]{2,1,0:T(8,128)(2,1)} %bitcast.7), calls=%async_computation.1 | async-start | bytes 2097152 | tf_op jit(solution)/shard_map/all_to_all | solution.py:28
  66.6 18.0 %collective-permute-start.6 = (bf16[128,768]{1,0:T(8,128)(2,1)S(1)}, bf16[128,768]{1,0:T(8,128)(2,1)S(1)}, u32[]{:S(2)}, u32[]{:S(2)}) collective-permute-start(bf16[128,768]{1,0:T(8,128)(2,1)S(1)} %bitcast.115), channel_id=1, source_target_pairs={{0,16},{16,32},{32,48},{48,0},{1,17},{17,33},{33,49},{49,1},{2,18}... | collective-permute-start | bytes 589832 | tf_op jit(solution)/shard_map/ppermute | solution.py:64
  69.7 19.6 %collective-permute-start.7 = (bf16[128,768]{1,0:T(8,128)(2,1)S(1)}, bf16[128,768]{1,0:T(8,128)(2,1)S(1)}, u32[]{:S(2)}, u32[]{:S(2)}) collective-permute-start(bf16[128,768]{1,0:T(8,128)(2,1)S(1)} %bitcast.116), channel_id=1, source_target_pairs={{0,48},{16,0},{32,16},{48,32},{1,49},{17,1},{33,17},{49,33},{2,50}... | collective-permute-start | bytes 589832 | tf_op jit(solution)/shard_map/ppermute | solution.py:64
  74.6 57.1 %collective-permute-start.12 = (bf16[8192,256]{1,0:T(8,128)(2,1)}, bf16[8192,256]{1,0:T(8,128)(2,1)}, u32[]{:S(2)}, u32[]{:S(2)}) collective-permute-start(bf16[8192,256]{1,0:T(8,128)(2,1)} %param.13), channel_id=1, source_target_pairs={{0,1},{1,0},{2,3},{3,2},{4,5},{5,4},{6,7},{7,6},{8,9},{9,8},{10,11... | collective-permute-start | bytes 12582920 | tf_op jit(solution)/shard_map/ppermute | solution.py:24
  76.5 21.6 %collective-permute-start.9 = (bf16[128,768]{1,0:T(8,128)(2,1)S(1)}, bf16[128,768]{1,0:T(8,128)(2,1)S(1)}, u32[]{:S(2)}, u32[]{:S(2)}) collective-permute-start(bf16[128,768]{1,0:T(8,128)(2,1)S(1)} %bitcast.117), channel_id=1, source_target_pairs={{0,32},{16,48},{32,0},{48,16},{1,33},{17,49},{33,1},{49,17},{2,34}... | collective-permute-start | bytes 589832 | tf_op jit(solution)/shard_map/ppermute | solution.py:64
  89.8 10.4 %collective-permute-start.8 = (bf16[4,64,256]{2,1,0:T(8,128)(2,1)S(1)}, bf16[4,64,256]{2,1,0:T(8,128)(2,1)S(1)}, u32[]{:S(2)}, u32[]{:S(2)}) collective-permute-start(bf16[4,64,256]{2,1,0:T(8,128)(2,1)S(1)} %gather_fusion.2), channel_id=1, source_target_pairs={{0,0},{2,66},{4,132},{6,198},{8,264},{10,330},{12,396},{14,462},{6... | collective-permute-start | bytes 393224 | tf_op jit(solution)/shard_map/ppermute | solution.py:102
  100.4 10.5 %copy-start.25 = (s32[32]{0:T(128)S(1)}, s32[32]{0:T(128)}, u32[]{:S(2)}) copy-start(s32[32]{0:T(128)} %param.17) | copy-start | bytes 388
  100.4 10.5 %copy-start.14 = (s32[128]{0:T(128)S(1)}, s32[128]{0:T(128)}, u32[]{:S(2)}) copy-start(s32[128]{0:T(128)} %param.16) | copy-start | bytes 1540
  102.0 20.4 %all-to-all-start.2 = ((bf16[8,64,1152]{2,1,0:T(8,128)(2,1)}), bf16[8,64,1152]{2,1,0:T(8,128)(2,1)S(1)}, u32[]{:S(2)}, u32[]{:S(2)}) async-start(bf16[8,64,1152]{2,1,0:T(8,128)(2,1)} %broadcast_in_dim.40), calls=%async_computation.2 | async-start | bytes 2359296 | tf_op jit(solution)/shard_map/all_to_all | solution.py:28
  113.0 4.6 %collective-permute-start.10 = (bf16[512,768]{1,0:T(8,128)(2,1)S(1)}, bf16[512,768]{1,0:T(8,128)(2,1)S(1)}, u32[]{:S(2)}, u32[]{:S(2)}) collective-permute-start(bf16[512,768]{1,0:T(8,128)(2,1)S(1)} %bitcast.105), channel_id=1, source_target_pairs={{0,1},{1,0},{2,3},{3,2},{4,5},{5,4},{6,7},{7,6},{8,9},{9,8},{10,11... | collective-permute-start | bytes 2359304 | tf_op jit(solution)/shard_map/ppermute | solution.py:24
  117.6 1.1 copy-start.1
  117.6 1.1 copy-start.3
  123.9 0.8 copy-start.22
  123.9 0.8 copy-start.23
  123.9 2.8 %copy-start.6 = (s32[512]{0:T(512)S(1)}, s32[512]{0:T(512)}, u32[]{:S(2)}) copy-start(s32[512]{0:T(512)} %fusion.55) | copy-start | bytes 6148
  123.9 2.8 %copy-start.19 = (s32[64]{0:T(128)S(1)}, s32[64]{0:T(128)}, u32[]{:S(2)}) copy-start(s32[64]{0:T(128)} %get-tuple-element.49) | copy-start | bytes 772
  124.7 4.0 %copy-start.13 = (f32[64]{0:T(128)S(1)}, f32[64]{0:T(128)}, u32[]{:S(2)}) copy-start(f32[64]{0:T(128)} %get-tuple-element.23) | copy-start | bytes 772
  124.8 3.9 %collective-permute-start.11 = (bf16[16,512]{1,0:T(8,128)(2,1)S(1)}, bf16[16,512]{1,0:T(8,128)(2,1)S(1)}, u32[]{:S(2)}, u32[]{:S(2)}) collective-permute-start(bf16[16,512]{1,0:T(8,128)(2,1)S(1)} %slice.192), channel_id=1, source_target_pairs={{0,1},{1,0},{2,3},{3,2},{4,5},{5,4},{6,7},{7,6},{8,9},{9,8},{10,11... | collective-permute-start | bytes 49160 | tf_op jit(solution)/shard_map/ppermute | solution.py:24
  131.7 3.1 %copy-start.2 = (bf16[512,256]{1,0:T(8,128)(2,1)S(1)}, bf16[512,256]{1,0:T(8,128)(2,1)}, u32[]{:S(2)}) copy-start(bf16[512,256]{1,0:T(8,128)(2,1)} %copy-done.1) | copy-start | bytes 786436
  131.7 3.1 %copy-start.4 = (bf16[512,256]{1,0:T(8,128)(2,1)S(1)}, bf16[512,256]{1,0:T(8,128)(2,1)}, u32[]{:S(2)}) copy-start(bf16[512,256]{1,0:T(8,128)(2,1)} %copy-done.3) | copy-start | bytes 786436
  131.7 3.1 %copy-start.7 = (s32[512]{0:T(512)S(1)}, s32[512]{0:T(512)}, u32[]{:S(2)}) copy-start(s32[512]{0:T(512)} %fusion.55) | copy-start | bytes 6148
  131.7 3.1 %copy-start.20 = (s32[64]{0:T(128)S(1)}, s32[64]{0:T(128)}, u32[]{:S(2)}) copy-start(s32[64]{0:T(128)} %get-tuple-element.49) | copy-start | bytes 772
  131.8 3.7 %copy-start.11 = (bf16[16,256]{1,0:T(8,128)(2,1)S(1)}, bf16[16,256]{1,0:T(8,128)(2,1)}, u32[]{:S(2)}) copy-start(bf16[16,256]{1,0:T(8,128)(2,1)} %reduce_sum.93) | copy-start | bytes 24580
  134.9 14.1 %copy-start.21 = (f32[64]{0:T(128)S(1)}, f32[64]{0:T(128)}, u32[]{:S(2)}) copy-start(f32[64]{0:T(128)} %get-tuple-element.22) | copy-start | bytes 772
  135.2 14.5 %copy-start.9 = (s32[32,16]{1,0:T(8,128)S(1)}, s32[32,16]{1,0:T(8,128)}, u32[]{:S(2)}) copy-start(s32[32,16]{1,0:T(8,128)} %fusion.43) | copy-start | bytes 6148
  136.2 12.3 %all-to-all-start.3 = ((bf16[16,16,512]{2,1,0:T(8,128)(2,1)}), bf16[16,16,512]{2,1,0:T(8,128)(2,1)S(1)}, u32[]{:S(2)}, u32[]{:S(2)}) async-start(bf16[16,16,512]{2,1,0:T(8,128)(2,1)} %broadcast_in_dim.47), calls=%async_computation.3 | async-start | bytes 524288 | tf_op jit(solution)/shard_map/all_to_all | solution.py:28
  142.6 7.7 %copy-start.8 = (s32[512]{0:T(512)S(1)}, s32[512]{0:T(512)}, u32[]{:S(2)}) copy-start(s32[512]{0:T(512)} %fusion.55) | copy-start | bytes 6148
  142.6 7.7 %copy-start.12 = (s32[64]{0:T(128)S(1)}, s32[64]{0:T(128)}, u32[]{:S(2)}) copy-start(s32[64]{0:T(128)} %get-tuple-element.48) | copy-start | bytes 772
  142.7 5.1 %collective-permute-start.13 = (bf16[64,384]{1,0:T(8,128)(2,1)S(1)}, bf16[64,384]{1,0:T(8,128)(2,1)S(1)}, u32[]{:S(2)}, u32[]{:S(2)}) collective-permute-start(bf16[64,384]{1,0:T(8,128)(2,1)S(1)} %pad_maximum_fusion.10), channel_id=1, source_target_pairs={{0,1},{1,0},{2,3},{3,2},{4,5},{5,4},{6,7},{7,6},{8,9},{9,8},{10,11... | collective-permute-start | bytes 147464 | tf_op jit(solution)/shard_map/ppermute | solution.py:24
  145.4 7.3 %collective-permute-start.14 = (bf16[64,512]{1,0:T(8,128)(2,1)}, bf16[64,512]{1,0:T(8,128)(2,1)}, u32[]{:S(2)}, u32[]{:S(2)}) collective-permute-start(bf16[64,512]{1,0:T(8,128)(2,1)} %dynamic-slice_bitcast_fusion), channel_id=1, source_target_pairs={{0,1},{1,0},{2,3},{3,2},{4,5},{5,4},{6,7},{7,6},{8,9},{9,8},{10,11... | collective-permute-start | bytes 196616 | tf_op jit(solution)/shard_map/ppermute | solution.py:24
  147.7 0.8 copy-start.10
  148.8 1.1 copy-start.15
  148.8 1.1 copy-start.17
  149.9 1.8 copy-start.16
  149.9 1.8 copy-start.18

commit v9 on v8

--- a/solution.py
+++ b/solution.py
@@ -1,6 +1,10 @@
+import functools
+
 import jax
 import jax.numpy as jnp
 from jax import lax
+from jax.experimental import pallas as pl
+from jax.experimental.pallas import tpu as pltpu
 from jax.sharding import Mesh
 from jax.sharding import PartitionSpec as P
 
@@ -39,6 +43,42 @@
 
 def half(value, which, length, axis=0):
     return lax.dynamic_slice_in_dim(value, which * length, length, axis)
+
+
+def product_kernel(mine, place, joined, *refs):
+    *pieces, out, rows = refs
+    came = pieces.pop() if len(pieces) > 4 else None
+    groups = joined.shape[0]
+    start = pl.multiple_of(place[0] * mine, mine)
+    for k in range(groups):
+        rows[pl.ds(k * mine, mine), :] = joined[(place[1] + k) % groups, pl.ds(start, mine), :]
+    cols = pieces[0].shape[1]
+    for s, piece in enumerate(pieces):
+        total = jnp.dot(rows[...], piece[...], preferred_element_type=F32)
+        total = total.reshape(groups, mine, cols)
+        lanes = pl.ds(s * cols, cols)
+        if came is not None:
+            total = total + came[:, :, lanes].astype(F32)
+        out[:, :, lanes] = total.astype(BF)
+
+
+def product(mine, which, z, joined, pieces, came=None):
+    groups, depth = joined.shape[0], joined.shape[2]
+    columns = sum(piece.shape[1] for piece in pieces)
+    place = jnp.stack([which, z]).astype(jnp.int32)
+    arrays = [joined, *pieces] + ([] if came is None else [came])
+    vmem = pl.BlockSpec(memory_space=pltpu.VMEM)
+    return pl.pallas_call(
+        functools.partial(product_kernel, mine),
+        out_shape=jax.ShapeDtypeStruct((groups, mine, columns), BF),
+        in_specs=[pl.BlockSpec(memory_space=pltpu.SMEM)] + [vmem] * len(arrays),
+        out_specs=vmem,
+        scratch_shapes=[pltpu.VMEM((groups * mine, depth), BF)],
+        compiler_params=pltpu.CompilerParams(vmem_limit_bytes=32 * 1024 * 1024),
+        cost_estimate=pl.CostEstimate(
+            flops=2 * groups * mine * depth * columns, bytes_accessed=4 * 1024 * 1024, transcendentals=0
+        ),
+    )(place, *arrays)
 
 
 def shards(attention, output_projection, residual, gain, draft_weight, down, up, tenant_of, tenant_count):
@@ -69,7 +109,7 @@
 
     upper = jnp.concatenate([up.T, jnp.zeros((rank, block - out_block), BF)], axis=1)
     joined = gather(jnp.concatenate([attention, down.T, upper], axis=0), "z", n_z)
-    proj = jnp.concatenate(around(output_projection), axis=1)
+    pieces = around(output_projection)
     draft_weight_other = swap(draft_weight)
     pad = jnp.broadcast_to(gain[None], (16, block))
     kept = swap(jnp.concatenate([half(residual, other, mine), pad], axis=0))
@@ -83,24 +123,19 @@
     joined, chip_rows = lax.optimization_barrier((joined, chip_rows))
     residual_part, gain_part = chip_rows[:mine].astype(F32), chip_rows[mine : mine + 1].astype(F32)
 
-    rows = n_z * mine
     z = lax.axis_index("z")
-    order = (z + jnp.arange(n_z, dtype=jnp.int32)) % n_z
-    send = half(joined[:, :tokens], other, mine, 1)[order].reshape(rows, block)
-    keep = half(joined[:, :tokens], core, mine, 1)[order].reshape(rows, block)
-    sent = swap(dot("tk,kn->tn", send, proj).astype(BF))
-    pair = (dot("tk,kn->tn", keep, proj) + sent.astype(F32)).astype(BF)
+    sent = swap(product(mine, other, z, joined, pieces))
+    pair = product(mine, core, z, joined, pieces, sent)
     adapters = jnp.concatenate(
         [joined[:, tokens : tokens + rank], joined[:, tokens + rank :, :out_block]], axis=2
     ).reshape(n_z * rank, block + out_block)
     pair, adapters = lax.optimization_barrier((pair, adapters))
     parts = around(adapters)
 
-    summed = jnp.sum(exchange(pair.reshape(n_chips, mine, n_yh * cols), CHIPS).astype(F32), axis=0).astype(BF)
-    summed, parts[1], parts[3] = lax.optimization_barrier((summed, parts[1], parts[3]))
+    summed = jnp.sum(exchange(pair, CHIPS).astype(F32), axis=0).astype(BF)
     summed = jnp.stack([summed[:, s * cols : (s + 1) * cols] for s in range(n_yh)])
     projected = lax.ppermute(summed[turned], ("z", "yl", "x"), homes)
-    projected, parts[2] = lax.optimization_barrier((projected, parts[2]))
+    projected, *parts = lax.optimization_barrier((projected, *parts))
 
     hidden = residual_part + jnp.concatenate([projected[j] for j in range(n_yh)], axis=1).astype(F32)
     squares = jnp.sum(hidden * hidden, axis=1, keepdims=True)
@@ -134,14 +169,14 @@
 
     chip_features = lax.dynamic_index_in_dim(features, chip, 0, keepdims=False)
     own_scaled = half(chip_features, core, block, 1)
-    partner_scaled = swap(half(chip_features, other, block, 1))
     low_part = select(dot("jd,td->jt", downs, chip_features)) * inv_row
 
     target = lax.dynamic_slice(
         features, (chip // 2, 0, (chip % 2) * 2 * out_block), (1, mine, 2 * out_block)
     )[0]
     target = (target.astype(F32) * inv_column).astype(BF)
-    next_row = swap(target[:16])[:1]
+    came = swap(jnp.concatenate([half(chip_features, other, block, 1), target[:16]], axis=0))
+    partner_scaled, next_row = came[:mine], came[mine : mine + 1]
     target = jnp.concatenate([target[1:], next_row], axis=0)
     target = jnp.concatenate([half(target, core, out_block, 1), half(target, other, out_block, 1)], axis=1)
 

time: 194 us -> 187 us (0.964)
  the two profiles are of different devices: /device:TPU:76 before, /device:TPU:6 now
where the time goes in v9:
time: 187 us; the launch traced here: 186 us
  starting transfers between devices  72.1 us (39%)
  waiting for transfers between devices  39.1 us (21%)
  blocking collectives  35.5 us (19%)
  local copies, waits for them, and re-layouts  12.7 us (7%)
  matrix products  12 us (6%)
  other arithmetic  9.85 us (5%)
  Pallas kernels  3.54 us (2%)
    all_to_all x1, blocking collectives, exchange(): return lax.all_to_all(value, axis, 0, 0)  35.5 us
    ppermute x6, starting transfers between devices, around(): lax.ppermute(value, 'yh', [(i, (i + s) % n_yh) for i in range(n_yh)])  28.3 us
    all_to_all x4, starting transfers between devices, exchange(): return lax.all_to_all(value, axis, 0, 0)  26.5 us
    ppermute x1, waiting for transfers between devices, shards(): chip_rows = lax.ppermute(chip_rows, ('z', 'yl', 'x'), chips)  19.5 us
    ppermute x6, starting transfers between devices, swap(): return lax.ppermute(value, 'c', [(0, 1), (1, 0)])  12 us
    dot_general x11, matrix products, dot(): return jnp.einsum(subscripts, left, right, preferred_element_type=F32)  12 us
    ppermute x6, waiting for transfers between devices, around(): lax.ppermute(value, 'yh', [(i, (i + s) % n_yh) for i in range(n_yh)])  11.2 us
    all_to_all x4, waiting for transfers between devices, exchange(): return lax.all_to_all(value, axis, 0, 0)  4.91 us
  transfers between devices with their start and end apart: 18, of which 9 were waited for; matrix products, arithmetic and copies ran while one was open for 11% of the time, Pallas kernels for 0%

profile of v9, /device:TPU:6, one launch (start us, length us, event | category | flops | bytes accessed | tf_op | source)
XLA Modules:
  0.0 186.4 jit_solution(14004093491737926357)
XLA Ops:
  0.6 1.0 fusion.22
  1.6 1.2 broadcast_in_dim.38
  2.8 10.3 %all-to-all-start = ((bf16[8,160,512]{2,1,0:T(8,128)(2,1)}), bf16[8,160,512]{2,1,0:T(8,128)(2,1)S(1)}, u32[]{:S(2)}, u32[]{:S(2)}) async-start(bf16[8,160,512]{2,1,0:T(8,128)(2,1)} %broadcast_in_dim.38), calls=%async_computation | async-start | bytes 2621440 | tf_op jit(solution)/shard_map/all_to_all | solution.py:32
  13.2 1.9 %collective-permute-start = (bf16[80,512]{1,0:T(8,128)(2,1)S(1)}, bf16[80,512]{1,0:T(8,128)(2,1)S(1)}, u32[]{:S(2)}, u32[]{:S(2)}) collective-permute-start(bf16[80,512]{1,0:T(8,128)(2,1)S(1)} %pad_maximum_fusion.8), channel_id=1, source_target_pairs={{0,1},{1,0},{2,3},{3,2},{4,5},{5,4},{6,7},{7,6},{8,9},{9,8},{10,11... | collective-permute-start | bytes 245768 | tf_op jit(solution)/shard_map/ppermute | solution.py:28
  15.1 4.5 %collective-permute-start.2 = (bf16[512,256]{1,0:T(8,128)(2,1)S(1)}, bf16[512,256]{1,0:T(8,128)(2,1)S(1)}, u32[]{:S(2)}, u32[]{:S(2)}) collective-permute-start(bf16[512,256]{1,0:T(8,128)(2,1)S(1)} %copy-done), channel_id=1, source_target_pairs={{0,16},{16,32},{32,48},{48,0},{1,17},{17,33},{33,49},{49,1},{2,18}... | collective-permute-start | bytes 786440 | tf_op jit(solution)/shard_map/ppermute | solution.py:104
  19.6 5.9 %collective-permute-start.3 = (bf16[512,256]{1,0:T(8,128)(2,1)S(1)}, bf16[512,256]{1,0:T(8,128)(2,1)S(1)}, u32[]{:S(2)}, u32[]{:S(2)}) collective-permute-start(bf16[512,256]{1,0:T(8,128)(2,1)S(1)} %copy-done), channel_id=1, source_target_pairs={{0,32},{16,48},{32,0},{48,16},{1,33},{17,49},{33,1},{49,17},{2,34}... | collective-permute-start | bytes 786440 | tf_op jit(solution)/shard_map/ppermute | solution.py:104
  25.6 5.3 %collective-permute-start.4 = (bf16[512,256]{1,0:T(8,128)(2,1)S(1)}, bf16[512,256]{1,0:T(8,128)(2,1)S(1)}, u32[]{:S(2)}, u32[]{:S(2)}) collective-permute-start(bf16[512,256]{1,0:T(8,128)(2,1)S(1)} %copy-done), channel_id=1, source_target_pairs={{0,48},{16,0},{32,16},{48,32},{1,49},{17,1},{33,17},{49,33},{2,50}... | collective-permute-start | bytes 786440 | tf_op jit(solution)/shard_map/ppermute | solution.py:104
  30.9 3.4 %collective-permute-start.1 = (bf16[80,1024]{1,0:T(8,128)(2,1)S(1)}, bf16[80,1024]{1,0:T(8,128)(2,1)S(1)}, u32[]{:S(2)}, u32[]{:S(2)}) collective-permute-start(bf16[80,1024]{1,0:T(8,128)(2,1)S(1)} %pad_maximum_fusion.5), channel_id=1, source_target_pairs={{0,0},{2,14},{4,12},{6,10},{8,8},{10,6},{12,4},{14,2},{64,66},{66,... | collective-permute-start | bytes 491528 | tf_op jit(solution)/shard_map/ppermute | solution.py:122
  34.4 19.5 %collective-permute-done.1 = bf16[80,1024]{1,0:T(8,128)(2,1)S(1)} collective-permute-done((bf16[80,1024]{1,0:T(8,128)(2,1)S(1)}, bf16[80,1024]{1,0:T(8,128)(2,1)S(1)}, u32[]{:S(2)}, u32[]{:S(2)}) %collective-permute-start.1) | collective-permute-done | bytes 163872 | tf_op jit(solution)/shard_map/ppermute | solution.py:122
  53.9 1.3 shard_map.104
  55.2 1.9 %collective-permute-start.5 = (bf16[8,64,1024]{2,1,0:T(8,128)(2,1)S(1)}, bf16[8,64,1024]{2,1,0:T(8,128)(2,1)S(1)}, u32[]{:S(2)}, u32[]{:S(2)}) collective-permute-start(bf16[8,64,1024]{2,1,0:T(8,128)(2,1)S(1)} %shard_map.104), channel_id=1, source_target_pairs={{0,1},{1,0},{2,3},{3,2},{4,5},{5,4},{6,7},{7,6},{8,9},{9,8},{10,11... | collective-permute-start | bytes 3145736 | tf_op jit(solution)/shard_map/ppermute | solution.py:28
  57.2 2.5 %collective-permute-done.5.refs_4_ = bf16[8,64,1024]{2,1,0:T(8,128)(2,1)S(1)} collective-permute-done((bf16[8,64,1024]{2,1,0:T(8,128)(2,1)S(1)}, bf16[8,64,1024]{2,1,0:T(8,128)(2,1)S(1)}, u32[]{:S(2)}, u32[]{:S(2)}) %collective-permute-start.5) | collective-permute-done | bytes 1048608 | tf_op jit(solution)/shard_map/ppermute | solution.py:28
  59.7 2.3 %shard_map.105 = bf16[8,64,1024]{2,1,0:T(8,128)(2,1)} custom-call(s32[2]{0:T(128)S(1)} %pad_add_fusion.place, bf16[8,160,512]{2,1,0:T(8,128)(2,1)S(1)} %all-to-all-done.joined, bf16[512,256]{1,0:T(8,128)(2,1)S(1)} %copy-done, bf16[512,256]{1,0:T(8,128)(2,1)S(1)} %collective-permute-done.2.refs_1_, bf16[512,256]{1,0:T(8,128)(2,1)S(1)} %collective-permute-done.3.refs_2_, ...), custom_call_target="tpu_custom_call" | custom-call | flops 536870912 | bytes 4194304 | tf_op jit(solution)/shard_map/pallas_call | solution.py:71
  62.0 4.5 %all-to-all-start.1 = ((bf16[8,64,1024]{2,1,0:T(8,128)(2,1)}), bf16[8,64,1024]{2,1,0:T(8,128)(2,1)S(1)}, u32[]{:S(2)}, u32[]{:S(2)}) async-start(bf16[8,64,1024]{2,1,0:T(8,128)(2,1)} %shard_map.105), calls=%async_computation.1 | async-start | bytes 2097152 | tf_op jit(solution)/shard_map/all_to_all | solution.py:32
  66.5 1.9 %collective-permute-start.12 = (bf16[8192,256]{1,0:T(8,128)(2,1)}, bf16[8192,256]{1,0:T(8,128)(2,1)}, u32[]{:S(2)}, u32[]{:S(2)}) collective-permute-start(bf16[8192,256]{1,0:T(8,128)(2,1)} %param.13), channel_id=1, source_target_pairs={{0,1},{1,0},{2,3},{3,2},{4,5},{5,4},{6,7},{7,6},{8,9},{9,8},{10,11... | collective-permute-start | bytes 12582920 | tf_op jit(solution)/shard_map/ppermute | solution.py:28
  68.5 2.6 %collective-permute-start.7 = (bf16[128,768]{1,0:T(8,128)(2,1)S(1)}, bf16[128,768]{1,0:T(8,128)(2,1)S(1)}, u32[]{:S(2)}, u32[]{:S(2)}) collective-permute-start(bf16[128,768]{1,0:T(8,128)(2,1)S(1)} %bitcast.108), channel_id=1, source_target_pairs={{0,16},{16,32},{32,48},{48,0},{1,17},{17,33},{33,49},{49,1},{2,18}... | collective-permute-start | bytes 589832 | tf_op jit(solution)/shard_map/ppermute | solution.py:104
  71.1 6.9 %collective-permute-start.8 = (bf16[128,768]{1,0:T(8,128)(2,1)S(1)}, bf16[128,768]{1,0:T(8,128)(2,1)S(1)}, u32[]{:S(2)}, u32[]{:S(2)}) collective-permute-start(bf16[128,768]{1,0:T(8,128)(2,1)S(1)} %bitcast.109), channel_id=1, source_target_pairs={{0,32},{16,48},{32,0},{48,16},{1,33},{17,49},{33,1},{49,17},{2,34}... | collective-permute-start | bytes 589832 | tf_op jit(solution)/shard_map/ppermute | solution.py:104
  78.0 3.1 %collective-permute-start.9 = (bf16[128,768]{1,0:T(8,128)(2,1)S(1)}, bf16[128,768]{1,0:T(8,128)(2,1)S(1)}, u32[]{:S(2)}, u32[]{:S(2)}) collective-permute-start(bf16[128,768]{1,0:T(8,128)(2,1)S(1)} %bitcast.110), channel_id=1, source_target_pairs={{0,48},{16,0},{32,16},{48,32},{1,49},{17,1},{33,17},{49,33},{2,50}... | collective-permute-start | bytes 589832 | tf_op jit(solution)/shard_map/ppermute | solution.py:104
  81.1 2.3 %all-to-all-done.1 = bf16[8,64,1024]{2,1,0:T(8,128)(2,1)S(1)} async-done(((bf16[8,64,1024]{2,1,0:T(8,128)(2,1)}), bf16[8,64,1024]{2,1,0:T(8,128)(2,1)S(1)}, u32[]{:S(2)}, u32[]{:S(2)}) %all-to-all-start.1) | async-done | bytes 1048608 | tf_op jit(solution)/shard_map/all_to_all | solution.py:32
  83.6 0.6 gather_fusion
  84.2 1.9 %collective-permute-start.6 = (bf16[4,64,256]{2,1,0:T(8,128)(2,1)S(1)}, bf16[4,64,256]{2,1,0:T(8,128)(2,1)S(1)}, u32[]{:S(2)}, u32[]{:S(2)}) collective-permute-start(bf16[4,64,256]{2,1,0:T(8,128)(2,1)S(1)} %gather_fusion), channel_id=1, source_target_pairs={{0,0},{2,66},{4,132},{6,198},{8,264},{10,330},{12,396},{14,462},{6... | collective-permute-start | bytes 393224 | tf_op jit(solution)/shard_map/ppermute | solution.py:137
  86.2 7.4 %collective-permute-done.7 = bf16[128,768]{1,0:T(8,128)(2,1)S(1)} collective-permute-done((bf16[128,768]{1,0:T(8,128)(2,1)S(1)}, bf16[128,768]{1,0:T(8,128)(2,1)S(1)}, u32[]{:S(2)}, u32[]{:S(2)}) %collective-permute-start.7) | collective-permute-done | bytes 196640 | tf_op jit(solution)/shard_map/ppermute | solution.py:104
  93.6 2.6 %collective-permute-done.8 = bf16[128,768]{1,0:T(8,128)(2,1)S(1)} collective-permute-done((bf16[128,768]{1,0:T(8,128)(2,1)S(1)}, bf16[128,768]{1,0:T(8,128)(2,1)S(1)}, u32[]{:S(2)}, u32[]{:S(2)}) %collective-permute-start.8) | collective-permute-done | bytes 196640 | tf_op jit(solution)/shard_map/ppermute | solution.py:104
  96.1 1.2 collective-permute-done.9
  97.9 1.2 broadcast_in_dim.40
  99.1 5.9 %all-to-all-start.2 = ((bf16[8,64,1152]{2,1,0:T(8,128)(2,1)}), bf16[8,64,1152]{2,1,0:T(8,128)(2,1)S(1)}, u32[]{:S(2)}, u32[]{:S(2)}) async-start(bf16[8,64,1152]{2,1,0:T(8,128)(2,1)} %broadcast_in_dim.40), calls=%async_computation.2 | async-start | bytes 2359296 | tf_op jit(solution)/shard_map/all_to_all | solution.py:32
  105.0 0.5 convert_element_type.151
  105.5 0.6 slice.154
  106.1 0.6 fusion.66
  106.8 0.7 gather_fusion.1
  107.6 1.9 %collective-permute-start.10 = (bf16[512,768]{1,0:T(8,128)(2,1)S(1)}, bf16[512,768]{1,0:T(8,128)(2,1)S(1)}, u32[]{:S(2)}, u32[]{:S(2)}) collective-permute-start(bf16[512,768]{1,0:T(8,128)(2,1)S(1)} %bitcast.98), channel_id=1, source_target_pairs={{0,1},{1,0},{2,3},{3,2},{4,5},{5,4},{6,7},{7,6},{8,9},{9,8},{10,11... | collective-permute-start | bytes 2359304 | tf_op jit(solution)/shard_map/ppermute | solution.py:28
  109.5 1.4 fusion.86
  110.9 0.8 select_reduce_fusion
  111.7 1.4 fusion.62
  113.0 0.7 broadcast_multiply_fusion.2
  113.7 0.6 fusion.56
  114.3 1.2 pad_clamp_fusion
  115.6 0.6 copy-done.1
  116.3 0.3 convolution_select_fusion
  116.5 0.4 copy-done.3
  117.0 0.6 reduce_sum.93
  117.6 0.9 broadcast_select_fusion.1
  118.7 0.6 copy.44
  119.3 0.6 copy.45
  120.1 0.7 gather_fusion.2
  121.1 2.3 %collective-permute-start.11 = (bf16[80,512]{1,0:T(8,128)(2,1)S(1)}, bf16[80,512]{1,0:T(8,128)(2,1)S(1)}, u32[]{:S(2)}, u32[]{:S(2)}) collective-permute-start(bf16[80,512]{1,0:T(8,128)(2,1)S(1)} %pad_maximum_fusion.10), channel_id=1, source_target_pairs={{0,1},{1,0},{2,3},{3,2},{4,5},{5,4},{6,7},{7,6},{8,9},{9,8},{10,11... | collective-permute-start | bytes 245768 | tf_op jit(solution)/shard_map/ppermute | solution.py:28
  123.4 1.5 convolution_select_fusion.2
  125.4 3.0 %fusion.35 = (bf16[64,256]{1,0:T(8,128)(2,1)S(1)}, f32[64,256]{1,0:T(8,128)S(1)}) fusion(f32[64]{0:T(128)S(1)} %copy-done.14, s32[]{:T(128)S(6)} %select_n.238, bf16[1,512]{1,0:T(2,128)(2,1)S(1)} %slice.192, bf16[63,512]{1,0:T(8,128)(2,1)S(1)} %slice.190, f32[64]{0:T(128)S(1)} %bitcast.124, bf16[8,64,1024]{2,1,0:T(8,128)(2,1)S(1)} %gather_fusion.2, ...), kind=kOutput, calls=%fused_computation.84 | convolution fusion | flops 268566528 | bytes 5407236 | tf_op jit(solution)/shard_map/ktd,kdn->tn/dot_general | solution.py:24
  128.4 3.0 %fusion.7 = bf16[64,256]{1,0:T(8,128)(2,1)S(1)} fusion(bf16[8,64,1024]{2,1,0:T(8,128)(2,1)S(1)} %gather_fusion.2, bf16[8,1024,256]{2,1,0:T(8,128)(2,1)} %bitcast.30, s32[]{:T(128)S(6)} %select_n.240, bf16[63,512]{1,0:T(8,128)(2,1)S(1)} %slice.190, bf16[1,512]{1,0:T(2,128)(2,1)S(1)} %slice.192, f32[64]{0:T(128)S(1)} %copy-done.14, f32[64]{0:T(128)S(1)} %bitcast.125), kind=kOutput, calls=%fused_computation.20 | convolution fusion | flops 268566528 | bytes 5341700 | tf_op jit(solution)/shard_map/ktd,kdn->tn/dot_general | solution.py:24
  131.6 0.3 convolution_select_fusion.1
  132.2 0.7 broadcast_in_dim.47
  132.9 5.7 %all-to-all-start.3 = ((bf16[16,16,512]{2,1,0:T(8,128)(2,1)}), bf16[16,16,512]{2,1,0:T(8,128)(2,1)S(1)}, u32[]{:S(2)}, u32[]{:S(2)}) async-start(bf16[16,16,512]{2,1,0:T(8,128)(2,1)} %broadcast_in_dim.47), calls=%async_computation.3 | async-start | bytes 524288 | tf_op jit(solution)/shard_map/all_to_all | solution.py:32
  138.7 2.1 %collective-permute-start.13 = (bf16[64,384]{1,0:T(8,128)(2,1)S(1)}, bf16[64,384]{1,0:T(8,128)(2,1)S(1)}, u32[]{:S(2)}, u32[]{:S(2)}) collective-permute-start(bf16[64,384]{1,0:T(8,128)(2,1)S(1)} %pad_maximum_fusion.11), channel_id=1, source_target_pairs={{0,1},{1,0},{2,3},{3,2},{4,5},{5,4},{6,7},{7,6},{8,9},{9,8},{10,11... | collective-permute-start | bytes 147464 | tf_op jit(solution)/shard_map/ppermute | solution.py:28
  140.8 1.0 collective-permute-done.13
  142.0 2.5 %all-to-all-done.3 = bf16[16,16,512]{2,1,0:T(8,128)(2,1)S(1)} async-done(((bf16[16,16,512]{2,1,0:T(8,128)(2,1)}), bf16[16,16,512]{2,1,0:T(8,128)(2,1)S(1)}, u32[]{:S(2)}, u32[]{:S(2)}) %all-to-all-start.3) | async-done | bytes 262176 | tf_op jit(solution)/shard_map/all_to_all | solution.py:32
  144.8 0.2 fusion.15
  145.5 0.5 fusion.9
  146.2 0.4 fusion.30
  146.7 1.3 fusion.1
  148.0 1.2 fusion
  149.3 0.3 copy.43
  149.6 35.5 %all_to_all.25 = bf16[32,16,768]{2,1,0:T(8,128)(2,1)S(1)} all-to-all(bf16[32,16,768]{2,1,0:T(8,128)(2,1)S(1)} %bitcast.104), channel_id=1, replica_groups=mesh['z'=8,'yh'=4,'yl'=2,'x'=4,'c'=2] {'yh','z'}, dimensions={0} | all-to-all | bytes 1572864 | tf_op jit(solution)/shard_map/all_to_all | solution.py:32
  185.2 0.6 slice_bitcast_fusion
  185.8 0.6 slice_bitcast_fusion.9
  (134 shorter events, 3.8 us)
Async XLA Ops:
  1.6 11.5 %copy-start.5 = (bf16[128,512]{1,0:T(8,128)(2,1)S(1)}, bf16[128,512]{1,0:T(8,128)(2,1)}, u32[]{:S(2)}) copy-start(bf16[128,512]{1,0:T(8,128)(2,1)} %param.11) | copy-start | bytes 393220
  1.6 11.6 %copy-start.25 = (bf16[512]{0:T(512)(128)(2,1)S(1)}, bf16[512]{0:T(512)(128)(2,1)}, u32[]{:S(2)}) copy-start(bf16[512]{0:T(512)(128)(2,1)} %param.12) | copy-start | bytes 3076
  1.6 13.5 %copy-start = (bf16[512,256]{1,0:T(8,128)(2,1)S(1)}, bf16[512,256]{1,0:T(8,128)(2,1)}, u32[]{:S(2)}) copy-start(bf16[512,256]{1,0:T(8,128)(2,1)} %refs_0_.3) | copy-start | bytes 786436
  2.8 51.1 %all-to-all-start = ((bf16[8,160,512]{2,1,0:T(8,128)(2,1)}), bf16[8,160,512]{2,1,0:T(8,128)(2,1)S(1)}, u32[]{:S(2)}, u32[]{:S(2)}) async-start(bf16[8,160,512]{2,1,0:T(8,128)(2,1)} %broadcast_in_dim.38), calls=%async_computation | async-start | bytes 2621440 | tf_op jit(solution)/shard_map/all_to_all | solution.py:32
  13.2 17.7 %collective-permute-start = (bf16[80,512]{1,0:T(8,128)(2,1)S(1)}, bf16[80,512]{1,0:T(8,128)(2,1)S(1)}, u32[]{:S(2)}, u32[]{:S(2)}) collective-permute-start(bf16[80,512]{1,0:T(8,128)(2,1)S(1)} %pad_maximum_fusion.8), channel_id=1, source_target_pairs={{0,1},{1,0},{2,3},{3,2},{4,5},{5,4},{6,7},{7,6},{8,9},{9,8},{10,11... | collective-permute-start | bytes 245768 | tf_op jit(solution)/shard_map/ppermute | solution.py:28
  15.1 38.8 %collective-permute-start.2 = (bf16[512,256]{1,0:T(8,128)(2,1)S(1)}, bf16[512,256]{1,0:T(8,128)(2,1)S(1)}, u32[]{:S(2)}, u32[]{:S(2)}) collective-permute-start(bf16[512,256]{1,0:T(8,128)(2,1)S(1)} %copy-done), channel_id=1, source_target_pairs={{0,16},{16,32},{32,48},{48,0},{1,17},{17,33},{33,49},{49,1},{2,18}... | collective-permute-start | bytes 786440 | tf_op jit(solution)/shard_map/ppermute | solution.py:104
  19.6 34.3 %collective-permute-start.3 = (bf16[512,256]{1,0:T(8,128)(2,1)S(1)}, bf16[512,256]{1,0:T(8,128)(2,1)S(1)}, u32[]{:S(2)}, u32[]{:S(2)}) collective-permute-start(bf16[512,256]{1,0:T(8,128)(2,1)S(1)} %copy-done), channel_id=1, source_target_pairs={{0,32},{16,48},{32,0},{48,16},{1,33},{17,49},{33,1},{49,17},{2,34}... | collective-permute-start | bytes 786440 | tf_op jit(solution)/shard_map/ppermute | solution.py:104
  25.6 28.3 %collective-permute-start.4 = (bf16[512,256]{1,0:T(8,128)(2,1)S(1)}, bf16[512,256]{1,0:T(8,128)(2,1)S(1)}, u32[]{:S(2)}, u32[]{:S(2)}) collective-permute-start(bf16[512,256]{1,0:T(8,128)(2,1)S(1)} %copy-done), channel_id=1, source_target_pairs={{0,48},{16,0},{32,16},{48,32},{1,49},{17,1},{33,17},{49,33},{2,50}... | collective-permute-start | bytes 786440 | tf_op jit(solution)/shard_map/ppermute | solution.py:104
  30.9 23.0 %collective-permute-start.1 = (bf16[80,1024]{1,0:T(8,128)(2,1)S(1)}, bf16[80,1024]{1,0:T(8,128)(2,1)S(1)}, u32[]{:S(2)}, u32[]{:S(2)}) collective-permute-start(bf16[80,1024]{1,0:T(8,128)(2,1)S(1)} %pad_maximum_fusion.5), channel_id=1, source_target_pairs={{0,0},{2,14},{4,12},{6,10},{8,8},{10,6},{12,4},{14,2},{64,66},{66,... | collective-permute-start | bytes 491528 | tf_op jit(solution)/shard_map/ppermute | solution.py:122
  55.2 4.6 %collective-permute-start.5 = (bf16[8,64,1024]{2,1,0:T(8,128)(2,1)S(1)}, bf16[8,64,1024]{2,1,0:T(8,128)(2,1)S(1)}, u32[]{:S(2)}, u32[]{:S(2)}) collective-permute-start(bf16[8,64,1024]{2,1,0:T(8,128)(2,1)S(1)} %shard_map.104), channel_id=1, source_target_pairs={{0,1},{1,0},{2,3},{3,2},{4,5},{5,4},{6,7},{7,6},{8,9},{9,8},{10,11... | collective-permute-start | bytes 3145736 | tf_op jit(solution)/shard_map/ppermute | solution.py:28
  62.0 21.4 %all-to-all-start.1 = ((bf16[8,64,1024]{2,1,0:T(8,128)(2,1)}), bf16[8,64,1024]{2,1,0:T(8,128)(2,1)S(1)}, u32[]{:S(2)}, u32[]{:S(2)}) async-start(bf16[8,64,1024]{2,1,0:T(8,128)(2,1)} %shard_map.105), calls=%async_computation.1 | async-start | bytes 2097152 | tf_op jit(solution)/shard_map/all_to_all | solution.py:32
  66.5 61.9 %collective-permute-start.12 = (bf16[8192,256]{1,0:T(8,128)(2,1)}, bf16[8192,256]{1,0:T(8,128)(2,1)}, u32[]{:S(2)}, u32[]{:S(2)}) collective-permute-start(bf16[8192,256]{1,0:T(8,128)(2,1)} %param.13), channel_id=1, source_target_pairs={{0,1},{1,0},{2,3},{3,2},{4,5},{5,4},{6,7},{7,6},{8,9},{9,8},{10,11... | collective-permute-start | bytes 12582920 | tf_op jit(solution)/shard_map/ppermute | solution.py:28
  68.5 15.7 %copy-start.18 = (s32[1024]{0:T(1024)}, s32[1024]{0:T(1024)S(1)}, u32[]{:S(2)}) copy-start(s32[1024]{0:T(1024)S(1)} %pad_clamp_fusion.1) | copy-start | bytes 12292
  68.5 25.1 %collective-permute-start.7 = (bf16[128,768]{1,0:T(8,128)(2,1)S(1)}, bf16[128,768]{1,0:T(8,128)(2,1)S(1)}, u32[]{:S(2)}, u32[]{:S(2)}) collective-permute-start(bf16[128,768]{1,0:T(8,128)(2,1)S(1)} %bitcast.108), channel_id=1, source_target_pairs={{0,16},{16,32},{32,48},{48,0},{1,17},{17,33},{33,49},{49,1},{2,18}... | collective-permute-start | bytes 589832 | tf_op jit(solution)/shard_map/ppermute | solution.py:104
  71.1 25.0 %collective-permute-start.8 = (bf16[128,768]{1,0:T(8,128)(2,1)S(1)}, bf16[128,768]{1,0:T(8,128)(2,1)S(1)}, u32[]{:S(2)}, u32[]{:S(2)}) collective-permute-start(bf16[128,768]{1,0:T(8,128)(2,1)S(1)} %bitcast.109), channel_id=1, source_target_pairs={{0,32},{16,48},{32,0},{48,16},{1,33},{17,49},{33,1},{49,17},{2,34}... | collective-permute-start | bytes 589832 | tf_op jit(solution)/shard_map/ppermute | solution.py:104
  78.0 19.3 %collective-permute-start.9 = (bf16[128,768]{1,0:T(8,128)(2,1)S(1)}, bf16[128,768]{1,0:T(8,128)(2,1)S(1)}, u32[]{:S(2)}, u32[]{:S(2)}) collective-permute-start(bf16[128,768]{1,0:T(8,128)(2,1)S(1)} %bitcast.110), channel_id=1, source_target_pairs={{0,48},{16,0},{32,16},{48,32},{1,49},{17,1},{33,17},{49,33},{2,50}... | collective-permute-start | bytes 589832 | tf_op jit(solution)/shard_map/ppermute | solution.py:104
  84.2 13.1 %collective-permute-start.6 = (bf16[4,64,256]{2,1,0:T(8,128)(2,1)S(1)}, bf16[4,64,256]{2,1,0:T(8,128)(2,1)S(1)}, u32[]{:S(2)}, u32[]{:S(2)}) collective-permute-start(bf16[4,64,256]{2,1,0:T(8,128)(2,1)S(1)} %gather_fusion), channel_id=1, source_target_pairs={{0,0},{2,66},{4,132},{6,198},{8,264},{10,330},{12,396},{14,462},{6... | collective-permute-start | bytes 393224 | tf_op jit(solution)/shard_map/ppermute | solution.py:137
  97.5 7.5 %copy-start.26 = (s32[32]{0:T(128)S(1)}, s32[32]{0:T(128)}, u32[]{:S(2)}) copy-start(s32[32]{0:T(128)} %param.17) | copy-start | bytes 388
  97.5 8.0 %copy-start.15 = (s32[128]{0:T(128)S(1)}, s32[128]{0:T(128)}, u32[]{:S(2)}) copy-start(s32[128]{0:T(128)} %param.16) | copy-start | bytes 1540
  99.1 19.5 %all-to-all-start.2 = ((bf16[8,64,1152]{2,1,0:T(8,128)(2,1)}), bf16[8,64,1152]{2,1,0:T(8,128)(2,1)S(1)}, u32[]{:S(2)}, u32[]{:S(2)}) async-start(bf16[8,64,1152]{2,1,0:T(8,128)(2,1)} %broadcast_in_dim.40), calls=%async_computation.2 | async-start | bytes 2359296 | tf_op jit(solution)/shard_map/all_to_all | solution.py:32
  106.1 0.6 copy-start.19
  106.8 9.4 %slice-start = ((s32[512]{0:T(512)}), s32[256]{0:T(256)S(1)}, s32[]{:S(2)}) async-start(s32[512]{0:T(512)} %copy-done.19), calls=%async_computation.5 | async-start | bytes 2048 | tf_op jit(solution)/shard_map/slice | solution.py:204
  107.6 8.0 %collective-permute-start.10 = (bf16[512,768]{1,0:T(8,128)(2,1)S(1)}, bf16[512,768]{1,0:T(8,128)(2,1)S(1)}, u32[]{:S(2)}, u32[]{:S(2)}) collective-permute-start(bf16[512,768]{1,0:T(8,128)(2,1)S(1)} %bitcast.98), channel_id=1, source_target_pairs={{0,1},{1,0},{2,3},{3,2},{4,5},{5,4},{6,7},{7,6},{8,9},{9,8},{10,11... | collective-permute-start | bytes 2359304 | tf_op jit(solution)/shard_map/ppermute | solution.py:28
  115.5 0.7 copy-start.1
  116.2 0.7 copy-start.3
  120.0 0.8 copy-start.23
  120.0 0.8 copy-start.24
  120.0 3.3 %copy-start.6 = (s32[512]{0:T(512)S(1)}, s32[512]{0:T(512)}, u32[]{:S(2)}) copy-start(s32[512]{0:T(512)} %fusion.56) | copy-start | bytes 6148
  120.1 3.3 %copy-start.16 = (s32[64]{0:T(128)S(1)}, s32[64]{0:T(128)}, u32[]{:S(2)}) copy-start(s32[64]{0:T(128)} %get-tuple-element.47) | copy-start | bytes 772
  120.8 4.5 %copy-start.14 = (f32[64]{0:T(128)S(1)}, f32[64]{0:T(128)}, u32[]{:S(2)}) copy-start(f32[64]{0:T(128)} %get-tuple-element.23) | copy-start | bytes 772
  121.1 4.3 %collective-permute-start.11 = (bf16[80,512]{1,0:T(8,128)(2,1)S(1)}, bf16[80,512]{1,0:T(8,128)(2,1)S(1)}, u32[]{:S(2)}, u32[]{:S(2)}) collective-permute-start(bf16[80,512]{1,0:T(8,128)(2,1)S(1)} %pad_maximum_fusion.10), channel_id=1, source_target_pairs={{0,1},{1,0},{2,3},{3,2},{4,5},{5,4},{6,7},{7,6},{8,9},{9,8},{10,11... | collective-permute-start | bytes 245768 | tf_op jit(solution)/shard_map/ppermute | solution.py:28
  125.3 6.7 %copy-start.9 = (bf16[80,512]{1,0:T(8,128)(2,1)}, bf16[80,512]{1,0:T(8,128)(2,1)S(1)}, u32[]{:S(2)}) copy-start(bf16[80,512]{1,0:T(8,128)(2,1)S(1)} %collective-permute-done.11) | copy-start | bytes 245764
  128.4 3.1 %copy-start.2 = (bf16[512,256]{1,0:T(8,128)(2,1)S(1)}, bf16[512,256]{1,0:T(8,128)(2,1)}, u32[]{:S(2)}) copy-start(bf16[512,256]{1,0:T(8,128)(2,1)} %copy-done.1) | copy-start | bytes 786436
  128.4 3.1 %copy-start.4 = (bf16[512,256]{1,0:T(8,128)(2,1)S(1)}, bf16[512,256]{1,0:T(8,128)(2,1)}, u32[]{:S(2)}) copy-start(bf16[512,256]{1,0:T(8,128)(2,1)} %copy-done.3) | copy-start | bytes 786436
  128.4 3.1 %copy-start.7 = (s32[512]{0:T(512)S(1)}, s32[512]{0:T(512)}, u32[]{:S(2)}) copy-start(s32[512]{0:T(512)} %fusion.56) | copy-start | bytes 6148
  128.4 3.1 %copy-start.17 = (s32[64]{0:T(128)S(1)}, s32[64]{0:T(128)}, u32[]{:S(2)}) copy-start(s32[64]{0:T(128)} %get-tuple-element.47) | copy-start | bytes 772
  128.4 3.8 %copy-start.11 = (bf16[16,256]{1,0:T(8,128)(2,1)S(1)}, bf16[16,256]{1,0:T(8,128)(2,1)}, u32[]{:S(2)}) copy-start(bf16[16,256]{1,0:T(8,128)(2,1)} %reduce_sum.93) | copy-start | bytes 24580
  131.5 13.3 %copy-start.12 = (s32[64]{0:T(128)S(1)}, s32[64]{0:T(128)}, u32[]{:S(2)}) copy-start(s32[64]{0:T(128)} %get-tuple-element.46) | copy-start | bytes 772
  131.5 13.3 %copy-start.20 = (f32[64]{0:T(128)S(1)}, f32[64]{0:T(128)}, u32[]{:S(2)}) copy-start(f32[64]{0:T(128)} %get-tuple-element.48) | copy-start | bytes 772
  131.5 13.8 %copy-start.22 = (f32[64]{0:T(128)S(1)}, f32[64]{0:T(128)}, u32[]{:S(2)}) copy-start(f32[64]{0:T(128)} %get-tuple-element.22) | copy-start | bytes 772
  132.9 11.6 %all-to-all-start.3 = ((bf16[16,16,512]{2,1,0:T(8,128)(2,1)}), bf16[16,16,512]{2,1,0:T(8,128)(2,1)S(1)}, u32[]{:S(2)}, u32[]{:S(2)}) async-start(bf16[16,16,512]{2,1,0:T(8,128)(2,1)} %broadcast_in_dim.47), calls=%async_computation.3 | async-start | bytes 524288 | tf_op jit(solution)/shard_map/all_to_all | solution.py:32
  138.7 3.1 %collective-permute-start.13 = (bf16[64,384]{1,0:T(8,128)(2,1)S(1)}, bf16[64,384]{1,0:T(8,128)(2,1)S(1)}, u32[]{:S(2)}, u32[]{:S(2)}) collective-permute-start(bf16[64,384]{1,0:T(8,128)(2,1)S(1)} %pad_maximum_fusion.11), channel_id=1, source_target_pairs={{0,1},{1,0},{2,3},{3,2},{4,5},{5,4},{6,7},{7,6},{8,9},{9,8},{10,11... | collective-permute-start | bytes 147464 | tf_op jit(solution)/shard_map/ppermute | solution.py:28
  141.8 4.4 %copy-start.10 = (bf16[64,384]{1,0:T(8,128)(2,1)}, bf16[64,384]{1,0:T(8,128)(2,1)S(1)}, u32[]{:S(2)}) copy-start(bf16[64,384]{1,0:T(8,128)(2,1)S(1)} %collective-permute-done.13) | copy-start | bytes 147460
  144.6 2.1 %copy-start.8 = (s32[512]{0:T(512)S(1)}, s32[512]{0:T(512)}, u32[]{:S(2)}) copy-start(s32[512]{0:T(512)} %fusion.56) | copy-start | bytes 6148
  144.6 2.1 %copy-start.13 = (s32[64]{0:T(128)S(1)}, s32[64]{0:T(128)}, u32[]{:S(2)}) copy-start(s32[64]{0:T(128)} %get-tuple-element.46) | copy-start | bytes 772
  144.6 2.1 %copy-start.21 = (f32[64]{0:T(128)S(1)}, f32[64]{0:T(128)}, u32[]{:S(2)}) copy-start(f32[64]{0:T(128)} %get-tuple-element.48) | copy-start | bytes 772

commit v10 on v9

--- a/solution.py
+++ b/solution.py
@@ -99,17 +99,15 @@
     yh = lax.axis_index("yh")
     turned = (yh - jnp.arange(n_yh, dtype=jnp.int32)) % n_yh
 
-    def around(value):
-        return [value] + [
-            lax.ppermute(value, "yh", [(i, (i + s) % n_yh) for i in range(n_yh)]) for s in range(1, n_yh)
-        ]
+    def shift(value, step):
+        return lax.ppermute(value, "yh", [(i, (i + step) % n_yh) for i in range(n_yh)])
 
     def ordered(own, others):
         return jnp.where(first, own, others), jnp.where(first, others, own)
 
     upper = jnp.concatenate([up.T, jnp.zeros((rank, block - out_block), BF)], axis=1)
     joined = gather(jnp.concatenate([attention, down.T, upper], axis=0), "z", n_z)
-    pieces = around(output_projection)
+    pieces = [output_projection] + [shift(output_projection, step) for step in range(1, n_yh)]
     draft_weight_other = swap(draft_weight)
     pad = jnp.broadcast_to(gain[None], (16, block))
     kept = swap(jnp.concatenate([half(residual, other, mine), pad], axis=0))
@@ -120,7 +118,21 @@
     homes = [(i * n_chips + k, (i + k) % n_z * n_chips + k) for i, k in places]
     chips = [(i * n_chips + k, i * n_chips + (i - k) % n_chips) for i, k in places]
     chip_rows = lax.ppermute(chip_rows, ("z", "yl", "x"), chips)
-    joined, chip_rows = lax.optimization_barrier((joined, chip_rows))
+    slot = jnp.arange(tenants * rank, dtype=jnp.int32) // rank
+    slot_tenant = (slot % n_z) * n_yh + slot // n_z
+    own_tenant = half(tenant_of, core, mine)
+    partner_tenant = half(tenant_of, other, mine)
+    own_mask = slot_tenant[:, None] == own_tenant[None, :]
+    partner_mask = slot_tenant[:, None] == partner_tenant[None, :]
+    following = jnp.roll(tenant_of, -1)
+    position = jnp.arange(tokens, dtype=jnp.int32)
+    keep_mask = (position < tokens - 1) & (tenant_of == following)
+    is_tenant = tenant_of[:, None] == jnp.arange(tenants, dtype=jnp.int32)[None, :]
+    count = jnp.sum(jnp.where(is_tenant, tenant_count.astype(F32)[None, :], 0.0), axis=1)
+    weights = keep_mask.astype(F32) / count
+    joined, chip_rows, draft_weight_other, own_mask, partner_mask, weights = lax.optimization_barrier(
+        (joined, chip_rows, draft_weight_other, own_mask, partner_mask, weights)
+    )
     residual_part, gain_part = chip_rows[:mine].astype(F32), chip_rows[mine : mine + 1].astype(F32)
 
     z = lax.axis_index("z")
@@ -130,12 +142,14 @@
         [joined[:, tokens : tokens + rank], joined[:, tokens + rank :, :out_block]], axis=2
     ).reshape(n_z * rank, block + out_block)
     pair, adapters = lax.optimization_barrier((pair, adapters))
-    parts = around(adapters)
+    before, after = shift(adapters, 1), shift(adapters, -1)
 
     summed = jnp.sum(exchange(pair, CHIPS).astype(F32), axis=0).astype(BF)
+    summed, before, after, adapters = lax.optimization_barrier((summed, before, after, adapters))
+    some = n_z * rank // 2
+    parts = [adapters, before, jnp.concatenate([shift(adapters[:some], 2), shift(after[some:], -1)], axis=0), after]
     summed = jnp.stack([summed[:, s * cols : (s + 1) * cols] for s in range(n_yh)])
     projected = lax.ppermute(summed[turned], ("z", "yl", "x"), homes)
-    projected, *parts = lax.optimization_barrier((projected, *parts))
 
     hidden = residual_part + jnp.concatenate([projected[j] for j in range(n_yh)], axis=1).astype(F32)
     squares = jnp.sum(hidden * hidden, axis=1, keepdims=True)
@@ -148,17 +162,11 @@
     inv_column = lax.rsqrt((totals[:, :1] + totals[:, 1:2]) / width + EPSILON)
     inv_row = jnp.broadcast_to(inv_column, (mine, 128)).T[:1]
 
-    adapters_all = jnp.stack(parts)[turned].reshape(tenants * rank, block + out_block)
+    _, later = lax.optimization_barrier((message, turned))
+    adapters_all = jnp.stack(parts)[later].reshape(tenants * rank, block + out_block)
     adapters_other = swap(adapters_all)
     downs = jnp.concatenate(ordered(adapters_all[:, :block], adapters_other[:, :block]), axis=1)
     ups = jnp.concatenate([adapters_all[:, block:], adapters_other[:, block:]], axis=1)
-
-    slot = jnp.arange(tenants * rank, dtype=jnp.int32) // rank
-    slot_tenant = (slot % n_z) * n_yh + slot // n_z
-    own_tenant = half(tenant_of, core, mine)
-    partner_tenant = half(tenant_of, other, mine)
-    own_mask = slot_tenant[:, None] == own_tenant[None, :]
-    partner_mask = slot_tenant[:, None] == partner_tenant[None, :]
 
     def select(values):
         chosen = jnp.where(own_mask, values, 0.0)
@@ -180,12 +188,6 @@
     target = jnp.concatenate([target[1:], next_row], axis=0)
     target = jnp.concatenate([half(target, core, out_block, 1), half(target, other, out_block, 1)], axis=1)
 
-    following = jnp.roll(tenant_of, -1)
-    position = jnp.arange(tokens, dtype=jnp.int32)
-    keep_mask = (position < tokens - 1) & (tenant_of == following)
-    is_tenant = tenant_of[:, None] == jnp.arange(tenants, dtype=jnp.int32)[None, :]
-    count = jnp.sum(jnp.where(is_tenant, tenant_count.astype(F32)[None, :], 0.0), axis=1)
-    weights = keep_mask.astype(F32) / count
     weight, weight_row = half(weights, core, mine)[:, None], half(weights, core, mine)[None]
     partner_weight, partner_weight_row = half(weights, other, mine)[:, None], half(weights, other, mine)[None]
 

time: 187 us -> 207 us (1.11)
  waiting for transfers between devices: 39.1 us -> 54.8 us
  starting transfers between devices: 72.1 us -> 84.3 us
  blocking collectives: 35.5 us -> 32.9 us
  other arithmetic: 9.85 us -> 7.43 us
    all_to_all x4, waiting for transfers between devices: 4.91 us -> 14.4 us  [exchange(): return lax.all_to_all(value, axis, 0, 0)]
    ppermute x1, waiting for transfers between devices: 0.01 us -> 8.82 us  [shards(): projected = lax.ppermute(summed[turned], ('z', 'yl', 'x'), homes)]
    all_to_all x4, starting transfers between devices: 26.5 us -> 33.4 us  [exchange(): return lax.all_to_all(value, axis, 0, 0)]
    ppermute x1, waiting for transfers between devices: 19.5 us -> 14.1 us  [shards(): chip_rows = lax.ppermute(chip_rows, ('z', 'yl', 'x'), chips)]
    ppermute x1, starting transfers between devices: 1.92 us -> 4.56 us  [shards(): projected = lax.ppermute(summed[turned], ('z', 'yl', 'x'), homes)]
    all_to_all x1, blocking collectives: 35.5 us -> 32.9 us  [exchange(): return lax.all_to_all(value, axis, 0, 0)]
    ppermute x6 -> x7, starting transfers between devices: 28.3 us -> 30.8 us  [shift(): lax.ppermute(value, 'yh', [(i, (i + step) % n_yh) for i in range(n_yh)])]
    ppermute x6 -> x7, waiting for transfers between devices: 11.2 us -> 13.5 us  [shift(): lax.ppermute(value, 'yh', [(i, (i + step) % n_yh) for i in range(n_yh)])]
  transfers between devices with their start and end apart: 18 -> 19, of which waited for: 9 -> 10; matrix products, arithmetic and copies ran while one was open for 11% -> 5% of each run, Pallas kernels for 0% -> 0%
where the time goes in v10:
time: 207 us; the launch traced here: 206 us
  starting transfers between devices  84.3 us (41%)
  waiting for transfers between devices  54.8 us (26%)
  blocking collectives  32.9 us (16%)
  local copies, waits for them, and re-layouts  10.9 us (5%)
  matrix products  10.1 us (5%)
  other arithmetic  7.43 us (4%)
  Pallas kernels  3.52 us (2%)
    all_to_all x4, starting transfers between devices, exchange(): return lax.all_to_all(value, axis, 0, 0)  33.4 us
    all_to_all x1, blocking collectives, exchange(): return lax.all_to_all(value, axis, 0, 0)  32.9 us
    ppermute x7, starting transfers between devices, shift(): lax.ppermute(value, 'yh', [(i, (i + step) % n_yh) for i in range(n_yh)])  30.8 us
    all_to_all x4, waiting for transfers between devices, exchange(): return lax.all_to_all(value, axis, 0, 0)  14.4 us
    ppermute x1, waiting for transfers between devices, shards(): chip_rows = lax.ppermute(chip_rows, ('z', 'yl', 'x'), chips)  14.1 us
    ppermute x7, waiting for transfers between devices, shift(): lax.ppermute(value, 'yh', [(i, (i + step) % n_yh) for i in range(n_yh)])  13.5 us
    ppermute x6, starting transfers between devices, swap(): return lax.ppermute(value, 'c', [(0, 1), (1, 0)])  12.2 us
    dot_general x11, matrix products, dot(): return jnp.einsum(subscripts, left, right, preferred_element_type=F32)  10.1 us
  transfers between devices with their start and end apart: 19, of which 10 were waited for; matrix products, arithmetic and copies ran while one was open for 5% of the time, Pallas kernels for 0%

profile of v10, /device:TPU:6, one launch (start us, length us, event | category | flops | bytes accessed | tf_op | source)
XLA Modules:
  0.0 205.6 jit_solution(15021003372386586613)
XLA Ops:
  0.6 1.9 collective-permute-start.2
  2.6 1.0 fusion.21
  3.6 1.2 broadcast_in_dim.38
  4.8 10.3 %all-to-all-start = ((bf16[8,160,512]{2,1,0:T(8,128)(2,1)}), bf16[8,160,512]{2,1,0:T(8,128)(2,1)S(1)}, u32[]{:S(2)}, u32[]{:S(2)}) async-start(bf16[8,160,512]{2,1,0:T(8,128)(2,1)} %broadcast_in_dim.38), calls=%async_computation | async-start | bytes 2621440 | tf_op jit(solution)/shard_map/all_to_all | solution.py:32
  15.1 6.2 %collective-permute-start.5 = (bf16[512,256]{1,0:T(8,128)(2,1)S(1)}, bf16[512,256]{1,0:T(8,128)(2,1)S(1)}, u32[]{:S(2)}, u32[]{:S(2)}) collective-permute-start(bf16[512,256]{1,0:T(8,128)(2,1)S(1)} %copy-done), channel_id=1, source_target_pairs={{0,48},{16,0},{32,16},{48,32},{1,49},{17,1},{33,17},{49,33},{2,50}... | collective-permute-start | bytes 786440 | tf_op jit(solution)/shard_map/ppermute | solution.py:103
  21.3 3.8 %collective-permute-start.4 = (bf16[512,256]{1,0:T(8,128)(2,1)S(1)}, bf16[512,256]{1,0:T(8,128)(2,1)S(1)}, u32[]{:S(2)}, u32[]{:S(2)}) collective-permute-start(bf16[512,256]{1,0:T(8,128)(2,1)S(1)} %copy-done), channel_id=1, source_target_pairs={{0,32},{16,48},{32,0},{48,16},{1,33},{17,49},{33,1},{49,17},{2,34}... | collective-permute-start | bytes 786440 | tf_op jit(solution)/shard_map/ppermute | solution.py:103
  25.1 4.5 %collective-permute-start.3 = (bf16[512,256]{1,0:T(8,128)(2,1)S(1)}, bf16[512,256]{1,0:T(8,128)(2,1)S(1)}, u32[]{:S(2)}, u32[]{:S(2)}) collective-permute-start(bf16[512,256]{1,0:T(8,128)(2,1)S(1)} %copy-done), channel_id=1, source_target_pairs={{0,16},{16,32},{32,48},{48,0},{1,17},{17,33},{33,49},{49,1},{2,18}... | collective-permute-start | bytes 786440 | tf_op jit(solution)/shard_map/ppermute | solution.py:103
  29.7 1.9 collective-permute-start
  31.8 0.7 broadcast_compare_fusion
  32.6 0.2 collective-permute-done
  32.9 3.4 %collective-permute-start.1 = (bf16[80,1024]{1,0:T(8,128)(2,1)S(1)}, bf16[80,1024]{1,0:T(8,128)(2,1)S(1)}, u32[]{:S(2)}, u32[]{:S(2)}) collective-permute-start(bf16[80,1024]{1,0:T(8,128)(2,1)S(1)} %pad_maximum_fusion.5), channel_id=1, source_target_pairs={{0,0},{2,14},{4,12},{6,10},{8,8},{10,6},{12,4},{14,2},{64,66},{66,... | collective-permute-start | bytes 491528 | tf_op jit(solution)/shard_map/ppermute | solution.py:120
  36.4 0.6 fusion.67
  37.1 14.1 %collective-permute-done.1 = bf16[80,1024]{1,0:T(8,128)(2,1)S(1)} collective-permute-done((bf16[80,1024]{1,0:T(8,128)(2,1)S(1)}, bf16[80,1024]{1,0:T(8,128)(2,1)S(1)}, u32[]{:S(2)}, u32[]{:S(2)}) %collective-permute-start.1) | collective-permute-done | bytes 163872 | tf_op jit(solution)/shard_map/ppermute | solution.py:120
  51.1 1.3 shard_map.104
  52.4 1.9 collective-permute-start.6
  54.5 2.5 %collective-permute-done.6.refs_4_ = bf16[8,64,1024]{2,1,0:T(8,128)(2,1)S(1)} collective-permute-done((bf16[8,64,1024]{2,1,0:T(8,128)(2,1)S(1)}, bf16[8,64,1024]{2,1,0:T(8,128)(2,1)S(1)}, u32[]{:S(2)}, u32[]{:S(2)}) %collective-permute-start.6) | collective-permute-done | bytes 1048608 | tf_op jit(solution)/shard_map/ppermute | solution.py:28
  57.0 2.3 %shard_map.105 = bf16[8,64,1024]{2,1,0:T(8,128)(2,1)} custom-call(s32[2]{0:T(128)S(1)} %pad_add_fusion.place, bf16[8,160,512]{2,1,0:T(8,128)(2,1)S(1)} %all-to-all-done.joined, bf16[512,256]{1,0:T(8,128)(2,1)S(1)} %copy-done, bf16[512,256]{1,0:T(8,128)(2,1)S(1)} %collective-permute-done.3.refs_1_, bf16[512,256]{1,0:T(8,128)(2,1)S(1)} %collective-permute-done.4.refs_2_, ...), custom_call_target="tpu_custom_call" | custom-call | flops 536870912 | bytes 4194304 | tf_op jit(solution)/shard_map/pallas_call | solution.py:71
  59.2 7.3 %all-to-all-start.1 = ((bf16[8,64,1024]{2,1,0:T(8,128)(2,1)}), bf16[8,64,1024]{2,1,0:T(8,128)(2,1)S(1)}, u32[]{:S(2)}, u32[]{:S(2)}) async-start(bf16[8,64,1024]{2,1,0:T(8,128)(2,1)} %shard_map.105), calls=%async_computation.1 | async-start | bytes 2097152 | tf_op jit(solution)/shard_map/all_to_all | solution.py:32
  66.5 2.8 %collective-permute-start.8 = (bf16[128,768]{1,0:T(8,128)(2,1)S(1)}, bf16[128,768]{1,0:T(8,128)(2,1)S(1)}, u32[]{:S(2)}, u32[]{:S(2)}) collective-permute-start(bf16[128,768]{1,0:T(8,128)(2,1)S(1)} %bitcast.105), channel_id=1, source_target_pairs={{0,48},{16,0},{32,16},{48,32},{1,49},{17,1},{33,17},{49,33},{2,50}... | collective-permute-start | bytes 589832 | tf_op jit(solution)/shard_map/ppermute | solution.py:103
  69.3 4.0 %collective-permute-start.7 = (bf16[128,768]{1,0:T(8,128)(2,1)S(1)}, bf16[128,768]{1,0:T(8,128)(2,1)S(1)}, u32[]{:S(2)}, u32[]{:S(2)}) collective-permute-start(bf16[128,768]{1,0:T(8,128)(2,1)S(1)} %bitcast.106), channel_id=1, source_target_pairs={{0,16},{16,32},{32,48},{48,0},{1,17},{17,33},{33,49},{49,1},{2,18}... | collective-permute-start | bytes 589832 | tf_op jit(solution)/shard_map/ppermute | solution.py:103
  73.3 11.9 %all-to-all-done.1 = bf16[8,64,1024]{2,1,0:T(8,128)(2,1)S(1)} async-done(((bf16[8,64,1024]{2,1,0:T(8,128)(2,1)}), bf16[8,64,1024]{2,1,0:T(8,128)(2,1)S(1)}, u32[]{:S(2)}, u32[]{:S(2)}) %all-to-all-start.1) | async-done | bytes 1048608 | tf_op jit(solution)/shard_map/all_to_all | solution.py:32
  85.2 0.2 reduce_sum.87
  85.4 2.3 %collective-permute-done.7 = bf16[128,768]{1,0:T(8,128)(2,1)S(1)} collective-permute-done((bf16[128,768]{1,0:T(8,128)(2,1)S(1)}, bf16[128,768]{1,0:T(8,128)(2,1)S(1)}, u32[]{:S(2)}, u32[]{:S(2)}) %collective-permute-start.7) | collective-permute-done | bytes 196640 | tf_op jit(solution)/shard_map/ppermute | solution.py:103
  87.7 0.6 gather_fusion
  88.3 4.6 %collective-permute-start.11 = (bf16[4,64,256]{2,1,0:T(8,128)(2,1)S(1)}, bf16[4,64,256]{2,1,0:T(8,128)(2,1)S(1)}, u32[]{:S(2)}, u32[]{:S(2)}) collective-permute-start(bf16[4,64,256]{2,1,0:T(8,128)(2,1)S(1)} %gather_fusion), channel_id=1, source_target_pairs={{0,0},{2,66},{4,132},{6,198},{8,264},{10,330},{12,396},{14,462},{6... | collective-permute-start | bytes 393224 | tf_op jit(solution)/shard_map/ppermute | solution.py:152
  92.9 8.8 %collective-permute-done.11 = bf16[4,64,256]{2,1,0:T(8,128)(2,1)S(1)} collective-permute-done((bf16[4,64,256]{2,1,0:T(8,128)(2,1)S(1)}, bf16[4,64,256]{2,1,0:T(8,128)(2,1)S(1)}, u32[]{:S(2)}, u32[]{:S(2)}) %collective-permute-start.11) | collective-permute-done | bytes 131104 | tf_op jit(solution)/shard_map/ppermute | solution.py:152
  101.7 0.2 multiply_reduce_fusion
  102.2 1.2 broadcast_in_dim.43
  103.4 5.9 %all-to-all-start.2 = ((bf16[8,64,1152]{2,1,0:T(8,128)(2,1)}), bf16[8,64,1152]{2,1,0:T(8,128)(2,1)S(1)}, u32[]{:S(2)}, u32[]{:S(2)}) async-start(bf16[8,64,1152]{2,1,0:T(8,128)(2,1)} %broadcast_in_dim.43), calls=%async_computation.2 | async-start | bytes 2359296 | tf_op jit(solution)/shard_map/all_to_all | solution.py:32
  109.3 4.1 %collective-permute-start.10 = (bf16[64,768]{1,0:T(8,128)(2,1)S(1)}, bf16[64,768]{1,0:T(8,128)(2,1)S(1)}, u32[]{:S(2)}, u32[]{:S(2)}) collective-permute-start(bf16[64,768]{1,0:T(8,128)(2,1)S(1)} %slice.142), channel_id=1, source_target_pairs={{0,48},{16,0},{32,16},{48,32},{1,49},{17,1},{33,17},{49,33},{2,50}... | collective-permute-start | bytes 294920 | tf_op jit(solution)/shard_map/ppermute | solution.py:103
  113.4 5.5 %collective-permute-start.9 = (bf16[64,768]{1,0:T(8,128)(2,1)S(1)}, bf16[64,768]{1,0:T(8,128)(2,1)S(1)}, u32[]{:S(2)}, u32[]{:S(2)}) collective-permute-start(bf16[64,768]{1,0:T(8,128)(2,1)S(1)} %slice.141), channel_id=1, source_target_pairs={{0,32},{16,48},{32,0},{48,16},{1,33},{17,49},{33,1},{49,17},{2,34}... | collective-permute-start | bytes 294920 | tf_op jit(solution)/shard_map/ppermute | solution.py:103
  118.9 11.1 %collective-permute-done.9 = bf16[64,768]{1,0:T(8,128)(2,1)S(1)} collective-permute-done((bf16[64,768]{1,0:T(8,128)(2,1)S(1)}, bf16[64,768]{1,0:T(8,128)(2,1)S(1)}, u32[]{:S(2)}, u32[]{:S(2)}) %collective-permute-start.9) | collective-permute-done | bytes 98336 | tf_op jit(solution)/shard_map/ppermute | solution.py:103
  130.2 0.6 gather_fusion.1
  130.8 1.9 collective-permute-start.12
  132.9 0.6 pad_clamp_fusion
  133.5 1.3 broadcast_multiply_fusion.2
  134.8 0.2 collective-permute-done.12
  135.0 0.5 copy-done.4
  135.5 0.3 convolution_select_fusion
  135.8 0.4 copy-done.6
  136.2 0.6 reduce_sum.93
  136.8 0.9 broadcast_select_fusion.1
  137.8 0.6 copy.49
  138.4 0.7 copy.48
  139.2 0.9 gather_fusion.2
  140.3 2.4 %collective-permute-start.13 = (bf16[80,512]{1,0:T(8,128)(2,1)S(1)}, bf16[80,512]{1,0:T(8,128)(2,1)S(1)}, u32[]{:S(2)}, u32[]{:S(2)}) collective-permute-start(bf16[80,512]{1,0:T(8,128)(2,1)S(1)} %pad_maximum_fusion.10), channel_id=1, source_target_pairs={{0,1},{1,0},{2,3},{3,2},{4,5},{5,4},{6,7},{7,6},{8,9},{9,8},{10,11... | collective-permute-start | bytes 245768 | tf_op jit(solution)/shard_map/ppermute | solution.py:28
  142.8 1.5 convolution_select_fusion.2
  144.7 3.0 %fusion.34 = (bf16[64,256]{1,0:T(8,128)(2,1)S(1)}, f32[64,256]{1,0:T(8,128)S(1)}) fusion(f32[64]{0:T(128)S(1)} %copy-done.12, s32[]{:T(128)S(6)} %select_n.222, bf16[1,512]{1,0:T(2,128)(2,1)S(1)} %slice.200, bf16[63,512]{1,0:T(8,128)(2,1)S(1)} %slice.198, f32[64]{0:T(128)S(1)} %bitcast.123, bf16[8,64,1024]{2,1,0:T(8,128)(2,1)S(1)} %gather_fusion.2, ...), kind=kOutput, calls=%fused_computation.82 | convolution fusion | flops 268566528 | bytes 5407236 | tf_op jit(solution)/shard_map/ktd,kdn->tn/dot_general | solution.py:24
  147.8 3.1 %fusion.7 = bf16[64,256]{1,0:T(8,128)(2,1)S(1)} fusion(bf16[8,64,1024]{2,1,0:T(8,128)(2,1)S(1)} %gather_fusion.2, bf16[8,1024,256]{2,1,0:T(8,128)(2,1)} %bitcast.30, s32[]{:T(128)S(6)} %select_n.223, bf16[63,512]{1,0:T(8,128)(2,1)S(1)} %slice.198, bf16[1,512]{1,0:T(2,128)(2,1)S(1)} %slice.200, f32[64]{0:T(128)S(1)} %copy-done.12, f32[64]{0:T(128)S(1)} %bitcast.124), kind=kOutput, calls=%fused_computation.20 | convolution fusion | flops 268566528 | bytes 5341700 | tf_op jit(solution)/shard_map/ktd,kdn->tn/dot_general | solution.py:24
  150.9 0.3 convolution_select_fusion.1
  151.6 0.7 broadcast_in_dim.48
  152.3 10.0 %all-to-all-start.3 = ((bf16[16,16,512]{2,1,0:T(8,128)(2,1)}), bf16[16,16,512]{2,1,0:T(8,128)(2,1)S(1)}, u32[]{:S(2)}, u32[]{:S(2)}) async-start(bf16[16,16,512]{2,1,0:T(8,128)(2,1)} %broadcast_in_dim.48), calls=%async_computation.3 | async-start | bytes 524288 | tf_op jit(solution)/shard_map/all_to_all | solution.py:32
  162.3 2.1 %collective-permute-start.14 = (bf16[64,384]{1,0:T(8,128)(2,1)S(1)}, bf16[64,384]{1,0:T(8,128)(2,1)S(1)}, u32[]{:S(2)}, u32[]{:S(2)}) collective-permute-start(bf16[64,384]{1,0:T(8,128)(2,1)S(1)} %pad_maximum_fusion.11), channel_id=1, source_target_pairs={{0,1},{1,0},{2,3},{3,2},{4,5},{5,4},{6,7},{7,6},{8,9},{9,8},{10,11... | collective-permute-start | bytes 147464 | tf_op jit(solution)/shard_map/ppermute | solution.py:28
  164.4 1.1 collective-permute-done.14
  165.5 0.2 multiply_reduce_fusion.1
  165.7 2.5 %all-to-all-done.3 = bf16[16,16,512]{2,1,0:T(8,128)(2,1)S(1)} async-done(((bf16[16,16,512]{2,1,0:T(8,128)(2,1)}), bf16[16,16,512]{2,1,0:T(8,128)(2,1)S(1)}, u32[]{:S(2)}, u32[]{:S(2)}) %all-to-all-start.3) | async-done | bytes 262176 | tf_op jit(solution)/shard_map/all_to_all | solution.py:32
  169.1 0.5 fusion.40
  169.7 0.5 fusion.1
  170.2 0.3 fusion.25
  170.5 0.4 fusion
  171.0 0.3 copy.47
  171.3 32.9 %all_to_all.25 = bf16[32,16,768]{2,1,0:T(8,128)(2,1)S(1)} all-to-all(bf16[32,16,768]{2,1,0:T(8,128)(2,1)S(1)} %bitcast.104), channel_id=1, replica_groups=mesh['z'=8,'yh'=4,'yl'=2,'x'=4,'c'=2] {'yh','z'}, dimensions={0} | all-to-all | bytes 1572864 | tf_op jit(solution)/shard_map/all_to_all | solution.py:32
  204.3 0.6 slice_bitcast_fusion.9
  204.9 0.6 slice_bitcast_fusion
  (130 shorter events, 3.5 us)
Async XLA Ops:
  0.6 50.5 %collective-permute-start.2 = (bf16[8192,256]{1,0:T(8,128)(2,1)}, bf16[8192,256]{1,0:T(8,128)(2,1)}, u32[]{:S(2)}, u32[]{:S(2)}) collective-permute-start(bf16[8192,256]{1,0:T(8,128)(2,1)} %param.13), channel_id=1, source_target_pairs={{0,1},{1,0},{2,3},{3,2},{4,5},{5,4},{6,7},{7,6},{8,9},{9,8},{10,11... | collective-permute-start | bytes 12582920 | tf_op jit(solution)/shard_map/ppermute | solution.py:28
  3.5 11.6 %copy-start = (bf16[512,256]{1,0:T(8,128)(2,1)S(1)}, bf16[512,256]{1,0:T(8,128)(2,1)}, u32[]{:S(2)}) copy-start(bf16[512,256]{1,0:T(8,128)(2,1)} %refs_0_.3) | copy-start | bytes 786436
  3.5 26.1 %copy-start.8 = (bf16[128,512]{1,0:T(8,128)(2,1)S(1)}, bf16[128,512]{1,0:T(8,128)(2,1)}, u32[]{:S(2)}) copy-start(bf16[128,512]{1,0:T(8,128)(2,1)} %param.11) | copy-start | bytes 393220
  3.5 26.1 %copy-start.19 = (bf16[512]{0:T(512)(128)(2,1)S(1)}, bf16[512]{0:T(512)(128)(2,1)}, u32[]{:S(2)}) copy-start(bf16[512]{0:T(512)(128)(2,1)} %param.12) | copy-start | bytes 3076
  3.6 28.1 %copy-start.20 = (s32[32]{0:T(128)S(1)}, s32[32]{0:T(128)}, u32[]{:S(2)}) copy-start(s32[32]{0:T(128)} %param.17) | copy-start | bytes 388
  3.6 28.1 %copy-start.14 = (s32[128]{0:T(128)S(1)}, s32[128]{0:T(128)}, u32[]{:S(2)}) copy-start(s32[128]{0:T(128)} %param.16) | copy-start | bytes 1540
  4.8 46.3 %all-to-all-start = ((bf16[8,160,512]{2,1,0:T(8,128)(2,1)}), bf16[8,160,512]{2,1,0:T(8,128)(2,1)S(1)}, u32[]{:S(2)}, u32[]{:S(2)}) async-start(bf16[8,160,512]{2,1,0:T(8,128)(2,1)} %broadcast_in_dim.38), calls=%async_computation | async-start | bytes 2621440 | tf_op jit(solution)/shard_map/all_to_all | solution.py:32
  15.1 36.0 %collective-permute-start.5 = (bf16[512,256]{1,0:T(8,128)(2,1)S(1)}, bf16[512,256]{1,0:T(8,128)(2,1)S(1)}, u32[]{:S(2)}, u32[]{:S(2)}) collective-permute-start(bf16[512,256]{1,0:T(8,128)(2,1)S(1)} %copy-done), channel_id=1, source_target_pairs={{0,48},{16,0},{32,16},{48,32},{1,49},{17,1},{33,17},{49,33},{2,50}... | collective-permute-start | bytes 786440 | tf_op jit(solution)/shard_map/ppermute | solution.py:103
  21.3 29.8 %collective-permute-start.4 = (bf16[512,256]{1,0:T(8,128)(2,1)S(1)}, bf16[512,256]{1,0:T(8,128)(2,1)S(1)}, u32[]{:S(2)}, u32[]{:S(2)}) collective-permute-start(bf16[512,256]{1,0:T(8,128)(2,1)S(1)} %copy-done), channel_id=1, source_target_pairs={{0,32},{16,48},{32,0},{48,16},{1,33},{17,49},{33,1},{49,17},{2,34}... | collective-permute-start | bytes 786440 | tf_op jit(solution)/shard_map/ppermute | solution.py:103
  25.1 26.0 %collective-permute-start.3 = (bf16[512,256]{1,0:T(8,128)(2,1)S(1)}, bf16[512,256]{1,0:T(8,128)(2,1)S(1)}, u32[]{:S(2)}, u32[]{:S(2)}) collective-permute-start(bf16[512,256]{1,0:T(8,128)(2,1)S(1)} %copy-done), channel_id=1, source_target_pairs={{0,16},{16,32},{32,48},{48,0},{1,17},{17,33},{33,49},{49,1},{2,18}... | collective-permute-start | bytes 786440 | tf_op jit(solution)/shard_map/ppermute | solution.py:103
  29.7 3.2 %collective-permute-start = (bf16[80,512]{1,0:T(8,128)(2,1)S(1)}, bf16[80,512]{1,0:T(8,128)(2,1)S(1)}, u32[]{:S(2)}, u32[]{:S(2)}) collective-permute-start(bf16[80,512]{1,0:T(8,128)(2,1)S(1)} %pad_maximum_fusion.8), channel_id=1, source_target_pairs={{0,1},{1,0},{2,3},{3,2},{4,5},{5,4},{6,7},{7,6},{8,9},{9,8},{10,11... | collective-permute-start | bytes 245768 | tf_op jit(solution)/shard_map/ppermute | solution.py:28
  32.9 18.2 %collective-permute-start.1 = (bf16[80,1024]{1,0:T(8,128)(2,1)S(1)}, bf16[80,1024]{1,0:T(8,128)(2,1)S(1)}, u32[]{:S(2)}, u32[]{:S(2)}) collective-permute-start(bf16[80,1024]{1,0:T(8,128)(2,1)S(1)} %pad_maximum_fusion.5), channel_id=1, source_target_pairs={{0,0},{2,14},{4,12},{6,10},{8,8},{10,6},{12,4},{14,2},{64,66},{66,... | collective-permute-start | bytes 491528 | tf_op jit(solution)/shard_map/ppermute | solution.py:120
  52.4 4.6 %collective-permute-start.6 = (bf16[8,64,1024]{2,1,0:T(8,128)(2,1)S(1)}, bf16[8,64,1024]{2,1,0:T(8,128)(2,1)S(1)}, u32[]{:S(2)}, u32[]{:S(2)}) collective-permute-start(bf16[8,64,1024]{2,1,0:T(8,128)(2,1)S(1)} %shard_map.104), channel_id=1, source_target_pairs={{0,1},{1,0},{2,3},{3,2},{4,5},{5,4},{6,7},{7,6},{8,9},{9,8},{10,11... | collective-permute-start | bytes 3145736 | tf_op jit(solution)/shard_map/ppermute | solution.py:28
  59.2 26.0 %all-to-all-start.1 = ((bf16[8,64,1024]{2,1,0:T(8,128)(2,1)}), bf16[8,64,1024]{2,1,0:T(8,128)(2,1)S(1)}, u32[]{:S(2)}, u32[]{:S(2)}) async-start(bf16[8,64,1024]{2,1,0:T(8,128)(2,1)} %shard_map.105), calls=%async_computation.1 | async-start | bytes 2097152 | tf_op jit(solution)/shard_map/all_to_all | solution.py:32
  66.5 18.9 %collective-permute-start.8 = (bf16[128,768]{1,0:T(8,128)(2,1)S(1)}, bf16[128,768]{1,0:T(8,128)(2,1)S(1)}, u32[]{:S(2)}, u32[]{:S(2)}) collective-permute-start(bf16[128,768]{1,0:T(8,128)(2,1)S(1)} %bitcast.105), channel_id=1, source_target_pairs={{0,48},{16,0},{32,16},{48,32},{1,49},{17,1},{33,17},{49,33},{2,50}... | collective-permute-start | bytes 589832 | tf_op jit(solution)/shard_map/ppermute | solution.py:103
  69.3 18.4 %collective-permute-start.7 = (bf16[128,768]{1,0:T(8,128)(2,1)S(1)}, bf16[128,768]{1,0:T(8,128)(2,1)S(1)}, u32[]{:S(2)}, u32[]{:S(2)}) collective-permute-start(bf16[128,768]{1,0:T(8,128)(2,1)S(1)} %bitcast.106), channel_id=1, source_target_pairs={{0,16},{16,32},{32,48},{48,0},{1,17},{17,33},{33,49},{49,1},{2,18}... | collective-permute-start | bytes 589832 | tf_op jit(solution)/shard_map/ppermute | solution.py:103
  88.3 13.4 %collective-permute-start.11 = (bf16[4,64,256]{2,1,0:T(8,128)(2,1)S(1)}, bf16[4,64,256]{2,1,0:T(8,128)(2,1)S(1)}, u32[]{:S(2)}, u32[]{:S(2)}) collective-permute-start(bf16[4,64,256]{2,1,0:T(8,128)(2,1)S(1)} %gather_fusion), channel_id=1, source_target_pairs={{0,0},{2,66},{4,132},{6,198},{8,264},{10,330},{12,396},{14,462},{6... | collective-permute-start | bytes 393224 | tf_op jit(solution)/shard_map/ppermute | solution.py:152
  103.4 34.2 %all-to-all-start.2 = ((bf16[8,64,1152]{2,1,0:T(8,128)(2,1)}), bf16[8,64,1152]{2,1,0:T(8,128)(2,1)S(1)}, u32[]{:S(2)}, u32[]{:S(2)}) async-start(bf16[8,64,1152]{2,1,0:T(8,128)(2,1)} %broadcast_in_dim.43), calls=%async_computation.2 | async-start | bytes 2359296 | tf_op jit(solution)/shard_map/all_to_all | solution.py:32
  109.3 9.6 %collective-permute-start.10 = (bf16[64,768]{1,0:T(8,128)(2,1)S(1)}, bf16[64,768]{1,0:T(8,128)(2,1)S(1)}, u32[]{:S(2)}, u32[]{:S(2)}) collective-permute-start(bf16[64,768]{1,0:T(8,128)(2,1)S(1)} %slice.142), channel_id=1, source_target_pairs={{0,48},{16,0},{32,16},{48,32},{1,49},{17,1},{33,17},{49,33},{2,50}... | collective-permute-start | bytes 294920 | tf_op jit(solution)/shard_map/ppermute | solution.py:103
  113.4 16.6 %collective-permute-start.9 = (bf16[64,768]{1,0:T(8,128)(2,1)S(1)}, bf16[64,768]{1,0:T(8,128)(2,1)S(1)}, u32[]{:S(2)}, u32[]{:S(2)}) collective-permute-start(bf16[64,768]{1,0:T(8,128)(2,1)S(1)} %slice.141), channel_id=1, source_target_pairs={{0,32},{16,48},{32,0},{48,16},{1,33},{17,49},{33,1},{49,17},{2,34}... | collective-permute-start | bytes 294920 | tf_op jit(solution)/shard_map/ppermute | solution.py:103
  130.8 4.2 %collective-permute-start.12 = (bf16[512,768]{1,0:T(8,128)(2,1)S(1)}, bf16[512,768]{1,0:T(8,128)(2,1)S(1)}, u32[]{:S(2)}, u32[]{:S(2)}) collective-permute-start(bf16[512,768]{1,0:T(8,128)(2,1)S(1)} %bitcast.98), channel_id=1, source_target_pairs={{0,1},{1,0},{2,3},{3,2},{4,5},{5,4},{6,7},{7,6},{8,9},{9,8},{10,11... | collective-permute-start | bytes 2359304 | tf_op jit(solution)/shard_map/ppermute | solution.py:28
  134.8 0.7 copy-start.4
  135.5 0.7 copy-start.6
  139.2 0.9 copy-start.17
  139.2 0.9 copy-start.18
  139.2 3.6 %copy-start.1 = (pred[512,64]{0,1:T(32,128)(4,1)S(1)}, pred[512,64]{0,1:T(32,128)(4,1)}, u32[]{:S(2)}) copy-start(pred[512,64]{0,1:T(32,128)(4,1)} %get-tuple-element.15) | copy-start | bytes 98308
  140.1 4.6 %copy-start.12 = (f32[64]{0:T(128)S(1)}, f32[64]{0:T(128)}, u32[]{:S(2)}) copy-start(f32[64]{0:T(128)} %get-tuple-element.31) | copy-start | bytes 772
  140.3 4.4 %collective-permute-start.13 = (bf16[80,512]{1,0:T(8,128)(2,1)S(1)}, bf16[80,512]{1,0:T(8,128)(2,1)S(1)}, u32[]{:S(2)}, u32[]{:S(2)}) collective-permute-start(bf16[80,512]{1,0:T(8,128)(2,1)S(1)} %pad_maximum_fusion.10), channel_id=1, source_target_pairs={{0,1},{1,0},{2,3},{3,2},{4,5},{5,4},{6,7},{7,6},{8,9},{9,8},{10,11... | collective-permute-start | bytes 245768 | tf_op jit(solution)/shard_map/ppermute | solution.py:28
  144.7 3.1 %copy-start.9 = (bf16[80,512]{1,0:T(8,128)(2,1)}, bf16[80,512]{1,0:T(8,128)(2,1)S(1)}, u32[]{:S(2)}) copy-start(bf16[80,512]{1,0:T(8,128)(2,1)S(1)} %collective-permute-done.13) | copy-start | bytes 245764
  147.8 3.1 %copy-start.2 = (pred[512,64]{0,1:T(32,128)(4,1)S(1)}, pred[512,64]{0,1:T(32,128)(4,1)}, u32[]{:S(2)}) copy-start(pred[512,64]{0,1:T(32,128)(4,1)} %get-tuple-element.15) | copy-start | bytes 98308
  147.8 3.1 %copy-start.5 = (bf16[512,256]{1,0:T(8,128)(2,1)S(1)}, bf16[512,256]{1,0:T(8,128)(2,1)}, u32[]{:S(2)}) copy-start(bf16[512,256]{1,0:T(8,128)(2,1)} %copy-done.4) | copy-start | bytes 786436
  147.8 3.1 %copy-start.7 = (bf16[512,256]{1,0:T(8,128)(2,1)S(1)}, bf16[512,256]{1,0:T(8,128)(2,1)}, u32[]{:S(2)}) copy-start(bf16[512,256]{1,0:T(8,128)(2,1)} %copy-done.6) | copy-start | bytes 786436
  147.8 3.7 %copy-start.11 = (bf16[16,256]{1,0:T(8,128)(2,1)S(1)}, bf16[16,256]{1,0:T(8,128)(2,1)}, u32[]{:S(2)}) copy-start(bf16[16,256]{1,0:T(8,128)(2,1)} %reduce_sum.93) | copy-start | bytes 24580
  150.9 17.6 %copy-start.3 = (pred[512,64]{0,1:T(32,128)(4,1)S(1)}, pred[512,64]{0,1:T(32,128)(4,1)}, u32[]{:S(2)}) copy-start(pred[512,64]{0,1:T(32,128)(4,1)} %get-tuple-element.27) | copy-start | bytes 98308
  150.9 17.6 %copy-start.15 = (f32[64]{0:T(128)S(1)}, f32[64]{0:T(128)}, u32[]{:S(2)}) copy-start(f32[64]{0:T(128)} %get-tuple-element.56) | copy-start | bytes 772
  150.9 17.9 %copy-start.16 = (f32[64]{0:T(128)S(1)}, f32[64]{0:T(128)}, u32[]{:S(2)}) copy-start(f32[64]{0:T(128)} %get-tuple-element.30) | copy-start | bytes 772
  151.5 18.1 %copy-start.13 = (f32[64]{0:T(128)S(1)}, f32[64]{0:T(128)}, u32[]{:S(2)}) copy-start(f32[64]{0:T(128)} %get-tuple-element.31) | copy-start | bytes 772
  152.3 15.9 %all-to-all-start.3 = ((bf16[16,16,512]{2,1,0:T(8,128)(2,1)}), bf16[16,16,512]{2,1,0:T(8,128)(2,1)S(1)}, u32[]{:S(2)}, u32[]{:S(2)}) async-start(bf16[16,16,512]{2,1,0:T(8,128)(2,1)} %broadcast_in_dim.48), calls=%async_computation.3 | async-start | bytes 524288 | tf_op jit(solution)/shard_map/all_to_all | solution.py:32
  162.3 3.1 %collective-permute-start.14 = (bf16[64,384]{1,0:T(8,128)(2,1)S(1)}, bf16[64,384]{1,0:T(8,128)(2,1)S(1)}, u32[]{:S(2)}, u32[]{:S(2)}) collective-permute-start(bf16[64,384]{1,0:T(8,128)(2,1)S(1)} %pad_maximum_fusion.11), channel_id=1, source_target_pairs={{0,1},{1,0},{2,3},{3,2},{4,5},{5,4},{6,7},{7,6},{8,9},{9,8},{10,11... | collective-permute-start | bytes 147464 | tf_op jit(solution)/shard_map/ppermute | solution.py:28
  168.2 2.0 copy-start.10

commit v11 on v10

--- a/solution.py
+++ b/solution.py
@@ -99,15 +99,20 @@
     yh = lax.axis_index("yh")
     turned = (yh - jnp.arange(n_yh, dtype=jnp.int32)) % n_yh
 
-    def shift(value, step):
-        return lax.ppermute(value, "yh", [(i, (i + step) % n_yh) for i in range(n_yh)])
+    def around(value):
+        return [value] + [
+            lax.ppermute(value, "yh", [(i, (i + s) % n_yh) for i in range(n_yh)]) for s in range(1, n_yh)
+        ]
 
     def ordered(own, others):
         return jnp.where(first, own, others), jnp.where(first, others, own)
 
     upper = jnp.concatenate([up.T, jnp.zeros((rank, block - out_block), BF)], axis=1)
-    joined = gather(jnp.concatenate([attention, down.T, upper], axis=0), "z", n_z)
-    pieces = [output_projection] + [shift(output_projection, step) for step in range(1, n_yh)]
+    joined = jnp.concatenate(
+        [jnp.broadcast_to(part[None], (n_z,) + part.shape) for part in (attention, down.T, upper)], axis=1
+    )
+    joined = exchange(joined, "z")
+    pieces = around(output_projection)
     draft_weight_other = swap(draft_weight)
     pad = jnp.broadcast_to(gain[None], (16, block))
     kept = swap(jnp.concatenate([half(residual, other, mine), pad], axis=0))
@@ -130,8 +135,8 @@
     is_tenant = tenant_of[:, None] == jnp.arange(tenants, dtype=jnp.int32)[None, :]
     count = jnp.sum(jnp.where(is_tenant, tenant_count.astype(F32)[None, :], 0.0), axis=1)
     weights = keep_mask.astype(F32) / count
-    joined, chip_rows, draft_weight_other, own_mask, partner_mask, weights = lax.optimization_barrier(
-        (joined, chip_rows, draft_weight_other, own_mask, partner_mask, weights)
+    joined, chip_rows, own_mask, partner_mask, weights = lax.optimization_barrier(
+        (joined, chip_rows, own_mask, partner_mask, weights)
     )
     residual_part, gain_part = chip_rows[:mine].astype(F32), chip_rows[mine : mine + 1].astype(F32)
 
@@ -142,14 +147,12 @@
         [joined[:, tokens : tokens + rank], joined[:, tokens + rank :, :out_block]], axis=2
     ).reshape(n_z * rank, block + out_block)
     pair, adapters = lax.optimization_barrier((pair, adapters))
-    before, after = shift(adapters, 1), shift(adapters, -1)
+    parts = around(adapters)
 
     summed = jnp.sum(exchange(pair, CHIPS).astype(F32), axis=0).astype(BF)
-    summed, before, after, adapters = lax.optimization_barrier((summed, before, after, adapters))
-    some = n_z * rank // 2
-    parts = [adapters, before, jnp.concatenate([shift(adapters[:some], 2), shift(after[some:], -1)], axis=0), after]
     summed = jnp.stack([summed[:, s * cols : (s + 1) * cols] for s in range(n_yh)])
     projected = lax.ppermute(summed[turned], ("z", "yl", "x"), homes)
+    projected, *parts = lax.optimization_barrier((projected, *parts))
 
     hidden = residual_part + jnp.concatenate([projected[j] for j in range(n_yh)], axis=1).astype(F32)
     squares = jnp.sum(hidden * hidden, axis=1, keepdims=True)
@@ -162,14 +165,11 @@
     inv_column = lax.rsqrt((totals[:, :1] + totals[:, 1:2]) / width + EPSILON)
     inv_row = jnp.broadcast_to(inv_column, (mine, 128)).T[:1]
 
-    _, later = lax.optimization_barrier((message, turned))
-    adapters_all = jnp.stack(parts)[later].reshape(tenants * rank, block + out_block)
-    adapters_other = swap(adapters_all)
-    downs = jnp.concatenate(ordered(adapters_all[:, :block], adapters_other[:, :block]), axis=1)
-    ups = jnp.concatenate([adapters_all[:, block:], adapters_other[:, block:]], axis=1)
-
-    def select(values):
-        chosen = jnp.where(own_mask, values, 0.0)
+    adapters_all = jnp.stack(parts)[turned].reshape(tenants * rank, block + out_block)
+    downs, ups = adapters_all[:, :block], adapters_all[:, block:]
+
+    def select(values, mask):
+        chosen = jnp.where(mask, values, 0.0)
         return jnp.sum(chosen.reshape(tenants, rank, mine), axis=0)
 
     def widen(values, mask):
@@ -177,14 +177,16 @@
 
     chip_features = lax.dynamic_index_in_dim(features, chip, 0, keepdims=False)
     own_scaled = half(chip_features, core, block, 1)
-    low_part = select(dot("jd,td->jt", downs, chip_features)) * inv_row
-
     target = lax.dynamic_slice(
         features, (chip // 2, 0, (chip % 2) * 2 * out_block), (1, mine, 2 * out_block)
     )[0]
     target = (target.astype(F32) * inv_column).astype(BF)
     came = swap(jnp.concatenate([half(chip_features, other, block, 1), target[:16]], axis=0))
     partner_scaled, next_row = came[:mine], came[mine : mine + 1]
+    low_parts = ordered(
+        select(dot("jd,td->jt", downs, own_scaled), own_mask),
+        select(dot("jd,td->jt", downs, partner_scaled), partner_mask),
+    )
     target = jnp.concatenate([target[1:], next_row], axis=0)
     target = jnp.concatenate([half(target, core, out_block, 1), half(target, other, out_block, 1)], axis=1)
 
@@ -200,32 +202,33 @@
     partner = swap(jnp.concatenate([plain_other, lanes], axis=1))
     plain_own = plain(draft_weight, 0)
 
-    back_part = select(dot("jc,tc->jt", ups, jnp.concatenate([plain_own.astype(BF), plain_other], axis=1)))
-    some = tenants * rank // 2
-    some_ups = half(ups, core, some)
-    same = slot[:some, None] == slot[None, :some]
-    square_part = jnp.where(same, dot("jc,ic->ji", some_ups, some_ups), 0.0)
-    square_part = jnp.sum(square_part.reshape(tenants // 2, rank, some), axis=0)
-    codes = jnp.concatenate([low_part, back_part], axis=1)
-    codes = gather(jnp.concatenate([*split(codes), square_part.astype(BF)], axis=1), MP, 2 * n_chips)
-    codes = jnp.sum(codes.reshape(n_chips, 2, rank, 4 * mine + some).astype(F32), axis=0)
-    square = jnp.concatenate([codes[0, :, 4 * mine :], codes[1, :, 4 * mine :]], axis=1).astype(BF)
-    codes = codes[:, :, : 2 * mine] + codes[:, :, 2 * mine : 4 * mine]
+    back_parts = ordered(
+        select(dot("jc,tc->jt", ups, plain_own.astype(BF)), own_mask),
+        select(dot("jc,tc->jt", ups, partner[:, :out_block]), partner_mask),
+    )
+    square = jnp.where(slot[:, None] == slot[None, :], dot("jc,ic->ji", ups, ups), 0.0)
+    square = jnp.sum(square.reshape(tenants, rank, tenants * rank), axis=0)
+    codes = jnp.concatenate([*low_parts, *back_parts, square], axis=1).astype(BF)
+    codes = jnp.sum(gather(codes, MP, 2 * n_chips).astype(F32), axis=0)
+    square = codes[:, 4 * mine :].astype(BF)
+    lows = ordered(codes[:, :mine], codes[:, mine : 2 * mine])
+    backs = ordered(codes[:, 2 * mine : 3 * mine], codes[:, 3 * mine : 4 * mine])
     partner_inv = partner[:, out_block:].T
     partner_inv = partner_inv[:1].astype(F32) + partner_inv[1:2].astype(F32)
 
-    def finish(code, mask, plain_grad, column, row, inv):
-        low_wide = widen(code[:, :mine].astype(BF), mask)
-        term = ADAPTER_SCALE * dot("jt,jn->tn", low_wide, ups[:, :out_block])
+    def finish(low, back, mask, plain_grad, column, row, inv):
+        low_wide = widen((low * inv).astype(BF), mask)
+        term = ADAPTER_SCALE * dot("jt,jn->tn", low_wide, ups)
         grad = (plain_grad + term * column).astype(BF)
-        back = code[:, mine:] + ADAPTER_SCALE * dot("rj,jt->rt", square, low_wide) * row
+        back = back + ADAPTER_SCALE * dot("rj,jt->rt", square, low_wide) * row
         return low_wide, grad, widen((ADAPTER_SCALE * back * inv).astype(BF), mask)
 
     low_wide, grad, back_wide = finish(
-        half(codes, core, 1)[0], own_mask, plain_own, weight, weight_row, inv_row
+        lows[0], backs[0], own_mask, plain_own, weight, weight_row, inv_row
     )
     partner_low, partner_grad, partner_back = finish(
-        half(codes, other, 1)[0],
+        lows[1],
+        backs[1],
         partner_mask,
         partner[:, :out_block].astype(F32),
         partner_weight,

time: 207 us -> 185 us (0.89)
  starting transfers between devices: 84.3 us -> 69.6 us
  other arithmetic: 7.43 us -> 3.29 us
  waiting for transfers between devices: 54.8 us -> 51.7 us
  blocking collectives: 32.9 us -> 35.5 us
    ppermute x1, waiting for transfers between devices: 8.82 us -> 0.01 us  [shards(): projected = lax.ppermute(summed[turned], ('z', 'yl', 'x'), homes)]
    all_to_all x4, starting transfers between devices: 33.4 us -> 25.8 us  [exchange(): return lax.all_to_all(value, axis, 0, 0)]
    all_to_all x4, waiting for transfers between devices: 14.4 us -> 21.9 us  [exchange(): return lax.all_to_all(value, axis, 0, 0)]
    ppermute x1, starting transfers between devices: 4.56 us -> 1.92 us  [shards(): projected = lax.ppermute(summed[turned], ('z', 'yl', 'x'), homes)]
    all_to_all x1, blocking collectives: 32.9 us -> 35.5 us  [exchange(): return lax.all_to_all(value, axis, 0, 0)]
    ppermute x7 -> x6, starting transfers between devices: 30.8 us -> 28.4 us  [around(): lax.ppermute(value, 'yh', [(i, (i + s) % n_yh) for i in range(n_yh)])]
    ppermute x7 -> x6, waiting for transfers between devices: 13.5 us -> 11.2 us  [around(): lax.ppermute(value, 'yh', [(i, (i + s) % n_yh) for i in range(n_yh)])]
    ppermute x6 -> x5, starting transfers between devices: 12.2 us -> 10.1 us  [swap(): return lax.ppermute(value, 'c', [(0, 1), (1, 0)])]
  transfers between devices with their start and end apart: 19 -> 17, of which waited for: 10 -> 9; matrix products, arithmetic and copies ran while one was open for 5% -> 6% of each run, Pallas kernels for 0% -> 0%
where the time goes in v11:
time: 185 us; the launch traced here: 184 us
  starting transfers between devices  69.6 us (38%)
  waiting for transfers between devices  51.7 us (28%)
  blocking collectives  35.5 us (19%)
  local copies, waits for them, and re-layouts  9.97 us (5%)
  matrix products  9.36 us (5%)
  Pallas kernels  3.48 us (2%)
  other arithmetic  3.29 us (2%)
    all_to_all x1, blocking collectives, exchange(): return lax.all_to_all(value, axis, 0, 0)  35.5 us
    ppermute x6, starting transfers between devices, around(): lax.ppermute(value, 'yh', [(i, (i + s) % n_yh) for i in range(n_yh)])  28.4 us
    all_to_all x4, starting transfers between devices, exchange(): return lax.all_to_all(value, axis, 0, 0)  25.8 us
    all_to_all x4, waiting for transfers between devices, exchange(): return lax.all_to_all(value, axis, 0, 0)  21.9 us
    ppermute x1, waiting for transfers between devices, shards(): chip_rows = lax.ppermute(chip_rows, ('z', 'yl', 'x'), chips)  15.2 us
    ppermute x6, waiting for transfers between devices, around(): lax.ppermute(value, 'yh', [(i, (i + s) % n_yh) for i in range(n_yh)])  11.2 us
    ppermute x5, starting transfers between devices, swap(): return lax.ppermute(value, 'c', [(0, 1), (1, 0)])  10.1 us
    dot_general x13, matrix products, dot(): return jnp.einsum(subscripts, left, right, preferred_element_type=F32)  9.36 us
  transfers between devices with their start and end apart: 17, of which 9 were waited for; matrix products, arithmetic and copies ran while one was open for 6% of the time, Pallas kernels for 0%

profile of v11, /device:TPU:6, one launch (start us, length us, event | category | flops | bytes accessed | tf_op | source)
XLA Modules:
  0.0 184.2 jit_solution(6744784826561429772)
XLA Ops:
  0.6 0.7 concatenate.48
  1.3 1.0 broadcast_in_dim.39
  2.3 0.7 broadcast_in_dim.40
  3.1 1.2 pad_maximum_fusion
  4.3 10.3 %all-to-all-start = ((bf16[8,160,512]{2,1,0:T(8,128)(2,1)}), bf16[8,160,512]{2,1,0:T(8,128)(2,1)S(1)}, u32[]{:S(2)}, u32[]{:S(2)}) async-start(bf16[8,160,512]{2,1,0:T(8,128)(2,1)} %pad_maximum_fusion), calls=%async_computation | async-start | bytes 2621440 | tf_op jit(solution)/shard_map/all_to_all | solution.py:32
  14.7 4.5 %collective-permute-start.2 = (bf16[512,256]{1,0:T(8,128)(2,1)S(1)}, bf16[512,256]{1,0:T(8,128)(2,1)S(1)}, u32[]{:S(2)}, u32[]{:S(2)}) collective-permute-start(bf16[512,256]{1,0:T(8,128)(2,1)S(1)} %copy-done), channel_id=1, source_target_pairs={{0,16},{16,32},{32,48},{48,0},{1,17},{17,33},{33,49},{49,1},{2,18}... | collective-permute-start | bytes 786440 | tf_op jit(solution)/shard_map/ppermute | solution.py:104
  19.2 5.9 %collective-permute-start.3 = (bf16[512,256]{1,0:T(8,128)(2,1)S(1)}, bf16[512,256]{1,0:T(8,128)(2,1)S(1)}, u32[]{:S(2)}, u32[]{:S(2)}) collective-permute-start(bf16[512,256]{1,0:T(8,128)(2,1)S(1)} %copy-done), channel_id=1, source_target_pairs={{0,32},{16,48},{32,0},{48,16},{1,33},{17,49},{33,1},{49,17},{2,34}... | collective-permute-start | bytes 786440 | tf_op jit(solution)/shard_map/ppermute | solution.py:104
  25.1 5.3 %collective-permute-start.4 = (bf16[512,256]{1,0:T(8,128)(2,1)S(1)}, bf16[512,256]{1,0:T(8,128)(2,1)S(1)}, u32[]{:S(2)}, u32[]{:S(2)}) collective-permute-start(bf16[512,256]{1,0:T(8,128)(2,1)S(1)} %copy-done), channel_id=1, source_target_pairs={{0,48},{16,0},{32,16},{48,32},{1,49},{17,1},{33,17},{49,33},{2,50}... | collective-permute-start | bytes 786440 | tf_op jit(solution)/shard_map/ppermute | solution.py:104
  30.4 1.9 %collective-permute-start = (bf16[80,512]{1,0:T(8,128)(2,1)S(1)}, bf16[80,512]{1,0:T(8,128)(2,1)S(1)}, u32[]{:S(2)}, u32[]{:S(2)}) collective-permute-start(bf16[80,512]{1,0:T(8,128)(2,1)S(1)} %pad_maximum_fusion.7), channel_id=1, source_target_pairs={{0,1},{1,0},{2,3},{3,2},{4,5},{5,4},{6,7},{7,6},{8,9},{9,8},{10,11... | collective-permute-start | bytes 245768 | tf_op jit(solution)/shard_map/ppermute | solution.py:28
  32.8 0.8 collective-permute-done
  33.7 3.4 %collective-permute-start.1 = (bf16[80,1024]{1,0:T(8,128)(2,1)S(1)}, bf16[80,1024]{1,0:T(8,128)(2,1)S(1)}, u32[]{:S(2)}, u32[]{:S(2)}) collective-permute-start(bf16[80,1024]{1,0:T(8,128)(2,1)S(1)} %pad_maximum_fusion.4), channel_id=1, source_target_pairs={{0,0},{2,14},{4,12},{6,10},{8,8},{10,6},{12,4},{14,2},{64,66},{66,... | collective-permute-start | bytes 491528 | tf_op jit(solution)/shard_map/ppermute | solution.py:125
  37.3 15.2 %collective-permute-done.1 = bf16[80,1024]{1,0:T(8,128)(2,1)S(1)} collective-permute-done((bf16[80,1024]{1,0:T(8,128)(2,1)S(1)}, bf16[80,1024]{1,0:T(8,128)(2,1)S(1)}, u32[]{:S(2)}, u32[]{:S(2)}) %collective-permute-start.1) | collective-permute-done | bytes 163872 | tf_op jit(solution)/shard_map/ppermute | solution.py:125
  52.5 1.3 shard_map.104
  53.8 1.9 %collective-permute-start.5 = (bf16[8,64,1024]{2,1,0:T(8,128)(2,1)S(1)}, bf16[8,64,1024]{2,1,0:T(8,128)(2,1)S(1)}, u32[]{:S(2)}, u32[]{:S(2)}) collective-permute-start(bf16[8,64,1024]{2,1,0:T(8,128)(2,1)S(1)} %shard_map.104), channel_id=1, source_target_pairs={{0,1},{1,0},{2,3},{3,2},{4,5},{5,4},{6,7},{7,6},{8,9},{9,8},{10,11... | collective-permute-start | bytes 3145736 | tf_op jit(solution)/shard_map/ppermute | solution.py:28
  55.8 2.5 %collective-permute-done.5.refs_4_ = bf16[8,64,1024]{2,1,0:T(8,128)(2,1)S(1)} collective-permute-done((bf16[8,64,1024]{2,1,0:T(8,128)(2,1)S(1)}, bf16[8,64,1024]{2,1,0:T(8,128)(2,1)S(1)}, u32[]{:S(2)}, u32[]{:S(2)}) %collective-permute-start.5) | collective-permute-done | bytes 1048608 | tf_op jit(solution)/shard_map/ppermute | solution.py:28
  58.3 2.2 %shard_map.105 = bf16[8,64,1024]{2,1,0:T(8,128)(2,1)} custom-call(s32[2]{0:T(128)S(1)} %pad_add_fusion.place, bf16[8,160,512]{2,1,0:T(8,128)(2,1)S(1)} %all-to-all-done.joined, bf16[512,256]{1,0:T(8,128)(2,1)S(1)} %copy-done, bf16[512,256]{1,0:T(8,128)(2,1)S(1)} %collective-permute-done.2.refs_1_, bf16[512,256]{1,0:T(8,128)(2,1)S(1)} %collective-permute-done.3.refs_2_, ...), custom_call_target="tpu_custom_call" | custom-call | flops 536870912 | bytes 4194304 | tf_op jit(solution)/shard_map/pallas_call | solution.py:71
  60.5 4.5 %all-to-all-start.1 = ((bf16[8,64,1024]{2,1,0:T(8,128)(2,1)}), bf16[8,64,1024]{2,1,0:T(8,128)(2,1)S(1)}, u32[]{:S(2)}, u32[]{:S(2)}) async-start(bf16[8,64,1024]{2,1,0:T(8,128)(2,1)} %shard_map.105), calls=%async_computation.1 | async-start | bytes 2097152 | tf_op jit(solution)/shard_map/all_to_all | solution.py:32
  65.0 1.9 %collective-permute-start.11 = (bf16[8192,256]{1,0:T(8,128)(2,1)}, bf16[8192,256]{1,0:T(8,128)(2,1)}, u32[]{:S(2)}, u32[]{:S(2)}) collective-permute-start(bf16[8192,256]{1,0:T(8,128)(2,1)} %param.13), channel_id=1, source_target_pairs={{0,1},{1,0},{2,3},{3,2},{4,5},{5,4},{6,7},{7,6},{8,9},{9,8},{10,11... | collective-permute-start | bytes 12582920 | tf_op jit(solution)/shard_map/ppermute | solution.py:28
  67.0 2.6 %collective-permute-start.7 = (bf16[128,768]{1,0:T(8,128)(2,1)S(1)}, bf16[128,768]{1,0:T(8,128)(2,1)S(1)}, u32[]{:S(2)}, u32[]{:S(2)}) collective-permute-start(bf16[128,768]{1,0:T(8,128)(2,1)S(1)} %bitcast.102), channel_id=1, source_target_pairs={{0,16},{16,32},{32,48},{48,0},{1,17},{17,33},{33,49},{49,1},{2,18}... | collective-permute-start | bytes 589832 | tf_op jit(solution)/shard_map/ppermute | solution.py:104
  69.7 6.9 %collective-permute-start.8 = (bf16[128,768]{1,0:T(8,128)(2,1)S(1)}, bf16[128,768]{1,0:T(8,128)(2,1)S(1)}, u32[]{:S(2)}, u32[]{:S(2)}) collective-permute-start(bf16[128,768]{1,0:T(8,128)(2,1)S(1)} %bitcast.103), channel_id=1, source_target_pairs={{0,32},{16,48},{32,0},{48,16},{1,33},{17,49},{33,1},{49,17},{2,34}... | collective-permute-start | bytes 589832 | tf_op jit(solution)/shard_map/ppermute | solution.py:104
  76.6 3.1 %collective-permute-start.9 = (bf16[128,768]{1,0:T(8,128)(2,1)S(1)}, bf16[128,768]{1,0:T(8,128)(2,1)S(1)}, u32[]{:S(2)}, u32[]{:S(2)}) collective-permute-start(bf16[128,768]{1,0:T(8,128)(2,1)S(1)} %bitcast.104), channel_id=1, source_target_pairs={{0,48},{16,0},{32,16},{48,32},{1,49},{17,1},{33,17},{49,33},{2,50}... | collective-permute-start | bytes 589832 | tf_op jit(solution)/shard_map/ppermute | solution.py:104
  79.7 2.2 %all-to-all-done.1 = bf16[8,64,1024]{2,1,0:T(8,128)(2,1)S(1)} async-done(((bf16[8,64,1024]{2,1,0:T(8,128)(2,1)}), bf16[8,64,1024]{2,1,0:T(8,128)(2,1)S(1)}, u32[]{:S(2)}, u32[]{:S(2)}) %all-to-all-start.1) | async-done | bytes 1048608 | tf_op jit(solution)/shard_map/all_to_all | solution.py:32
  81.9 0.2 reduce_sum.105
  82.2 0.6 gather_fusion
  82.7 1.9 %collective-permute-start.6 = (bf16[4,64,256]{2,1,0:T(8,128)(2,1)S(1)}, bf16[4,64,256]{2,1,0:T(8,128)(2,1)S(1)}, u32[]{:S(2)}, u32[]{:S(2)}) collective-permute-start(bf16[4,64,256]{2,1,0:T(8,128)(2,1)S(1)} %gather_fusion), channel_id=1, source_target_pairs={{0,0},{2,66},{4,132},{6,198},{8,264},{10,330},{12,396},{14,462},{6... | collective-permute-start | bytes 393224 | tf_op jit(solution)/shard_map/ppermute | solution.py:154
  84.7 7.4 %collective-permute-done.7 = bf16[128,768]{1,0:T(8,128)(2,1)S(1)} collective-permute-done((bf16[128,768]{1,0:T(8,128)(2,1)S(1)}, bf16[128,768]{1,0:T(8,128)(2,1)S(1)}, u32[]{:S(2)}, u32[]{:S(2)}) %collective-permute-start.7) | collective-permute-done | bytes 196640 | tf_op jit(solution)/shard_map/ppermute | solution.py:104
  92.0 2.7 %collective-permute-done.8 = bf16[128,768]{1,0:T(8,128)(2,1)S(1)} collective-permute-done((bf16[128,768]{1,0:T(8,128)(2,1)S(1)}, bf16[128,768]{1,0:T(8,128)(2,1)S(1)}, u32[]{:S(2)}, u32[]{:S(2)}) %collective-permute-start.8) | collective-permute-done | bytes 196640 | tf_op jit(solution)/shard_map/ppermute | solution.py:104
  94.7 1.1 collective-permute-done.9
  95.9 0.2 multiply_reduce_fusion
  96.2 0.1 copy.40
  96.4 1.2 broadcast_in_dim.46
  97.5 5.6 %all-to-all-start.2 = ((bf16[8,64,1152]{2,1,0:T(8,128)(2,1)}), bf16[8,64,1152]{2,1,0:T(8,128)(2,1)S(1)}, u32[]{:S(2)}, u32[]{:S(2)}) async-start(bf16[8,64,1152]{2,1,0:T(8,128)(2,1)} %broadcast_in_dim.46), calls=%async_computation.2 | async-start | bytes 2359296 | tf_op jit(solution)/shard_map/all_to_all | solution.py:32
  103.4 0.6 gather_fusion.1
  104.0 0.3 convolution_select_fusion
  104.4 12.6 %all-to-all-done.2 = bf16[8,64,1152]{2,1,0:T(8,128)(2,1)S(1)} async-done(((bf16[8,64,1152]{2,1,0:T(8,128)(2,1)}), bf16[8,64,1152]{2,1,0:T(8,128)(2,1)S(1)}, u32[]{:S(2)}, u32[]{:S(2)}) %all-to-all-start.2) | async-done | bytes 1179680 | tf_op jit(solution)/shard_map/all_to_all | solution.py:32
  117.2 0.2 slice.156
  117.4 0.6 gather_fusion.2
  118.3 1.9 %collective-permute-start.10 = (bf16[80,512]{1,0:T(8,128)(2,1)S(1)}, bf16[80,512]{1,0:T(8,128)(2,1)S(1)}, u32[]{:S(2)}, u32[]{:S(2)}) collective-permute-start(bf16[80,512]{1,0:T(8,128)(2,1)S(1)} %pad_maximum_fusion.9), channel_id=1, source_target_pairs={{0,1},{1,0},{2,3},{3,2},{4,5},{5,4},{6,7},{7,6},{8,9},{9,8},{10,11... | collective-permute-start | bytes 245768 | tf_op jit(solution)/shard_map/ppermute | solution.py:28
  120.2 0.3 convolution_select_fusion.2
  120.5 3.0 %fusion.3 = f32[64,256]{1,0:T(8,128)S(1)} fusion(bf16[8,64,1024]{2,1,0:T(8,128)(2,1)S(1)} %gather_fusion.2, bf16[8,1024,256]{2,1,0:T(8,128)(2,1)} %bitcast.95, f32[64]{0:T(128)S(1)} %bitcast.116), kind=kOutput, calls=%fused_computation.17 | convolution fusion | flops 268451840 | bytes 5308672 | tf_op jit(solution)/shard_map/ktd,kdn->tn/dot_general | solution.py:24
  123.7 0.1 copy.41
  124.0 3.0 %fusion.7 = bf16[64,256]{1,0:T(8,128)(2,1)S(1)} fusion(bf16[8,64,1024]{2,1,0:T(8,128)(2,1)S(1)} %gather_fusion.2, bf16[8,1024,256]{2,1,0:T(8,128)(2,1)} %bitcast.32, s32[]{:T(128)S(6)} %select_n.259, bf16[63,512]{1,0:T(8,128)(2,1)S(1)} %slice.163, bf16[1,512]{1,0:T(2,128)(2,1)S(1)} %slice.164, f32[64]{0:T(128)S(1)} %get-tuple-element.29, f32[64]{0:T(128)S(1)} %bitcast.117), kind=kOutput, calls=%fused_computation.23 | convolution fusion | flops 268566528 | bytes 5341700 | tf_op jit(solution)/shard_map/ktd,kdn->tn/dot_general | solution.py:24
  127.1 2.4 %collective-permute-start.12 = (bf16[64,384]{1,0:T(8,128)(2,1)S(1)}, bf16[64,384]{1,0:T(8,128)(2,1)S(1)}, u32[]{:S(2)}, u32[]{:S(2)}) collective-permute-start(bf16[64,384]{1,0:T(8,128)(2,1)S(1)} %pad_maximum_fusion.10), channel_id=1, source_target_pairs={{0,1},{1,0},{2,3},{3,2},{4,5},{5,4},{6,7},{7,6},{8,9},{9,8},{10,11... | collective-permute-start | bytes 147464 | tf_op jit(solution)/shard_map/ppermute | solution.py:28
  129.5 0.3 convolution_select_fusion.1
  129.8 0.1 copy.44
  129.9 0.2 convolution_select_fusion.4
  130.2 0.1 copy.45
  130.4 0.2 convolution_select_fusion.3
  130.6 0.1 copy.48
  130.8 0.8 broadcast_in_dim.49
  131.6 5.4 %all-to-all-start.3 = ((bf16[16,16,768]{2,1,0:T(8,128)(2,1)}), bf16[16,16,768]{2,1,0:T(8,128)(2,1)S(1)}, u32[]{:S(2)}, u32[]{:S(2)}) async-start(bf16[16,16,768]{2,1,0:T(8,128)(2,1)} %broadcast_in_dim.49), calls=%async_computation.3 | async-start | bytes 786432 | tf_op jit(solution)/shard_map/all_to_all | solution.py:32
  137.0 0.2 add_reduce_fusion
  137.2 7.1 %all-to-all-done.3 = bf16[16,16,768]{2,1,0:T(8,128)(2,1)S(1)} async-done(((bf16[16,16,768]{2,1,0:T(8,128)(2,1)}), bf16[16,16,768]{2,1,0:T(8,128)(2,1)S(1)}, u32[]{:S(2)}, u32[]{:S(2)}) %all-to-all-start.3) | async-done | bytes 393248 | tf_op jit(solution)/shard_map/all_to_all | solution.py:32
  144.6 0.1 fusion.13
  145.0 0.1 fusion.14
  145.2 0.5 fusion.40
  145.7 0.5 fusion.1
  146.3 0.3 fusion.26
  146.6 0.4 fusion
  147.1 0.3 copy.53
  147.4 35.5 %all_to_all.25 = bf16[32,16,768]{2,1,0:T(8,128)(2,1)S(1)} all-to-all(bf16[32,16,768]{2,1,0:T(8,128)(2,1)S(1)} %bitcast.96), channel_id=1, replica_groups=mesh['z'=8,'yh'=4,'yl'=2,'x'=4,'c'=2] {'yh','z'}, dimensions={0} | all-to-all | bytes 1572864 | tf_op jit(solution)/shard_map/all_to_all | solution.py:32
  182.9 0.1 convert_reduce_fusion
  183.0 0.6 slice_bitcast_fusion
  183.6 0.6 slice_bitcast_fusion.9
  (87 shorter events, 3.1 us)
Async XLA Ops:
  3.1 11.6 %copy-start = (bf16[512,256]{1,0:T(8,128)(2,1)S(1)}, bf16[512,256]{1,0:T(8,128)(2,1)}, u32[]{:S(2)}) copy-start(bf16[512,256]{1,0:T(8,128)(2,1)} %refs_0_.3) | copy-start | bytes 786436
  3.1 27.3 %copy-start.1 = (bf16[128,512]{1,0:T(8,128)(2,1)S(1)}, bf16[128,512]{1,0:T(8,128)(2,1)}, u32[]{:S(2)}) copy-start(bf16[128,512]{1,0:T(8,128)(2,1)} %param.11) | copy-start | bytes 393220
  3.1 27.3 %copy-start.3 = (bf16[512]{0:T(512)(128)(2,1)S(1)}, bf16[512]{0:T(512)(128)(2,1)}, u32[]{:S(2)}) copy-start(bf16[512]{0:T(512)(128)(2,1)} %param.12) | copy-start | bytes 3076
  3.1 29.3 %copy-start.4 = (s32[32]{0:T(128)S(1)}, s32[32]{0:T(128)}, u32[]{:S(2)}) copy-start(s32[32]{0:T(128)} %param.17) | copy-start | bytes 388
  3.1 29.3 %copy-start.2 = (s32[128]{0:T(128)S(1)}, s32[128]{0:T(128)}, u32[]{:S(2)}) copy-start(s32[128]{0:T(128)} %param.16) | copy-start | bytes 1540
  4.3 48.1 %all-to-all-start = ((bf16[8,160,512]{2,1,0:T(8,128)(2,1)}), bf16[8,160,512]{2,1,0:T(8,128)(2,1)S(1)}, u32[]{:S(2)}, u32[]{:S(2)}) async-start(bf16[8,160,512]{2,1,0:T(8,128)(2,1)} %pad_maximum_fusion), calls=%async_computation | async-start | bytes 2621440 | tf_op jit(solution)/shard_map/all_to_all | solution.py:32
  14.7 37.8 %collective-permute-start.2 = (bf16[512,256]{1,0:T(8,128)(2,1)S(1)}, bf16[512,256]{1,0:T(8,128)(2,1)S(1)}, u32[]{:S(2)}, u32[]{:S(2)}) collective-permute-start(bf16[512,256]{1,0:T(8,128)(2,1)S(1)} %copy-done), channel_id=1, source_target_pairs={{0,16},{16,32},{32,48},{48,0},{1,17},{17,33},{33,49},{49,1},{2,18}... | collective-permute-start | bytes 786440 | tf_op jit(solution)/shard_map/ppermute | solution.py:104
  19.2 33.3 %collective-permute-start.3 = (bf16[512,256]{1,0:T(8,128)(2,1)S(1)}, bf16[512,256]{1,0:T(8,128)(2,1)S(1)}, u32[]{:S(2)}, u32[]{:S(2)}) collective-permute-start(bf16[512,256]{1,0:T(8,128)(2,1)S(1)} %copy-done), channel_id=1, source_target_pairs={{0,32},{16,48},{32,0},{48,16},{1,33},{17,49},{33,1},{49,17},{2,34}... | collective-permute-start | bytes 786440 | tf_op jit(solution)/shard_map/ppermute | solution.py:104
  25.1 27.4 %collective-permute-start.4 = (bf16[512,256]{1,0:T(8,128)(2,1)S(1)}, bf16[512,256]{1,0:T(8,128)(2,1)S(1)}, u32[]{:S(2)}, u32[]{:S(2)}) collective-permute-start(bf16[512,256]{1,0:T(8,128)(2,1)S(1)} %copy-done), channel_id=1, source_target_pairs={{0,48},{16,0},{32,16},{48,32},{1,49},{17,1},{33,17},{49,33},{2,50}... | collective-permute-start | bytes 786440 | tf_op jit(solution)/shard_map/ppermute | solution.py:104
  30.4 3.2 %collective-permute-start = (bf16[80,512]{1,0:T(8,128)(2,1)S(1)}, bf16[80,512]{1,0:T(8,128)(2,1)S(1)}, u32[]{:S(2)}, u32[]{:S(2)}) collective-permute-start(bf16[80,512]{1,0:T(8,128)(2,1)S(1)} %pad_maximum_fusion.7), channel_id=1, source_target_pairs={{0,1},{1,0},{2,3},{3,2},{4,5},{5,4},{6,7},{7,6},{8,9},{9,8},{10,11... | collective-permute-start | bytes 245768 | tf_op jit(solution)/shard_map/ppermute | solution.py:28
  33.7 18.8 %collective-permute-start.1 = (bf16[80,1024]{1,0:T(8,128)(2,1)S(1)}, bf16[80,1024]{1,0:T(8,128)(2,1)S(1)}, u32[]{:S(2)}, u32[]{:S(2)}) collective-permute-start(bf16[80,1024]{1,0:T(8,128)(2,1)S(1)} %pad_maximum_fusion.4), channel_id=1, source_target_pairs={{0,0},{2,14},{4,12},{6,10},{8,8},{10,6},{12,4},{14,2},{64,66},{66,... | collective-permute-start | bytes 491528 | tf_op jit(solution)/shard_map/ppermute | solution.py:125
  53.8 4.6 %collective-permute-start.5 = (bf16[8,64,1024]{2,1,0:T(8,128)(2,1)S(1)}, bf16[8,64,1024]{2,1,0:T(8,128)(2,1)S(1)}, u32[]{:S(2)}, u32[]{:S(2)}) collective-permute-start(bf16[8,64,1024]{2,1,0:T(8,128)(2,1)S(1)} %shard_map.104), channel_id=1, source_target_pairs={{0,1},{1,0},{2,3},{3,2},{4,5},{5,4},{6,7},{7,6},{8,9},{9,8},{10,11... | collective-permute-start | bytes 3145736 | tf_op jit(solution)/shard_map/ppermute | solution.py:28
  60.5 21.4 %all-to-all-start.1 = ((bf16[8,64,1024]{2,1,0:T(8,128)(2,1)}), bf16[8,64,1024]{2,1,0:T(8,128)(2,1)S(1)}, u32[]{:S(2)}, u32[]{:S(2)}) async-start(bf16[8,64,1024]{2,1,0:T(8,128)(2,1)} %shard_map.105), calls=%async_computation.1 | async-start | bytes 2097152 | tf_op jit(solution)/shard_map/all_to_all | solution.py:32
  65.0 58.9 %collective-permute-start.11 = (bf16[8192,256]{1,0:T(8,128)(2,1)}, bf16[8192,256]{1,0:T(8,128)(2,1)}, u32[]{:S(2)}, u32[]{:S(2)}) collective-permute-start(bf16[8192,256]{1,0:T(8,128)(2,1)} %param.13), channel_id=1, source_target_pairs={{0,1},{1,0},{2,3},{3,2},{4,5},{5,4},{6,7},{7,6},{8,9},{9,8},{10,11... | collective-permute-start | bytes 12582920 | tf_op jit(solution)/shard_map/ppermute | solution.py:28
  67.0 25.0 %collective-permute-start.7 = (bf16[128,768]{1,0:T(8,128)(2,1)S(1)}, bf16[128,768]{1,0:T(8,128)(2,1)S(1)}, u32[]{:S(2)}, u32[]{:S(2)}) collective-permute-start(bf16[128,768]{1,0:T(8,128)(2,1)S(1)} %bitcast.102), channel_id=1, source_target_pairs={{0,16},{16,32},{32,48},{48,0},{1,17},{17,33},{33,49},{49,1},{2,18}... | collective-permute-start | bytes 589832 | tf_op jit(solution)/shard_map/ppermute | solution.py:104
  69.7 25.1 %collective-permute-start.8 = (bf16[128,768]{1,0:T(8,128)(2,1)S(1)}, bf16[128,768]{1,0:T(8,128)(2,1)S(1)}, u32[]{:S(2)}, u32[]{:S(2)}) collective-permute-start(bf16[128,768]{1,0:T(8,128)(2,1)S(1)} %bitcast.103), channel_id=1, source_target_pairs={{0,32},{16,48},{32,0},{48,16},{1,33},{17,49},{33,1},{49,17},{2,34}... | collective-permute-start | bytes 589832 | tf_op jit(solution)/shard_map/ppermute | solution.py:104
  76.6 19.3 %collective-permute-start.9 = (bf16[128,768]{1,0:T(8,128)(2,1)S(1)}, bf16[128,768]{1,0:T(8,128)(2,1)S(1)}, u32[]{:S(2)}, u32[]{:S(2)}) collective-permute-start(bf16[128,768]{1,0:T(8,128)(2,1)S(1)} %bitcast.104), channel_id=1, source_target_pairs={{0,48},{16,0},{32,16},{48,32},{1,49},{17,1},{33,17},{49,33},{2,50}... | collective-permute-start | bytes 589832 | tf_op jit(solution)/shard_map/ppermute | solution.py:104
  82.7 13.1 %collective-permute-start.6 = (bf16[4,64,256]{2,1,0:T(8,128)(2,1)S(1)}, bf16[4,64,256]{2,1,0:T(8,128)(2,1)S(1)}, u32[]{:S(2)}, u32[]{:S(2)}) collective-permute-start(bf16[4,64,256]{2,1,0:T(8,128)(2,1)S(1)} %gather_fusion), channel_id=1, source_target_pairs={{0,0},{2,66},{4,132},{6,198},{8,264},{10,330},{12,396},{14,462},{6... | collective-permute-start | bytes 393224 | tf_op jit(solution)/shard_map/ppermute | solution.py:154
  97.5 19.5 %all-to-all-start.2 = ((bf16[8,64,1152]{2,1,0:T(8,128)(2,1)}), bf16[8,64,1152]{2,1,0:T(8,128)(2,1)S(1)}, u32[]{:S(2)}, u32[]{:S(2)}) async-start(bf16[8,64,1152]{2,1,0:T(8,128)(2,1)} %broadcast_in_dim.46), calls=%async_computation.2 | async-start | bytes 2359296 | tf_op jit(solution)/shard_map/all_to_all | solution.py:32
  118.3 5.7 %collective-permute-start.10 = (bf16[80,512]{1,0:T(8,128)(2,1)S(1)}, bf16[80,512]{1,0:T(8,128)(2,1)S(1)}, u32[]{:S(2)}, u32[]{:S(2)}) collective-permute-start(bf16[80,512]{1,0:T(8,128)(2,1)S(1)} %pad_maximum_fusion.9), channel_id=1, source_target_pairs={{0,1},{1,0},{2,3},{3,2},{4,5},{5,4},{6,7},{7,6},{8,9},{9,8},{10,11... | collective-permute-start | bytes 245768 | tf_op jit(solution)/shard_map/ppermute | solution.py:28
  127.1 3.3 %collective-permute-start.12 = (bf16[64,384]{1,0:T(8,128)(2,1)S(1)}, bf16[64,384]{1,0:T(8,128)(2,1)S(1)}, u32[]{:S(2)}, u32[]{:S(2)}) collective-permute-start(bf16[64,384]{1,0:T(8,128)(2,1)S(1)} %pad_maximum_fusion.10), channel_id=1, source_target_pairs={{0,1},{1,0},{2,3},{3,2},{4,5},{5,4},{6,7},{7,6},{8,9},{9,8},{10,11... | collective-permute-start | bytes 147464 | tf_op jit(solution)/shard_map/ppermute | solution.py:28
  131.6 12.7 %all-to-all-start.3 = ((bf16[16,16,768]{2,1,0:T(8,128)(2,1)}), bf16[16,16,768]{2,1,0:T(8,128)(2,1)S(1)}, u32[]{:S(2)}, u32[]{:S(2)}) async-start(bf16[16,16,768]{2,1,0:T(8,128)(2,1)} %broadcast_in_dim.49), calls=%async_computation.3 | async-start | bytes 786432 | tf_op jit(solution)/shard_map/all_to_all | solution.py:32

commit v12 on v11

--- a/solution.py
+++ b/solution.py
@@ -108,10 +108,7 @@
         return jnp.where(first, own, others), jnp.where(first, others, own)
 
     upper = jnp.concatenate([up.T, jnp.zeros((rank, block - out_block), BF)], axis=1)
-    joined = jnp.concatenate(
-        [jnp.broadcast_to(part[None], (n_z,) + part.shape) for part in (attention, down.T, upper)], axis=1
-    )
-    joined = exchange(joined, "z")
+    joined = gather(jnp.concatenate([attention, down.T, upper], axis=0), "z", n_z)
     pieces = around(output_projection)
     draft_weight_other = swap(draft_weight)
     pad = jnp.broadcast_to(gain[None], (16, block))
@@ -152,7 +149,6 @@
     summed = jnp.sum(exchange(pair, CHIPS).astype(F32), axis=0).astype(BF)
     summed = jnp.stack([summed[:, s * cols : (s + 1) * cols] for s in range(n_yh)])
     projected = lax.ppermute(summed[turned], ("z", "yl", "x"), homes)
-    projected, *parts = lax.optimization_barrier((projected, *parts))
 
     hidden = residual_part + jnp.concatenate([projected[j] for j in range(n_yh)], axis=1).astype(F32)
     squares = jnp.sum(hidden * hidden, axis=1, keepdims=True)
@@ -165,7 +161,8 @@
     inv_column = lax.rsqrt((totals[:, :1] + totals[:, 1:2]) / width + EPSILON)
     inv_row = jnp.broadcast_to(inv_column, (mine, 128)).T[:1]
 
-    adapters_all = jnp.stack(parts)[turned].reshape(tenants * rank, block + out_block)
+    _, later = lax.optimization_barrier((message, turned))
+    adapters_all = jnp.stack(parts)[later].reshape(tenants * rank, block + out_block)
     downs, ups = adapters_all[:, :block], adapters_all[:, block:]
 
     def select(values, mask):

time: 185 us -> 201 us (1.086)
  waiting for transfers between devices: 51.7 us -> 63.7 us
  blocking collectives: 35.5 us -> 39 us
    ppermute x1, waiting for transfers between devices: 0.01 us -> 9.71 us  [shards(): projected = lax.ppermute(summed[turned], ('z', 'yl', 'x'), homes)]
    ppermute x6, waiting for transfers between devices: 11.2 us -> 16.9 us  [around(): lax.ppermute(value, 'yh', [(i, (i + s) % n_yh) for i in range(n_yh)])]
    all_to_all x1, blocking collectives: 35.5 us -> 39 us  [exchange(): return lax.all_to_all(value, axis, 0, 0)]
    all_to_all x4, waiting for transfers between devices: 21.9 us -> 18.7 us  [exchange(): return lax.all_to_all(value, axis, 0, 0)]
  transfers between devices with their start and end apart: 17 -> 17, of which waited for: 9 -> 8; matrix products, arithmetic and copies ran while one was open for 6% -> 5% of each run, Pallas kernels for 0% -> 0%
where the time goes in v12:
time: 201 us; the launch traced here: 200 us
  starting transfers between devices  71.5 us (36%)
  waiting for transfers between devices  63.7 us (32%)
  blocking collectives  39 us (19%)
  matrix products  9.36 us (5%)
  local copies, waits for them, and re-layouts  8.72 us (4%)
  Pallas kernels  3.48 us (2%)
  other arithmetic  3.06 us (2%)
    all_to_all x1, blocking collectives, exchange(): return lax.all_to_all(value, axis, 0, 0)  39 us
    ppermute x6, starting transfers between devices, around(): lax.ppermute(value, 'yh', [(i, (i + s) % n_yh) for i in range(n_yh)])  28.3 us
    all_to_all x4, starting transfers between devices, exchange(): return lax.all_to_all(value, axis, 0, 0)  27.8 us
    all_to_all x4, waiting for transfers between devices, exchange(): return lax.all_to_all(value, axis, 0, 0)  18.7 us
    ppermute x6, waiting for transfers between devices, around(): lax.ppermute(value, 'yh', [(i, (i + s) % n_yh) for i in range(n_yh)])  16.9 us
    ppermute x1, waiting for transfers between devices, shards(): chip_rows = lax.ppermute(chip_rows, ('z', 'yl', 'x'), chips)  15.2 us
    ppermute x5, starting transfers between devices, swap(): return lax.ppermute(value, 'c', [(0, 1), (1, 0)])  10.1 us
    ppermute x1, waiting for transfers between devices, shards(): projected = lax.ppermute(summed[turned], ('z', 'yl', 'x'), homes)  9.71 us
  transfers between devices with their start and end apart: 17, of which 8 were waited for; matrix products, arithmetic and copies ran while one was open for 5% of the time, Pallas kernels for 0%

profile of v12, /device:TPU:6, one launch (start us, length us, event | category | flops | bytes accessed | tf_op | source)
XLA Modules:
  0.0 200.3 jit_solution(13964561642926215490)
XLA Ops:
  0.6 1.0 fusion.18
  1.6 1.2 broadcast_in_dim.38
  2.8 10.5 %all-to-all-start = ((bf16[8,160,512]{2,1,0:T(8,128)(2,1)}), bf16[8,160,512]{2,1,0:T(8,128)(2,1)S(1)}, u32[]{:S(2)}, u32[]{:S(2)}) async-start(bf16[8,160,512]{2,1,0:T(8,128)(2,1)} %broadcast_in_dim.38), calls=%async_computation | async-start | bytes 2621440 | tf_op jit(solution)/shard_map/all_to_all | solution.py:32
  13.3 4.5 %collective-permute-start.2 = (bf16[512,256]{1,0:T(8,128)(2,1)S(1)}, bf16[512,256]{1,0:T(8,128)(2,1)S(1)}, u32[]{:S(2)}, u32[]{:S(2)}) collective-permute-start(bf16[512,256]{1,0:T(8,128)(2,1)S(1)} %copy-done), channel_id=1, source_target_pairs={{0,16},{16,32},{32,48},{48,0},{1,17},{17,33},{33,49},{49,1},{2,18}... | collective-permute-start | bytes 786440 | tf_op jit(solution)/shard_map/ppermute | solution.py:104
  17.8 5.9 %collective-permute-start.3 = (bf16[512,256]{1,0:T(8,128)(2,1)S(1)}, bf16[512,256]{1,0:T(8,128)(2,1)S(1)}, u32[]{:S(2)}, u32[]{:S(2)}) collective-permute-start(bf16[512,256]{1,0:T(8,128)(2,1)S(1)} %copy-done), channel_id=1, source_target_pairs={{0,32},{16,48},{32,0},{48,16},{1,33},{17,49},{33,1},{49,17},{2,34}... | collective-permute-start | bytes 786440 | tf_op jit(solution)/shard_map/ppermute | solution.py:104
  23.7 5.3 %collective-permute-start.4 = (bf16[512,256]{1,0:T(8,128)(2,1)S(1)}, bf16[512,256]{1,0:T(8,128)(2,1)S(1)}, u32[]{:S(2)}, u32[]{:S(2)}) collective-permute-start(bf16[512,256]{1,0:T(8,128)(2,1)S(1)} %copy-done), channel_id=1, source_target_pairs={{0,48},{16,0},{32,16},{48,32},{1,49},{17,1},{33,17},{49,33},{2,50}... | collective-permute-start | bytes 786440 | tf_op jit(solution)/shard_map/ppermute | solution.py:104
  29.0 1.9 collective-permute-start
  31.4 0.8 collective-permute-done
  32.3 3.4 %collective-permute-start.1 = (bf16[80,1024]{1,0:T(8,128)(2,1)S(1)}, bf16[80,1024]{1,0:T(8,128)(2,1)S(1)}, u32[]{:S(2)}, u32[]{:S(2)}) collective-permute-start(bf16[80,1024]{1,0:T(8,128)(2,1)S(1)} %pad_maximum_fusion.3), channel_id=1, source_target_pairs={{0,0},{2,14},{4,12},{6,10},{8,8},{10,6},{12,4},{14,2},{64,66},{66,... | collective-permute-start | bytes 491528 | tf_op jit(solution)/shard_map/ppermute | solution.py:122
  35.9 15.2 %collective-permute-done.1 = bf16[80,1024]{1,0:T(8,128)(2,1)S(1)} collective-permute-done((bf16[80,1024]{1,0:T(8,128)(2,1)S(1)}, bf16[80,1024]{1,0:T(8,128)(2,1)S(1)}, u32[]{:S(2)}, u32[]{:S(2)}) %collective-permute-start.1) | collective-permute-done | bytes 163872 | tf_op jit(solution)/shard_map/ppermute | solution.py:122
  51.1 1.3 shard_map.104
  52.3 1.9 collective-permute-start.5
  54.4 2.5 %collective-permute-done.5.refs_4_ = bf16[8,64,1024]{2,1,0:T(8,128)(2,1)S(1)} collective-permute-done((bf16[8,64,1024]{2,1,0:T(8,128)(2,1)S(1)}, bf16[8,64,1024]{2,1,0:T(8,128)(2,1)S(1)}, u32[]{:S(2)}, u32[]{:S(2)}) %collective-permute-start.5) | collective-permute-done | bytes 1048608 | tf_op jit(solution)/shard_map/ppermute | solution.py:28
  56.9 2.2 %shard_map.105 = bf16[8,64,1024]{2,1,0:T(8,128)(2,1)} custom-call(s32[2]{0:T(128)S(1)} %pad_add_fusion.place, bf16[8,160,512]{2,1,0:T(8,128)(2,1)S(1)} %all-to-all-done.joined, bf16[512,256]{1,0:T(8,128)(2,1)S(1)} %copy-done, bf16[512,256]{1,0:T(8,128)(2,1)S(1)} %collective-permute-done.2.refs_1_, bf16[512,256]{1,0:T(8,128)(2,1)S(1)} %collective-permute-done.3.refs_2_, ...), custom_call_target="tpu_custom_call" | custom-call | flops 536870912 | bytes 4194304 | tf_op jit(solution)/shard_map/pallas_call | solution.py:71
  59.1 4.5 %all-to-all-start.1 = ((bf16[8,64,1024]{2,1,0:T(8,128)(2,1)}), bf16[8,64,1024]{2,1,0:T(8,128)(2,1)S(1)}, u32[]{:S(2)}, u32[]{:S(2)}) async-start(bf16[8,64,1024]{2,1,0:T(8,128)(2,1)} %shard_map.105), calls=%async_computation.1 | async-start | bytes 2097152 | tf_op jit(solution)/shard_map/all_to_all | solution.py:32
  63.6 1.9 collective-permute-start.11
  65.6 11.5 %all-to-all-done.1 = bf16[8,64,1024]{2,1,0:T(8,128)(2,1)S(1)} async-done(((bf16[8,64,1024]{2,1,0:T(8,128)(2,1)}), bf16[8,64,1024]{2,1,0:T(8,128)(2,1)S(1)}, u32[]{:S(2)}, u32[]{:S(2)}) %all-to-all-start.1) | async-done | bytes 1048608 | tf_op jit(solution)/shard_map/all_to_all | solution.py:32
  77.1 0.2 reduce_sum.105
  77.4 0.6 gather_fusion
  77.9 1.9 collective-permute-start.9
  79.9 9.7 %collective-permute-done.9 = bf16[4,64,256]{2,1,0:T(8,128)(2,1)S(1)} collective-permute-done((bf16[4,64,256]{2,1,0:T(8,128)(2,1)S(1)}, bf16[4,64,256]{2,1,0:T(8,128)(2,1)S(1)}, u32[]{:S(2)}, u32[]{:S(2)}) %collective-permute-start.9) | collective-permute-done | bytes 131104 | tf_op jit(solution)/shard_map/ppermute | solution.py:151
  89.6 0.2 multiply_reduce_fusion
  89.8 0.1 copy.39
  89.9 0.1 copy.40
  90.1 1.2 broadcast_in_dim.43
  91.3 8.0 %all-to-all-start.2 = ((bf16[8,64,1152]{2,1,0:T(8,128)(2,1)}), bf16[8,64,1152]{2,1,0:T(8,128)(2,1)S(1)}, u32[]{:S(2)}, u32[]{:S(2)}) async-start(bf16[8,64,1152]{2,1,0:T(8,128)(2,1)} %broadcast_in_dim.43), calls=%async_computation.2 | async-start | bytes 2359296 | tf_op jit(solution)/shard_map/all_to_all | solution.py:32
  99.3 2.6 %collective-permute-start.6 = (bf16[128,768]{1,0:T(8,128)(2,1)S(1)}, bf16[128,768]{1,0:T(8,128)(2,1)S(1)}, u32[]{:S(2)}, u32[]{:S(2)}) collective-permute-start(bf16[128,768]{1,0:T(8,128)(2,1)S(1)} %bitcast.102), channel_id=1, source_target_pairs={{0,16},{16,32},{32,48},{48,0},{1,17},{17,33},{33,49},{49,1},{2,18}... | collective-permute-start | bytes 589832 | tf_op jit(solution)/shard_map/ppermute | solution.py:104
  102.0 6.9 %collective-permute-start.7 = (bf16[128,768]{1,0:T(8,128)(2,1)S(1)}, bf16[128,768]{1,0:T(8,128)(2,1)S(1)}, u32[]{:S(2)}, u32[]{:S(2)}) collective-permute-start(bf16[128,768]{1,0:T(8,128)(2,1)S(1)} %bitcast.103), channel_id=1, source_target_pairs={{0,32},{16,48},{32,0},{48,16},{1,33},{17,49},{33,1},{49,17},{2,34}... | collective-permute-start | bytes 589832 | tf_op jit(solution)/shard_map/ppermute | solution.py:104
  108.9 3.1 %collective-permute-start.8 = (bf16[128,768]{1,0:T(8,128)(2,1)S(1)}, bf16[128,768]{1,0:T(8,128)(2,1)S(1)}, u32[]{:S(2)}, u32[]{:S(2)}) collective-permute-start(bf16[128,768]{1,0:T(8,128)(2,1)S(1)} %bitcast.104), channel_id=1, source_target_pairs={{0,48},{16,0},{32,16},{48,32},{1,49},{17,1},{33,17},{49,33},{2,50}... | collective-permute-start | bytes 589832 | tf_op jit(solution)/shard_map/ppermute | solution.py:104
  112.1 14.6 %collective-permute-done.6 = bf16[128,768]{1,0:T(8,128)(2,1)S(1)} collective-permute-done((bf16[128,768]{1,0:T(8,128)(2,1)S(1)}, bf16[128,768]{1,0:T(8,128)(2,1)S(1)}, u32[]{:S(2)}, u32[]{:S(2)}) %collective-permute-start.6) | collective-permute-done | bytes 196640 | tf_op jit(solution)/shard_map/ppermute | solution.py:104
  126.6 2.3 %collective-permute-done.7 = bf16[128,768]{1,0:T(8,128)(2,1)S(1)} collective-permute-done((bf16[128,768]{1,0:T(8,128)(2,1)S(1)}, bf16[128,768]{1,0:T(8,128)(2,1)S(1)}, u32[]{:S(2)}, u32[]{:S(2)}) %collective-permute-start.7) | collective-permute-done | bytes 196640 | tf_op jit(solution)/shard_map/ppermute | solution.py:104
  129.0 0.6 gather_fusion.1
  129.6 0.3 convolution_select_fusion
  130.3 0.2 slice.160
  130.5 0.6 gather_fusion.2
  131.3 1.9 collective-permute-start.10
  133.3 0.3 convolution_select_fusion.2
  133.6 3.0 %fusion.3 = f32[64,256]{1,0:T(8,128)S(1)} fusion(bf16[8,64,1024]{2,1,0:T(8,128)(2,1)S(1)} %gather_fusion.2, bf16[8,1024,256]{2,1,0:T(8,128)(2,1)} %bitcast.95, f32[64]{0:T(128)S(1)} %bitcast.116), kind=kOutput, calls=%fused_computation.16 | convolution fusion | flops 268451840 | bytes 5308672 | tf_op jit(solution)/shard_map/ktd,kdn->tn/dot_general | solution.py:24
  136.6 0.1 copy.46
  136.7 0.1 copy.47
  136.8 0.1 copy.41
  137.0 3.0 %fusion.7 = bf16[64,256]{1,0:T(8,128)(2,1)S(1)} fusion(bf16[8,64,1024]{2,1,0:T(8,128)(2,1)S(1)} %gather_fusion.2, bf16[8,1024,256]{2,1,0:T(8,128)(2,1)} %bitcast.32, s32[]{:T(128)S(6)} %select_n.265, bf16[63,512]{1,0:T(8,128)(2,1)S(1)} %slice.167, bf16[1,512]{1,0:T(2,128)(2,1)S(1)} %slice.168, f32[64]{0:T(128)S(1)} %get-tuple-element.21, f32[64]{0:T(128)S(1)} %bitcast.117), kind=kOutput, calls=%fused_computation.22 | convolution fusion | flops 268566528 | bytes 5341700 | tf_op jit(solution)/shard_map/ktd,kdn->tn/dot_general | solution.py:24
  140.1 2.4 %collective-permute-start.12 = (bf16[64,384]{1,0:T(8,128)(2,1)S(1)}, bf16[64,384]{1,0:T(8,128)(2,1)S(1)}, u32[]{:S(2)}, u32[]{:S(2)}) collective-permute-start(bf16[64,384]{1,0:T(8,128)(2,1)S(1)} %pad_maximum_fusion.9), channel_id=1, source_target_pairs={{0,1},{1,0},{2,3},{3,2},{4,5},{5,4},{6,7},{7,6},{8,9},{9,8},{10,11... | collective-permute-start | bytes 147464 | tf_op jit(solution)/shard_map/ppermute | solution.py:28
  142.5 0.3 convolution_select_fusion.1
  142.8 0.1 copy.44
  143.0 0.2 convolution_select_fusion.4
  143.2 0.1 copy.45
  143.4 0.2 convolution_select_fusion.3
  143.6 0.1 copy.48
  143.9 0.8 broadcast_in_dim.47
  144.7 4.8 %all-to-all-start.3 = ((bf16[16,16,768]{2,1,0:T(8,128)(2,1)}), bf16[16,16,768]{2,1,0:T(8,128)(2,1)S(1)}, u32[]{:S(2)}, u32[]{:S(2)}) async-start(bf16[16,16,768]{2,1,0:T(8,128)(2,1)} %broadcast_in_dim.47), calls=%async_computation.3 | async-start | bytes 786432 | tf_op jit(solution)/shard_map/all_to_all | solution.py:32
  149.5 0.2 add_reduce_fusion
  149.7 7.1 %all-to-all-done.3 = bf16[16,16,768]{2,1,0:T(8,128)(2,1)S(1)} async-done(((bf16[16,16,768]{2,1,0:T(8,128)(2,1)}), bf16[16,16,768]{2,1,0:T(8,128)(2,1)S(1)}, u32[]{:S(2)}, u32[]{:S(2)}) %all-to-all-start.3) | async-done | bytes 393248 | tf_op jit(solution)/shard_map/all_to_all | solution.py:32
  157.1 0.1 fusion.13
  157.5 0.1 fusion.14
  157.7 0.5 fusion.42
  158.3 0.5 fusion.1
  158.8 0.3 fusion.28
  159.1 0.4 fusion
  159.6 0.3 copy.53
  159.9 39.0 %all_to_all.25 = bf16[32,16,768]{2,1,0:T(8,128)(2,1)S(1)} all-to-all(bf16[32,16,768]{2,1,0:T(8,128)(2,1)S(1)} %bitcast.96), channel_id=1, replica_groups=mesh['z'=8,'yh'=4,'yl'=2,'x'=4,'c'=2] {'yh','z'}, dimensions={0} | all-to-all | bytes 1572864 | tf_op jit(solution)/shard_map/all_to_all | solution.py:32
  198.9 0.1 convert_reduce_fusion
  199.1 0.6 slice_bitcast_fusion
  199.7 0.6 slice_bitcast_fusion.9
  (87 shorter events, 2.8 us)
Async XLA Ops:
  2.8 10.5 %copy-start = (bf16[512,256]{1,0:T(8,128)(2,1)S(1)}, bf16[512,256]{1,0:T(8,128)(2,1)}, u32[]{:S(2)}) copy-start(bf16[512,256]{1,0:T(8,128)(2,1)} %refs_0_.3) | copy-start | bytes 786436
  2.8 26.2 %copy-start.1 = (bf16[128,512]{1,0:T(8,128)(2,1)S(1)}, bf16[128,512]{1,0:T(8,128)(2,1)}, u32[]{:S(2)}) copy-start(bf16[128,512]{1,0:T(8,128)(2,1)} %param.11) | copy-start | bytes 393220
  2.8 26.2 %copy-start.3 = (bf16[512]{0:T(512)(128)(2,1)S(1)}, bf16[512]{0:T(512)(128)(2,1)}, u32[]{:S(2)}) copy-start(bf16[512]{0:T(512)(128)(2,1)} %param.12) | copy-start | bytes 3076
  2.8 28.2 %copy-start.4 = (s32[32]{0:T(128)S(1)}, s32[32]{0:T(128)}, u32[]{:S(2)}) copy-start(s32[32]{0:T(128)} %param.17) | copy-start | bytes 388
  2.8 28.2 %copy-start.2 = (s32[128]{0:T(128)S(1)}, s32[128]{0:T(128)}, u32[]{:S(2)}) copy-start(s32[128]{0:T(128)} %param.16) | copy-start | bytes 1540
  2.8 48.3 %all-to-all-start = ((bf16[8,160,512]{2,1,0:T(8,128)(2,1)}), bf16[8,160,512]{2,1,0:T(8,128)(2,1)S(1)}, u32[]{:S(2)}, u32[]{:S(2)}) async-start(bf16[8,160,512]{2,1,0:T(8,128)(2,1)} %broadcast_in_dim.38), calls=%async_computation | async-start | bytes 2621440 | tf_op jit(solution)/shard_map/all_to_all | solution.py:32
  13.3 37.8 %collective-permute-start.2 = (bf16[512,256]{1,0:T(8,128)(2,1)S(1)}, bf16[512,256]{1,0:T(8,128)(2,1)S(1)}, u32[]{:S(2)}, u32[]{:S(2)}) collective-permute-start(bf16[512,256]{1,0:T(8,128)(2,1)S(1)} %copy-done), channel_id=1, source_target_pairs={{0,16},{16,32},{32,48},{48,0},{1,17},{17,33},{33,49},{49,1},{2,18}... | collective-permute-start | bytes 786440 | tf_op jit(solution)/shard_map/ppermute | solution.py:104
  17.8 33.3 %collective-permute-start.3 = (bf16[512,256]{1,0:T(8,128)(2,1)S(1)}, bf16[512,256]{1,0:T(8,128)(2,1)S(1)}, u32[]{:S(2)}, u32[]{:S(2)}) collective-permute-start(bf16[512,256]{1,0:T(8,128)(2,1)S(1)} %copy-done), channel_id=1, source_target_pairs={{0,32},{16,48},{32,0},{48,16},{1,33},{17,49},{33,1},{49,17},{2,34}... | collective-permute-start | bytes 786440 | tf_op jit(solution)/shard_map/ppermute | solution.py:104
  23.7 27.4 %collective-permute-start.4 = (bf16[512,256]{1,0:T(8,128)(2,1)S(1)}, bf16[512,256]{1,0:T(8,128)(2,1)S(1)}, u32[]{:S(2)}, u32[]{:S(2)}) collective-permute-start(bf16[512,256]{1,0:T(8,128)(2,1)S(1)} %copy-done), channel_id=1, source_target_pairs={{0,48},{16,0},{32,16},{48,32},{1,49},{17,1},{33,17},{49,33},{2,50}... | collective-permute-start | bytes 786440 | tf_op jit(solution)/shard_map/ppermute | solution.py:104
  29.0 3.2 %collective-permute-start = (bf16[80,512]{1,0:T(8,128)(2,1)S(1)}, bf16[80,512]{1,0:T(8,128)(2,1)S(1)}, u32[]{:S(2)}, u32[]{:S(2)}) collective-permute-start(bf16[80,512]{1,0:T(8,128)(2,1)S(1)} %pad_maximum_fusion.6), channel_id=1, source_target_pairs={{0,1},{1,0},{2,3},{3,2},{4,5},{5,4},{6,7},{7,6},{8,9},{9,8},{10,11... | collective-permute-start | bytes 245768 | tf_op jit(solution)/shard_map/ppermute | solution.py:28
  32.3 18.8 %collective-permute-start.1 = (bf16[80,1024]{1,0:T(8,128)(2,1)S(1)}, bf16[80,1024]{1,0:T(8,128)(2,1)S(1)}, u32[]{:S(2)}, u32[]{:S(2)}) collective-permute-start(bf16[80,1024]{1,0:T(8,128)(2,1)S(1)} %pad_maximum_fusion.3), channel_id=1, source_target_pairs={{0,0},{2,14},{4,12},{6,10},{8,8},{10,6},{12,4},{14,2},{64,66},{66,... | collective-permute-start | bytes 491528 | tf_op jit(solution)/shard_map/ppermute | solution.py:122
  52.3 4.6 %collective-permute-start.5 = (bf16[8,64,1024]{2,1,0:T(8,128)(2,1)S(1)}, bf16[8,64,1024]{2,1,0:T(8,128)(2,1)S(1)}, u32[]{:S(2)}, u32[]{:S(2)}) collective-permute-start(bf16[8,64,1024]{2,1,0:T(8,128)(2,1)S(1)} %shard_map.104), channel_id=1, source_target_pairs={{0,1},{1,0},{2,3},{3,2},{4,5},{5,4},{6,7},{7,6},{8,9},{9,8},{10,11... | collective-permute-start | bytes 3145736 | tf_op jit(solution)/shard_map/ppermute | solution.py:28
  59.1 18.0 %all-to-all-start.1 = ((bf16[8,64,1024]{2,1,0:T(8,128)(2,1)}), bf16[8,64,1024]{2,1,0:T(8,128)(2,1)S(1)}, u32[]{:S(2)}, u32[]{:S(2)}) async-start(bf16[8,64,1024]{2,1,0:T(8,128)(2,1)} %shard_map.105), calls=%async_computation.1 | async-start | bytes 2097152 | tf_op jit(solution)/shard_map/all_to_all | solution.py:32
  63.6 73.4 %collective-permute-start.11 = (bf16[8192,256]{1,0:T(8,128)(2,1)}, bf16[8192,256]{1,0:T(8,128)(2,1)}, u32[]{:S(2)}, u32[]{:S(2)}) collective-permute-start(bf16[8192,256]{1,0:T(8,128)(2,1)} %param.13), channel_id=1, source_target_pairs={{0,1},{1,0},{2,3},{3,2},{4,5},{5,4},{6,7},{7,6},{8,9},{9,8},{10,11... | collective-permute-start | bytes 12582920 | tf_op jit(solution)/shard_map/ppermute | solution.py:28
  77.9 11.7 %collective-permute-start.9 = (bf16[4,64,256]{2,1,0:T(8,128)(2,1)S(1)}, bf16[4,64,256]{2,1,0:T(8,128)(2,1)S(1)}, u32[]{:S(2)}, u32[]{:S(2)}) collective-permute-start(bf16[4,64,256]{2,1,0:T(8,128)(2,1)S(1)} %gather_fusion), channel_id=1, source_target_pairs={{0,0},{2,66},{4,132},{6,198},{8,264},{10,330},{12,396},{14,462},{6... | collective-permute-start | bytes 393224 | tf_op jit(solution)/shard_map/ppermute | solution.py:151
  91.3 38.8 %all-to-all-start.2 = ((bf16[8,64,1152]{2,1,0:T(8,128)(2,1)}), bf16[8,64,1152]{2,1,0:T(8,128)(2,1)S(1)}, u32[]{:S(2)}, u32[]{:S(2)}) async-start(bf16[8,64,1152]{2,1,0:T(8,128)(2,1)} %broadcast_in_dim.43), calls=%async_computation.2 | async-start | bytes 2359296 | tf_op jit(solution)/shard_map/all_to_all | solution.py:32
  99.3 27.3 %collective-permute-start.6 = (bf16[128,768]{1,0:T(8,128)(2,1)S(1)}, bf16[128,768]{1,0:T(8,128)(2,1)S(1)}, u32[]{:S(2)}, u32[]{:S(2)}) collective-permute-start(bf16[128,768]{1,0:T(8,128)(2,1)S(1)} %bitcast.102), channel_id=1, source_target_pairs={{0,16},{16,32},{32,48},{48,0},{1,17},{17,33},{33,49},{49,1},{2,18}... | collective-permute-start | bytes 589832 | tf_op jit(solution)/shard_map/ppermute | solution.py:104
  102.0 26.9 %collective-permute-start.7 = (bf16[128,768]{1,0:T(8,128)(2,1)S(1)}, bf16[128,768]{1,0:T(8,128)(2,1)S(1)}, u32[]{:S(2)}, u32[]{:S(2)}) collective-permute-start(bf16[128,768]{1,0:T(8,128)(2,1)S(1)} %bitcast.103), channel_id=1, source_target_pairs={{0,32},{16,48},{32,0},{48,16},{1,33},{17,49},{33,1},{49,17},{2,34}... | collective-permute-start | bytes 589832 | tf_op jit(solution)/shard_map/ppermute | solution.py:104
  108.9 20.0 %collective-permute-start.8 = (bf16[128,768]{1,0:T(8,128)(2,1)S(1)}, bf16[128,768]{1,0:T(8,128)(2,1)S(1)}, u32[]{:S(2)}, u32[]{:S(2)}) collective-permute-start(bf16[128,768]{1,0:T(8,128)(2,1)S(1)} %bitcast.104), channel_id=1, source_target_pairs={{0,48},{16,0},{32,16},{48,32},{1,49},{17,1},{33,17},{49,33},{2,50}... | collective-permute-start | bytes 589832 | tf_op jit(solution)/shard_map/ppermute | solution.py:104
  131.3 5.7 %collective-permute-start.10 = (bf16[80,512]{1,0:T(8,128)(2,1)S(1)}, bf16[80,512]{1,0:T(8,128)(2,1)S(1)}, u32[]{:S(2)}, u32[]{:S(2)}) collective-permute-start(bf16[80,512]{1,0:T(8,128)(2,1)S(1)} %pad_maximum_fusion.8), channel_id=1, source_target_pairs={{0,1},{1,0},{2,3},{3,2},{4,5},{5,4},{6,7},{7,6},{8,9},{9,8},{10,11... | collective-permute-start | bytes 245768 | tf_op jit(solution)/shard_map/ppermute | solution.py:28
  140.1 3.3 %collective-permute-start.12 = (bf16[64,384]{1,0:T(8,128)(2,1)S(1)}, bf16[64,384]{1,0:T(8,128)(2,1)S(1)}, u32[]{:S(2)}, u32[]{:S(2)}) collective-permute-start(bf16[64,384]{1,0:T(8,128)(2,1)S(1)} %pad_maximum_fusion.9), channel_id=1, source_target_pairs={{0,1},{1,0},{2,3},{3,2},{4,5},{5,4},{6,7},{7,6},{8,9},{9,8},{10,11... | collective-permute-start | bytes 147464 | tf_op jit(solution)/shard_map/ppermute | solution.py:28
  144.7 12.1 %all-to-all-start.3 = ((bf16[16,16,768]{2,1,0:T(8,128)(2,1)}), bf16[16,16,768]{2,1,0:T(8,128)(2,1)S(1)}, u32[]{:S(2)}, u32[]{:S(2)}) async-start(bf16[16,16,768]{2,1,0:T(8,128)(2,1)} %broadcast_in_dim.47), calls=%async_computation.3 | async-start | bytes 786432 | tf_op jit(solution)/shard_map/all_to_all | solution.py:32

commit v13 on v12

--- a/solution.py
+++ b/solution.py
@@ -99,17 +99,15 @@
     yh = lax.axis_index("yh")
     turned = (yh - jnp.arange(n_yh, dtype=jnp.int32)) % n_yh
 
-    def around(value):
-        return [value] + [
-            lax.ppermute(value, "yh", [(i, (i + s) % n_yh) for i in range(n_yh)]) for s in range(1, n_yh)
-        ]
+    def shift(value, step):
+        return lax.ppermute(value, "yh", [(i, (i + step) % n_yh) for i in range(n_yh)])
 
     def ordered(own, others):
         return jnp.where(first, own, others), jnp.where(first, others, own)
 
     upper = jnp.concatenate([up.T, jnp.zeros((rank, block - out_block), BF)], axis=1)
     joined = gather(jnp.concatenate([attention, down.T, upper], axis=0), "z", n_z)
-    pieces = around(output_projection)
+    pieces = [output_projection] + [shift(output_projection, step) for step in range(1, n_yh)]
     draft_weight_other = swap(draft_weight)
     pad = jnp.broadcast_to(gain[None], (16, block))
     kept = swap(jnp.concatenate([half(residual, other, mine), pad], axis=0))
@@ -144,11 +142,16 @@
         [joined[:, tokens : tokens + rank], joined[:, tokens + rank :, :out_block]], axis=2
     ).reshape(n_z * rank, block + out_block)
     pair, adapters = lax.optimization_barrier((pair, adapters))
-    parts = around(adapters)
+    before, after = shift(adapters, 1), shift(adapters, -1)
 
     summed = jnp.sum(exchange(pair, CHIPS).astype(F32), axis=0).astype(BF)
     summed = jnp.stack([summed[:, s * cols : (s + 1) * cols] for s in range(n_yh)])
     projected = lax.ppermute(summed[turned], ("z", "yl", "x"), homes)
+
+    projected, before, after = lax.optimization_barrier((projected, before, after))
+    some = n_z * rank // 2
+    far = jnp.concatenate([shift(before[:some], 1), shift(after[some:], -1)], axis=0)
+    parts = [adapters, before, far, after]
 
     hidden = residual_part + jnp.concatenate([projected[j] for j in range(n_yh)], axis=1).astype(F32)
     squares = jnp.sum(hidden * hidden, axis=1, keepdims=True)

time: 201 us -> 193 us (0.960)
  waiting for transfers between devices: 63.7 us -> 55.5 us
    ppermute x6 -> x7, waiting for transfers between devices: 16.9 us -> 12.7 us  [shift(): lax.ppermute(value, 'yh', [(i, (i + step) % n_yh) for i in range(n_yh)])]
    all_to_all x4, starting transfers between devices: 27.8 us -> 24.3 us  [exchange(): return lax.all_to_all(value, axis, 0, 0)]
    all_to_all x4, waiting for transfers between devices: 18.7 us -> 15.9 us  [exchange(): return lax.all_to_all(value, axis, 0, 0)]
    ppermute x6 -> x7, starting transfers between devices: 28.3 us -> 30.9 us  [shift(): lax.ppermute(value, 'yh', [(i, (i + step) % n_yh) for i in range(n_yh)])]
  transfers between devices with their start and end apart: 17 -> 18, of which waited for: 8 -> 9; matrix products, arithmetic and copies ran while one was open for 5% -> 5% of each run, Pallas kernels for 0% -> 0%
where the time goes in v13:
time: 193 us; the launch traced here: 192 us
  starting transfers between devices  70.6 us (37%)
  waiting for transfers between devices  55.5 us (29%)
  blocking collectives  40.1 us (21%)
  matrix products  9.35 us (5%)
  local copies, waits for them, and re-layouts  8.76 us (5%)
  Pallas kernels  3.47 us (2%)
  other arithmetic  3.08 us (2%)
    all_to_all x1, blocking collectives, exchange(): return lax.all_to_all(value, axis, 0, 0)  40.1 us
    ppermute x7, starting transfers between devices, shift(): lax.ppermute(value, 'yh', [(i, (i + step) % n_yh) for i in range(n_yh)])  30.9 us
    all_to_all x4, starting transfers between devices, exchange(): return lax.all_to_all(value, axis, 0, 0)  24.3 us
    all_to_all x4, waiting for transfers between devices, exchange(): return lax.all_to_all(value, axis, 0, 0)  15.9 us
    ppermute x1, waiting for transfers between devices, shards(): chip_rows = lax.ppermute(chip_rows, ('z', 'yl', 'x'), chips)  15.2 us
    ppermute x7, waiting for transfers between devices, shift(): lax.ppermute(value, 'yh', [(i, (i + step) % n_yh) for i in range(n_yh)])  12.7 us
    ppermute x5, starting transfers between devices, swap(): return lax.ppermute(value, 'c', [(0, 1), (1, 0)])  10.1 us
    dot_general x13, matrix products, dot(): return jnp.einsum(subscripts, left, right, preferred_element_type=F32)  9.35 us
  transfers between devices with their start and end apart: 18, of which 9 were waited for; matrix products, arithmetic and copies ran while one was open for 5% of the time, Pallas kernels for 0%

profile of v13, /device:TPU:6, one launch (start us, length us, event | category | flops | bytes accessed | tf_op | source)
XLA Modules:
  0.0 192.2 jit_solution(18044666881095208925)
XLA Ops:
  0.6 1.0 fusion.18
  1.6 1.2 broadcast_in_dim.38
  2.8 10.5 %all-to-all-start = ((bf16[8,160,512]{2,1,0:T(8,128)(2,1)}), bf16[8,160,512]{2,1,0:T(8,128)(2,1)S(1)}, u32[]{:S(2)}, u32[]{:S(2)}) async-start(bf16[8,160,512]{2,1,0:T(8,128)(2,1)} %broadcast_in_dim.38), calls=%async_computation | async-start | bytes 2621440 | tf_op jit(solution)/shard_map/all_to_all | solution.py:32
  13.3 4.5 %collective-permute-start.2 = (bf16[512,256]{1,0:T(8,128)(2,1)S(1)}, bf16[512,256]{1,0:T(8,128)(2,1)S(1)}, u32[]{:S(2)}, u32[]{:S(2)}) collective-permute-start(bf16[512,256]{1,0:T(8,128)(2,1)S(1)} %copy-done), channel_id=1, source_target_pairs={{0,16},{16,32},{32,48},{48,0},{1,17},{17,33},{33,49},{49,1},{2,18}... | collective-permute-start | bytes 786440 | tf_op jit(solution)/shard_map/ppermute | solution.py:103
  17.8 5.9 %collective-permute-start.3 = (bf16[512,256]{1,0:T(8,128)(2,1)S(1)}, bf16[512,256]{1,0:T(8,128)(2,1)S(1)}, u32[]{:S(2)}, u32[]{:S(2)}) collective-permute-start(bf16[512,256]{1,0:T(8,128)(2,1)S(1)} %copy-done), channel_id=1, source_target_pairs={{0,32},{16,48},{32,0},{48,16},{1,33},{17,49},{33,1},{49,17},{2,34}... | collective-permute-start | bytes 786440 | tf_op jit(solution)/shard_map/ppermute | solution.py:103
  23.7 5.3 %collective-permute-start.4 = (bf16[512,256]{1,0:T(8,128)(2,1)S(1)}, bf16[512,256]{1,0:T(8,128)(2,1)S(1)}, u32[]{:S(2)}, u32[]{:S(2)}) collective-permute-start(bf16[512,256]{1,0:T(8,128)(2,1)S(1)} %copy-done), channel_id=1, source_target_pairs={{0,48},{16,0},{32,16},{48,32},{1,49},{17,1},{33,17},{49,33},{2,50}... | collective-permute-start | bytes 786440 | tf_op jit(solution)/shard_map/ppermute | solution.py:103
  29.0 1.9 collective-permute-start
  31.4 0.8 collective-permute-done
  32.3 3.4 %collective-permute-start.1 = (bf16[80,1024]{1,0:T(8,128)(2,1)S(1)}, bf16[80,1024]{1,0:T(8,128)(2,1)S(1)}, u32[]{:S(2)}, u32[]{:S(2)}) collective-permute-start(bf16[80,1024]{1,0:T(8,128)(2,1)S(1)} %pad_maximum_fusion.3), channel_id=1, source_target_pairs={{0,0},{2,14},{4,12},{6,10},{8,8},{10,6},{12,4},{14,2},{64,66},{66,... | collective-permute-start | bytes 491528 | tf_op jit(solution)/shard_map/ppermute | solution.py:120
  35.9 15.2 %collective-permute-done.1 = bf16[80,1024]{1,0:T(8,128)(2,1)S(1)} collective-permute-done((bf16[80,1024]{1,0:T(8,128)(2,1)S(1)}, bf16[80,1024]{1,0:T(8,128)(2,1)S(1)}, u32[]{:S(2)}, u32[]{:S(2)}) %collective-permute-start.1) | collective-permute-done | bytes 163872 | tf_op jit(solution)/shard_map/ppermute | solution.py:120
  51.1 1.3 shard_map.104
  52.4 1.9 collective-permute-start.5
  54.4 2.5 %collective-permute-done.5.refs_4_ = bf16[8,64,1024]{2,1,0:T(8,128)(2,1)S(1)} collective-permute-done((bf16[8,64,1024]{2,1,0:T(8,128)(2,1)S(1)}, bf16[8,64,1024]{2,1,0:T(8,128)(2,1)S(1)}, u32[]{:S(2)}, u32[]{:S(2)}) %collective-permute-start.5) | collective-permute-done | bytes 1048608 | tf_op jit(solution)/shard_map/ppermute | solution.py:28
  56.9 2.2 %shard_map.105 = bf16[8,64,1024]{2,1,0:T(8,128)(2,1)} custom-call(s32[2]{0:T(128)S(1)} %pad_add_fusion.place, bf16[8,160,512]{2,1,0:T(8,128)(2,1)S(1)} %all-to-all-done.joined, bf16[512,256]{1,0:T(8,128)(2,1)S(1)} %copy-done, bf16[512,256]{1,0:T(8,128)(2,1)S(1)} %collective-permute-done.2.refs_1_, bf16[512,256]{1,0:T(8,128)(2,1)S(1)} %collective-permute-done.3.refs_2_, ...), custom_call_target="tpu_custom_call" | custom-call | flops 536870912 | bytes 4194304 | tf_op jit(solution)/shard_map/pallas_call | solution.py:71
  59.1 4.6 %all-to-all-start.1 = ((bf16[8,64,1024]{2,1,0:T(8,128)(2,1)}), bf16[8,64,1024]{2,1,0:T(8,128)(2,1)S(1)}, u32[]{:S(2)}, u32[]{:S(2)}) async-start(bf16[8,64,1024]{2,1,0:T(8,128)(2,1)} %shard_map.105), calls=%async_computation.1 | async-start | bytes 2097152 | tf_op jit(solution)/shard_map/all_to_all | solution.py:32
  63.8 1.9 collective-permute-start.12
  65.7 2.6 %collective-permute-start.7 = (bf16[128,768]{1,0:T(8,128)(2,1)S(1)}, bf16[128,768]{1,0:T(8,128)(2,1)S(1)}, u32[]{:S(2)}, u32[]{:S(2)}) collective-permute-start(bf16[128,768]{1,0:T(8,128)(2,1)S(1)} %bitcast.103), channel_id=1, source_target_pairs={{0,16},{16,32},{32,48},{48,0},{1,17},{17,33},{33,49},{49,1},{2,18}... | collective-permute-start | bytes 589832 | tf_op jit(solution)/shard_map/ppermute | solution.py:103
  68.4 5.3 %collective-permute-start.8 = (bf16[128,768]{1,0:T(8,128)(2,1)S(1)}, bf16[128,768]{1,0:T(8,128)(2,1)S(1)}, u32[]{:S(2)}, u32[]{:S(2)}) collective-permute-start(bf16[128,768]{1,0:T(8,128)(2,1)S(1)} %bitcast.104), channel_id=1, source_target_pairs={{0,48},{16,0},{32,16},{48,32},{1,49},{17,1},{33,17},{49,33},{2,50}... | collective-permute-start | bytes 589832 | tf_op jit(solution)/shard_map/ppermute | solution.py:103
  73.7 8.7 %all-to-all-done.1 = bf16[8,64,1024]{2,1,0:T(8,128)(2,1)S(1)} async-done(((bf16[8,64,1024]{2,1,0:T(8,128)(2,1)}), bf16[8,64,1024]{2,1,0:T(8,128)(2,1)S(1)}, u32[]{:S(2)}, u32[]{:S(2)}) %all-to-all-start.1) | async-done | bytes 1048608 | tf_op jit(solution)/shard_map/all_to_all | solution.py:32
  82.4 0.2 reduce_sum.105
  82.7 0.6 gather_fusion
  83.2 1.9 collective-permute-start.6
  85.2 2.3 %collective-permute-done.7 = bf16[128,768]{1,0:T(8,128)(2,1)S(1)} collective-permute-done((bf16[128,768]{1,0:T(8,128)(2,1)S(1)}, bf16[128,768]{1,0:T(8,128)(2,1)S(1)}, u32[]{:S(2)}, u32[]{:S(2)}) %collective-permute-start.7) | collective-permute-done | bytes 196640 | tf_op jit(solution)/shard_map/ppermute | solution.py:103
  87.5 8.4 %collective-permute-done.6 = bf16[4,64,256]{2,1,0:T(8,128)(2,1)S(1)} collective-permute-done((bf16[4,64,256]{2,1,0:T(8,128)(2,1)S(1)}, bf16[4,64,256]{2,1,0:T(8,128)(2,1)S(1)}, u32[]{:S(2)}, u32[]{:S(2)}) %collective-permute-start.6) | collective-permute-done | bytes 131104 | tf_op jit(solution)/shard_map/ppermute | solution.py:149
  95.9 0.2 multiply_reduce_fusion
  96.0 0.1 copy.39
  96.2 0.1 copy.40
  96.4 1.2 broadcast_in_dim.43
  97.6 4.5 %all-to-all-start.2 = ((bf16[8,64,1152]{2,1,0:T(8,128)(2,1)}), bf16[8,64,1152]{2,1,0:T(8,128)(2,1)S(1)}, u32[]{:S(2)}, u32[]{:S(2)}) async-start(bf16[8,64,1152]{2,1,0:T(8,128)(2,1)} %broadcast_in_dim.43), calls=%async_computation.2 | async-start | bytes 2359296 | tf_op jit(solution)/shard_map/all_to_all | solution.py:32
  102.2 5.3 %collective-permute-start.10 = (bf16[64,768]{1,0:T(8,128)(2,1)S(1)}, bf16[64,768]{1,0:T(8,128)(2,1)S(1)}, u32[]{:S(2)}, u32[]{:S(2)}) collective-permute-start(bf16[64,768]{1,0:T(8,128)(2,1)S(1)} %slice.125), channel_id=1, source_target_pairs={{0,48},{16,0},{32,16},{48,32},{1,49},{17,1},{33,17},{49,33},{2,50}... | collective-permute-start | bytes 294920 | tf_op jit(solution)/shard_map/ppermute | solution.py:103
  107.6 1.9 collective-permute-start.9
  109.5 0.9 collective-permute-done.10
  110.4 9.6 %collective-permute-done.9 = bf16[64,768]{1,0:T(8,128)(2,1)S(1)} collective-permute-done((bf16[64,768]{1,0:T(8,128)(2,1)S(1)}, bf16[64,768]{1,0:T(8,128)(2,1)S(1)}, u32[]{:S(2)}, u32[]{:S(2)}) %collective-permute-start.9) | collective-permute-done | bytes 98336 | tf_op jit(solution)/shard_map/ppermute | solution.py:103
  120.1 0.6 gather_fusion.1
  120.7 0.3 convolution_select_fusion
  121.3 0.2 slice.164
  121.5 0.6 gather_fusion.2
  122.4 1.9 collective-permute-start.11
  124.3 0.3 convolution_select_fusion.2
  124.6 3.0 %fusion.3 = f32[64,256]{1,0:T(8,128)S(1)} fusion(bf16[8,64,1024]{2,1,0:T(8,128)(2,1)S(1)} %gather_fusion.2, bf16[8,1024,256]{2,1,0:T(8,128)(2,1)} %bitcast.96, f32[64]{0:T(128)S(1)} %bitcast.115), kind=kOutput, calls=%fused_computation.16 | convolution fusion | flops 268451840 | bytes 5308672 | tf_op jit(solution)/shard_map/ktd,kdn->tn/dot_general | solution.py:24
  127.8 0.1 copy.41
  128.1 3.0 %fusion.7 = bf16[64,256]{1,0:T(8,128)(2,1)S(1)} fusion(bf16[8,64,1024]{2,1,0:T(8,128)(2,1)S(1)} %gather_fusion.2, bf16[8,1024,256]{2,1,0:T(8,128)(2,1)} %bitcast.32, s32[]{:T(128)S(6)} %select_n.265, bf16[63,512]{1,0:T(8,128)(2,1)S(1)} %slice.171, bf16[1,512]{1,0:T(2,128)(2,1)S(1)} %slice.172, f32[64]{0:T(128)S(1)} %get-tuple-element.27, f32[64]{0:T(128)S(1)} %bitcast.116), kind=kOutput, calls=%fused_computation.22 | convolution fusion | flops 268566528 | bytes 5341700 | tf_op jit(solution)/shard_map/ktd,kdn->tn/dot_general | solution.py:24
  131.2 2.4 %collective-permute-start.13 = (bf16[64,384]{1,0:T(8,128)(2,1)S(1)}, bf16[64,384]{1,0:T(8,128)(2,1)S(1)}, u32[]{:S(2)}, u32[]{:S(2)}) collective-permute-start(bf16[64,384]{1,0:T(8,128)(2,1)S(1)} %pad_maximum_fusion.9), channel_id=1, source_target_pairs={{0,1},{1,0},{2,3},{3,2},{4,5},{5,4},{6,7},{7,6},{8,9},{9,8},{10,11... | collective-permute-start | bytes 147464 | tf_op jit(solution)/shard_map/ppermute | solution.py:28
  133.6 0.3 convolution_select_fusion.1
  133.9 0.1 copy.44
  134.0 0.2 convolution_select_fusion.4
  134.3 0.1 copy.45
  134.5 0.2 convolution_select_fusion.3
  134.7 0.1 copy.48
  134.9 0.8 broadcast_in_dim.47
  135.7 4.7 %all-to-all-start.3 = ((bf16[16,16,768]{2,1,0:T(8,128)(2,1)}), bf16[16,16,768]{2,1,0:T(8,128)(2,1)S(1)}, u32[]{:S(2)}, u32[]{:S(2)}) async-start(bf16[16,16,768]{2,1,0:T(8,128)(2,1)} %broadcast_in_dim.47), calls=%async_computation.3 | async-start | bytes 786432 | tf_op jit(solution)/shard_map/all_to_all | solution.py:32
  140.4 0.2 add_reduce_fusion
  140.6 7.1 %all-to-all-done.3 = bf16[16,16,768]{2,1,0:T(8,128)(2,1)S(1)} async-done(((bf16[16,16,768]{2,1,0:T(8,128)(2,1)}), bf16[16,16,768]{2,1,0:T(8,128)(2,1)S(1)}, u32[]{:S(2)}, u32[]{:S(2)}) %all-to-all-start.3) | async-done | bytes 393248 | tf_op jit(solution)/shard_map/all_to_all | solution.py:32
  147.9 0.1 fusion.13
  148.3 0.1 fusion.14
  148.6 0.5 fusion.42
  149.1 0.5 fusion.1
  149.6 0.3 fusion.28
  150.0 0.4 fusion
  150.5 0.3 copy.53
  150.8 40.1 %all_to_all.25 = bf16[32,16,768]{2,1,0:T(8,128)(2,1)S(1)} all-to-all(bf16[32,16,768]{2,1,0:T(8,128)(2,1)S(1)} %bitcast.97), channel_id=1, replica_groups=mesh['z'=8,'yh'=4,'yl'=2,'x'=4,'c'=2] {'yh','z'}, dimensions={0} | all-to-all | bytes 1572864 | tf_op jit(solution)/shard_map/all_to_all | solution.py:32
  190.9 0.1 convert_reduce_fusion
  191.0 0.6 slice_bitcast_fusion
  191.6 0.6 slice_bitcast_fusion.9
  (96 shorter events, 3.0 us)
Async XLA Ops:
  2.8 10.5 %copy-start = (bf16[512,256]{1,0:T(8,128)(2,1)S(1)}, bf16[512,256]{1,0:T(8,128)(2,1)}, u32[]{:S(2)}) copy-start(bf16[512,256]{1,0:T(8,128)(2,1)} %refs_0_.3) | copy-start | bytes 786436
  2.8 26.2 %copy-start.1 = (bf16[128,512]{1,0:T(8,128)(2,1)S(1)}, bf16[128,512]{1,0:T(8,128)(2,1)}, u32[]{:S(2)}) copy-start(bf16[128,512]{1,0:T(8,128)(2,1)} %param.11) | copy-start | bytes 393220
  2.8 26.2 %copy-start.5 = (bf16[512]{0:T(512)(128)(2,1)S(1)}, bf16[512]{0:T(512)(128)(2,1)}, u32[]{:S(2)}) copy-start(bf16[512]{0:T(512)(128)(2,1)} %param.12) | copy-start | bytes 3076
  2.8 28.2 %copy-start.6 = (s32[32]{0:T(128)S(1)}, s32[32]{0:T(128)}, u32[]{:S(2)}) copy-start(s32[32]{0:T(128)} %param.17) | copy-start | bytes 388
  2.8 28.2 %copy-start.4 = (s32[128]{0:T(128)S(1)}, s32[128]{0:T(128)}, u32[]{:S(2)}) copy-start(s32[128]{0:T(128)} %param.16) | copy-start | bytes 1540
  2.8 48.3 %all-to-all-start = ((bf16[8,160,512]{2,1,0:T(8,128)(2,1)}), bf16[8,160,512]{2,1,0:T(8,128)(2,1)S(1)}, u32[]{:S(2)}, u32[]{:S(2)}) async-start(bf16[8,160,512]{2,1,0:T(8,128)(2,1)} %broadcast_in_dim.38), calls=%async_computation | async-start | bytes 2621440 | tf_op jit(solution)/shard_map/all_to_all | solution.py:32
  13.3 37.8 %collective-permute-start.2 = (bf16[512,256]{1,0:T(8,128)(2,1)S(1)}, bf16[512,256]{1,0:T(8,128)(2,1)S(1)}, u32[]{:S(2)}, u32[]{:S(2)}) collective-permute-start(bf16[512,256]{1,0:T(8,128)(2,1)S(1)} %copy-done), channel_id=1, source_target_pairs={{0,16},{16,32},{32,48},{48,0},{1,17},{17,33},{33,49},{49,1},{2,18}... | collective-permute-start | bytes 786440 | tf_op jit(solution)/shard_map/ppermute | solution.py:103
  17.8 33.3 %collective-permute-start.3 = (bf16[512,256]{1,0:T(8,128)(2,1)S(1)}, bf16[512,256]{1,0:T(8,128)(2,1)S(1)}, u32[]{:S(2)}, u32[]{:S(2)}) collective-permute-start(bf16[512,256]{1,0:T(8,128)(2,1)S(1)} %copy-done), channel_id=1, source_target_pairs={{0,32},{16,48},{32,0},{48,16},{1,33},{17,49},{33,1},{49,17},{2,34}... | collective-permute-start | bytes 786440 | tf_op jit(solution)/shard_map/ppermute | solution.py:103
  23.7 27.4 %collective-permute-start.4 = (bf16[512,256]{1,0:T(8,128)(2,1)S(1)}, bf16[512,256]{1,0:T(8,128)(2,1)S(1)}, u32[]{:S(2)}, u32[]{:S(2)}) collective-permute-start(bf16[512,256]{1,0:T(8,128)(2,1)S(1)} %copy-done), channel_id=1, source_target_pairs={{0,48},{16,0},{32,16},{48,32},{1,49},{17,1},{33,17},{49,33},{2,50}... | collective-permute-start | bytes 786440 | tf_op jit(solution)/shard_map/ppermute | solution.py:103
  29.0 3.2 %collective-permute-start = (bf16[80,512]{1,0:T(8,128)(2,1)S(1)}, bf16[80,512]{1,0:T(8,128)(2,1)S(1)}, u32[]{:S(2)}, u32[]{:S(2)}) collective-permute-start(bf16[80,512]{1,0:T(8,128)(2,1)S(1)} %pad_maximum_fusion.6), channel_id=1, source_target_pairs={{0,1},{1,0},{2,3},{3,2},{4,5},{5,4},{6,7},{7,6},{8,9},{9,8},{10,11... | collective-permute-start | bytes 245768 | tf_op jit(solution)/shard_map/ppermute | solution.py:28
  32.3 18.8 %collective-permute-start.1 = (bf16[80,1024]{1,0:T(8,128)(2,1)S(1)}, bf16[80,1024]{1,0:T(8,128)(2,1)S(1)}, u32[]{:S(2)}, u32[]{:S(2)}) collective-permute-start(bf16[80,1024]{1,0:T(8,128)(2,1)S(1)} %pad_maximum_fusion.3), channel_id=1, source_target_pairs={{0,0},{2,14},{4,12},{6,10},{8,8},{10,6},{12,4},{14,2},{64,66},{66,... | collective-permute-start | bytes 491528 | tf_op jit(solution)/shard_map/ppermute | solution.py:120
  51.1 1.3 copy-start.2
  52.4 4.6 %collective-permute-start.5 = (bf16[8,64,1024]{2,1,0:T(8,128)(2,1)S(1)}, bf16[8,64,1024]{2,1,0:T(8,128)(2,1)S(1)}, u32[]{:S(2)}, u32[]{:S(2)}) collective-permute-start(bf16[8,64,1024]{2,1,0:T(8,128)(2,1)S(1)} %shard_map.104), channel_id=1, source_target_pairs={{0,1},{1,0},{2,3},{3,2},{4,5},{5,4},{6,7},{7,6},{8,9},{9,8},{10,11... | collective-permute-start | bytes 3145736 | tf_op jit(solution)/shard_map/ppermute | solution.py:28
  59.1 26.0 %copy-start.3 = (bf16[80,1024]{1,0:T(8,128)(2,1)S(1)}, bf16[80,1024]{1,0:T(8,128)(2,1)}, u32[]{:S(2)}) copy-start(bf16[80,1024]{1,0:T(8,128)(2,1)} %copy-done.2) | copy-start | bytes 491524
  59.1 23.3 %all-to-all-start.1 = ((bf16[8,64,1024]{2,1,0:T(8,128)(2,1)}), bf16[8,64,1024]{2,1,0:T(8,128)(2,1)S(1)}, u32[]{:S(2)}, u32[]{:S(2)}) async-start(bf16[8,64,1024]{2,1,0:T(8,128)(2,1)} %shard_map.105), calls=%async_computation.1 | async-start | bytes 2097152 | tf_op jit(solution)/shard_map/all_to_all | solution.py:32
  63.8 64.3 %collective-permute-start.12 = (bf16[8192,256]{1,0:T(8,128)(2,1)}, bf16[8192,256]{1,0:T(8,128)(2,1)}, u32[]{:S(2)}, u32[]{:S(2)}) collective-permute-start(bf16[8192,256]{1,0:T(8,128)(2,1)} %param.13), channel_id=1, source_target_pairs={{0,1},{1,0},{2,3},{3,2},{4,5},{5,4},{6,7},{7,6},{8,9},{9,8},{10,11... | collective-permute-start | bytes 12582920 | tf_op jit(solution)/shard_map/ppermute | solution.py:28
  65.7 21.7 %collective-permute-start.7 = (bf16[128,768]{1,0:T(8,128)(2,1)S(1)}, bf16[128,768]{1,0:T(8,128)(2,1)S(1)}, u32[]{:S(2)}, u32[]{:S(2)}) collective-permute-start(bf16[128,768]{1,0:T(8,128)(2,1)S(1)} %bitcast.103), channel_id=1, source_target_pairs={{0,16},{16,32},{32,48},{48,0},{1,17},{17,33},{33,49},{49,1},{2,18}... | collective-permute-start | bytes 589832 | tf_op jit(solution)/shard_map/ppermute | solution.py:103
  68.4 19.1 %collective-permute-start.8 = (bf16[128,768]{1,0:T(8,128)(2,1)S(1)}, bf16[128,768]{1,0:T(8,128)(2,1)S(1)}, u32[]{:S(2)}, u32[]{:S(2)}) collective-permute-start(bf16[128,768]{1,0:T(8,128)(2,1)S(1)} %bitcast.104), channel_id=1, source_target_pairs={{0,48},{16,0},{32,16},{48,32},{1,49},{17,1},{33,17},{49,33},{2,50}... | collective-permute-start | bytes 589832 | tf_op jit(solution)/shard_map/ppermute | solution.py:103
  83.2 12.6 %collective-permute-start.6 = (bf16[4,64,256]{2,1,0:T(8,128)(2,1)S(1)}, bf16[4,64,256]{2,1,0:T(8,128)(2,1)S(1)}, u32[]{:S(2)}, u32[]{:S(2)}) collective-permute-start(bf16[4,64,256]{2,1,0:T(8,128)(2,1)S(1)} %gather_fusion), channel_id=1, source_target_pairs={{0,0},{2,66},{4,132},{6,198},{8,264},{10,330},{12,396},{14,462},{6... | collective-permute-start | bytes 393224 | tf_op jit(solution)/shard_map/ppermute | solution.py:149
  97.6 23.5 %all-to-all-start.2 = ((bf16[8,64,1152]{2,1,0:T(8,128)(2,1)}), bf16[8,64,1152]{2,1,0:T(8,128)(2,1)S(1)}, u32[]{:S(2)}, u32[]{:S(2)}) async-start(bf16[8,64,1152]{2,1,0:T(8,128)(2,1)} %broadcast_in_dim.43), calls=%async_computation.2 | async-start | bytes 2359296 | tf_op jit(solution)/shard_map/all_to_all | solution.py:32
  102.2 8.2 %collective-permute-start.10 = (bf16[64,768]{1,0:T(8,128)(2,1)S(1)}, bf16[64,768]{1,0:T(8,128)(2,1)S(1)}, u32[]{:S(2)}, u32[]{:S(2)}) collective-permute-start(bf16[64,768]{1,0:T(8,128)(2,1)S(1)} %slice.125), channel_id=1, source_target_pairs={{0,48},{16,0},{32,16},{48,32},{1,49},{17,1},{33,17},{49,33},{2,50}... | collective-permute-start | bytes 294920 | tf_op jit(solution)/shard_map/ppermute | solution.py:103
  107.6 12.4 %collective-permute-start.9 = (bf16[64,768]{1,0:T(8,128)(2,1)S(1)}, bf16[64,768]{1,0:T(8,128)(2,1)S(1)}, u32[]{:S(2)}, u32[]{:S(2)}) collective-permute-start(bf16[64,768]{1,0:T(8,128)(2,1)S(1)} %slice.124), channel_id=1, source_target_pairs={{0,16},{16,32},{32,48},{48,0},{1,17},{17,33},{33,49},{49,1},{2,18}... | collective-permute-start | bytes 294920 | tf_op jit(solution)/shard_map/ppermute | solution.py:103
  122.4 5.7 %collective-permute-start.11 = (bf16[80,512]{1,0:T(8,128)(2,1)S(1)}, bf16[80,512]{1,0:T(8,128)(2,1)S(1)}, u32[]{:S(2)}, u32[]{:S(2)}) collective-permute-start(bf16[80,512]{1,0:T(8,128)(2,1)S(1)} %pad_maximum_fusion.8), channel_id=1, source_target_pairs={{0,1},{1,0},{2,3},{3,2},{4,5},{5,4},{6,7},{7,6},{8,9},{9,8},{10,11... | collective-permute-start | bytes 245768 | tf_op jit(solution)/shard_map/ppermute | solution.py:28
  131.2 3.3 %collective-permute-start.13 = (bf16[64,384]{1,0:T(8,128)(2,1)S(1)}, bf16[64,384]{1,0:T(8,128)(2,1)S(1)}, u32[]{:S(2)}, u32[]{:S(2)}) collective-permute-start(bf16[64,384]{1,0:T(8,128)(2,1)S(1)} %pad_maximum_fusion.9), channel_id=1, source_target_pairs={{0,1},{1,0},{2,3},{3,2},{4,5},{5,4},{6,7},{7,6},{8,9},{9,8},{10,11... | collective-permute-start | bytes 147464 | tf_op jit(solution)/shard_map/ppermute | solution.py:28
  135.7 12.0 %all-to-all-start.3 = ((bf16[16,16,768]{2,1,0:T(8,128)(2,1)}), bf16[16,16,768]{2,1,0:T(8,128)(2,1)S(1)}, u32[]{:S(2)}, u32[]{:S(2)}) async-start(bf16[16,16,768]{2,1,0:T(8,128)(2,1)} %broadcast_in_dim.47), calls=%async_computation.3 | async-start | bytes 786432 | tf_op jit(solution)/shard_map/all_to_all | solution.py:32

commit v14 on v12

--- a/solution.py
+++ b/solution.py
@@ -149,6 +149,7 @@
     summed = jnp.sum(exchange(pair, CHIPS).astype(F32), axis=0).astype(BF)
     summed = jnp.stack([summed[:, s * cols : (s + 1) * cols] for s in range(n_yh)])
     projected = lax.ppermute(summed[turned], ("z", "yl", "x"), homes)
+    projected, *parts = lax.optimization_barrier((projected, *parts))
 
     hidden = residual_part + jnp.concatenate([projected[j] for j in range(n_yh)], axis=1).astype(F32)
     squares = jnp.sum(hidden * hidden, axis=1, keepdims=True)
@@ -161,8 +162,7 @@
     inv_column = lax.rsqrt((totals[:, :1] + totals[:, 1:2]) / width + EPSILON)
     inv_row = jnp.broadcast_to(inv_column, (mine, 128)).T[:1]
 
-    _, later = lax.optimization_barrier((message, turned))
-    adapters_all = jnp.stack(parts)[later].reshape(tenants * rank, block + out_block)
+    adapters_all = jnp.stack(parts)[turned].reshape(tenants * rank, block + out_block)
     downs, ups = adapters_all[:, :block], adapters_all[:, block:]
 
     def select(values, mask):

time: 201 us -> 184 us (0.915)
  waiting for transfers between devices: 63.7 us -> 51.6 us
  blocking collectives: 39 us -> 35.5 us
    ppermute x1, waiting for transfers between devices: 9.71 us -> 0.01 us  [shards(): projected = lax.ppermute(summed[turned], ('z', 'yl', 'x'), homes)]
    ppermute x6, waiting for transfers between devices: 16.9 us -> 11.2 us  [around(): lax.ppermute(value, 'yh', [(i, (i + s) % n_yh) for i in range(n_yh)])]
    all_to_all x1, blocking collectives: 39 us -> 35.5 us  [exchange(): return lax.all_to_all(value, axis, 0, 0)]
    all_to_all x4, waiting for transfers between devices: 18.7 us -> 21.9 us  [exchange(): return lax.all_to_all(value, axis, 0, 0)]
  transfers between devices with their start and end apart: 17 -> 17, of which waited for: 8 -> 9; matrix products, arithmetic and copies ran while one was open for 5% -> 6% of each run, Pallas kernels for 0% -> 0%
where the time goes in v14:
time: 184 us; the launch traced here: 183 us
  starting transfers between devices  69.8 us (38%)
  waiting for transfers between devices  51.6 us (28%)
  blocking collectives  35.5 us (19%)
  matrix products  9.36 us (5%)
  local copies, waits for them, and re-layouts  8.72 us (5%)
  Pallas kernels  3.48 us (2%)
  other arithmetic  3.04 us (2%)
    all_to_all x1, blocking collectives, exchange(): return lax.all_to_all(value, axis, 0, 0)  35.5 us
    ppermute x6, starting transfers between devices, around(): lax.ppermute(value, 'yh', [(i, (i + s) % n_yh) for i in range(n_yh)])  28.4 us
    all_to_all x4, starting transfers between devices, exchange(): return lax.all_to_all(value, axis, 0, 0)  26 us
    all_to_all x4, waiting for transfers between devices, exchange(): return lax.all_to_all(value, axis, 0, 0)  21.9 us
    ppermute x1, waiting for transfers between devices, shards(): chip_rows = lax.ppermute(chip_rows, ('z', 'yl', 'x'), chips)  15.2 us
    ppermute x6, waiting for transfers between devices, around(): lax.ppermute(value, 'yh', [(i, (i + s) % n_yh) for i in range(n_yh)])  11.2 us
    ppermute x5, starting transfers between devices, swap(): return lax.ppermute(value, 'c', [(0, 1), (1, 0)])  10.1 us
    dot_general x13, matrix products, dot(): return jnp.einsum(subscripts, left, right, preferred_element_type=F32)  9.36 us
  transfers between devices with their start and end apart: 17, of which 9 were waited for; matrix products, arithmetic and copies ran while one was open for 6% of the time, Pallas kernels for 0%

profile of v14, /device:TPU:6, one launch (start us, length us, event | category | flops | bytes accessed | tf_op | source)
XLA Modules:
  0.0 182.8 jit_solution(15940018260215132052)
XLA Ops:
  0.6 1.0 fusion.18
  1.6 1.2 broadcast_in_dim.35
  2.8 10.5 %all-to-all-start = ((bf16[8,160,512]{2,1,0:T(8,128)(2,1)}), bf16[8,160,512]{2,1,0:T(8,128)(2,1)S(1)}, u32[]{:S(2)}, u32[]{:S(2)}) async-start(bf16[8,160,512]{2,1,0:T(8,128)(2,1)} %broadcast_in_dim.35), calls=%async_computation | async-start | bytes 2621440 | tf_op jit(solution)/shard_map/all_to_all | solution.py:32
  13.3 4.5 %collective-permute-start.2 = (bf16[512,256]{1,0:T(8,128)(2,1)S(1)}, bf16[512,256]{1,0:T(8,128)(2,1)S(1)}, u32[]{:S(2)}, u32[]{:S(2)}) collective-permute-start(bf16[512,256]{1,0:T(8,128)(2,1)S(1)} %copy-done), channel_id=1, source_target_pairs={{0,16},{16,32},{32,48},{48,0},{1,17},{17,33},{33,49},{49,1},{2,18}... | collective-permute-start | bytes 786440 | tf_op jit(solution)/shard_map/ppermute | solution.py:104
  17.8 5.9 %collective-permute-start.3 = (bf16[512,256]{1,0:T(8,128)(2,1)S(1)}, bf16[512,256]{1,0:T(8,128)(2,1)S(1)}, u32[]{:S(2)}, u32[]{:S(2)}) collective-permute-start(bf16[512,256]{1,0:T(8,128)(2,1)S(1)} %copy-done), channel_id=1, source_target_pairs={{0,32},{16,48},{32,0},{48,16},{1,33},{17,49},{33,1},{49,17},{2,34}... | collective-permute-start | bytes 786440 | tf_op jit(solution)/shard_map/ppermute | solution.py:104
  23.7 5.3 %collective-permute-start.4 = (bf16[512,256]{1,0:T(8,128)(2,1)S(1)}, bf16[512,256]{1,0:T(8,128)(2,1)S(1)}, u32[]{:S(2)}, u32[]{:S(2)}) collective-permute-start(bf16[512,256]{1,0:T(8,128)(2,1)S(1)} %copy-done), channel_id=1, source_target_pairs={{0,48},{16,0},{32,16},{48,32},{1,49},{17,1},{33,17},{49,33},{2,50}... | collective-permute-start | bytes 786440 | tf_op jit(solution)/shard_map/ppermute | solution.py:104
  29.0 1.9 %collective-permute-start = (bf16[80,512]{1,0:T(8,128)(2,1)S(1)}, bf16[80,512]{1,0:T(8,128)(2,1)S(1)}, u32[]{:S(2)}, u32[]{:S(2)}) collective-permute-start(bf16[80,512]{1,0:T(8,128)(2,1)S(1)} %pad_maximum_fusion.6), channel_id=1, source_target_pairs={{0,1},{1,0},{2,3},{3,2},{4,5},{5,4},{6,7},{7,6},{8,9},{9,8},{10,11... | collective-permute-start | bytes 245768 | tf_op jit(solution)/shard_map/ppermute | solution.py:28
  31.4 0.8 collective-permute-done
  32.3 3.4 %collective-permute-start.1 = (bf16[80,1024]{1,0:T(8,128)(2,1)S(1)}, bf16[80,1024]{1,0:T(8,128)(2,1)S(1)}, u32[]{:S(2)}, u32[]{:S(2)}) collective-permute-start(bf16[80,1024]{1,0:T(8,128)(2,1)S(1)} %pad_maximum_fusion.3), channel_id=1, source_target_pairs={{0,0},{2,14},{4,12},{6,10},{8,8},{10,6},{12,4},{14,2},{64,66},{66,... | collective-permute-start | bytes 491528 | tf_op jit(solution)/shard_map/ppermute | solution.py:122
  35.9 15.2 %collective-permute-done.1 = bf16[80,1024]{1,0:T(8,128)(2,1)S(1)} collective-permute-done((bf16[80,1024]{1,0:T(8,128)(2,1)S(1)}, bf16[80,1024]{1,0:T(8,128)(2,1)S(1)}, u32[]{:S(2)}, u32[]{:S(2)}) %collective-permute-start.1) | collective-permute-done | bytes 163872 | tf_op jit(solution)/shard_map/ppermute | solution.py:122
  51.1 1.3 shard_map.104
  52.3 1.9 %collective-permute-start.5 = (bf16[8,64,1024]{2,1,0:T(8,128)(2,1)S(1)}, bf16[8,64,1024]{2,1,0:T(8,128)(2,1)S(1)}, u32[]{:S(2)}, u32[]{:S(2)}) collective-permute-start(bf16[8,64,1024]{2,1,0:T(8,128)(2,1)S(1)} %shard_map.104), channel_id=1, source_target_pairs={{0,1},{1,0},{2,3},{3,2},{4,5},{5,4},{6,7},{7,6},{8,9},{9,8},{10,11... | collective-permute-start | bytes 3145736 | tf_op jit(solution)/shard_map/ppermute | solution.py:28
  54.4 2.5 %collective-permute-done.5.refs_4_ = bf16[8,64,1024]{2,1,0:T(8,128)(2,1)S(1)} collective-permute-done((bf16[8,64,1024]{2,1,0:T(8,128)(2,1)S(1)}, bf16[8,64,1024]{2,1,0:T(8,128)(2,1)S(1)}, u32[]{:S(2)}, u32[]{:S(2)}) %collective-permute-start.5) | collective-permute-done | bytes 1048608 | tf_op jit(solution)/shard_map/ppermute | solution.py:28
  56.9 2.2 %shard_map.105 = bf16[8,64,1024]{2,1,0:T(8,128)(2,1)} custom-call(s32[2]{0:T(128)S(1)} %pad_add_fusion.place, bf16[8,160,512]{2,1,0:T(8,128)(2,1)S(1)} %all-to-all-done.joined, bf16[512,256]{1,0:T(8,128)(2,1)S(1)} %copy-done, bf16[512,256]{1,0:T(8,128)(2,1)S(1)} %collective-permute-done.2.refs_1_, bf16[512,256]{1,0:T(8,128)(2,1)S(1)} %collective-permute-done.3.refs_2_, ...), custom_call_target="tpu_custom_call" | custom-call | flops 536870912 | bytes 4194304 | tf_op jit(solution)/shard_map/pallas_call | solution.py:71
  59.1 4.5 %all-to-all-start.1 = ((bf16[8,64,1024]{2,1,0:T(8,128)(2,1)}), bf16[8,64,1024]{2,1,0:T(8,128)(2,1)S(1)}, u32[]{:S(2)}, u32[]{:S(2)}) async-start(bf16[8,64,1024]{2,1,0:T(8,128)(2,1)} %shard_map.105), calls=%async_computation.1 | async-start | bytes 2097152 | tf_op jit(solution)/shard_map/all_to_all | solution.py:32
  63.6 1.9 %collective-permute-start.11 = (bf16[8192,256]{1,0:T(8,128)(2,1)}, bf16[8192,256]{1,0:T(8,128)(2,1)}, u32[]{:S(2)}, u32[]{:S(2)}) collective-permute-start(bf16[8192,256]{1,0:T(8,128)(2,1)} %param.13), channel_id=1, source_target_pairs={{0,1},{1,0},{2,3},{3,2},{4,5},{5,4},{6,7},{7,6},{8,9},{9,8},{10,11... | collective-permute-start | bytes 12582920 | tf_op jit(solution)/shard_map/ppermute | solution.py:28
  65.6 2.6 %collective-permute-start.7 = (bf16[128,768]{1,0:T(8,128)(2,1)S(1)}, bf16[128,768]{1,0:T(8,128)(2,1)S(1)}, u32[]{:S(2)}, u32[]{:S(2)}) collective-permute-start(bf16[128,768]{1,0:T(8,128)(2,1)S(1)} %bitcast.102), channel_id=1, source_target_pairs={{0,16},{16,32},{32,48},{48,0},{1,17},{17,33},{33,49},{49,1},{2,18}... | collective-permute-start | bytes 589832 | tf_op jit(solution)/shard_map/ppermute | solution.py:104
  68.2 6.9 %collective-permute-start.8 = (bf16[128,768]{1,0:T(8,128)(2,1)S(1)}, bf16[128,768]{1,0:T(8,128)(2,1)S(1)}, u32[]{:S(2)}, u32[]{:S(2)}) collective-permute-start(bf16[128,768]{1,0:T(8,128)(2,1)S(1)} %bitcast.103), channel_id=1, source_target_pairs={{0,32},{16,48},{32,0},{48,16},{1,33},{17,49},{33,1},{49,17},{2,34}... | collective-permute-start | bytes 589832 | tf_op jit(solution)/shard_map/ppermute | solution.py:104
  75.1 3.1 %collective-permute-start.9 = (bf16[128,768]{1,0:T(8,128)(2,1)S(1)}, bf16[128,768]{1,0:T(8,128)(2,1)S(1)}, u32[]{:S(2)}, u32[]{:S(2)}) collective-permute-start(bf16[128,768]{1,0:T(8,128)(2,1)S(1)} %bitcast.104), channel_id=1, source_target_pairs={{0,48},{16,0},{32,16},{48,32},{1,49},{17,1},{33,17},{49,33},{2,50}... | collective-permute-start | bytes 589832 | tf_op jit(solution)/shard_map/ppermute | solution.py:104
  78.3 2.2 %all-to-all-done.1 = bf16[8,64,1024]{2,1,0:T(8,128)(2,1)S(1)} async-done(((bf16[8,64,1024]{2,1,0:T(8,128)(2,1)}), bf16[8,64,1024]{2,1,0:T(8,128)(2,1)S(1)}, u32[]{:S(2)}, u32[]{:S(2)}) %all-to-all-start.1) | async-done | bytes 1048608 | tf_op jit(solution)/shard_map/all_to_all | solution.py:32
  80.5 0.2 reduce_sum.105
  80.8 0.6 gather_fusion
  81.3 1.9 %collective-permute-start.6 = (bf16[4,64,256]{2,1,0:T(8,128)(2,1)S(1)}, bf16[4,64,256]{2,1,0:T(8,128)(2,1)S(1)}, u32[]{:S(2)}, u32[]{:S(2)}) collective-permute-start(bf16[4,64,256]{2,1,0:T(8,128)(2,1)S(1)} %gather_fusion), channel_id=1, source_target_pairs={{0,0},{2,66},{4,132},{6,198},{8,264},{10,330},{12,396},{14,462},{6... | collective-permute-start | bytes 393224 | tf_op jit(solution)/shard_map/ppermute | solution.py:151
  83.3 7.4 %collective-permute-done.7 = bf16[128,768]{1,0:T(8,128)(2,1)S(1)} collective-permute-done((bf16[128,768]{1,0:T(8,128)(2,1)S(1)}, bf16[128,768]{1,0:T(8,128)(2,1)S(1)}, u32[]{:S(2)}, u32[]{:S(2)}) %collective-permute-start.7) | collective-permute-done | bytes 196640 | tf_op jit(solution)/shard_map/ppermute | solution.py:104
  90.6 2.7 %collective-permute-done.8 = bf16[128,768]{1,0:T(8,128)(2,1)S(1)} collective-permute-done((bf16[128,768]{1,0:T(8,128)(2,1)S(1)}, bf16[128,768]{1,0:T(8,128)(2,1)S(1)}, u32[]{:S(2)}, u32[]{:S(2)}) %collective-permute-start.8) | collective-permute-done | bytes 196640 | tf_op jit(solution)/shard_map/ppermute | solution.py:104
  93.3 1.1 collective-permute-done.9
  94.5 0.2 multiply_reduce_fusion
  94.6 0.1 copy.39
  94.7 0.1 copy.40
  95.0 1.2 broadcast_in_dim.40
  96.1 5.6 %all-to-all-start.2 = ((bf16[8,64,1152]{2,1,0:T(8,128)(2,1)}), bf16[8,64,1152]{2,1,0:T(8,128)(2,1)S(1)}, u32[]{:S(2)}, u32[]{:S(2)}) async-start(bf16[8,64,1152]{2,1,0:T(8,128)(2,1)} %broadcast_in_dim.40), calls=%async_computation.2 | async-start | bytes 2359296 | tf_op jit(solution)/shard_map/all_to_all | solution.py:32
  102.0 0.6 gather_fusion.1
  102.6 0.3 convolution_select_fusion
  103.0 12.6 %all-to-all-done.2 = bf16[8,64,1152]{2,1,0:T(8,128)(2,1)S(1)} async-done(((bf16[8,64,1152]{2,1,0:T(8,128)(2,1)}), bf16[8,64,1152]{2,1,0:T(8,128)(2,1)S(1)}, u32[]{:S(2)}, u32[]{:S(2)}) %all-to-all-start.2) | async-done | bytes 1179680 | tf_op jit(solution)/shard_map/all_to_all | solution.py:32
  115.8 0.2 slice.156
  116.0 0.6 gather_fusion.2
  116.9 1.9 %collective-permute-start.10 = (bf16[80,512]{1,0:T(8,128)(2,1)S(1)}, bf16[80,512]{1,0:T(8,128)(2,1)S(1)}, u32[]{:S(2)}, u32[]{:S(2)}) collective-permute-start(bf16[80,512]{1,0:T(8,128)(2,1)S(1)} %pad_maximum_fusion.8), channel_id=1, source_target_pairs={{0,1},{1,0},{2,3},{3,2},{4,5},{5,4},{6,7},{7,6},{8,9},{9,8},{10,11... | collective-permute-start | bytes 245768 | tf_op jit(solution)/shard_map/ppermute | solution.py:28
  118.8 0.3 convolution_select_fusion.2
  119.1 3.0 %fusion.3 = f32[64,256]{1,0:T(8,128)S(1)} fusion(bf16[8,64,1024]{2,1,0:T(8,128)(2,1)S(1)} %gather_fusion.2, bf16[8,1024,256]{2,1,0:T(8,128)(2,1)} %bitcast.95, f32[64]{0:T(128)S(1)} %bitcast.116), kind=kOutput, calls=%fused_computation.16 | convolution fusion | flops 268451840 | bytes 5308672 | tf_op jit(solution)/shard_map/ktd,kdn->tn/dot_general | solution.py:24
  122.1 0.1 copy.46
  122.3 0.1 copy.41
  122.6 3.0 %fusion.7 = bf16[64,256]{1,0:T(8,128)(2,1)S(1)} fusion(bf16[8,64,1024]{2,1,0:T(8,128)(2,1)S(1)} %gather_fusion.2, bf16[8,1024,256]{2,1,0:T(8,128)(2,1)} %bitcast.32, s32[]{:T(128)S(6)} %select_n.259, bf16[63,512]{1,0:T(8,128)(2,1)S(1)} %slice.163, bf16[1,512]{1,0:T(2,128)(2,1)S(1)} %slice.164, f32[64]{0:T(128)S(1)} %get-tuple-element.29, f32[64]{0:T(128)S(1)} %bitcast.117), kind=kOutput, calls=%fused_computation.22 | convolution fusion | flops 268566528 | bytes 5341700 | tf_op jit(solution)/shard_map/ktd,kdn->tn/dot_general | solution.py:24
  125.6 2.4 %collective-permute-start.12 = (bf16[64,384]{1,0:T(8,128)(2,1)S(1)}, bf16[64,384]{1,0:T(8,128)(2,1)S(1)}, u32[]{:S(2)}, u32[]{:S(2)}) collective-permute-start(bf16[64,384]{1,0:T(8,128)(2,1)S(1)} %pad_maximum_fusion.9), channel_id=1, source_target_pairs={{0,1},{1,0},{2,3},{3,2},{4,5},{5,4},{6,7},{7,6},{8,9},{9,8},{10,11... | collective-permute-start | bytes 147464 | tf_op jit(solution)/shard_map/ppermute | solution.py:28
  128.1 0.3 convolution_select_fusion.1
  128.3 0.1 copy.44
  128.5 0.2 convolution_select_fusion.4
  128.8 0.1 copy.45
  128.9 0.2 convolution_select_fusion.3
  129.1 0.1 copy.48
  129.4 0.8 broadcast_in_dim.43
  130.2 5.4 %all-to-all-start.3 = ((bf16[16,16,768]{2,1,0:T(8,128)(2,1)}), bf16[16,16,768]{2,1,0:T(8,128)(2,1)S(1)}, u32[]{:S(2)}, u32[]{:S(2)}) async-start(bf16[16,16,768]{2,1,0:T(8,128)(2,1)} %broadcast_in_dim.43), calls=%async_computation.3 | async-start | bytes 786432 | tf_op jit(solution)/shard_map/all_to_all | solution.py:32
  135.6 0.2 add_reduce_fusion
  135.8 7.1 %all-to-all-done.3 = bf16[16,16,768]{2,1,0:T(8,128)(2,1)S(1)} async-done(((bf16[16,16,768]{2,1,0:T(8,128)(2,1)}), bf16[16,16,768]{2,1,0:T(8,128)(2,1)S(1)}, u32[]{:S(2)}, u32[]{:S(2)}) %all-to-all-start.3) | async-done | bytes 393248 | tf_op jit(solution)/shard_map/all_to_all | solution.py:32
  143.1 0.1 fusion.13
  143.6 0.1 fusion.14
  143.8 0.5 fusion.42
  144.3 0.5 fusion.1
  144.8 0.3 fusion.28
  145.2 0.4 fusion
  145.7 0.3 copy.53
  146.0 35.5 %all_to_all.25 = bf16[32,16,768]{2,1,0:T(8,128)(2,1)S(1)} all-to-all(bf16[32,16,768]{2,1,0:T(8,128)(2,1)S(1)} %bitcast.96), channel_id=1, replica_groups=mesh['z'=8,'yh'=4,'yl'=2,'x'=4,'c'=2] {'yh','z'}, dimensions={0} | all-to-all | bytes 1572864 | tf_op jit(solution)/shard_map/all_to_all | solution.py:32
  181.5 0.1 convert_reduce_fusion
  181.6 0.6 slice_bitcast_fusion
  182.2 0.6 slice_bitcast_fusion.9
  (84 shorter events, 2.8 us)
Async XLA Ops:
  2.8 10.5 %copy-start = (bf16[512,256]{1,0:T(8,128)(2,1)S(1)}, bf16[512,256]{1,0:T(8,128)(2,1)}, u32[]{:S(2)}) copy-start(bf16[512,256]{1,0:T(8,128)(2,1)} %refs_0_.3) | copy-start | bytes 786436
  2.8 26.2 %copy-start.1 = (bf16[128,512]{1,0:T(8,128)(2,1)S(1)}, bf16[128,512]{1,0:T(8,128)(2,1)}, u32[]{:S(2)}) copy-start(bf16[128,512]{1,0:T(8,128)(2,1)} %param.11) | copy-start | bytes 393220
  2.8 26.2 %copy-start.3 = (bf16[512]{0:T(512)(128)(2,1)S(1)}, bf16[512]{0:T(512)(128)(2,1)}, u32[]{:S(2)}) copy-start(bf16[512]{0:T(512)(128)(2,1)} %param.12) | copy-start | bytes 3076
  2.8 28.2 %copy-start.4 = (s32[32]{0:T(128)S(1)}, s32[32]{0:T(128)}, u32[]{:S(2)}) copy-start(s32[32]{0:T(128)} %param.17) | copy-start | bytes 388
  2.8 28.2 %copy-start.2 = (s32[128]{0:T(128)S(1)}, s32[128]{0:T(128)}, u32[]{:S(2)}) copy-start(s32[128]{0:T(128)} %param.16) | copy-start | bytes 1540
  2.8 48.3 %all-to-all-start = ((bf16[8,160,512]{2,1,0:T(8,128)(2,1)}), bf16[8,160,512]{2,1,0:T(8,128)(2,1)S(1)}, u32[]{:S(2)}, u32[]{:S(2)}) async-start(bf16[8,160,512]{2,1,0:T(8,128)(2,1)} %broadcast_in_dim.35), calls=%async_computation | async-start | bytes 2621440 | tf_op jit(solution)/shard_map/all_to_all | solution.py:32
  13.3 37.8 %collective-permute-start.2 = (bf16[512,256]{1,0:T(8,128)(2,1)S(1)}, bf16[512,256]{1,0:T(8,128)(2,1)S(1)}, u32[]{:S(2)}, u32[]{:S(2)}) collective-permute-start(bf16[512,256]{1,0:T(8,128)(2,1)S(1)} %copy-done), channel_id=1, source_target_pairs={{0,16},{16,32},{32,48},{48,0},{1,17},{17,33},{33,49},{49,1},{2,18}... | collective-permute-start | bytes 786440 | tf_op jit(solution)/shard_map/ppermute | solution.py:104
  17.8 33.3 %collective-permute-start.3 = (bf16[512,256]{1,0:T(8,128)(2,1)S(1)}, bf16[512,256]{1,0:T(8,128)(2,1)S(1)}, u32[]{:S(2)}, u32[]{:S(2)}) collective-permute-start(bf16[512,256]{1,0:T(8,128)(2,1)S(1)} %copy-done), channel_id=1, source_target_pairs={{0,32},{16,48},{32,0},{48,16},{1,33},{17,49},{33,1},{49,17},{2,34}... | collective-permute-start | bytes 786440 | tf_op jit(solution)/shard_map/ppermute | solution.py:104
  23.7 27.4 %collective-permute-start.4 = (bf16[512,256]{1,0:T(8,128)(2,1)S(1)}, bf16[512,256]{1,0:T(8,128)(2,1)S(1)}, u32[]{:S(2)}, u32[]{:S(2)}) collective-permute-start(bf16[512,256]{1,0:T(8,128)(2,1)S(1)} %copy-done), channel_id=1, source_target_pairs={{0,48},{16,0},{32,16},{48,32},{1,49},{17,1},{33,17},{49,33},{2,50}... | collective-permute-start | bytes 786440 | tf_op jit(solution)/shard_map/ppermute | solution.py:104
  29.0 3.2 %collective-permute-start = (bf16[80,512]{1,0:T(8,128)(2,1)S(1)}, bf16[80,512]{1,0:T(8,128)(2,1)S(1)}, u32[]{:S(2)}, u32[]{:S(2)}) collective-permute-start(bf16[80,512]{1,0:T(8,128)(2,1)S(1)} %pad_maximum_fusion.6), channel_id=1, source_target_pairs={{0,1},{1,0},{2,3},{3,2},{4,5},{5,4},{6,7},{7,6},{8,9},{9,8},{10,11... | collective-permute-start | bytes 245768 | tf_op jit(solution)/shard_map/ppermute | solution.py:28
  32.3 18.8 %collective-permute-start.1 = (bf16[80,1024]{1,0:T(8,128)(2,1)S(1)}, bf16[80,1024]{1,0:T(8,128)(2,1)S(1)}, u32[]{:S(2)}, u32[]{:S(2)}) collective-permute-start(bf16[80,1024]{1,0:T(8,128)(2,1)S(1)} %pad_maximum_fusion.3), channel_id=1, source_target_pairs={{0,0},{2,14},{4,12},{6,10},{8,8},{10,6},{12,4},{14,2},{64,66},{66,... | collective-permute-start | bytes 491528 | tf_op jit(solution)/shard_map/ppermute | solution.py:122
  52.3 4.6 %collective-permute-start.5 = (bf16[8,64,1024]{2,1,0:T(8,128)(2,1)S(1)}, bf16[8,64,1024]{2,1,0:T(8,128)(2,1)S(1)}, u32[]{:S(2)}, u32[]{:S(2)}) collective-permute-start(bf16[8,64,1024]{2,1,0:T(8,128)(2,1)S(1)} %shard_map.104), channel_id=1, source_target_pairs={{0,1},{1,0},{2,3},{3,2},{4,5},{5,4},{6,7},{7,6},{8,9},{9,8},{10,11... | collective-permute-start | bytes 3145736 | tf_op jit(solution)/shard_map/ppermute | solution.py:28
  59.1 21.4 %all-to-all-start.1 = ((bf16[8,64,1024]{2,1,0:T(8,128)(2,1)}), bf16[8,64,1024]{2,1,0:T(8,128)(2,1)S(1)}, u32[]{:S(2)}, u32[]{:S(2)}) async-start(bf16[8,64,1024]{2,1,0:T(8,128)(2,1)} %shard_map.105), calls=%async_computation.1 | async-start | bytes 2097152 | tf_op jit(solution)/shard_map/all_to_all | solution.py:32
  63.6 58.9 %collective-permute-start.11 = (bf16[8192,256]{1,0:T(8,128)(2,1)}, bf16[8192,256]{1,0:T(8,128)(2,1)}, u32[]{:S(2)}, u32[]{:S(2)}) collective-permute-start(bf16[8192,256]{1,0:T(8,128)(2,1)} %param.13), channel_id=1, source_target_pairs={{0,1},{1,0},{2,3},{3,2},{4,5},{5,4},{6,7},{7,6},{8,9},{9,8},{10,11... | collective-permute-start | bytes 12582920 | tf_op jit(solution)/shard_map/ppermute | solution.py:28
  65.6 25.0 %collective-permute-start.7 = (bf16[128,768]{1,0:T(8,128)(2,1)S(1)}, bf16[128,768]{1,0:T(8,128)(2,1)S(1)}, u32[]{:S(2)}, u32[]{:S(2)}) collective-permute-start(bf16[128,768]{1,0:T(8,128)(2,1)S(1)} %bitcast.102), channel_id=1, source_target_pairs={{0,16},{16,32},{32,48},{48,0},{1,17},{17,33},{33,49},{49,1},{2,18}... | collective-permute-start | bytes 589832 | tf_op jit(solution)/shard_map/ppermute | solution.py:104
  68.2 25.1 %collective-permute-start.8 = (bf16[128,768]{1,0:T(8,128)(2,1)S(1)}, bf16[128,768]{1,0:T(8,128)(2,1)S(1)}, u32[]{:S(2)}, u32[]{:S(2)}) collective-permute-start(bf16[128,768]{1,0:T(8,128)(2,1)S(1)} %bitcast.103), channel_id=1, source_target_pairs={{0,32},{16,48},{32,0},{48,16},{1,33},{17,49},{33,1},{49,17},{2,34}... | collective-permute-start | bytes 589832 | tf_op jit(solution)/shard_map/ppermute | solution.py:104
  75.1 19.3 %collective-permute-start.9 = (bf16[128,768]{1,0:T(8,128)(2,1)S(1)}, bf16[128,768]{1,0:T(8,128)(2,1)S(1)}, u32[]{:S(2)}, u32[]{:S(2)}) collective-permute-start(bf16[128,768]{1,0:T(8,128)(2,1)S(1)} %bitcast.104), channel_id=1, source_target_pairs={{0,48},{16,0},{32,16},{48,32},{1,49},{17,1},{33,17},{49,33},{2,50}... | collective-permute-start | bytes 589832 | tf_op jit(solution)/shard_map/ppermute | solution.py:104
  81.3 13.1 %collective-permute-start.6 = (bf16[4,64,256]{2,1,0:T(8,128)(2,1)S(1)}, bf16[4,64,256]{2,1,0:T(8,128)(2,1)S(1)}, u32[]{:S(2)}, u32[]{:S(2)}) collective-permute-start(bf16[4,64,256]{2,1,0:T(8,128)(2,1)S(1)} %gather_fusion), channel_id=1, source_target_pairs={{0,0},{2,66},{4,132},{6,198},{8,264},{10,330},{12,396},{14,462},{6... | collective-permute-start | bytes 393224 | tf_op jit(solution)/shard_map/ppermute | solution.py:151
  96.1 19.5 %all-to-all-start.2 = ((bf16[8,64,1152]{2,1,0:T(8,128)(2,1)}), bf16[8,64,1152]{2,1,0:T(8,128)(2,1)S(1)}, u32[]{:S(2)}, u32[]{:S(2)}) async-start(bf16[8,64,1152]{2,1,0:T(8,128)(2,1)} %broadcast_in_dim.40), calls=%async_computation.2 | async-start | bytes 2359296 | tf_op jit(solution)/shard_map/all_to_all | solution.py:32
  116.9 5.7 %collective-permute-start.10 = (bf16[80,512]{1,0:T(8,128)(2,1)S(1)}, bf16[80,512]{1,0:T(8,128)(2,1)S(1)}, u32[]{:S(2)}, u32[]{:S(2)}) collective-permute-start(bf16[80,512]{1,0:T(8,128)(2,1)S(1)} %pad_maximum_fusion.8), channel_id=1, source_target_pairs={{0,1},{1,0},{2,3},{3,2},{4,5},{5,4},{6,7},{7,6},{8,9},{9,8},{10,11... | collective-permute-start | bytes 245768 | tf_op jit(solution)/shard_map/ppermute | solution.py:28
  125.6 3.3 %collective-permute-start.12 = (bf16[64,384]{1,0:T(8,128)(2,1)S(1)}, bf16[64,384]{1,0:T(8,128)(2,1)S(1)}, u32[]{:S(2)}, u32[]{:S(2)}) collective-permute-start(bf16[64,384]{1,0:T(8,128)(2,1)S(1)} %pad_maximum_fusion.9), channel_id=1, source_target_pairs={{0,1},{1,0},{2,3},{3,2},{4,5},{5,4},{6,7},{7,6},{8,9},{9,8},{10,11... | collective-permute-start | bytes 147464 | tf_op jit(solution)/shard_map/ppermute | solution.py:28
  130.2 12.7 %all-to-all-start.3 = ((bf16[16,16,768]{2,1,0:T(8,128)(2,1)}), bf16[16,16,768]{2,1,0:T(8,128)(2,1)S(1)}, u32[]{:S(2)}, u32[]{:S(2)}) async-start(bf16[16,16,768]{2,1,0:T(8,128)(2,1)} %broadcast_in_dim.43), calls=%async_computation.3 | async-start | bytes 786432 | tf_op jit(solution)/shard_map/all_to_all | solution.py:32

commit v15 on v14

--- a/solution.py
+++ b/solution.py
@@ -107,7 +107,7 @@
     def ordered(own, others):
         return jnp.where(first, own, others), jnp.where(first, others, own)
 
-    upper = jnp.concatenate([up.T, jnp.zeros((rank, block - out_block), BF)], axis=1)
+    upper = jnp.concatenate([up.T[: rank // 2], up.T[rank // 2 :]], axis=1)
     joined = gather(jnp.concatenate([attention, down.T, upper], axis=0), "z", n_z)
     pieces = around(output_projection)
     draft_weight_other = swap(draft_weight)
@@ -140,9 +140,9 @@
     z = lax.axis_index("z")
     sent = swap(product(mine, other, z, joined, pieces))
     pair = product(mine, core, z, joined, pieces, sent)
-    adapters = jnp.concatenate(
-        [joined[:, tokens : tokens + rank], joined[:, tokens + rank :, :out_block]], axis=2
-    ).reshape(n_z * rank, block + out_block)
+    uppers = joined[:, tokens + rank :]
+    uppers = jnp.concatenate([uppers[:, :, :out_block], uppers[:, :, out_block:]], axis=1)
+    adapters = jnp.concatenate([joined[:, tokens : tokens + rank], uppers], axis=2).reshape(n_z * rank, block + out_block)
     pair, adapters = lax.optimization_barrier((pair, adapters))
     parts = around(adapters)
 

time: 184 us -> 184 us (level)
  no operation moved by 1% of the time
where the time goes in v15:
time: 184 us
  starting transfers between devices  69.7 us (38%)
  waiting for transfers between devices  51.7 us (28%)
  blocking collectives  35.6 us (19%)
  local copies, waits for them, and re-layouts  9.37 us (5%)
  matrix products  9.36 us (5%)
  Pallas kernels  3.47 us (2%)
  other arithmetic  3.02 us (2%)
    all_to_all x1, blocking collectives, exchange(): return lax.all_to_all(value, axis, 0, 0)  35.6 us
    ppermute x6, starting transfers between devices, around(): lax.ppermute(value, 'yh', [(i, (i + s) % n_yh) for i in range(n_yh)])  28.3 us
    all_to_all x4, starting transfers between devices, exchange(): return lax.all_to_all(value, axis, 0, 0)  26 us
    all_to_all x4, waiting for transfers between devices, exchange(): return lax.all_to_all(value, axis, 0, 0)  22 us
    ppermute x1, waiting for transfers between devices, shards(): chip_rows = lax.ppermute(chip_rows, ('z', 'yl', 'x'), chips)  15.2 us
    ppermute x6, waiting for transfers between devices, around(): lax.ppermute(value, 'yh', [(i, (i + s) % n_yh) for i in range(n_yh)])  11.2 us
    ppermute x5, starting transfers between devices, swap(): return lax.ppermute(value, 'c', [(0, 1), (1, 0)])  10.1 us
    dot_general x13, matrix products, dot(): return jnp.einsum(subscripts, left, right, preferred_element_type=F32)  9.36 us
  transfers between devices with their start and end apart: 17, of which 9 were waited for; matrix products, arithmetic and copies ran while one was open for 6% of the time, Pallas kernels for 0%

profile of v15, /device:TPU:6, one launch (start us, length us, event | category | flops | bytes accessed | tf_op | source)
XLA Modules:
  0.0 183.5 jit_solution(12318816029915188171)
XLA Ops:
  0.6 0.7 fusion.89
  1.3 0.9 maximum_maximum_fusion.1
  2.3 1.1 broadcast_in_dim.36
  3.4 10.5 %all-to-all-start = ((bf16[8,152,512]{2,1,0:T(8,128)(2,1)}), bf16[8,152,512]{2,1,0:T(8,128)(2,1)S(1)}, u32[]{:S(2)}, u32[]{:S(2)}) async-start(bf16[8,152,512]{2,1,0:T(8,128)(2,1)} %broadcast_in_dim.36), calls=%async_computation | async-start | bytes 2490368 | tf_op jit(solution)/shard_map/all_to_all | solution.py:32
  13.9 4.5 %collective-permute-start.2 = (bf16[512,256]{1,0:T(8,128)(2,1)S(1)}, bf16[512,256]{1,0:T(8,128)(2,1)S(1)}, u32[]{:S(2)}, u32[]{:S(2)}) collective-permute-start(bf16[512,256]{1,0:T(8,128)(2,1)S(1)} %copy-done), channel_id=1, source_target_pairs={{0,16},{16,32},{32,48},{48,0},{1,17},{17,33},{33,49},{49,1},{2,18}... | collective-permute-start | bytes 786440 | tf_op jit(solution)/shard_map/ppermute | solution.py:104
  18.4 5.9 %collective-permute-start.3 = (bf16[512,256]{1,0:T(8,128)(2,1)S(1)}, bf16[512,256]{1,0:T(8,128)(2,1)S(1)}, u32[]{:S(2)}, u32[]{:S(2)}) collective-permute-start(bf16[512,256]{1,0:T(8,128)(2,1)S(1)} %copy-done), channel_id=1, source_target_pairs={{0,32},{16,48},{32,0},{48,16},{1,33},{17,49},{33,1},{49,17},{2,34}... | collective-permute-start | bytes 786440 | tf_op jit(solution)/shard_map/ppermute | solution.py:104
  24.3 5.3 %collective-permute-start.4 = (bf16[512,256]{1,0:T(8,128)(2,1)S(1)}, bf16[512,256]{1,0:T(8,128)(2,1)S(1)}, u32[]{:S(2)}, u32[]{:S(2)}) collective-permute-start(bf16[512,256]{1,0:T(8,128)(2,1)S(1)} %copy-done), channel_id=1, source_target_pairs={{0,48},{16,0},{32,16},{48,32},{1,49},{17,1},{33,17},{49,33},{2,50}... | collective-permute-start | bytes 786440 | tf_op jit(solution)/shard_map/ppermute | solution.py:104
  29.7 1.9 %collective-permute-start = (bf16[80,512]{1,0:T(8,128)(2,1)S(1)}, bf16[80,512]{1,0:T(8,128)(2,1)S(1)}, u32[]{:S(2)}, u32[]{:S(2)}) collective-permute-start(bf16[80,512]{1,0:T(8,128)(2,1)S(1)} %pad_maximum_fusion.5), channel_id=1, source_target_pairs={{0,1},{1,0},{2,3},{3,2},{4,5},{5,4},{6,7},{7,6},{8,9},{9,8},{10,11... | collective-permute-start | bytes 245768 | tf_op jit(solution)/shard_map/ppermute | solution.py:28
  32.0 0.8 collective-permute-done
  32.9 3.4 %collective-permute-start.1 = (bf16[80,1024]{1,0:T(8,128)(2,1)S(1)}, bf16[80,1024]{1,0:T(8,128)(2,1)S(1)}, u32[]{:S(2)}, u32[]{:S(2)}) collective-permute-start(bf16[80,1024]{1,0:T(8,128)(2,1)S(1)} %pad_maximum_fusion.2), channel_id=1, source_target_pairs={{0,0},{2,14},{4,12},{6,10},{8,8},{10,6},{12,4},{14,2},{64,66},{66,... | collective-permute-start | bytes 491528 | tf_op jit(solution)/shard_map/ppermute | solution.py:122
  36.5 15.2 %collective-permute-done.1 = bf16[80,1024]{1,0:T(8,128)(2,1)S(1)} collective-permute-done((bf16[80,1024]{1,0:T(8,128)(2,1)S(1)}, bf16[80,1024]{1,0:T(8,128)(2,1)S(1)}, u32[]{:S(2)}, u32[]{:S(2)}) %collective-permute-start.1) | collective-permute-done | bytes 163872 | tf_op jit(solution)/shard_map/ppermute | solution.py:122
  51.7 1.3 shard_map.104
  53.0 1.9 %collective-permute-start.5 = (bf16[8,64,1024]{2,1,0:T(8,128)(2,1)S(1)}, bf16[8,64,1024]{2,1,0:T(8,128)(2,1)S(1)}, u32[]{:S(2)}, u32[]{:S(2)}) collective-permute-start(bf16[8,64,1024]{2,1,0:T(8,128)(2,1)S(1)} %shard_map.104), channel_id=1, source_target_pairs={{0,1},{1,0},{2,3},{3,2},{4,5},{5,4},{6,7},{7,6},{8,9},{9,8},{10,11... | collective-permute-start | bytes 3145736 | tf_op jit(solution)/shard_map/ppermute | solution.py:28
  55.0 2.5 %collective-permute-done.5.refs_4_ = bf16[8,64,1024]{2,1,0:T(8,128)(2,1)S(1)} collective-permute-done((bf16[8,64,1024]{2,1,0:T(8,128)(2,1)S(1)}, bf16[8,64,1024]{2,1,0:T(8,128)(2,1)S(1)}, u32[]{:S(2)}, u32[]{:S(2)}) %collective-permute-start.5) | collective-permute-done | bytes 1048608 | tf_op jit(solution)/shard_map/ppermute | solution.py:28
  57.5 2.2 %shard_map.105 = bf16[8,64,1024]{2,1,0:T(8,128)(2,1)} custom-call(s32[2]{0:T(128)S(1)} %pad_add_fusion.place, bf16[8,152,512]{2,1,0:T(8,128)(2,1)S(1)} %all-to-all-done.joined, bf16[512,256]{1,0:T(8,128)(2,1)S(1)} %copy-done, bf16[512,256]{1,0:T(8,128)(2,1)S(1)} %collective-permute-done.2.refs_1_, bf16[512,256]{1,0:T(8,128)(2,1)S(1)} %collective-permute-done.3.refs_2_, ...), custom_call_target="tpu_custom_call" | custom-call | flops 536870912 | bytes 4194304 | tf_op jit(solution)/shard_map/pallas_call | solution.py:71
  59.8 4.5 %all-to-all-start.1 = ((bf16[8,64,1024]{2,1,0:T(8,128)(2,1)}), bf16[8,64,1024]{2,1,0:T(8,128)(2,1)S(1)}, u32[]{:S(2)}, u32[]{:S(2)}) async-start(bf16[8,64,1024]{2,1,0:T(8,128)(2,1)} %shard_map.105), calls=%async_computation.1 | async-start | bytes 2097152 | tf_op jit(solution)/shard_map/all_to_all | solution.py:32
  64.3 1.9 %collective-permute-start.11 = (bf16[8192,256]{1,0:T(8,128)(2,1)}, bf16[8192,256]{1,0:T(8,128)(2,1)}, u32[]{:S(2)}, u32[]{:S(2)}) collective-permute-start(bf16[8192,256]{1,0:T(8,128)(2,1)} %param.13), channel_id=1, source_target_pairs={{0,1},{1,0},{2,3},{3,2},{4,5},{5,4},{6,7},{7,6},{8,9},{9,8},{10,11... | collective-permute-start | bytes 12582920 | tf_op jit(solution)/shard_map/ppermute | solution.py:28
  66.2 2.6 %collective-permute-start.7 = (bf16[128,768]{1,0:T(8,128)(2,1)S(1)}, bf16[128,768]{1,0:T(8,128)(2,1)S(1)}, u32[]{:S(2)}, u32[]{:S(2)}) collective-permute-start(bf16[128,768]{1,0:T(8,128)(2,1)S(1)} %bitcast.102), channel_id=1, source_target_pairs={{0,16},{16,32},{32,48},{48,0},{1,17},{17,33},{33,49},{49,1},{2,18}... | collective-permute-start | bytes 589832 | tf_op jit(solution)/shard_map/ppermute | solution.py:104
  68.9 6.9 %collective-permute-start.8 = (bf16[128,768]{1,0:T(8,128)(2,1)S(1)}, bf16[128,768]{1,0:T(8,128)(2,1)S(1)}, u32[]{:S(2)}, u32[]{:S(2)}) collective-permute-start(bf16[128,768]{1,0:T(8,128)(2,1)S(1)} %bitcast.103), channel_id=1, source_target_pairs={{0,32},{16,48},{32,0},{48,16},{1,33},{17,49},{33,1},{49,17},{2,34}... | collective-permute-start | bytes 589832 | tf_op jit(solution)/shard_map/ppermute | solution.py:104
  75.8 3.1 %collective-permute-start.9 = (bf16[128,768]{1,0:T(8,128)(2,1)S(1)}, bf16[128,768]{1,0:T(8,128)(2,1)S(1)}, u32[]{:S(2)}, u32[]{:S(2)}) collective-permute-start(bf16[128,768]{1,0:T(8,128)(2,1)S(1)} %bitcast.104), channel_id=1, source_target_pairs={{0,48},{16,0},{32,16},{48,32},{1,49},{17,1},{33,17},{49,33},{2,50}... | collective-permute-start | bytes 589832 | tf_op jit(solution)/shard_map/ppermute | solution.py:104
  78.9 2.3 %all-to-all-done.1 = bf16[8,64,1024]{2,1,0:T(8,128)(2,1)S(1)} async-done(((bf16[8,64,1024]{2,1,0:T(8,128)(2,1)}), bf16[8,64,1024]{2,1,0:T(8,128)(2,1)S(1)}, u32[]{:S(2)}, u32[]{:S(2)}) %all-to-all-start.1) | async-done | bytes 1048608 | tf_op jit(solution)/shard_map/all_to_all | solution.py:32
  81.2 0.2 reduce_sum.105
  81.4 0.6 gather_fusion
  81.9 1.9 %collective-permute-start.6 = (bf16[4,64,256]{2,1,0:T(8,128)(2,1)S(1)}, bf16[4,64,256]{2,1,0:T(8,128)(2,1)S(1)}, u32[]{:S(2)}, u32[]{:S(2)}) collective-permute-start(bf16[4,64,256]{2,1,0:T(8,128)(2,1)S(1)} %gather_fusion), channel_id=1, source_target_pairs={{0,0},{2,66},{4,132},{6,198},{8,264},{10,330},{12,396},{14,462},{6... | collective-permute-start | bytes 393224 | tf_op jit(solution)/shard_map/ppermute | solution.py:151
  83.9 7.4 %collective-permute-done.7 = bf16[128,768]{1,0:T(8,128)(2,1)S(1)} collective-permute-done((bf16[128,768]{1,0:T(8,128)(2,1)S(1)}, bf16[128,768]{1,0:T(8,128)(2,1)S(1)}, u32[]{:S(2)}, u32[]{:S(2)}) %collective-permute-start.7) | collective-permute-done | bytes 196640 | tf_op jit(solution)/shard_map/ppermute | solution.py:104
  91.3 2.6 %collective-permute-done.8 = bf16[128,768]{1,0:T(8,128)(2,1)S(1)} collective-permute-done((bf16[128,768]{1,0:T(8,128)(2,1)S(1)}, bf16[128,768]{1,0:T(8,128)(2,1)S(1)}, u32[]{:S(2)}, u32[]{:S(2)}) %collective-permute-start.8) | collective-permute-done | bytes 196640 | tf_op jit(solution)/shard_map/ppermute | solution.py:104
  93.8 1.2 collective-permute-done.9
  95.1 0.2 multiply_reduce_fusion
  95.2 0.1 copy.39
  95.4 0.1 copy.40
  95.6 1.2 broadcast_in_dim.40
  96.8 5.6 %all-to-all-start.2 = ((bf16[8,64,1152]{2,1,0:T(8,128)(2,1)}), bf16[8,64,1152]{2,1,0:T(8,128)(2,1)S(1)}, u32[]{:S(2)}, u32[]{:S(2)}) async-start(bf16[8,64,1152]{2,1,0:T(8,128)(2,1)} %broadcast_in_dim.40), calls=%async_computation.2 | async-start | bytes 2359296 | tf_op jit(solution)/shard_map/all_to_all | solution.py:32
  102.6 0.6 gather_fusion.1
  103.2 0.3 convolution_select_fusion
  103.6 12.6 %all-to-all-done.2 = bf16[8,64,1152]{2,1,0:T(8,128)(2,1)S(1)} async-done(((bf16[8,64,1152]{2,1,0:T(8,128)(2,1)}), bf16[8,64,1152]{2,1,0:T(8,128)(2,1)S(1)}, u32[]{:S(2)}, u32[]{:S(2)}) %all-to-all-start.2) | async-done | bytes 1179680 | tf_op jit(solution)/shard_map/all_to_all | solution.py:32
  116.5 0.2 slice.173
  116.6 0.6 gather_fusion.2
  117.5 1.9 %collective-permute-start.10 = (bf16[80,512]{1,0:T(8,128)(2,1)S(1)}, bf16[80,512]{1,0:T(8,128)(2,1)S(1)}, u32[]{:S(2)}, u32[]{:S(2)}) collective-permute-start(bf16[80,512]{1,0:T(8,128)(2,1)S(1)} %pad_maximum_fusion.7), channel_id=1, source_target_pairs={{0,1},{1,0},{2,3},{3,2},{4,5},{5,4},{6,7},{7,6},{8,9},{9,8},{10,11... | collective-permute-start | bytes 245768 | tf_op jit(solution)/shard_map/ppermute | solution.py:28
  119.4 0.3 convolution_select_fusion.2
  119.7 3.0 %fusion.3 = f32[64,256]{1,0:T(8,128)S(1)} fusion(bf16[8,64,1024]{2,1,0:T(8,128)(2,1)S(1)} %gather_fusion.2, bf16[8,1024,256]{2,1,0:T(8,128)(2,1)} %bitcast.95, f32[64]{0:T(128)S(1)} %bitcast.116), kind=kOutput, calls=%fused_computation.16 | convolution fusion | flops 268451840 | bytes 5308672 | tf_op jit(solution)/shard_map/ktd,kdn->tn/dot_general | solution.py:24
  123.0 0.1 copy.41
  123.2 3.0 %fusion.7 = bf16[64,256]{1,0:T(8,128)(2,1)S(1)} fusion(bf16[8,64,1024]{2,1,0:T(8,128)(2,1)S(1)} %gather_fusion.2, bf16[8,1024,256]{2,1,0:T(8,128)(2,1)} %bitcast.32, s32[]{:T(128)S(6)} %select_n.259, bf16[63,512]{1,0:T(8,128)(2,1)S(1)} %slice.180, bf16[1,512]{1,0:T(2,128)(2,1)S(1)} %slice.181, f32[64]{0:T(128)S(1)} %get-tuple-element.29, f32[64]{0:T(128)S(1)} %bitcast.117), kind=kOutput, calls=%fused_computation.22 | convolution fusion | flops 268566528 | bytes 5341700 | tf_op jit(solution)/shard_map/ktd,kdn->tn/dot_general | solution.py:24
  126.3 2.4 %collective-permute-start.12 = (bf16[64,384]{1,0:T(8,128)(2,1)S(1)}, bf16[64,384]{1,0:T(8,128)(2,1)S(1)}, u32[]{:S(2)}, u32[]{:S(2)}) collective-permute-start(bf16[64,384]{1,0:T(8,128)(2,1)S(1)} %pad_maximum_fusion.8), channel_id=1, source_target_pairs={{0,1},{1,0},{2,3},{3,2},{4,5},{5,4},{6,7},{7,6},{8,9},{9,8},{10,11... | collective-permute-start | bytes 147464 | tf_op jit(solution)/shard_map/ppermute | solution.py:28
  128.7 0.3 convolution_select_fusion.1
  129.0 0.1 copy.44
  129.2 0.2 convolution_select_fusion.4
  129.4 0.1 copy.45
  129.6 0.2 convolution_select_fusion.3
  129.8 0.1 copy.48
  130.1 0.8 broadcast_in_dim.44
  130.8 5.4 %all-to-all-start.3 = ((bf16[16,16,768]{2,1,0:T(8,128)(2,1)}), bf16[16,16,768]{2,1,0:T(8,128)(2,1)S(1)}, u32[]{:S(2)}, u32[]{:S(2)}) async-start(bf16[16,16,768]{2,1,0:T(8,128)(2,1)} %broadcast_in_dim.44), calls=%async_computation.3 | async-start | bytes 786432 | tf_op jit(solution)/shard_map/all_to_all | solution.py:32
  136.2 0.2 add_reduce_fusion
  136.4 7.1 %all-to-all-done.3 = bf16[16,16,768]{2,1,0:T(8,128)(2,1)S(1)} async-done(((bf16[16,16,768]{2,1,0:T(8,128)(2,1)}), bf16[16,16,768]{2,1,0:T(8,128)(2,1)S(1)}, u32[]{:S(2)}, u32[]{:S(2)}) %all-to-all-start.3) | async-done | bytes 393248 | tf_op jit(solution)/shard_map/all_to_all | solution.py:32
  143.8 0.1 fusion.13
  144.2 0.1 fusion.14
  144.5 0.5 fusion.40
  145.0 0.5 fusion.1
  145.5 0.3 fusion.26
  145.8 0.4 fusion
  146.3 0.3 copy.53
  146.6 35.6 %all_to_all.25 = bf16[32,16,768]{2,1,0:T(8,128)(2,1)S(1)} all-to-all(bf16[32,16,768]{2,1,0:T(8,128)(2,1)S(1)} %bitcast.96), channel_id=1, replica_groups=mesh['z'=8,'yh'=4,'yl'=2,'x'=4,'c'=2] {'yh','z'}, dimensions={0} | all-to-all | bytes 1572864 | tf_op jit(solution)/shard_map/all_to_all | solution.py:32
  182.2 0.1 convert_reduce_fusion
  182.3 0.6 slice_bitcast_fusion
  182.9 0.6 slice_bitcast_fusion.9
  (85 shorter events, 3.0 us)
Async XLA Ops:
  3.4 10.5 %copy-start = (bf16[512,256]{1,0:T(8,128)(2,1)S(1)}, bf16[512,256]{1,0:T(8,128)(2,1)}, u32[]{:S(2)}) copy-start(bf16[512,256]{1,0:T(8,128)(2,1)} %refs_0_.3) | copy-start | bytes 786436
  3.4 26.2 %copy-start.1 = (bf16[128,512]{1,0:T(8,128)(2,1)S(1)}, bf16[128,512]{1,0:T(8,128)(2,1)}, u32[]{:S(2)}) copy-start(bf16[128,512]{1,0:T(8,128)(2,1)} %param.11) | copy-start | bytes 393220
  3.4 26.2 %copy-start.3 = (bf16[512]{0:T(512)(128)(2,1)S(1)}, bf16[512]{0:T(512)(128)(2,1)}, u32[]{:S(2)}) copy-start(bf16[512]{0:T(512)(128)(2,1)} %param.12) | copy-start | bytes 3076
  3.4 28.2 %copy-start.4 = (s32[32]{0:T(128)S(1)}, s32[32]{0:T(128)}, u32[]{:S(2)}) copy-start(s32[32]{0:T(128)} %param.17) | copy-start | bytes 388
  3.4 28.2 %copy-start.2 = (s32[128]{0:T(128)S(1)}, s32[128]{0:T(128)}, u32[]{:S(2)}) copy-start(s32[128]{0:T(128)} %param.16) | copy-start | bytes 1540
  3.4 48.3 %all-to-all-start = ((bf16[8,152,512]{2,1,0:T(8,128)(2,1)}), bf16[8,152,512]{2,1,0:T(8,128)(2,1)S(1)}, u32[]{:S(2)}, u32[]{:S(2)}) async-start(bf16[8,152,512]{2,1,0:T(8,128)(2,1)} %broadcast_in_dim.36), calls=%async_computation | async-start | bytes 2490368 | tf_op jit(solution)/shard_map/all_to_all | solution.py:32
  13.9 37.8 %collective-permute-start.2 = (bf16[512,256]{1,0:T(8,128)(2,1)S(1)}, bf16[512,256]{1,0:T(8,128)(2,1)S(1)}, u32[]{:S(2)}, u32[]{:S(2)}) collective-permute-start(bf16[512,256]{1,0:T(8,128)(2,1)S(1)} %copy-done), channel_id=1, source_target_pairs={{0,16},{16,32},{32,48},{48,0},{1,17},{17,33},{33,49},{49,1},{2,18}... | collective-permute-start | bytes 786440 | tf_op jit(solution)/shard_map/ppermute | solution.py:104
  18.4 33.3 %collective-permute-start.3 = (bf16[512,256]{1,0:T(8,128)(2,1)S(1)}, bf16[512,256]{1,0:T(8,128)(2,1)S(1)}, u32[]{:S(2)}, u32[]{:S(2)}) collective-permute-start(bf16[512,256]{1,0:T(8,128)(2,1)S(1)} %copy-done), channel_id=1, source_target_pairs={{0,32},{16,48},{32,0},{48,16},{1,33},{17,49},{33,1},{49,17},{2,34}... | collective-permute-start | bytes 786440 | tf_op jit(solution)/shard_map/ppermute | solution.py:104
  24.3 27.4 %collective-permute-start.4 = (bf16[512,256]{1,0:T(8,128)(2,1)S(1)}, bf16[512,256]{1,0:T(8,128)(2,1)S(1)}, u32[]{:S(2)}, u32[]{:S(2)}) collective-permute-start(bf16[512,256]{1,0:T(8,128)(2,1)S(1)} %copy-done), channel_id=1, source_target_pairs={{0,48},{16,0},{32,16},{48,32},{1,49},{17,1},{33,17},{49,33},{2,50}... | collective-permute-start | bytes 786440 | tf_op jit(solution)/shard_map/ppermute | solution.py:104
  29.7 3.2 %collective-permute-start = (bf16[80,512]{1,0:T(8,128)(2,1)S(1)}, bf16[80,512]{1,0:T(8,128)(2,1)S(1)}, u32[]{:S(2)}, u32[]{:S(2)}) collective-permute-start(bf16[80,512]{1,0:T(8,128)(2,1)S(1)} %pad_maximum_fusion.5), channel_id=1, source_target_pairs={{0,1},{1,0},{2,3},{3,2},{4,5},{5,4},{6,7},{7,6},{8,9},{9,8},{10,11... | collective-permute-start | bytes 245768 | tf_op jit(solution)/shard_map/ppermute | solution.py:28
  32.9 18.8 %collective-permute-start.1 = (bf16[80,1024]{1,0:T(8,128)(2,1)S(1)}, bf16[80,1024]{1,0:T(8,128)(2,1)S(1)}, u32[]{:S(2)}, u32[]{:S(2)}) collective-permute-start(bf16[80,1024]{1,0:T(8,128)(2,1)S(1)} %pad_maximum_fusion.2), channel_id=1, source_target_pairs={{0,0},{2,14},{4,12},{6,10},{8,8},{10,6},{12,4},{14,2},{64,66},{66,... | collective-permute-start | bytes 491528 | tf_op jit(solution)/shard_map/ppermute | solution.py:122
  53.0 4.6 %collective-permute-start.5 = (bf16[8,64,1024]{2,1,0:T(8,128)(2,1)S(1)}, bf16[8,64,1024]{2,1,0:T(8,128)(2,1)S(1)}, u32[]{:S(2)}, u32[]{:S(2)}) collective-permute-start(bf16[8,64,1024]{2,1,0:T(8,128)(2,1)S(1)} %shard_map.104), channel_id=1, source_target_pairs={{0,1},{1,0},{2,3},{3,2},{4,5},{5,4},{6,7},{7,6},{8,9},{9,8},{10,11... | collective-permute-start | bytes 3145736 | tf_op jit(solution)/shard_map/ppermute | solution.py:28
  59.8 21.4 %all-to-all-start.1 = ((bf16[8,64,1024]{2,1,0:T(8,128)(2,1)}), bf16[8,64,1024]{2,1,0:T(8,128)(2,1)S(1)}, u32[]{:S(2)}, u32[]{:S(2)}) async-start(bf16[8,64,1024]{2,1,0:T(8,128)(2,1)} %shard_map.105), calls=%async_computation.1 | async-start | bytes 2097152 | tf_op jit(solution)/shard_map/all_to_all | solution.py:32
  64.3 58.9 %collective-permute-start.11 = (bf16[8192,256]{1,0:T(8,128)(2,1)}, bf16[8192,256]{1,0:T(8,128)(2,1)}, u32[]{:S(2)}, u32[]{:S(2)}) collective-permute-start(bf16[8192,256]{1,0:T(8,128)(2,1)} %param.13), channel_id=1, source_target_pairs={{0,1},{1,0},{2,3},{3,2},{4,5},{5,4},{6,7},{7,6},{8,9},{9,8},{10,11... | collective-permute-start | bytes 12582920 | tf_op jit(solution)/shard_map/ppermute | solution.py:28
  66.2 25.1 %collective-permute-start.7 = (bf16[128,768]{1,0:T(8,128)(2,1)S(1)}, bf16[128,768]{1,0:T(8,128)(2,1)S(1)}, u32[]{:S(2)}, u32[]{:S(2)}) collective-permute-start(bf16[128,768]{1,0:T(8,128)(2,1)S(1)} %bitcast.102), channel_id=1, source_target_pairs={{0,16},{16,32},{32,48},{48,0},{1,17},{17,33},{33,49},{49,1},{2,18}... | collective-permute-start | bytes 589832 | tf_op jit(solution)/shard_map/ppermute | solution.py:104
  68.9 25.0 %collective-permute-start.8 = (bf16[128,768]{1,0:T(8,128)(2,1)S(1)}, bf16[128,768]{1,0:T(8,128)(2,1)S(1)}, u32[]{:S(2)}, u32[]{:S(2)}) collective-permute-start(bf16[128,768]{1,0:T(8,128)(2,1)S(1)} %bitcast.103), channel_id=1, source_target_pairs={{0,32},{16,48},{32,0},{48,16},{1,33},{17,49},{33,1},{49,17},{2,34}... | collective-permute-start | bytes 589832 | tf_op jit(solution)/shard_map/ppermute | solution.py:104
  75.8 19.3 %collective-permute-start.9 = (bf16[128,768]{1,0:T(8,128)(2,1)S(1)}, bf16[128,768]{1,0:T(8,128)(2,1)S(1)}, u32[]{:S(2)}, u32[]{:S(2)}) collective-permute-start(bf16[128,768]{1,0:T(8,128)(2,1)S(1)} %bitcast.104), channel_id=1, source_target_pairs={{0,48},{16,0},{32,16},{48,32},{1,49},{17,1},{33,17},{49,33},{2,50}... | collective-permute-start | bytes 589832 | tf_op jit(solution)/shard_map/ppermute | solution.py:104
  81.9 13.1 %collective-permute-start.6 = (bf16[4,64,256]{2,1,0:T(8,128)(2,1)S(1)}, bf16[4,64,256]{2,1,0:T(8,128)(2,1)S(1)}, u32[]{:S(2)}, u32[]{:S(2)}) collective-permute-start(bf16[4,64,256]{2,1,0:T(8,128)(2,1)S(1)} %gather_fusion), channel_id=1, source_target_pairs={{0,0},{2,66},{4,132},{6,198},{8,264},{10,330},{12,396},{14,462},{6... | collective-permute-start | bytes 393224 | tf_op jit(solution)/shard_map/ppermute | solution.py:151
  96.8 19.5 %all-to-all-start.2 = ((bf16[8,64,1152]{2,1,0:T(8,128)(2,1)}), bf16[8,64,1152]{2,1,0:T(8,128)(2,1)S(1)}, u32[]{:S(2)}, u32[]{:S(2)}) async-start(bf16[8,64,1152]{2,1,0:T(8,128)(2,1)} %broadcast_in_dim.40), calls=%async_computation.2 | async-start | bytes 2359296 | tf_op jit(solution)/shard_map/all_to_all | solution.py:32
  117.5 5.7 %collective-permute-start.10 = (bf16[80,512]{1,0:T(8,128)(2,1)S(1)}, bf16[80,512]{1,0:T(8,128)(2,1)S(1)}, u32[]{:S(2)}, u32[]{:S(2)}) collective-permute-start(bf16[80,512]{1,0:T(8,128)(2,1)S(1)} %pad_maximum_fusion.7), channel_id=1, source_target_pairs={{0,1},{1,0},{2,3},{3,2},{4,5},{5,4},{6,7},{7,6},{8,9},{9,8},{10,11... | collective-permute-start | bytes 245768 | tf_op jit(solution)/shard_map/ppermute | solution.py:28
  126.3 3.3 %collective-permute-start.12 = (bf16[64,384]{1,0:T(8,128)(2,1)S(1)}, bf16[64,384]{1,0:T(8,128)(2,1)S(1)}, u32[]{:S(2)}, u32[]{:S(2)}) collective-permute-start(bf16[64,384]{1,0:T(8,128)(2,1)S(1)} %pad_maximum_fusion.8), channel_id=1, source_target_pairs={{0,1},{1,0},{2,3},{3,2},{4,5},{5,4},{6,7},{7,6},{8,9},{9,8},{10,11... | collective-permute-start | bytes 147464 | tf_op jit(solution)/shard_map/ppermute | solution.py:28
  130.8 12.7 %all-to-all-start.3 = ((bf16[16,16,768]{2,1,0:T(8,128)(2,1)}), bf16[16,16,768]{2,1,0:T(8,128)(2,1)S(1)}, u32[]{:S(2)}, u32[]{:S(2)}) async-start(bf16[16,16,768]{2,1,0:T(8,128)(2,1)} %broadcast_in_dim.44), calls=%async_computation.3 | async-start | bytes 786432 | tf_op jit(solution)/shard_map/all_to_all | solution.py:32
